TPU v7x, 32 devices: a whole 2x2x4 slice. The times are simulated.
32 devices in a mesh: span: 4 (over z), wall: 4 (over y, core), stream: 2 (over x).
Axes of the slice: x: 2, y: 2, z: 4, core: 2. Of those that a mesh axis runs over, the one named last changes fastest.
Arguments:
- fields: float32 [4, 16, 64, 512], P(None, 'stream', 'wall', 'span'), may hold values from -67.5 to 67.5, as said below
Outputs:
- clark_model: float32 [3, 16, 64, 512], P(None, 'stream', 'wall', 'span')
- similar_model: float32 [3, 16, 64, 512], P(None, 'stream', 'wall', 'span')
- clark_corr: float32 [3, 64], P(None, 'wall')
- similar_corr: float32 [3, 64], P(None, 'wall')
Inputs may be any that keep to these rules, and one draw needn't show every extreme that they name: The fields are rough from cell to cell.
All inputs are finite; a program needn't handle non-finite values.
Results may differ from a plain program's by a relative error of at most 0.00024.
Values sent between devices are 32-bit elements; how exact they have to be, the bound alone decides.
No kernel may reach another device: no remote copies, remote signals or barrier semaphores. Data moves between devices by JAX's collectives and lax.ppermute only.
A program may use at most 64 MiB of HBM per device.

v0:
```python
import math

import jax
import jax.numpy as jnp
from jax import lax
from jax.sharding import PartitionSpec as P

raw_taps = [math.exp(-((k - 8) ** 2) / 18.0) for k in range(17)]
filter_taps = [value / sum(raw_taps) for value in raw_taps]
clark_coef = 9.0
small_eps = 1e-06


def with_halo(cells, sides, width, closed):
    for axis, dim in sides:
        count = lax.axis_size(axis)
        ends = count if closed else count - 1
        head = lax.slice_in_dim(cells, 0, width, axis=dim)
        tail = lax.slice_in_dim(cells, cells.shape[dim] - width, cells.shape[dim], axis=dim)
        cells = jnp.concatenate(
            [
                lax.ppermute(tail, axis, [(i, (i + 1) % count) for i in range(ends)]),
                cells,
                lax.ppermute(head, axis, [((i + 1) % count, i) for i in range(ends)]),
            ],
            axis=dim,
        )
    return cells


def band_matrix(length):
    offset = (
        jnp.arange(length + 16, dtype=jnp.int32)[:, None]
        - jnp.arange(length, dtype=jnp.int32)[None, :]
    )
    matrix = jnp.zeros((length + 16, length), jnp.float32)
    for k in range(17):
        matrix = matrix + jnp.where(offset == k, filter_taps[k], 0.0).astype(jnp.float32)
    return matrix


def smooth(padded, direction, length):
    matrix = band_matrix(length)
    if direction == 3:
        return jnp.einsum("fswz,zk->fswk", padded, matrix, precision=lax.Precision.HIGHEST)
    if direction == 2:
        return jnp.einsum("fswz,wk->fskz", padded, matrix, precision=lax.Precision.HIGHEST)
    return jnp.einsum("fswz,sk->fkwz", padded, matrix, precision=lax.Precision.HIGHEST)


def with_products(quad):
    return jnp.concatenate([quad, quad[:3] * quad[3:4]], axis=0)


def filter_all(quad):
    stream_len, wall_len, span_len = (quad.shape[1], quad.shape[2], quad.shape[3])
    payload = with_products(quad)
    spanned = with_halo(payload, (("span", 3),), 8, True)
    extended = with_halo(spanned, (("wall", 2), ("stream", 1)), 8, False)
    kept = extended[:4]
    result = smooth(extended, 3, span_len)
    result = smooth(result, 2, wall_len)
    return (smooth(result, 1, stream_len), kept)


def clark_flux(means):
    padded = with_halo(means, (("span", 3),), 1, True)
    along_span = (padded[..., 2:] - padded[..., :-2]) * 0.5
    plane = with_halo(means, (("wall", 2), ("stream", 1)), 1, False)
    along_wall = (plane[:, 1:-1, 2:, :] - plane[:, 1:-1, :-2, :]) * 0.5
    along_stream = (plane[:, 2:, 1:-1, :] - plane[:, :-2, 1:-1, :]) * 0.5
    total = along_span[:3] * along_span[3:4] + along_wall[:3] * along_wall[3:4]
    total = total + along_stream[:3] * along_stream[3:4]
    return clark_coef * total


def shards(fields):
    first, unused_rim = filter_all(fields)
    means = first[:4]
    exact = first[4:] - means[:3] * means[3:4]
    second, mean_rim = filter_all(means)
    similar = second[4:] - second[:3] * second[3:4]
    clark = clark_flux(means)
    sums = (
        jnp.sum(exact * clark, axis=(1, 3)),
        jnp.sum(exact * similar, axis=(1, 3)),
        jnp.sum(exact * exact, axis=(1, 3)),
        jnp.sum(clark * clark, axis=(1, 3)),
        jnp.sum(similar * similar, axis=(1, 3)),
    )
    cross_c, cross_s, power_e, power_c, power_s = lax.psum(
        (sums[0], sums[1], sums[2], sums[3], sums[4]), ("span", "stream")
    )
    plane_cells = float(
        fields.shape[1] * fields.shape[3] * lax.axis_size("stream") * lax.axis_size("span")
    )
    cross_c = cross_c / plane_cells
    cross_s = cross_s / plane_cells
    power_e = power_e / plane_cells
    power_c = power_c / plane_cells
    power_s = power_s / plane_cells
    clark_corr = cross_c / jnp.sqrt((power_e + small_eps) * (power_c + small_eps))
    similar_corr = cross_s / jnp.sqrt((power_e + small_eps) * (power_s + small_eps))
    clark_model = clark / jnp.sqrt(power_c + small_eps)[:, None, :, None]
    similar_model = similar / jnp.sqrt(power_s + small_eps)[:, None, :, None]
    return (clark_model, similar_model, clark_corr, similar_corr)


def solution(mesh):
    return jax.shard_map(
        shards,
        mesh=mesh,
        in_specs=(P(None, "stream", "wall", "span"),),
        out_specs=(
            P(None, "stream", "wall", "span"),
            P(None, "stream", "wall", "span"),
            P(None, "wall"),
            P(None, "wall"),
        ),
        check_vma=False,
    )
```

profile of v0, /device:TPU:4, one launch (start us, length us, event | category | flops | bytes accessed | tf_op | source)
XLA Modules:
  0.0 213.2 jit_solution(17370033378872534033)
XLA Ops:
  3.7 3.7 %collective-permute-start.1 = (f32[7,8,16,8]{3,2,1,0:T(8,128)S(1)}, f32[7,8,16,8]{3,2,1,0:T(8,128)S(1)}, u32[]{:S(2)}, u32[]{:S(2)}) collective-permute-start(f32[7,8,16,8]{3,2,1,0:T(8,128)S(1)} %get-tuple-element.31), channel_id=1, source_target_pairs={{8,0},{16,8},{24,16},{0,24},{9,1},{17,9},{25,17},{1,25},{10,2},{18... | collective-permute-start | bytes 86024 | tf_op jit(solution)/shard_map/ppermute | solution.py:24
  7.4 10.9 %collective-permute-done.1 = f32[7,8,16,8]{3,2,1,0:T(8,128)S(1)} collective-permute-done((f32[7,8,16,8]{3,2,1,0:T(8,128)S(1)}, f32[7,8,16,8]{3,2,1,0:T(8,128)S(1)}, u32[]{:S(2)}, u32[]{:S(2)}) %collective-permute-start.1) | collective-permute-done | bytes 28704 | tf_op jit(solution)/shard_map/ppermute | solution.py:24
  18.3 9.6 %collective-permute-done = f32[7,8,16,8]{3,2,1,0:T(8,128)S(1)} collective-permute-done((f32[7,8,16,8]{3,2,1,0:T(8,128)S(1)}, f32[7,8,16,8]{3,2,1,0:T(8,128)S(1)}, u32[]{:S(2)}, u32[]{:S(2)}) %collective-permute-start) | collective-permute-done | bytes 28704 | tf_op jit(solution)/shard_map/ppermute | solution.py:22
  29.4 1.9 collective-permute-start.3
  31.3 2.4 %collective-permute-start.2 = (f32[7,8,8,144]{3,2,1,0:T(8,128)S(1)}, f32[7,8,8,144]{3,2,1,0:T(8,128)S(1)}, u32[]{:S(2)}, u32[]{:S(2)}) collective-permute-start(f32[7,8,8,144]{3,2,1,0:T(8,128)S(1)} %get-tuple-element.22), channel_id=1, source_target_pairs={{0,2},{2,4},{4,6},{1,3},{3,5},{5,7},{8,10},{10,12},{12,14},{9,11},... | collective-permute-start | bytes 774152 | tf_op jit(solution)/shard_map/ppermute | solution.py:22
  33.8 3.5 %collective-permute-done.3 = f32[7,8,8,144]{3,2,1,0:T(8,128)S(1)} collective-permute-done((f32[7,8,8,144]{3,2,1,0:T(8,128)S(1)}, f32[7,8,8,144]{3,2,1,0:T(8,128)S(1)}, u32[]{:S(2)}, u32[]{:S(2)}) %collective-permute-start.3) | collective-permute-done | bytes 258080 | tf_op jit(solution)/shard_map/ppermute | solution.py:24
  37.3 3.8 %collective-permute-done.2 = f32[7,8,8,144]{3,2,1,0:T(8,128)S(1)} collective-permute-done((f32[7,8,8,144]{3,2,1,0:T(8,128)S(1)}, f32[7,8,8,144]{3,2,1,0:T(8,128)S(1)}, u32[]{:S(2)}, u32[]{:S(2)}) %collective-permute-start.2) | collective-permute-done | bytes 258080 | tf_op jit(solution)/shard_map/ppermute | solution.py:22
  42.9 4.8 %collective-permute-start.4 = (f32[7,8,32,144]{3,2,1,0:T(8,128)S(1)}, f32[7,8,32,144]{3,2,1,0:T(8,128)S(1)}, u32[]{:S(2)}, u32[]{:S(2)}) collective-permute-start(f32[7,8,32,144]{3,2,1,0:T(8,128)S(1)} %pad_maximum_fusion.1), channel_id=1, source_target_pairs={{0,1},{2,3},{4,5},{6,7},{8,9},{10,11},{12,13},{14,15},{16,17},{18,... | collective-permute-start | bytes 3096584 | tf_op jit(solution)/shard_map/ppermute | solution.py:22
  47.6 32.2 %collective-permute-done.5 = f32[7,8,32,144]{3,2,1,0:T(8,128)S(1)} collective-permute-done((f32[7,8,32,144]{3,2,1,0:T(8,128)S(1)}, f32[7,8,32,144]{3,2,1,0:T(8,128)S(1)}, u32[]{:S(2)}, u32[]{:S(2)}) %collective-permute-start.5) | collective-permute-done | bytes 1032224 | tf_op jit(solution)/shard_map/ppermute | solution.py:24
  81.1 4.7 %fusion = f32[7,24,32,128]{3,2,1,0:T(8,128)S(1)} fusion(f32[7,8,32,144]{3,2,1,0:T(8,128)S(1)} %collective-permute-done.5, f32[7,8,8,144]{3,2,1,0:T(8,128)S(1)} %collective-permute-done.3, f32[7,8,16,8]{3,2,1,0:T(8,128)S(1)} %collective-permute-done.1, f32[3,8,16,128]{3,2,1,0:T(8,128)S(1)} %slice_multiply_fusion.5, f32[4,8,16,128]{3,2,1,0:T(8,128)S(1)} %copy-done, ...), kind=kOutput, calls=%fused_computation | convolution fusion | flops 1195444224 | bytes 5849088 | tf_op jit(solution)/shard_map/fswz,zk->fswk/dot_general | solution.py:45
  90.9 8.8 %collective-permute-done.13 = f32[7,8,16,8]{3,1,2,0:T(8,128)S(1)} collective-permute-done((f32[7,8,16,8]{3,1,2,0:T(8,128)S(1)}, f32[7,8,16,8]{3,1,2,0:T(8,128)S(1)}, u32[]{:S(2)}, u32[]{:S(2)}) %collective-permute-start.13) | collective-permute-done | bytes 28704 | tf_op jit(solution)/shard_map/ppermute | solution.py:24
  99.7 5.0 %collective-permute-done.12 = f32[7,8,16,8]{3,1,2,0:T(8,128)S(1)} collective-permute-done((f32[7,8,16,8]{3,1,2,0:T(8,128)S(1)}, f32[7,8,16,8]{3,1,2,0:T(8,128)S(1)}, u32[]{:S(2)}, u32[]{:S(2)}) %collective-permute-start.12) | collective-permute-done | bytes 28704 | tf_op jit(solution)/shard_map/ppermute | solution.py:22
  105.1 6.5 %collective-permute-start.15 = (f32[7,8,8,144]{3,1,2,0:T(8,128)S(1)}, f32[7,8,8,144]{3,1,2,0:T(8,128)S(1)}, u32[]{:S(2)}, u32[]{:S(2)}) collective-permute-start(f32[7,8,8,144]{3,1,2,0:T(8,128)S(1)} %get-tuple-element.21), channel_id=1, source_target_pairs={{2,0},{4,2},{6,4},{3,1},{5,3},{7,5},{10,8},{12,10},{14,12},{11,9},... | collective-permute-start | bytes 774152 | tf_op jit(solution)/shard_map/ppermute | solution.py:24
  111.6 1.9 collective-permute-start.14
  113.5 4.0 %collective-permute-done.15 = f32[7,8,8,144]{3,1,2,0:T(8,128)S(1)} collective-permute-done((f32[7,8,8,144]{3,1,2,0:T(8,128)S(1)}, f32[7,8,8,144]{3,1,2,0:T(8,128)S(1)}, u32[]{:S(2)}, u32[]{:S(2)}) %collective-permute-start.15) | collective-permute-done | bytes 258080 | tf_op jit(solution)/shard_map/ppermute | solution.py:24
  117.6 3.8 %collective-permute-done.14 = f32[7,8,8,144]{3,1,2,0:T(8,128)S(1)} collective-permute-done((f32[7,8,8,144]{3,1,2,0:T(8,128)S(1)}, f32[7,8,8,144]{3,1,2,0:T(8,128)S(1)}, u32[]{:S(2)}, u32[]{:S(2)}) %collective-permute-start.14) | collective-permute-done | bytes 258080 | tf_op jit(solution)/shard_map/ppermute | solution.py:22
  123.1 4.8 %collective-permute-start.16 = (f32[7,8,32,144]{3,1,2,0:T(8,128)S(1)}, f32[7,8,32,144]{3,1,2,0:T(8,128)S(1)}, u32[]{:S(2)}, u32[]{:S(2)}) collective-permute-start(f32[7,8,32,144]{3,1,2,0:T(8,128)S(1)} %pad_maximum_fusion.2), channel_id=1, source_target_pairs={{0,1},{2,3},{4,5},{6,7},{8,9},{10,11},{12,13},{14,15},{16,17},{18,... | collective-permute-start | bytes 3096584 | tf_op jit(solution)/shard_map/ppermute | solution.py:22
  129.9 3.8 %collective-permute-start.8 = (f32[4,8,1,128]{3,1,2,0:T(8,128)S(1)}, f32[4,8,1,128]{3,1,2,0:T(8,128)S(1)}, u32[]{:S(2)}, u32[]{:S(2)}) collective-permute-start(f32[4,8,1,128]{3,1,2,0:T(8,128)S(1)} %get-tuple-element.27), channel_id=1, source_target_pairs={{2,0},{4,2},{6,4},{3,1},{5,3},{7,5},{10,8},{12,10},{14,12},{11,9},... | collective-permute-start | bytes 49160 | tf_op jit(solution)/shard_map/ppermute | solution.py:24
  139.5 6.8 %collective-permute-done.7 = f32[4,8,16,1]{3,1,2,0:T(8,128)S(1)} collective-permute-done((f32[4,8,16,1]{3,1,2,0:T(8,128)S(1)}, f32[4,8,16,1]{3,1,2,0:T(8,128)S(1)}, u32[]{:S(2)}, u32[]{:S(2)}) %collective-permute-start.7) | collective-permute-done | bytes 2080 | tf_op jit(solution)/shard_map/ppermute | solution.py:22
  146.6 6.0 %collective-permute-done.6 = f32[4,8,16,1]{3,1,2,0:T(8,128)S(1)} collective-permute-done((f32[4,8,16,1]{3,1,2,0:T(8,128)S(1)}, f32[4,8,16,1]{3,1,2,0:T(8,128)S(1)}, u32[]{:S(2)}, u32[]{:S(2)}) %collective-permute-start.6) | collective-permute-done | bytes 2080 | tf_op jit(solution)/shard_map/ppermute | solution.py:24
  152.6 9.2 %collective-permute-done.11 = f32[4,1,18,128]{3,1,2,0:T(1,128)S(1)} collective-permute-done((f32[4,1,18,128]{3,1,2,0:T(1,128)S(1)}, f32[4,1,18,128]{3,1,2,0:T(1,128)S(1)}, u32[]{:S(2)}, u32[]{:S(2)}) %collective-permute-start.11) | collective-permute-done | bytes 36896 | tf_op jit(solution)/shard_map/ppermute | solution.py:22
  162.2 2.6 %pad_maximum_fusion = f32[7,24,32,144]{3,1,2,0:T(8,128)S(1)} fusion(f32[7,8,32,144]{3,1,2,0:T(8,128)S(1)} %collective-permute-done.17, f32[7,8,8,144]{3,1,2,0:T(8,128)S(1)} %collective-permute-done.15, f32[7,8,16,8]{3,1,2,0:T(8,128)S(1)} %collective-permute-done.13, f32[3,8,16,128]{3,1,2,0:T(8,128)S(1)} %slice_multiply_fusion.1, ...), kind=kLoop, calls=%fused_computation.16 | loop fusion | flops 5419008 | bytes 6193152 | tf_op jit(solution)/shard_map/concatenate | solution.py:20
  164.8 5.8 %fusion.16 = f32[7,24,32,128]{3,2,1,0:T(8,128)S(1)} fusion(f32[7,24,32,144]{3,1,2,0:T(8,128)S(1)} %pad_maximum_fusion), kind=kOutput, calls=%fused_computation.17 | convolution fusion | flops 1190025216 | bytes 5849088 | tf_op jit(solution)/shard_map/fswz,zk->fswk/dot_general | solution.py:45
  173.9 37.0 %all-reduce = (f32[3,16]{1,0:T(4,128)S(1)}, f32[3,16]{1,0:T(4,128)S(1)}, f32[3,16]{1,0:T(4,128)S(1)}, f32[3,16]{1,0:T(4,128)S(1)}, f32[3,16]{1,0:T(4,128)S(1)}) all-reduce(f32[3,16]{1,0:T(4,128)S(1)} %get-tuple-element.11, f32[3,16]{1,0:T(4,128)S(1)} %get-tuple-element.12, ...), channel_id=1, replica_groups=mesh['span'=4,'wall'=4,'stream'=2] {'span','stream'}, use_global_device_ids=true, to_apply=%region_1.2 | all-reduce | flops 240 | bytes 1920 | tf_op jit(solution)/shard_map/psum | solution.py:91
  (48 shorter events, 28.8 us)
Async XLA Ops:
  2.4 38.7 %copy-start = (f32[4,8,16,128]{3,2,1,0:T(8,128)S(1)}, f32[4,8,16,128]{3,2,1,0:T(8,128)}, u32[]{:S(2)}) copy-start(f32[4,8,16,128]{3,2,1,0:T(8,128)} %param.1) | copy-start | bytes 786436
  3.7 14.6 %collective-permute-start.1 = (f32[7,8,16,8]{3,2,1,0:T(8,128)S(1)}, f32[7,8,16,8]{3,2,1,0:T(8,128)S(1)}, u32[]{:S(2)}, u32[]{:S(2)}) collective-permute-start(f32[7,8,16,8]{3,2,1,0:T(8,128)S(1)} %get-tuple-element.31), channel_id=1, source_target_pairs={{8,0},{16,8},{24,16},{0,24},{9,1},{17,9},{25,17},{1,25},{10,2},{18... | collective-permute-start | bytes 86024 | tf_op jit(solution)/shard_map/ppermute | solution.py:24
  7.4 20.5 %collective-permute-start = (f32[7,8,16,8]{3,2,1,0:T(8,128)S(1)}, f32[7,8,16,8]{3,2,1,0:T(8,128)S(1)}, u32[]{:S(2)}, u32[]{:S(2)}) collective-permute-start(f32[7,8,16,8]{3,2,1,0:T(8,128)S(1)} %get-tuple-element.30), channel_id=1, source_target_pairs={{0,8},{8,16},{16,24},{24,0},{1,9},{9,17},{17,25},{25,1},{2,10},{10... | collective-permute-start | bytes 86024 | tf_op jit(solution)/shard_map/ppermute | solution.py:22
  29.4 7.9 %collective-permute-start.3 = (f32[7,8,8,144]{3,2,1,0:T(8,128)S(1)}, f32[7,8,8,144]{3,2,1,0:T(8,128)S(1)}, u32[]{:S(2)}, u32[]{:S(2)}) collective-permute-start(f32[7,8,8,144]{3,2,1,0:T(8,128)S(1)} %get-tuple-element.23), channel_id=1, source_target_pairs={{2,0},{4,2},{6,4},{3,1},{5,3},{7,5},{10,8},{12,10},{14,12},{11,9},... | collective-permute-start | bytes 774152 | tf_op jit(solution)/shard_map/ppermute | solution.py:24
  31.3 9.8 %collective-permute-start.2 = (f32[7,8,8,144]{3,2,1,0:T(8,128)S(1)}, f32[7,8,8,144]{3,2,1,0:T(8,128)S(1)}, u32[]{:S(2)}, u32[]{:S(2)}) collective-permute-start(f32[7,8,8,144]{3,2,1,0:T(8,128)S(1)} %get-tuple-element.22), channel_id=1, source_target_pairs={{0,2},{2,4},{4,6},{1,3},{3,5},{5,7},{8,10},{10,12},{12,14},{9,11},... | collective-permute-start | bytes 774152 | tf_op jit(solution)/shard_map/ppermute | solution.py:22
  41.6 38.2 %collective-permute-start.5 = (f32[7,8,32,144]{3,2,1,0:T(8,128)S(1)}, f32[7,8,32,144]{3,2,1,0:T(8,128)S(1)}, u32[]{:S(2)}, u32[]{:S(2)}) collective-permute-start(f32[7,8,32,144]{3,2,1,0:T(8,128)S(1)} %pad_maximum_fusion.1), channel_id=1, source_target_pairs={{1,0},{3,2},{5,4},{7,6},{9,8},{11,10},{13,12},{15,14},{17,16},{19,... | collective-permute-start | bytes 3096584 | tf_op jit(solution)/shard_map/ppermute | solution.py:24
  42.9 38.2 %collective-permute-start.4 = (f32[7,8,32,144]{3,2,1,0:T(8,128)S(1)}, f32[7,8,32,144]{3,2,1,0:T(8,128)S(1)}, u32[]{:S(2)}, u32[]{:S(2)}) collective-permute-start(f32[7,8,32,144]{3,2,1,0:T(8,128)S(1)} %pad_maximum_fusion.1), channel_id=1, source_target_pairs={{0,1},{2,3},{4,5},{6,7},{8,9},{10,11},{12,13},{14,15},{16,17},{18,... | collective-permute-start | bytes 3096584 | tf_op jit(solution)/shard_map/ppermute | solution.py:22
  88.8 10.9 %collective-permute-start.13 = (f32[7,8,16,8]{3,1,2,0:T(8,128)S(1)}, f32[7,8,16,8]{3,1,2,0:T(8,128)S(1)}, u32[]{:S(2)}, u32[]{:S(2)}) collective-permute-start(f32[7,8,16,8]{3,1,2,0:T(8,128)S(1)} %get-tuple-element.29), channel_id=1, source_target_pairs={{8,0},{16,8},{24,16},{0,24},{9,1},{17,9},{25,17},{1,25},{10,2},{18... | collective-permute-start | bytes 86024 | tf_op jit(solution)/shard_map/ppermute | solution.py:24
  90.6 14.1 %collective-permute-start.12 = (f32[7,8,16,8]{3,1,2,0:T(8,128)S(1)}, f32[7,8,16,8]{3,1,2,0:T(8,128)S(1)}, u32[]{:S(2)}, u32[]{:S(2)}) collective-permute-start(f32[7,8,16,8]{3,1,2,0:T(8,128)S(1)} %get-tuple-element.28), channel_id=1, source_target_pairs={{0,8},{8,16},{16,24},{24,0},{1,9},{9,17},{17,25},{25,1},{2,10},{10... | collective-permute-start | bytes 86024 | tf_op jit(solution)/shard_map/ppermute | solution.py:22
  105.1 12.4 %collective-permute-start.15 = (f32[7,8,8,144]{3,1,2,0:T(8,128)S(1)}, f32[7,8,8,144]{3,1,2,0:T(8,128)S(1)}, u32[]{:S(2)}, u32[]{:S(2)}) collective-permute-start(f32[7,8,8,144]{3,1,2,0:T(8,128)S(1)} %get-tuple-element.21), channel_id=1, source_target_pairs={{2,0},{4,2},{6,4},{3,1},{5,3},{7,5},{10,8},{12,10},{14,12},{11,9},... | collective-permute-start | bytes 774152 | tf_op jit(solution)/shard_map/ppermute | solution.py:24
  111.6 9.8 %collective-permute-start.14 = (f32[7,8,8,144]{3,1,2,0:T(8,128)S(1)}, f32[7,8,8,144]{3,1,2,0:T(8,128)S(1)}, u32[]{:S(2)}, u32[]{:S(2)}) collective-permute-start(f32[7,8,8,144]{3,1,2,0:T(8,128)S(1)} %get-tuple-element.20), channel_id=1, source_target_pairs={{0,2},{2,4},{4,6},{1,3},{3,5},{5,7},{8,10},{10,12},{12,14},{9,11},... | collective-permute-start | bytes 774152 | tf_op jit(solution)/shard_map/ppermute | solution.py:22
  121.8 40.3 %collective-permute-start.17 = (f32[7,8,32,144]{3,1,2,0:T(8,128)S(1)}, f32[7,8,32,144]{3,1,2,0:T(8,128)S(1)}, u32[]{:S(2)}, u32[]{:S(2)}) collective-permute-start(f32[7,8,32,144]{3,1,2,0:T(8,128)S(1)} %pad_maximum_fusion.2), channel_id=1, source_target_pairs={{1,0},{3,2},{5,4},{7,6},{9,8},{11,10},{13,12},{15,14},{17,16},{19,... | collective-permute-start | bytes 3096584 | tf_op jit(solution)/shard_map/ppermute | solution.py:24
  123.1 39.0 %collective-permute-start.16 = (f32[7,8,32,144]{3,1,2,0:T(8,128)S(1)}, f32[7,8,32,144]{3,1,2,0:T(8,128)S(1)}, u32[]{:S(2)}, u32[]{:S(2)}) collective-permute-start(f32[7,8,32,144]{3,1,2,0:T(8,128)S(1)} %pad_maximum_fusion.2), channel_id=1, source_target_pairs={{0,1},{2,3},{4,5},{6,7},{8,9},{10,11},{12,13},{14,15},{16,17},{18,... | collective-permute-start | bytes 3096584 | tf_op jit(solution)/shard_map/ppermute | solution.py:22
  127.9 5.8 %collective-permute-start.9 = (f32[4,8,1,128]{3,1,2,0:T(8,128)S(1)}, f32[4,8,1,128]{3,1,2,0:T(8,128)S(1)}, u32[]{:S(2)}, u32[]{:S(2)}) collective-permute-start(f32[4,8,1,128]{3,1,2,0:T(8,128)S(1)} %get-tuple-element.26), channel_id=1, source_target_pairs={{0,2},{2,4},{4,6},{1,3},{3,5},{5,7},{8,10},{10,12},{12,14},{9,11},... | collective-permute-start | bytes 49160 | tf_op jit(solution)/shard_map/ppermute | solution.py:22
  129.9 5.3 %collective-permute-start.8 = (f32[4,8,1,128]{3,1,2,0:T(8,128)S(1)}, f32[4,8,1,128]{3,1,2,0:T(8,128)S(1)}, u32[]{:S(2)}, u32[]{:S(2)}) collective-permute-start(f32[4,8,1,128]{3,1,2,0:T(8,128)S(1)} %get-tuple-element.27), channel_id=1, source_target_pairs={{2,0},{4,2},{6,4},{3,1},{5,3},{7,5},{10,8},{12,10},{14,12},{11,9},... | collective-permute-start | bytes 49160 | tf_op jit(solution)/shard_map/ppermute | solution.py:24
  135.2 26.6 %collective-permute-start.11 = (f32[4,1,18,128]{3,1,2,0:T(1,128)S(1)}, f32[4,1,18,128]{3,1,2,0:T(1,128)S(1)}, u32[]{:S(2)}, u32[]{:S(2)}) collective-permute-start(f32[4,1,18,128]{3,1,2,0:T(1,128)S(1)} %get-tuple-element.35), channel_id=1, source_target_pairs={{0,1},{2,3},{4,5},{6,7},{8,9},{10,11},{12,13},{14,15},{16,17},{18,... | collective-permute-start | bytes 110600 | tf_op jit(solution)/shard_map/ppermute | solution.py:22
  136.5 25.3 %collective-permute-start.10 = (f32[4,1,18,128]{3,1,2,0:T(1,128)S(1)}, f32[4,1,18,128]{3,1,2,0:T(1,128)S(1)}, u32[]{:S(2)}, u32[]{:S(2)}) collective-permute-start(f32[4,1,18,128]{3,1,2,0:T(1,128)S(1)} %get-tuple-element.34), channel_id=1, source_target_pairs={{1,0},{3,2},{5,4},{7,6},{9,8},{11,10},{13,12},{15,14},{17,16},{19,... | collective-permute-start | bytes 110600 | tf_op jit(solution)/shard_map/ppermute | solution.py:24
  137.9 8.3 %collective-permute-start.7 = (f32[4,8,16,1]{3,1,2,0:T(8,128)S(1)}, f32[4,8,16,1]{3,1,2,0:T(8,128)S(1)}, u32[]{:S(2)}, u32[]{:S(2)}) collective-permute-start(f32[4,8,16,1]{3,1,2,0:T(8,128)S(1)} %get-tuple-element.25), channel_id=1, source_target_pairs={{0,8},{8,16},{16,24},{24,0},{1,9},{9,17},{17,25},{25,1},{2,10},{10... | collective-permute-start | bytes 6152 | tf_op jit(solution)/shard_map/ppermute | solution.py:22
  146.2 6.4 %collective-permute-start.6 = (f32[4,8,16,1]{3,1,2,0:T(8,128)S(1)}, f32[4,8,16,1]{3,1,2,0:T(8,128)S(1)}, u32[]{:S(2)}, u32[]{:S(2)}) collective-permute-start(f32[4,8,16,1]{3,1,2,0:T(8,128)S(1)} %get-tuple-element.24), channel_id=1, source_target_pairs={{8,0},{16,8},{24,16},{0,24},{9,1},{17,9},{25,17},{1,25},{10,2},{18... | collective-permute-start | bytes 6152 | tf_op jit(solution)/shard_map/ppermute | solution.py:24
where the time goes:
time: 214 us; the launch traced here: 213 us
  waiting for transfers between devices  106 us (50%)
  starting transfers between devices  40.9 us (19%)
  blocking collectives  37 us (17%)
  matrix products  15.9 us (7%)
  other arithmetic  9.48 us (4%)
  local copies, waits for them, and re-layouts  2.62 us (1%)
    ppermute x9, waiting for transfers between devices, with_halo(): lax.ppermute(head, axis, [((i + 1) % count, i) for i in range(ends)])  66.9 us
    ppermute x9, waiting for transfers between devices, with_halo(): lax.ppermute(tail, axis, [(i, (i + 1) % count) for i in range(ends)])  39.4 us
    psum x1, blocking collectives, shards(): lax.psum((sums[0], sums[1], sums[2], sums[3], sums[4]), ('span', 'stream'))  37 us
    ppermute x9, starting transfers between devices, with_halo(): lax.ppermute(head, axis, [((i + 1) % count, i) for i in range(ends)])  21.9 us
    ppermute x9, starting transfers between devices, with_halo(): lax.ppermute(tail, axis, [(i, (i + 1) % count) for i in range(ends)])  19 us
    dot_general x2, matrix products, smooth(): jnp.einsum('fswz,zk->fswk', padded, matrix, precision=lax.Precision.HIGHEST)  10.5 us
    concatenate x5, other arithmetic, with_halo(): jnp.concatenate([lax.ppermute(tail, axis, [(i, (i + 1) % count) for i in...  5.3 us
  transfers between devices with their start and end apart: 18, of which 14 were waited for; matrix products, arithmetic and copies ran while one was open for 0% of the time, Pallas kernels for 0%

commit v1 on v0

v1 whole, which is shorter than its diff:
```python
import functools
import math

import jax
import jax.numpy as jnp
import ml_dtypes
import numpy as np
from jax import lax
from jax.experimental import pallas as pl
from jax.experimental.pallas import tpu as pltpu
from jax.sharding import PartitionSpec as P

raw_taps = [math.exp(-((k - 8) ** 2) / 18.0) for k in range(17)]
filter_taps = [value / sum(raw_taps) for value in raw_taps]
clark_coef = 9.0
small_eps = 1e-06

reach = 8
rim = 2 * reach


def split_constant(matrix):
    high = matrix.astype(ml_dtypes.bfloat16)
    low = (matrix - high.astype(np.float64)).astype(ml_dtypes.bfloat16)
    return high, low


def band(outs, ins, offset):
    matrix = np.zeros((outs, ins))
    for o in range(outs):
        for i in range(ins):
            k = i - o - offset + reach
            if 0 <= k <= 2 * reach:
                matrix[o, i] = filter_taps[k]
    return matrix


def plane_constants(layers, rows):
    stream = band(layers, layers, 0)
    wall = band(rows, 2 * rows, reach)
    blocks = [np.kron(stream, wall[:, :rows]), np.kron(stream, wall[:, rows:])]
    return split_constant(np.concatenate(blocks, axis=1))


def span_constants(width):
    everything = band(width + 2 * rim, width + 2 * rim, 0)
    weights = np.zeros((4, 2 * width, 2 * width))
    for f in range(4):
        place = np.full(width + 2 * rim, -1)
        for c in range(rim):
            place[c] = width + 64 + f * rim + c
            place[rim + width + c] = width + f * rim + c
        place[rim : rim + width] = np.arange(width)
        swapped = np.where(place >= width, place - width, place + width)
        weights[f][np.ix_(place, swapped)] = everything.T
    high, low = split_constant(weights)
    low = np.concatenate([low[..., width:], low[..., :width]], axis=2)
    return np.concatenate([high, low], axis=2)


def halves(value):
    high = value.astype(jnp.bfloat16)
    return high, (value - high.astype(jnp.float32)).astype(jnp.bfloat16)


def dot(a, b):
    return lax.dot_general(a, b, (((1,), (0,)), ((), ())), preferred_element_type=jnp.float32)


def lane_index(shape):
    return lax.broadcasted_iota(jnp.int32, shape, len(shape) - 1)


def edge_kernel(own, edges):
    _, layers, rows, width = own.shape
    lane = lane_index((layers * rows, width))
    total = jnp.zeros((layers * rows, width), jnp.float32)
    for f in range(4):
        cells = own[f].reshape(layers * rows, width)
        first = pltpu.roll(cells, f * rim, 1) if f else cells
        total = jnp.where((lane >= f * rim) & (lane < (f + 1) * rim), first, total)
        last = pltpu.roll(cells, (64 + f * rim + rim) % width, 1) if (f + 1) * rim != 64 else cells
        start = 64 + f * rim
        total = jnp.where((lane >= start) & (lane < start + rim), last, total)
    edges[...] = total.reshape(layers, rows, width)


def spread_temperature(strip):
    width = strip.shape[1]
    field = lax.rem(lane_index(strip.shape), 64) // rim
    result = strip
    for f in range(3):
        moved = pltpu.roll(strip, width - (3 - f) * rim, 1)
        result = jnp.where(field == f, moved, result)
    return result


def flux_kernel(
    walls, own, part, a_own, b_own, a_part, b_part, s_own, s_part, a_strip, b_strip,
    plane_h, plane_l, span_w, clark_ref, similar_ref, sums_ref,
    raw, in_h, in_l, prod_h, prod_l, mean, mid_h, mid_l,
):
    _, layers, rows, width = own.shape
    both = 2 * layers
    cells = both * rows
    here = layers * rows
    me_s = lax.axis_index("stream")
    me_w = lax.axis_index("wall")
    odd = lax.rem(me_w, 2)
    mine = pl.multiple_of(me_s * layers, layers)
    other = pl.multiple_of((1 - me_s) * layers, layers)
    row_a = pl.multiple_of((1 - odd) * (2 * rows), rows)
    row_b = pl.multiple_of(odd * (2 * rows), rows)
    at_end = (me_w == 0) | (me_w == walls - 1)
    keep_b = jnp.where(at_end, 0.0, 1.0).astype(jnp.float32)

    for where, blocks in ((mine, (own, a_own, b_own)), (other, (part, a_part, b_part))):
        raw[:4, pl.ds(where, layers), rows : 2 * rows, :] = blocks[0][...]
        raw[:4, pl.ds(where, layers), pl.ds(row_a, rows), :] = blocks[1][...]
        raw[:4, pl.ds(where, layers), pl.ds(row_b, rows), :] = blocks[2][...] * keep_b
    for k, where, block in ((0, mine, s_own), (1, other, s_part)):
        raw[4, pl.ds(where, layers), rows : 2 * rows, :] = block[...]
        raw[4, pl.ds(where, layers), pl.ds(row_a, rows), :] = a_strip[k]
        raw[4, pl.ds(where, layers), pl.ds(row_b, rows), :] = b_strip[k] * keep_b

    for block in range(3):
        for t in range(5):
            value = raw[t, :, block * rows : (block + 1) * rows, :].reshape(cells, width)
            high, low = halves(value)
            in_h[block * cells : (block + 1) * cells, t * width : (t + 1) * width] = high
            in_l[block * cells : (block + 1) * cells, t * width : (t + 1) * width] = low

    for t in range(4):
        mean[t, 0] = jnp.zeros((2 * rows, width), jnp.float32)
        mean[t, both + 1] = jnp.zeros((2 * rows, width), jnp.float32)
    for half in range(2):
        part_h = in_h[half * cells : (half + 2) * cells, :]
        part_l = in_l[half * cells : (half + 2) * cells, :]
        planes = dot(plane_h[...], part_h) + dot(plane_l[...], part_h) + dot(plane_h[...], part_l)
        row = lax.rem(lax.broadcasted_iota(jnp.int32, planes.shape, 0), rows)
        if half == 0:
            inside = (me_w > 0) | (row >= reach)
        else:
            inside = (me_w < walls - 1) | (row < rows - reach)
        planes = jnp.where(inside, planes, 0.0)
        high, low = halves(planes)
        strip = jnp.zeros((cells, width), jnp.float32)
        for f in range(4):
            lhs_h = jnp.concatenate([high[:, f * width : (f + 1) * width], high[:, 4 * width :]], axis=1)
            lhs_l = jnp.concatenate([low[:, f * width : (f + 1) * width], low[:, 4 * width :]], axis=1)
            one = dot(lhs_h, span_w[f])
            two = dot(lhs_l, span_w[f, :, : 2 * width])
            value = one[:, width : 2 * width] + one[:, 2 * width : 3 * width] + two[:, width:]
            strip = strip + one[:, :width] + one[:, 3 * width :] + two[:, :width]
            mean[f, 1 : both + 1, half * rows : (half + 1) * rows, :] = value.reshape(both, rows, width)
        mean[4, 1 : both + 1, half * rows : (half + 1) * rows, :] = strip.reshape(both, rows, width)

    own_rows = pl.ds(pl.multiple_of(me_s * here, here), here)

    def filtered(high, low, tiles):
        lhs_h = plane_h[own_rows, :]
        planes = dot(lhs_h, high[...]) + dot(plane_l[own_rows, :], high[...]) + dot(lhs_h, low[...])
        high, low = halves(planes)
        results = []
        for t, s, f in tiles:
            pick_h = jnp.concatenate([high[:, t * width : (t + 1) * width], high[:, s * width : (s + 1) * width]], axis=1)
            pick_l = jnp.concatenate([low[:, t * width : (t + 1) * width], low[:, s * width : (s + 1) * width]], axis=1)
            one = dot(pick_h, span_w[f, :, width : 3 * width])
            two = dot(pick_l, span_w[f, :, width : 2 * width])
            results.append((one[:, :width] + one[:, width:] + two).reshape(layers, rows, width))
        return results

    for half in range(2):
        span = slice(reach + half * rows, reach + (half + 1) * rows)
        down = slice(half * cells, (half + 1) * cells)
        temperature = raw[3, :, span, :].reshape(cells, width)
        strip = raw[4, :, span, :].reshape(cells, width)
        factors = [(raw[i, :, span, :].reshape(cells, width), temperature) for i in range(3)]
        factors.append((strip, spread_temperature(strip)))
        for t, (left, right) in enumerate(factors):
            high, low = halves(left * right)
            prod_h[down, t * width : (t + 1) * width] = high
            prod_l[down, t * width : (t + 1) * width] = low
    flux = filtered(prod_h, prod_l, [(i, 3, i) for i in range(3)])

    for half in range(2):
        span = slice(half * rows, (half + 1) * rows)
        down = slice(half * cells, (half + 1) * cells)
        tiles = [mean[t, 1 : both + 1, span, :].reshape(cells, width) for t in range(5)]
        tiles += [tiles[i] * tiles[3] for i in range(3)]
        tiles.append(tiles[4] * spread_temperature(tiles[4]))
        for t, value in enumerate(tiles):
            high, low = halves(value)
            mid_h[down, t * width : (t + 1) * width] = high
            mid_l[down, t * width : (t + 1) * width] = low
    second = filtered(mid_h, mid_l, [(f, 4, f) for f in range(4)] + [(5 + i, 8, i) for i in range(3)])

    lane = lane_index((layers, rows, width))
    mid = slice(reach, reach + rows)
    centre, along_span, along_wall, along_stream = [], [], [], []
    strip = mean[4, pl.ds(mine + 1, layers), mid, :]
    for f in range(4):
        here_f = mean[f, pl.ds(mine + 1, layers), mid, :]
        centre.append(here_f)
        after = pltpu.roll(here_f, width - 1, 2)
        after = jnp.where(lane == width - 1, pltpu.roll(strip, (width - 1 - f * rim) % width, 2), after)
        before = pltpu.roll(here_f, 1, 2)
        before = jnp.where(lane == 0, pltpu.roll(strip, (width - (64 + f * rim + rim - 1)) % width, 2), before)
        along_span.append((after - before) * 0.5)
        below = mean[f, pl.ds(mine + 1, layers), reach + 1 : reach + rows + 1, :]
        above = mean[f, pl.ds(mine + 1, layers), reach - 1 : reach + rows - 1, :]
        along_wall.append((below - above) * 0.5)
        ahead = mean[f, pl.ds(mine + 2, layers), mid, :]
        behind = mean[f, pl.ds(mine, layers), mid, :]
        along_stream.append((ahead - behind) * 0.5)

    lane = lane_index((rows, width))
    table = jnp.zeros((rows, width), jnp.float32)
    for i in range(3):
        exact = flux[i] - centre[i] * centre[3]
        similar = second[4 + i] - second[i] * second[3]
        total = along_span[i] * along_span[3] + along_wall[i] * along_wall[3]
        clark = clark_coef * (total + along_stream[i] * along_stream[3])
        clark_ref[i] = clark
        similar_ref[i] = similar
        terms = (exact * clark, exact * similar, exact * exact, clark * clark, similar * similar)
        for q, term in enumerate(terms):
            value = jnp.sum(jnp.sum(term, axis=0), axis=1, keepdims=True)
            table = jnp.where(lane == 3 * q + i, value, table)
    sums_ref[...] = table


def finish_kernel(plane_cells, *refs):
    sums = refs[:-6]
    clark, similar, clark_model, similar_model, clark_corr, similar_corr = refs[-6:]
    rows, width = sums[0].shape
    table = sums[0][...]
    for more in sums[1:]:
        table = table + more[...]
    table = table / plane_cells
    lane = lane_index((rows, width))
    corr = jnp.zeros((rows, width), jnp.float32)
    for i in range(3):
        cross_c, cross_s, power_e, power_c, power_s = (
            table[:, 3 * q + i : 3 * q + i + 1] for q in range(5)
        )
        clark_model[i] = clark[i] / jnp.sqrt(power_c + small_eps)[None]
        similar_model[i] = similar[i] / jnp.sqrt(power_s + small_eps)[None]
        value = cross_c / jnp.sqrt((power_e + small_eps) * (power_c + small_eps))
        corr = jnp.where(lane == i, value, corr)
        value = cross_s / jnp.sqrt((power_e + small_eps) * (power_s + small_eps))
        corr = jnp.where(lane == 8 + i, value, corr)
    square = jnp.concatenate([corr, jnp.zeros((width - rows, width), jnp.float32)], axis=0)
    turned = square.T
    clark_corr[...] = turned[:3, :rows]
    similar_corr[...] = turned[8:11, :rows]


def vmem(count):
    return [pl.BlockSpec(memory_space=pltpu.VMEM)] * count


def shards(fields):
    _, layers, rows, width = fields.shape
    spans = lax.axis_size("span")
    walls = lax.axis_size("wall")
    streams = lax.axis_size("stream")
    cells = 2 * layers * rows

    def swap(value):
        return lax.ppermute(value, "stream", [(0, 1), (1, 0)])

    def pair_a(value):
        return lax.ppermute(value, "wall", [(w, w ^ 1) for w in range(walls)])

    def pair_b(value):
        return lax.ppermute(
            value, "wall", [(w, min(max(((w + 1) ^ 1) - 1, 0), walls - 1)) for w in range(walls)]
        )

    edges = pl.pallas_call(
        edge_kernel,
        out_shape=jax.ShapeDtypeStruct((layers, rows, width), jnp.float32),
        in_specs=vmem(1),
        out_specs=vmem(1)[0],
        name="edges",
    )(fields)
    before = lax.ppermute(edges, "span", [(p, (p + 1) % spans) for p in range(spans)])
    after = lax.ppermute(edges, "span", [(p, (p - 1) % spans) for p in range(spans)])
    part = swap(fields)
    a_own, b_own = pair_a(fields), pair_b(fields)
    a_part, b_part = pair_a(part), pair_b(part)
    s_own = jnp.where(lane_index(edges.shape) < width // 2, after, before)
    s_part = swap(s_own)
    strips = jnp.stack([s_own, s_part])
    a_strip, b_strip = pair_a(strips), pair_b(strips)

    plane_h, plane_l = plane_constants(2 * layers, rows)
    span_w = span_constants(width)
    block = jax.ShapeDtypeStruct((3, layers, rows, width), jnp.float32)
    clark, similar, sums = pl.pallas_call(
        functools.partial(flux_kernel, walls),
        out_shape=(block, block, jax.ShapeDtypeStruct((rows, width), jnp.float32)),
        in_specs=vmem(13),
        out_specs=tuple(vmem(3)),
        scratch_shapes=[
            pltpu.VMEM((5, 2 * layers, 3 * rows, width), jnp.float32),
            pltpu.VMEM((3 * cells, 5 * width), jnp.bfloat16),
            pltpu.VMEM((3 * cells, 5 * width), jnp.bfloat16),
            pltpu.VMEM((2 * cells, 4 * width), jnp.bfloat16),
            pltpu.VMEM((2 * cells, 4 * width), jnp.bfloat16),
            pltpu.VMEM((5, 2 * layers + 2, 2 * rows, width), jnp.float32),
            pltpu.VMEM((2 * cells, 9 * width), jnp.bfloat16),
            pltpu.VMEM((2 * cells, 9 * width), jnp.bfloat16),
        ],
        compiler_params=pltpu.CompilerParams(vmem_limit_bytes=40 * 1024 * 1024),
        name="flux",
    )(
        fields, part, a_own, b_own, a_part, b_part, s_own, s_part, a_strip, b_strip,
        jnp.asarray(plane_h), jnp.asarray(plane_l), jnp.asarray(span_w),
    )

    group = spans * streams
    tables = [sums]
    for step in range(1, group):
        tables.append(
            lax.ppermute(sums, ("span", "stream"), [(g, (g + step) % group) for g in range(group)])
        )
    corr = jax.ShapeDtypeStruct((3, rows), jnp.float32)
    return pl.pallas_call(
        functools.partial(finish_kernel, float(layers * width * group)),
        out_shape=(block, block, corr, corr),
        in_specs=vmem(group + 2),
        out_specs=tuple(vmem(4)),
        name="finish",
    )(*tables, clark, similar)


def solution(mesh):
    return jax.shard_map(
        shards,
        mesh=mesh,
        in_specs=(P(None, "stream", "wall", "span"),),
        out_specs=(
            P(None, "stream", "wall", "span"),
            P(None, "stream", "wall", "span"),
            P(None, "wall"),
            P(None, "wall"),
        ),
        check_vma=False,
    )
```

time: 214 us -> 52.7 us (0.25)
  waiting for transfers between devices: 106 us -> 16.3 us
  blocking collectives: 37 us -> 0 us
  starting transfers between devices: 40.9 us -> 24.1 us
  matrix products: 15.9 us -> 0 us
  other arithmetic: 9.48 us -> 0.02 us
  Pallas kernels: 0 us -> 8.16 us
    ppermute x18 -> x17, waiting for transfers between devices: 106 us -> 16.3 us  [the longest x7 5.2 us: shards(): lax.ppermute(sums, ('span', 'stream'), [(g, (g + step) % group) for g in...]
    psum x1 -> x0, blocking collectives: 37 us -> none  [shards(): lax.psum((sums[0], sums[1], sums[2], sums[3], sums[4]), ('span', 'stream'))]
    ppermute x18 -> x17, starting transfers between devices: 40.9 us -> 24.1 us  [the longest x7 9.09 us: shards(): lax.ppermute(sums, ('span', 'stream'), [(g, (g + step) % group) for g in...]
    dot_general x6 -> x0, matrix products: 15.9 us -> none  [the longest x2 10.5 us: smooth(): jnp.einsum('fswz,zk->fswk', padded, matrix, precision=lax.Precision.HIGHEST)]
    pallas_call x0 -> x3, Pallas kernels: none -> 8.16 us  [the longest x1 4.19 us: shards(): pl.pallas_call(functools.partial(flux_kernel, walls), out_shape=(block, b...]
    concatenate x7 -> x0, other arithmetic: 6.76 us -> none  [the longest x5 5.3 us: with_halo(): jnp.concatenate([lax.ppermute(tail, axis, [(i, (i + 1) % count) for i in...]
  transfers between devices with their start and end apart: 18 -> 17, of which waited for: 14 -> 9; matrix products, arithmetic and copies ran while one was open for 0% -> 0% of each run, Pallas kernels for 0% -> 0%
where the time goes in v1:
time: 52.7 us; the launch traced here: 52.5 us
  starting transfers between devices  24.1 us (46%)
  waiting for transfers between devices  16.3 us (31%)
  Pallas kernels  8.16 us (15%)
  local copies, waits for them, and re-layouts  3.16 us (6%)
  between operations  0.79 us (1%)
    ppermute x7, starting transfers between devices, shards(): lax.ppermute(sums, ('span', 'stream'), [(g, (g + step) % group) for g in...  9.09 us
    ppermute x3, starting transfers between devices, pair_b(): lax.ppermute(value, 'wall', [(w, min(max((w + 1 ^ 1) - 1, 0), walls - 1))...  7.48 us
    ppermute x7, waiting for transfers between devices, shards(): lax.ppermute(sums, ('span', 'stream'), [(g, (g + step) % group) for g in...  5.2 us
    ppermute x2, waiting for transfers between devices, swap(): return lax.ppermute(value, 'stream', [(0, 1), (1, 0)])  4.46 us
    pallas_call x1, Pallas kernels, shards(): pl.pallas_call(functools.partial(flux_kernel, walls), out_shape=(block, b...  4.19 us
    ppermute x3, waiting for transfers between devices, pair_b(): lax.ppermute(value, 'wall', [(w, min(max((w + 1 ^ 1) - 1, 0), walls - 1))...  3.97 us
    unnamed x28, local copies, waits for them, and re-layouts  3.16 us
    ppermute x2, starting transfers between devices, swap(): return lax.ppermute(value, 'stream', [(0, 1), (1, 0)])  3.05 us
  transfers between devices with their start and end apart: 17, of which 9 were waited for; matrix products, arithmetic and copies ran while one was open for 0% of the time, Pallas kernels for 0%

profile of v1, /device:TPU:4, one launch (start us, length us, event | category | flops | bytes accessed | tf_op | source)
XLA Modules:
  0.0 52.5 jit_solution(1825149958111371663)
XLA Ops:
  0.7 1.8 %edges.1 = f32[8,16,128]{2,1,0:T(8,128)} custom-call(f32[4,8,16,128]{3,2,1,0:T(8,128)} %own.3), custom_call_target="tpu_custom_call" | custom-call | tf_op jit(solution)/shard_map/edges/pallas_call | solution.py:281
  2.5 1.6 %collective-permute-start.6 = (f32[8,16,128]{2,1,0:T(8,128)}, f32[8,16,128]{2,1,0:T(8,128)S(1)}, u32[]{:S(2)}, u32[]{:S(2)}) collective-permute-start(f32[8,16,128]{2,1,0:T(8,128)} %edges.1), channel_id=1, source_target_pairs={{0,8},{8,16},{16,24},{24,0},{1,9},{9,17},{17,25},{25,1},{2,10},{10... | collective-permute-start | bytes 196616 | tf_op jit(solution)/shard_map/ppermute | solution.py:288
  4.0 2.2 %collective-permute-start.5 = (f32[8,16,128]{2,1,0:T(8,128)}, f32[8,16,128]{2,1,0:T(8,128)S(1)}, u32[]{:S(2)}, u32[]{:S(2)}) collective-permute-start(f32[8,16,128]{2,1,0:T(8,128)} %edges.1), channel_id=1, source_target_pairs={{0,24},{8,0},{16,8},{24,16},{1,25},{9,1},{17,9},{25,17},{2,26},{10... | collective-permute-start | bytes 196616 | tf_op jit(solution)/shard_map/ppermute | solution.py:289
  6.3 1.5 %collective-permute-start = (f32[4,8,16,128]{3,2,1,0:T(8,128)S(1)}, f32[4,8,16,128]{3,2,1,0:T(8,128)S(1)}, u32[]{:S(2)}, u32[]{:S(2)}) collective-permute-start(f32[4,8,16,128]{3,2,1,0:T(8,128)S(1)} %copy-done.1), channel_id=1, source_target_pairs={{0,1},{1,0},{2,3},{3,2},{4,5},{5,4},{6,7},{7,6},{8,9},{9,8},{10,11... | collective-permute-start | bytes 786440 | tf_op jit(solution)/shard_map/ppermute | solution.py:271
  7.8 1.4 %collective-permute-done.6 = f32[8,16,128]{2,1,0:T(8,128)S(1)} collective-permute-done((f32[8,16,128]{2,1,0:T(8,128)}, f32[8,16,128]{2,1,0:T(8,128)S(1)}, u32[]{:S(2)}, u32[]{:S(2)}) %collective-permute-start.6) | collective-permute-done | bytes 65568 | tf_op jit(solution)/shard_map/ppermute | solution.py:288
  9.2 1.6 %collective-permute-start.7 = (f32[8,16,128]{2,1,0:T(8,128)S(1)}, f32[8,16,128]{2,1,0:T(8,128)S(1)}, u32[]{:S(2)}, u32[]{:S(2)}) collective-permute-start(f32[8,16,128]{2,1,0:T(8,128)S(1)} %broadcast_select_fusion.s_own), channel_id=1, source_target_pairs={{0,1},{1,0},{2,3},{3,2},{4,5},{5,4},{6,7},{7,6},{8,9},{9,8},{10,11... | collective-permute-start | bytes 196616 | tf_op jit(solution)/shard_map/ppermute | solution.py:271
  10.8 4.5 %collective-permute-done.7.s_part = f32[8,16,128]{2,1,0:T(8,128)S(1)} collective-permute-done((f32[8,16,128]{2,1,0:T(8,128)S(1)}, f32[8,16,128]{2,1,0:T(8,128)S(1)}, u32[]{:S(2)}, u32[]{:S(2)}) %collective-permute-start.7) | collective-permute-done | bytes 65568 | tf_op jit(solution)/shard_map/ppermute | solution.py:271
  15.3 1.9 %collective-permute-start.9 = (f32[2,8,16,128]{3,2,1,0:T(8,128)S(1)}, f32[2,8,16,128]{3,2,1,0:T(8,128)S(1)}, u32[]{:S(2)}, u32[]{:S(2)}) collective-permute-start(f32[2,8,16,128]{3,2,1,0:T(8,128)S(1)} %pad_maximum_fusion), channel_id=1, source_target_pairs={{0,0},{2,4},{4,2},{6,6},{1,1},{3,5},{5,3},{7,7},{8,8},{10,12},{12,... | collective-permute-start | bytes 393224 | tf_op jit(solution)/shard_map/ppermute | solution.py:277
  17.2 3.6 %collective-permute-start.2 = (f32[4,8,16,128]{3,2,1,0:T(8,128)S(1)}, f32[4,8,16,128]{3,2,1,0:T(8,128)S(1)}, u32[]{:S(2)}, u32[]{:S(2)}) collective-permute-start(f32[4,8,16,128]{3,2,1,0:T(8,128)S(1)} %copy-done.1), channel_id=1, source_target_pairs={{0,0},{2,4},{4,2},{6,6},{1,1},{3,5},{5,3},{7,7},{8,8},{10,12},{12,... | collective-permute-start | bytes 786440 | tf_op jit(solution)/shard_map/ppermute | solution.py:277
  20.9 1.9 %collective-permute-start.4 = (f32[4,8,16,128]{3,2,1,0:T(8,128)S(1)}, f32[4,8,16,128]{3,2,1,0:T(8,128)S(1)}, u32[]{:S(2)}, u32[]{:S(2)}) collective-permute-start(f32[4,8,16,128]{3,2,1,0:T(8,128)S(1)} %collective-permute-done.part), channel_id=1, source_target_pairs={{0,0},{2,4},{4,2},{6,6},{1,1},{3,5},{5,3},{7,7},{8,8},{10,12},{12,... | collective-permute-start | bytes 786440 | tf_op jit(solution)/shard_map/ppermute | solution.py:277
  23.4 1.2 %collective-permute-done.8.a_strip = f32[2,8,16,128]{3,2,1,0:T(8,128)S(1)} collective-permute-done((f32[2,8,16,128]{3,2,1,0:T(8,128)S(1)}, f32[2,8,16,128]{3,2,1,0:T(8,128)S(1)}, u32[]{:S(2)}, u32[]{:S(2)}) %collective-permute-start.8) | collective-permute-done | bytes 131104 | tf_op jit(solution)/shard_map/ppermute | solution.py:274
  24.9 3.7 %collective-permute-done.4.b_part = f32[4,8,16,128]{3,2,1,0:T(8,128)S(1)} collective-permute-done((f32[4,8,16,128]{3,2,1,0:T(8,128)S(1)}, f32[4,8,16,128]{3,2,1,0:T(8,128)S(1)}, u32[]{:S(2)}, u32[]{:S(2)}) %collective-permute-start.4) | collective-permute-done | bytes 262176 | tf_op jit(solution)/shard_map/ppermute | solution.py:277
  28.6 1.2 %copy-done = bf16[4,256,512]{2,1,0:T(8,128)(2,1)S(1)} copy-done((bf16[4,256,512]{2,1,0:T(8,128)(2,1)S(1)}, bf16[4,256,512]{2,1,0:T(8,128)(2,1)}, u32[]{:S(2)}) %copy-start) | copy-done | bytes 1048600
  29.9 4.2 %flux.1 = (f32[3,8,16,128]{3,2,1,0:T(8,128)S(1)}, f32[3,8,16,128]{3,2,1,0:T(8,128)S(1)}, f32[16,128]{1,0:T(8,128)S(1)}) custom-call(f32[4,8,16,128]{3,2,1,0:T(8,128)S(1)} %copy-done.1, f32[4,8,16,128]{3,2,1,0:T(8,128)S(1)} %collective-permute-done.part, f32[4,8,16,128]{3,2,1,0:T(8,128)S(1)} %collective-permute-done.1.a_own, ...), custom_call_target="tpu_custom_call" | custom-call | tf_op jit(solution)/shard_map/flux/pallas_call | solution.py:301
  34.0 0.7 %copy-done.4 = f32[3,8,16,128]{3,2,1,0:T(8,128)} copy-done((f32[3,8,16,128]{3,2,1,0:T(8,128)}, f32[3,8,16,128]{3,2,1,0:T(8,128)S(1)}, u32[]{:S(2)}) %copy-start.4) | copy-done | bytes 196632
  34.7 0.7 %copy-done.5 = f32[3,8,16,128]{3,2,1,0:T(8,128)} copy-done((f32[3,8,16,128]{3,2,1,0:T(8,128)}, f32[3,8,16,128]{3,2,1,0:T(8,128)S(1)}, u32[]{:S(2)}) %copy-start.5) | copy-done | bytes 196632
  35.4 2.7 %collective-permute-start.16 = (f32[16,128]{1,0:T(8,128)S(1)}, f32[16,128]{1,0:T(8,128)S(1)}, u32[]{:S(2)}, u32[]{:S(2)}) collective-permute-start(f32[16,128]{1,0:T(8,128)S(1)} %get-tuple-element.7.refs_0_), channel_id=1, source_target_pairs={{0,25},{1,0},{8,1},{9,8},{16,9},{17,16},{24,17},{25,24},{2,27},{3,... | collective-permute-start | bytes 24584 | tf_op jit(solution)/shard_map/ppermute | solution.py:327
  38.5 3.0 %collective-permute-start.13 = (f32[16,128]{1,0:T(8,128)S(1)}, f32[16,128]{1,0:T(8,128)S(1)}, u32[]{:S(2)}, u32[]{:S(2)}) collective-permute-start(f32[16,128]{1,0:T(8,128)S(1)} %get-tuple-element.7.refs_0_), channel_id=1, source_target_pairs={{0,16},{1,17},{8,24},{9,25},{16,0},{17,1},{24,8},{25,9},{2,18},{3,... | collective-permute-start | bytes 24584 | tf_op jit(solution)/shard_map/ppermute | solution.py:327
  41.5 1.2 %collective-permute-start.12 = (f32[16,128]{1,0:T(8,128)S(1)}, f32[16,128]{1,0:T(8,128)S(1)}, u32[]{:S(2)}, u32[]{:S(2)}) collective-permute-start(f32[16,128]{1,0:T(8,128)S(1)} %get-tuple-element.7.refs_0_), channel_id=1, source_target_pairs={{0,9},{1,16},{8,17},{9,24},{16,25},{17,0},{24,1},{25,8},{2,11},{3,... | collective-permute-start | bytes 24584 | tf_op jit(solution)/shard_map/ppermute | solution.py:327
  43.4 1.1 %collective-permute-start.10 = (f32[16,128]{1,0:T(8,128)S(1)}, f32[16,128]{1,0:T(8,128)S(1)}, u32[]{:S(2)}, u32[]{:S(2)}) collective-permute-start(f32[16,128]{1,0:T(8,128)S(1)} %get-tuple-element.7.refs_0_), channel_id=1, source_target_pairs={{0,1},{1,8},{8,9},{9,16},{16,17},{17,24},{24,25},{25,0},{2,3},{3,1... | collective-permute-start | bytes 24584 | tf_op jit(solution)/shard_map/ppermute | solution.py:327
  44.5 2.5 %collective-permute-done.12.refs_3_ = f32[16,128]{1,0:T(8,128)S(1)} collective-permute-done((f32[16,128]{1,0:T(8,128)S(1)}, f32[16,128]{1,0:T(8,128)S(1)}, u32[]{:S(2)}, u32[]{:S(2)}) %collective-permute-start.12) | collective-permute-done | bytes 8224 | tf_op jit(solution)/shard_map/ppermute | solution.py:327
  47.0 1.2 %collective-permute-done.11.refs_2_ = f32[16,128]{1,0:T(8,128)S(1)} collective-permute-done((f32[16,128]{1,0:T(8,128)S(1)}, f32[16,128]{1,0:T(8,128)S(1)}, u32[]{:S(2)}, u32[]{:S(2)}) %collective-permute-start.11) | collective-permute-done | bytes 8224 | tf_op jit(solution)/shard_map/ppermute | solution.py:327
  48.2 1.5 %collective-permute-done.10.refs_1_ = f32[16,128]{1,0:T(8,128)S(1)} collective-permute-done((f32[16,128]{1,0:T(8,128)S(1)}, f32[16,128]{1,0:T(8,128)S(1)}, u32[]{:S(2)}, u32[]{:S(2)}) %collective-permute-start.10) | collective-permute-done | bytes 8224 | tf_op jit(solution)/shard_map/ppermute | solution.py:327
  50.3 2.2 %finish.1 = (f32[3,8,16,128]{3,2,1,0:T(8,128)}, f32[3,8,16,128]{3,2,1,0:T(8,128)}, f32[3,16]{1,0:T(4,128)}, f32[3,16]{1,0:T(4,128)}) custom-call(f32[16,128]{1,0:T(8,128)} %copy-done.6, f32[16,128]{1,0:T(8,128)} %copy-done.13, f32[16,128]{1,0:T(8,128)} %copy-done.12, f32[16,128]{1,0:T(8,128)} %copy-done.11, f32[16,128]{1,0:T(8,128)} %copy-done.10, ...), custom_call_target="tpu_custom_call" | custom-call | tf_op jit(solution)/shard_map/finish/pallas_call | solution.py:330
  (44 shorter events, 2.6 us)
Async XLA Ops:
  0.6 5.7 %copy-start.1 = (f32[4,8,16,128]{3,2,1,0:T(8,128)S(1)}, f32[4,8,16,128]{3,2,1,0:T(8,128)}, u32[]{:S(2)}) copy-start(f32[4,8,16,128]{3,2,1,0:T(8,128)} %own.3) | copy-start | bytes 786436
  0.6 28.0 %copy-start.3 = (bf16[256,512]{1,0:T(8,128)(2,1)S(1)}, bf16[256,512]{1,0:T(8,128)(2,1)}, u32[]{:S(2)}) copy-start(bf16[256,512]{1,0:T(8,128)(2,1)} %constant.8.clone.plane_h) | copy-start | bytes 786436
  2.5 26.2 %copy-start.2 = (bf16[256,512]{1,0:T(8,128)(2,1)S(1)}, bf16[256,512]{1,0:T(8,128)(2,1)}, u32[]{:S(2)}) copy-start(bf16[256,512]{1,0:T(8,128)(2,1)} %constant.9.clone.plane_l) | copy-start | bytes 786436
  2.5 6.7 %collective-permute-start.6 = (f32[8,16,128]{2,1,0:T(8,128)}, f32[8,16,128]{2,1,0:T(8,128)S(1)}, u32[]{:S(2)}, u32[]{:S(2)}) collective-permute-start(f32[8,16,128]{2,1,0:T(8,128)} %edges.1), channel_id=1, source_target_pairs={{0,8},{8,16},{16,24},{24,0},{1,9},{9,17},{17,25},{25,1},{2,10},{10... | collective-permute-start | bytes 196616 | tf_op jit(solution)/shard_map/ppermute | solution.py:288
  4.0 5.2 %collective-permute-start.5 = (f32[8,16,128]{2,1,0:T(8,128)}, f32[8,16,128]{2,1,0:T(8,128)S(1)}, u32[]{:S(2)}, u32[]{:S(2)}) collective-permute-start(f32[8,16,128]{2,1,0:T(8,128)} %edges.1), channel_id=1, source_target_pairs={{0,24},{8,0},{16,8},{24,16},{1,25},{9,1},{17,9},{25,17},{2,26},{10... | collective-permute-start | bytes 196616 | tf_op jit(solution)/shard_map/ppermute | solution.py:289
  6.3 14.6 %collective-permute-start = (f32[4,8,16,128]{3,2,1,0:T(8,128)S(1)}, f32[4,8,16,128]{3,2,1,0:T(8,128)S(1)}, u32[]{:S(2)}, u32[]{:S(2)}) collective-permute-start(f32[4,8,16,128]{3,2,1,0:T(8,128)S(1)} %copy-done.1), channel_id=1, source_target_pairs={{0,1},{1,0},{2,3},{3,2},{4,5},{5,4},{6,7},{7,6},{8,9},{9,8},{10,11... | collective-permute-start | bytes 786440 | tf_op jit(solution)/shard_map/ppermute | solution.py:271
  9.2 6.0 %collective-permute-start.7 = (f32[8,16,128]{2,1,0:T(8,128)S(1)}, f32[8,16,128]{2,1,0:T(8,128)S(1)}, u32[]{:S(2)}, u32[]{:S(2)}) collective-permute-start(f32[8,16,128]{2,1,0:T(8,128)S(1)} %broadcast_select_fusion.s_own), channel_id=1, source_target_pairs={{0,1},{1,0},{2,3},{3,2},{4,5},{5,4},{6,7},{7,6},{8,9},{9,8},{10,11... | collective-permute-start | bytes 196616 | tf_op jit(solution)/shard_map/ppermute | solution.py:271
  15.3 7.7 %collective-permute-start.9 = (f32[2,8,16,128]{3,2,1,0:T(8,128)S(1)}, f32[2,8,16,128]{3,2,1,0:T(8,128)S(1)}, u32[]{:S(2)}, u32[]{:S(2)}) collective-permute-start(f32[2,8,16,128]{3,2,1,0:T(8,128)S(1)} %pad_maximum_fusion), channel_id=1, source_target_pairs={{0,0},{2,4},{4,2},{6,6},{1,1},{3,5},{5,3},{7,7},{8,8},{10,12},{12,... | collective-permute-start | bytes 393224 | tf_op jit(solution)/shard_map/ppermute | solution.py:277
  17.2 7.7 %collective-permute-start.2 = (f32[4,8,16,128]{3,2,1,0:T(8,128)S(1)}, f32[4,8,16,128]{3,2,1,0:T(8,128)S(1)}, u32[]{:S(2)}, u32[]{:S(2)}) collective-permute-start(f32[4,8,16,128]{3,2,1,0:T(8,128)S(1)} %copy-done.1), channel_id=1, source_target_pairs={{0,0},{2,4},{4,2},{6,6},{1,1},{3,5},{5,3},{7,7},{8,8},{10,12},{12,... | collective-permute-start | bytes 786440 | tf_op jit(solution)/shard_map/ppermute | solution.py:277
  20.8 4.0 %collective-permute-start.1 = (f32[4,8,16,128]{3,2,1,0:T(8,128)S(1)}, f32[4,8,16,128]{3,2,1,0:T(8,128)S(1)}, u32[]{:S(2)}, u32[]{:S(2)}) collective-permute-start(f32[4,8,16,128]{3,2,1,0:T(8,128)S(1)} %copy-done.1), channel_id=1, source_target_pairs={{0,2},{2,0},{4,6},{6,4},{1,3},{3,1},{5,7},{7,5},{8,10},{10,8},{12,... | collective-permute-start | bytes 786440 | tf_op jit(solution)/shard_map/ppermute | solution.py:274
  20.9 7.7 %collective-permute-start.4 = (f32[4,8,16,128]{3,2,1,0:T(8,128)S(1)}, f32[4,8,16,128]{3,2,1,0:T(8,128)S(1)}, u32[]{:S(2)}, u32[]{:S(2)}) collective-permute-start(f32[4,8,16,128]{3,2,1,0:T(8,128)S(1)} %collective-permute-done.part), channel_id=1, source_target_pairs={{0,0},{2,4},{4,2},{6,6},{1,1},{3,5},{5,3},{7,7},{8,8},{10,12},{12,... | collective-permute-start | bytes 786440 | tf_op jit(solution)/shard_map/ppermute | solution.py:277
  22.8 5.8 %collective-permute-start.3 = (f32[4,8,16,128]{3,2,1,0:T(8,128)S(1)}, f32[4,8,16,128]{3,2,1,0:T(8,128)S(1)}, u32[]{:S(2)}, u32[]{:S(2)}) collective-permute-start(f32[4,8,16,128]{3,2,1,0:T(8,128)S(1)} %collective-permute-done.part), channel_id=1, source_target_pairs={{0,2},{2,0},{4,6},{6,4},{1,3},{3,1},{5,7},{7,5},{8,10},{10,8},{12,... | collective-permute-start | bytes 786440 | tf_op jit(solution)/shard_map/ppermute | solution.py:274
  22.9 1.7 %collective-permute-start.8 = (f32[2,8,16,128]{3,2,1,0:T(8,128)S(1)}, f32[2,8,16,128]{3,2,1,0:T(8,128)S(1)}, u32[]{:S(2)}, u32[]{:S(2)}) collective-permute-start(f32[2,8,16,128]{3,2,1,0:T(8,128)S(1)} %pad_maximum_fusion), channel_id=1, source_target_pairs={{0,2},{2,0},{4,6},{6,4},{1,3},{3,1},{5,7},{7,5},{8,10},{10,8},{12,... | collective-permute-start | bytes 393224 | tf_op jit(solution)/shard_map/ppermute | solution.py:274
  35.4 14.3 %copy-start.6 = (f32[16,128]{1,0:T(8,128)}, f32[16,128]{1,0:T(8,128)S(1)}, u32[]{:S(2)}) copy-start(f32[16,128]{1,0:T(8,128)S(1)} %get-tuple-element.7.refs_0_) | copy-start | bytes 24580
  35.4 7.3 %collective-permute-start.16 = (f32[16,128]{1,0:T(8,128)S(1)}, f32[16,128]{1,0:T(8,128)S(1)}, u32[]{:S(2)}, u32[]{:S(2)}) collective-permute-start(f32[16,128]{1,0:T(8,128)S(1)} %get-tuple-element.7.refs_0_), channel_id=1, source_target_pairs={{0,25},{1,0},{8,1},{9,8},{16,9},{17,16},{24,17},{25,24},{2,27},{3,... | collective-permute-start | bytes 24584 | tf_op jit(solution)/shard_map/ppermute | solution.py:327
  38.1 5.3 %collective-permute-start.15 = (f32[16,128]{1,0:T(8,128)S(1)}, f32[16,128]{1,0:T(8,128)S(1)}, u32[]{:S(2)}, u32[]{:S(2)}) collective-permute-start(f32[16,128]{1,0:T(8,128)S(1)} %get-tuple-element.7.refs_0_), channel_id=1, source_target_pairs={{0,24},{1,25},{8,0},{9,1},{16,8},{17,9},{24,16},{25,17},{2,26},{3,... | collective-permute-start | bytes 24584 | tf_op jit(solution)/shard_map/ppermute | solution.py:327
  38.5 6.0 %collective-permute-start.14 = (f32[16,128]{1,0:T(8,128)S(1)}, f32[16,128]{1,0:T(8,128)S(1)}, u32[]{:S(2)}, u32[]{:S(2)}) collective-permute-start(f32[16,128]{1,0:T(8,128)S(1)} %get-tuple-element.7.refs_0_), channel_id=1, source_target_pairs={{0,17},{1,24},{8,25},{9,0},{16,1},{17,8},{24,9},{25,16},{2,19},{3,... | collective-permute-start | bytes 24584 | tf_op jit(solution)/shard_map/ppermute | solution.py:327
  38.5 6.0 %collective-permute-start.13 = (f32[16,128]{1,0:T(8,128)S(1)}, f32[16,128]{1,0:T(8,128)S(1)}, u32[]{:S(2)}, u32[]{:S(2)}) collective-permute-start(f32[16,128]{1,0:T(8,128)S(1)} %get-tuple-element.7.refs_0_), channel_id=1, source_target_pairs={{0,16},{1,17},{8,24},{9,25},{16,0},{17,1},{24,8},{25,9},{2,18},{3,... | collective-permute-start | bytes 24584 | tf_op jit(solution)/shard_map/ppermute | solution.py:327
  41.5 5.4 %collective-permute-start.12 = (f32[16,128]{1,0:T(8,128)S(1)}, f32[16,128]{1,0:T(8,128)S(1)}, u32[]{:S(2)}, u32[]{:S(2)}) collective-permute-start(f32[16,128]{1,0:T(8,128)S(1)} %get-tuple-element.7.refs_0_), channel_id=1, source_target_pairs={{0,9},{1,16},{8,17},{9,24},{16,25},{17,0},{24,1},{25,8},{2,11},{3,... | collective-permute-start | bytes 24584 | tf_op jit(solution)/shard_map/ppermute | solution.py:327
  42.7 7.0 %copy-start.7 = (f32[16,128]{1,0:T(8,128)}, f32[16,128]{1,0:T(8,128)S(1)}, u32[]{:S(2)}) copy-start(f32[16,128]{1,0:T(8,128)S(1)} %collective-permute-done.16.refs_7_) | copy-start | bytes 24580
  42.8 5.4 %collective-permute-start.11 = (f32[16,128]{1,0:T(8,128)S(1)}, f32[16,128]{1,0:T(8,128)S(1)}, u32[]{:S(2)}, u32[]{:S(2)}) collective-permute-start(f32[16,128]{1,0:T(8,128)S(1)} %get-tuple-element.7.refs_0_), channel_id=1, source_target_pairs={{0,8},{1,9},{8,16},{9,17},{16,24},{17,25},{24,0},{25,1},{2,10},{3,... | collective-permute-start | bytes 24584 | tf_op jit(solution)/shard_map/ppermute | solution.py:327
  43.4 6.4 %copy-start.8 = (f32[16,128]{1,0:T(8,128)}, f32[16,128]{1,0:T(8,128)S(1)}, u32[]{:S(2)}) copy-start(f32[16,128]{1,0:T(8,128)S(1)} %collective-permute-done.15.refs_6_) | copy-start | bytes 24580
  43.4 6.3 %collective-permute-start.10 = (f32[16,128]{1,0:T(8,128)S(1)}, f32[16,128]{1,0:T(8,128)S(1)}, u32[]{:S(2)}, u32[]{:S(2)}) collective-permute-start(f32[16,128]{1,0:T(8,128)S(1)} %get-tuple-element.7.refs_0_), channel_id=1, source_target_pairs={{0,1},{1,8},{8,9},{9,16},{16,17},{17,24},{24,25},{25,0},{2,3},{3,1... | collective-permute-start | bytes 24584 | tf_op jit(solution)/shard_map/ppermute | solution.py:327
  44.5 5.2 %copy-start.10 = (f32[16,128]{1,0:T(8,128)}, f32[16,128]{1,0:T(8,128)S(1)}, u32[]{:S(2)}) copy-start(f32[16,128]{1,0:T(8,128)S(1)} %collective-permute-done.13.refs_4_) | copy-start | bytes 24580
  (7 other events, 12.7 us)

commit v2 on v1

--- a/solution.py
+++ b/solution.py
@@ -230,14 +230,11 @@
     sums_ref[...] = table
 
 
-def finish_kernel(plane_cells, *refs):
-    sums = refs[:-6]
-    clark, similar, clark_model, similar_model, clark_corr, similar_corr = refs[-6:]
-    rows, width = sums[0].shape
-    table = sums[0][...]
-    for more in sums[1:]:
-        table = table + more[...]
-    table = table / plane_cells
+def finish_kernel(
+    plane_cells, sums, clark, similar, clark_model, similar_model, clark_corr, similar_corr
+):
+    rows, width = sums.shape
+    table = sums[...] / plane_cells
     lane = lane_index((rows, width))
     corr = jnp.zeros((rows, width), jnp.float32)
     for i in range(3):
@@ -283,6 +280,7 @@
         out_shape=jax.ShapeDtypeStruct((layers, rows, width), jnp.float32),
         in_specs=vmem(1),
         out_specs=vmem(1)[0],
+        compiler_params=pltpu.CompilerParams(vmem_limit_bytes=4 * 1024 * 1024),
         name="edges",
     )(fields)
     before = lax.ppermute(edges, "span", [(p, (p + 1) % spans) for p in range(spans)])
@@ -321,19 +319,20 @@
     )
 
     group = spans * streams
-    tables = [sums]
-    for step in range(1, group):
-        tables.append(
-            lax.ppermute(sums, ("span", "stream"), [(g, (g + step) % group) for g in range(group)])
-        )
+    step = 1
+    while step < group:
+        pairs = [(g, g ^ step) for g in range(group)]
+        sums = sums + lax.ppermute(sums, ("span", "stream"), pairs)
+        step *= 2
     corr = jax.ShapeDtypeStruct((3, rows), jnp.float32)
     return pl.pallas_call(
         functools.partial(finish_kernel, float(layers * width * group)),
         out_shape=(block, block, corr, corr),
-        in_specs=vmem(group + 2),
+        in_specs=vmem(3),
         out_specs=tuple(vmem(4)),
+        compiler_params=pltpu.CompilerParams(vmem_limit_bytes=4 * 1024 * 1024),
         name="finish",
-    )(*tables, clark, similar)
+    )(sums, clark, similar)
 
 
 def solution(mesh):

time: 52.7 us -> 47.9 us (0.909)
  starting transfers between devices: 24.1 us -> 17.3 us
  waiting for transfers between devices: 16.3 us -> 21 us
  local copies, waits for them, and re-layouts: 3.16 us -> 1.23 us
  Pallas kernels: 8.16 us -> 7.29 us
    ppermute x7 -> x3, starting transfers between devices: 9.09 us -> 2.23 us  [shards(): sums = sums + lax.ppermute(sums, ('span', 'stream'), pairs)]
    ppermute x7 -> x3, waiting for transfers between devices: 5.2 us -> 9.67 us  [shards(): sums = sums + lax.ppermute(sums, ('span', 'stream'), pairs)]
    unnamed x28 -> x6, local copies, waits for them, and re-layouts: 3.16 us -> 1.23 us
    pallas_call x1, Pallas kernels: 2.16 us -> 1 us  [shards(): pl.pallas_call(functools.partial(finish_kernel, float(layers * width * gr...]
    pallas_call x1, Pallas kernels: 4.19 us -> 5.13 us  [shards(): pl.pallas_call(functools.partial(flux_kernel, walls), out_shape=(block, b...]
    pallas_call x1, Pallas kernels: 1.8 us -> 1.16 us  [shards(): pl.pallas_call(edge_kernel, out_shape=jax.ShapeDtypeStruct((layers, rows,...]
  transfers between devices with their start and end apart: 17 -> 13, of which waited for: 9 -> 9; matrix products, arithmetic and copies ran while one was open for 0% -> 0% of each run, Pallas kernels for 0% -> 0%
where the time goes in v2:
time: 47.9 us; the launch traced here: 47.6 us
  waiting for transfers between devices  21 us (44%)
  starting transfers between devices  17.3 us (36%)
  Pallas kernels  7.29 us (15%)
  local copies, waits for them, and re-layouts  1.23 us (3%)
  between operations  0.74 us (2%)
    ppermute x3, waiting for transfers between devices, shards(): sums = sums + lax.ppermute(sums, ('span', 'stream'), pairs)  9.67 us
    ppermute x3, starting transfers between devices, pair_b(): lax.ppermute(value, 'wall', [(w, min(max((w + 1 ^ 1) - 1, 0), walls - 1))...  7.48 us
    pallas_call x1, Pallas kernels, shards(): pl.pallas_call(functools.partial(flux_kernel, walls), out_shape=(block, b...  5.13 us
    ppermute x2, waiting for transfers between devices, swap(): return lax.ppermute(value, 'stream', [(0, 1), (1, 0)])  4.94 us
    ppermute x3, waiting for transfers between devices, pair_b(): lax.ppermute(value, 'wall', [(w, min(max((w + 1 ^ 1) - 1, 0), walls - 1))...  3.97 us
    ppermute x2, starting transfers between devices, swap(): return lax.ppermute(value, 'stream', [(0, 1), (1, 0)])  3.05 us
    ppermute x1, starting transfers between devices, shards(): lax.ppermute(edges, 'span', [(p, (p - 1) % spans) for p in range(spans)])  2.25 us
    ppermute x3, starting transfers between devices, shards(): sums = sums + lax.ppermute(sums, ('span', 'stream'), pairs)  2.23 us
  transfers between devices with their start and end apart: 13, of which 9 were waited for; matrix products, arithmetic and copies ran while one was open for 0% of the time, Pallas kernels for 0%

profile of v2, /device:TPU:4, one launch (start us, length us, event | category | flops | bytes accessed | tf_op | source)
XLA Modules:
  0.0 47.6 jit_solution(11731971846704916594)
XLA Ops:
  0.6 1.2 %edges.1 = f32[8,16,128]{2,1,0:T(8,128)S(1)} custom-call(f32[4,8,16,128]{3,2,1,0:T(8,128)} %own.3), custom_call_target="tpu_custom_call" | custom-call | tf_op jit(solution)/shard_map/edges/pallas_call | solution.py:278
  1.8 1.6 %collective-permute-start.6 = (f32[8,16,128]{2,1,0:T(8,128)S(1)}, f32[8,16,128]{2,1,0:T(8,128)S(1)}, u32[]{:S(2)}, u32[]{:S(2)}) collective-permute-start(f32[8,16,128]{2,1,0:T(8,128)S(1)} %edges.1), channel_id=1, source_target_pairs={{0,8},{8,16},{16,24},{24,0},{1,9},{9,17},{17,25},{25,1},{2,10},{10... | collective-permute-start | bytes 196616 | tf_op jit(solution)/shard_map/ppermute | solution.py:286
  3.5 2.2 %collective-permute-start.5 = (f32[8,16,128]{2,1,0:T(8,128)S(1)}, f32[8,16,128]{2,1,0:T(8,128)S(1)}, u32[]{:S(2)}, u32[]{:S(2)}) collective-permute-start(f32[8,16,128]{2,1,0:T(8,128)S(1)} %edges.1), channel_id=1, source_target_pairs={{0,24},{8,0},{16,8},{24,16},{1,25},{9,1},{17,9},{25,17},{2,26},{10... | collective-permute-start | bytes 196616 | tf_op jit(solution)/shard_map/ppermute | solution.py:287
  5.7 1.5 %collective-permute-start = (f32[4,8,16,128]{3,2,1,0:T(8,128)}, f32[4,8,16,128]{3,2,1,0:T(8,128)S(1)}, u32[]{:S(2)}, u32[]{:S(2)}) collective-permute-start(f32[4,8,16,128]{3,2,1,0:T(8,128)} %own.3), channel_id=1, source_target_pairs={{0,1},{1,0},{2,3},{3,2},{4,5},{5,4},{6,7},{7,6},{8,9},{9,8},{10,11... | collective-permute-start | bytes 786440 | tf_op jit(solution)/shard_map/ppermute | solution.py:268
  7.2 1.1 %collective-permute-done.6 = f32[8,16,128]{2,1,0:T(8,128)S(1)} collective-permute-done((f32[8,16,128]{2,1,0:T(8,128)S(1)}, f32[8,16,128]{2,1,0:T(8,128)S(1)}, u32[]{:S(2)}, u32[]{:S(2)}) %collective-permute-start.6) | collective-permute-done | bytes 65568 | tf_op jit(solution)/shard_map/ppermute | solution.py:286
  8.3 0.1 collective-permute-done.5
  8.4 1.6 %collective-permute-start.7 = (f32[8,16,128]{2,1,0:T(8,128)S(1)}, f32[8,16,128]{2,1,0:T(8,128)S(1)}, u32[]{:S(2)}, u32[]{:S(2)}) collective-permute-start(f32[8,16,128]{2,1,0:T(8,128)S(1)} %broadcast_select_fusion.s_own), channel_id=1, source_target_pairs={{0,1},{1,0},{2,3},{3,2},{4,5},{5,4},{6,7},{7,6},{8,9},{9,8},{10,11... | collective-permute-start | bytes 196616 | tf_op jit(solution)/shard_map/ppermute | solution.py:268
  10.0 4.9 %collective-permute-done.7.s_part = f32[8,16,128]{2,1,0:T(8,128)S(1)} collective-permute-done((f32[8,16,128]{2,1,0:T(8,128)S(1)}, f32[8,16,128]{2,1,0:T(8,128)S(1)}, u32[]{:S(2)}, u32[]{:S(2)}) %collective-permute-start.7) | collective-permute-done | bytes 65568 | tf_op jit(solution)/shard_map/ppermute | solution.py:268
  14.9 1.9 %collective-permute-start.9 = (f32[2,8,16,128]{3,2,1,0:T(8,128)S(1)}, f32[2,8,16,128]{3,2,1,0:T(8,128)S(1)}, u32[]{:S(2)}, u32[]{:S(2)}) collective-permute-start(f32[2,8,16,128]{3,2,1,0:T(8,128)S(1)} %pad_maximum_fusion), channel_id=1, source_target_pairs={{0,0},{2,4},{4,2},{6,6},{1,1},{3,5},{5,3},{7,7},{8,8},{10,12},{12,... | collective-permute-start | bytes 393224 | tf_op jit(solution)/shard_map/ppermute | solution.py:274
  16.9 3.6 %collective-permute-start.2 = (f32[4,8,16,128]{3,2,1,0:T(8,128)}, f32[4,8,16,128]{3,2,1,0:T(8,128)S(1)}, u32[]{:S(2)}, u32[]{:S(2)}) collective-permute-start(f32[4,8,16,128]{3,2,1,0:T(8,128)} %own.3), channel_id=1, source_target_pairs={{0,0},{2,4},{4,2},{6,6},{1,1},{3,5},{5,3},{7,7},{8,8},{10,12},{12,... | collective-permute-start | bytes 786440 | tf_op jit(solution)/shard_map/ppermute | solution.py:274
  20.5 0.1 collective-permute-start.1
  20.6 1.9 %collective-permute-start.4 = (f32[4,8,16,128]{3,2,1,0:T(8,128)S(1)}, f32[4,8,16,128]{3,2,1,0:T(8,128)S(1)}, u32[]{:S(2)}, u32[]{:S(2)}) collective-permute-start(f32[4,8,16,128]{3,2,1,0:T(8,128)S(1)} %collective-permute-done.part), channel_id=1, source_target_pairs={{0,0},{2,4},{4,2},{6,6},{1,1},{3,5},{5,3},{7,7},{8,8},{10,12},{12,... | collective-permute-start | bytes 786440 | tf_op jit(solution)/shard_map/ppermute | solution.py:274
  22.6 0.5 %collective-permute-start.8 = (f32[2,8,16,128]{3,2,1,0:T(8,128)S(1)}, f32[2,8,16,128]{3,2,1,0:T(8,128)S(1)}, u32[]{:S(2)}, u32[]{:S(2)}) collective-permute-start(f32[2,8,16,128]{3,2,1,0:T(8,128)S(1)} %pad_maximum_fusion), channel_id=1, source_target_pairs={{0,2},{2,0},{4,6},{6,4},{1,3},{3,1},{5,7},{7,5},{8,10},{10,8},{12,... | collective-permute-start | bytes 393224 | tf_op jit(solution)/shard_map/ppermute | solution.py:271
  23.1 1.2 %collective-permute-done.8.a_strip = f32[2,8,16,128]{3,2,1,0:T(8,128)S(1)} collective-permute-done((f32[2,8,16,128]{3,2,1,0:T(8,128)S(1)}, f32[2,8,16,128]{3,2,1,0:T(8,128)S(1)}, u32[]{:S(2)}, u32[]{:S(2)}) %collective-permute-start.8) | collective-permute-done | bytes 131104 | tf_op jit(solution)/shard_map/ppermute | solution.py:271
  24.3 0.4 collective-permute-done.2.b_own
  24.8 3.5 %collective-permute-done.4.b_part = f32[4,8,16,128]{3,2,1,0:T(8,128)S(1)} collective-permute-done((f32[4,8,16,128]{3,2,1,0:T(8,128)S(1)}, f32[4,8,16,128]{3,2,1,0:T(8,128)S(1)}, u32[]{:S(2)}, u32[]{:S(2)}) %collective-permute-start.4) | collective-permute-done | bytes 262176 | tf_op jit(solution)/shard_map/ppermute | solution.py:274
  28.3 1.2 %copy-done = bf16[4,256,512]{2,1,0:T(8,128)(2,1)S(1)} copy-done((bf16[4,256,512]{2,1,0:T(8,128)(2,1)S(1)}, bf16[4,256,512]{2,1,0:T(8,128)(2,1)}, u32[]{:S(2)}) %copy-start) | copy-done | bytes 1048600
  29.5 5.1 %flux.1 = (f32[3,8,16,128]{3,2,1,0:T(8,128)S(1)}, f32[3,8,16,128]{3,2,1,0:T(8,128)S(1)}, f32[16,128]{1,0:T(8,128)S(1)}) custom-call(f32[4,8,16,128]{3,2,1,0:T(8,128)} %own.3, f32[4,8,16,128]{3,2,1,0:T(8,128)S(1)} %collective-permute-done.part, f32[4,8,16,128]{3,2,1,0:T(8,128)S(1)} %collective-permute-done.1.a_own, ...), custom_call_target="tpu_custom_call" | custom-call | tf_op jit(solution)/shard_map/flux/pallas_call | solution.py:299
  34.7 1.5 %collective-permute-start.10 = (f32[16,128]{1,0:T(8,128)S(1)}, f32[16,128]{1,0:T(8,128)S(1)}, u32[]{:S(2)}, u32[]{:S(2)}) collective-permute-start(f32[16,128]{1,0:T(8,128)S(1)} %get-tuple-element.7), channel_id=1, source_target_pairs={{0,1},{1,0},{8,9},{9,8},{16,17},{17,16},{24,25},{25,24},{2,3},{3,2... | collective-permute-start | bytes 24584 | tf_op jit(solution)/shard_map/ppermute | solution.py:325
  36.2 2.2 %collective-permute-done.10 = f32[16,128]{1,0:T(8,128)S(1)} collective-permute-done((f32[16,128]{1,0:T(8,128)S(1)}, f32[16,128]{1,0:T(8,128)S(1)}, u32[]{:S(2)}, u32[]{:S(2)}) %collective-permute-start.10) | collective-permute-done | bytes 8224 | tf_op jit(solution)/shard_map/ppermute | solution.py:325
  38.4 3.6 %collective-permute-done.11 = f32[16,128]{1,0:T(8,128)S(1)} collective-permute-done((f32[16,128]{1,0:T(8,128)S(1)}, f32[16,128]{1,0:T(8,128)S(1)}, u32[]{:S(2)}, u32[]{:S(2)}) %collective-permute-start.11) | collective-permute-done | bytes 8224 | tf_op jit(solution)/shard_map/ppermute | solution.py:325
  42.0 0.7 %collective-permute-start.12 = (f32[16,128]{1,0:T(8,128)S(1)}, f32[16,128]{1,0:T(8,128)S(1)}, u32[]{:S(2)}, u32[]{:S(2)}) collective-permute-start(f32[16,128]{1,0:T(8,128)S(1)} %add.10), channel_id=1, source_target_pairs={{0,16},{1,17},{8,24},{9,25},{16,0},{17,1},{24,8},{25,9},{2,18},{3,... | collective-permute-start | bytes 24584 | tf_op jit(solution)/shard_map/ppermute | solution.py:325
  42.7 3.9 %collective-permute-done.12 = f32[16,128]{1,0:T(8,128)S(1)} collective-permute-done((f32[16,128]{1,0:T(8,128)S(1)}, f32[16,128]{1,0:T(8,128)S(1)}, u32[]{:S(2)}, u32[]{:S(2)}) %collective-permute-start.12) | collective-permute-done | bytes 8224 | tf_op jit(solution)/shard_map/ppermute | solution.py:325
  46.6 1.0 %finish.1 = (f32[3,8,16,128]{3,2,1,0:T(8,128)}, f32[3,8,16,128]{3,2,1,0:T(8,128)}, f32[3,16]{1,0:T(4,128)}, f32[3,16]{1,0:T(4,128)}) custom-call(f32[16,128]{1,0:T(8,128)S(1)} %add.11.sums, f32[3,8,16,128]{3,2,1,0:T(8,128)S(1)} %get-tuple-element.8.clark, f32[3,8,16,128]{3,2,1,0:T(8,128)S(1)} %get-tuple-element.9.similar), custom_call_target="tpu_custom_call" | custom-call | tf_op jit(solution)/shard_map/finish/pallas_call | solution.py:328
  (17 shorter events, 0.1 us)
Async XLA Ops:
  0.6 27.7 %copy-start.2 = (bf16[256,512]{1,0:T(8,128)(2,1)S(1)}, bf16[256,512]{1,0:T(8,128)(2,1)}, u32[]{:S(2)}) copy-start(bf16[256,512]{1,0:T(8,128)(2,1)} %constant.8.clone.plane_h) | copy-start | bytes 786436
  1.8 26.5 %copy-start.1 = (bf16[256,512]{1,0:T(8,128)(2,1)S(1)}, bf16[256,512]{1,0:T(8,128)(2,1)}, u32[]{:S(2)}) copy-start(bf16[256,512]{1,0:T(8,128)(2,1)} %constant.9.clone.plane_l) | copy-start | bytes 786436
  1.8 6.5 %collective-permute-start.6 = (f32[8,16,128]{2,1,0:T(8,128)S(1)}, f32[8,16,128]{2,1,0:T(8,128)S(1)}, u32[]{:S(2)}, u32[]{:S(2)}) collective-permute-start(f32[8,16,128]{2,1,0:T(8,128)S(1)} %edges.1), channel_id=1, source_target_pairs={{0,8},{8,16},{16,24},{24,0},{1,9},{9,17},{17,25},{25,1},{2,10},{10... | collective-permute-start | bytes 196616 | tf_op jit(solution)/shard_map/ppermute | solution.py:286
  3.5 5.0 %collective-permute-start.5 = (f32[8,16,128]{2,1,0:T(8,128)S(1)}, f32[8,16,128]{2,1,0:T(8,128)S(1)}, u32[]{:S(2)}, u32[]{:S(2)}) collective-permute-start(f32[8,16,128]{2,1,0:T(8,128)S(1)} %edges.1), channel_id=1, source_target_pairs={{0,24},{8,0},{16,8},{24,16},{1,25},{9,1},{17,9},{25,17},{2,26},{10... | collective-permute-start | bytes 196616 | tf_op jit(solution)/shard_map/ppermute | solution.py:287
  5.7 14.9 %collective-permute-start = (f32[4,8,16,128]{3,2,1,0:T(8,128)}, f32[4,8,16,128]{3,2,1,0:T(8,128)S(1)}, u32[]{:S(2)}, u32[]{:S(2)}) collective-permute-start(f32[4,8,16,128]{3,2,1,0:T(8,128)} %own.3), channel_id=1, source_target_pairs={{0,1},{1,0},{2,3},{3,2},{4,5},{5,4},{6,7},{7,6},{8,9},{9,8},{10,11... | collective-permute-start | bytes 786440 | tf_op jit(solution)/shard_map/ppermute | solution.py:268
  8.4 6.5 %collective-permute-start.7 = (f32[8,16,128]{2,1,0:T(8,128)S(1)}, f32[8,16,128]{2,1,0:T(8,128)S(1)}, u32[]{:S(2)}, u32[]{:S(2)}) collective-permute-start(f32[8,16,128]{2,1,0:T(8,128)S(1)} %broadcast_select_fusion.s_own), channel_id=1, source_target_pairs={{0,1},{1,0},{2,3},{3,2},{4,5},{5,4},{6,7},{7,6},{8,9},{9,8},{10,11... | collective-permute-start | bytes 196616 | tf_op jit(solution)/shard_map/ppermute | solution.py:268
  14.9 7.7 %collective-permute-start.9 = (f32[2,8,16,128]{3,2,1,0:T(8,128)S(1)}, f32[2,8,16,128]{3,2,1,0:T(8,128)S(1)}, u32[]{:S(2)}, u32[]{:S(2)}) collective-permute-start(f32[2,8,16,128]{3,2,1,0:T(8,128)S(1)} %pad_maximum_fusion), channel_id=1, source_target_pairs={{0,0},{2,4},{4,2},{6,6},{1,1},{3,5},{5,3},{7,7},{8,8},{10,12},{12,... | collective-permute-start | bytes 393224 | tf_op jit(solution)/shard_map/ppermute | solution.py:274
  16.9 7.9 %collective-permute-start.2 = (f32[4,8,16,128]{3,2,1,0:T(8,128)}, f32[4,8,16,128]{3,2,1,0:T(8,128)S(1)}, u32[]{:S(2)}, u32[]{:S(2)}) collective-permute-start(f32[4,8,16,128]{3,2,1,0:T(8,128)} %own.3), channel_id=1, source_target_pairs={{0,0},{2,4},{4,2},{6,6},{1,1},{3,5},{5,3},{7,7},{8,8},{10,12},{12,... | collective-permute-start | bytes 786440 | tf_op jit(solution)/shard_map/ppermute | solution.py:274
  20.5 4.3 %collective-permute-start.1 = (f32[4,8,16,128]{3,2,1,0:T(8,128)}, f32[4,8,16,128]{3,2,1,0:T(8,128)S(1)}, u32[]{:S(2)}, u32[]{:S(2)}) collective-permute-start(f32[4,8,16,128]{3,2,1,0:T(8,128)} %own.3), channel_id=1, source_target_pairs={{0,2},{2,0},{4,6},{6,4},{1,3},{3,1},{5,7},{7,5},{8,10},{10,8},{12,... | collective-permute-start | bytes 786440 | tf_op jit(solution)/shard_map/ppermute | solution.py:271
  20.6 7.7 %collective-permute-start.4 = (f32[4,8,16,128]{3,2,1,0:T(8,128)S(1)}, f32[4,8,16,128]{3,2,1,0:T(8,128)S(1)}, u32[]{:S(2)}, u32[]{:S(2)}) collective-permute-start(f32[4,8,16,128]{3,2,1,0:T(8,128)S(1)} %collective-permute-done.part), channel_id=1, source_target_pairs={{0,0},{2,4},{4,2},{6,6},{1,1},{3,5},{5,3},{7,7},{8,8},{10,12},{12,... | collective-permute-start | bytes 786440 | tf_op jit(solution)/shard_map/ppermute | solution.py:274
  22.5 5.8 %collective-permute-start.3 = (f32[4,8,16,128]{3,2,1,0:T(8,128)S(1)}, f32[4,8,16,128]{3,2,1,0:T(8,128)S(1)}, u32[]{:S(2)}, u32[]{:S(2)}) collective-permute-start(f32[4,8,16,128]{3,2,1,0:T(8,128)S(1)} %collective-permute-done.part), channel_id=1, source_target_pairs={{0,2},{2,0},{4,6},{6,4},{1,3},{3,1},{5,7},{7,5},{8,10},{10,8},{12,... | collective-permute-start | bytes 786440 | tf_op jit(solution)/shard_map/ppermute | solution.py:271
  22.6 1.7 %collective-permute-start.8 = (f32[2,8,16,128]{3,2,1,0:T(8,128)S(1)}, f32[2,8,16,128]{3,2,1,0:T(8,128)S(1)}, u32[]{:S(2)}, u32[]{:S(2)}) collective-permute-start(f32[2,8,16,128]{3,2,1,0:T(8,128)S(1)} %pad_maximum_fusion), channel_id=1, source_target_pairs={{0,2},{2,0},{4,6},{6,4},{1,3},{3,1},{5,7},{7,5},{8,10},{10,8},{12,... | collective-permute-start | bytes 393224 | tf_op jit(solution)/shard_map/ppermute | solution.py:271
  28.3 1.2 %copy-start = (bf16[4,256,512]{2,1,0:T(8,128)(2,1)S(1)}, bf16[4,256,512]{2,1,0:T(8,128)(2,1)}, u32[]{:S(2)}) copy-start(bf16[4,256,512]{2,1,0:T(8,128)(2,1)} %constant.10.clone.span_w) | copy-start | bytes 3145732
  34.7 3.7 %collective-permute-start.10 = (f32[16,128]{1,0:T(8,128)S(1)}, f32[16,128]{1,0:T(8,128)S(1)}, u32[]{:S(2)}, u32[]{:S(2)}) collective-permute-start(f32[16,128]{1,0:T(8,128)S(1)} %get-tuple-element.7), channel_id=1, source_target_pairs={{0,1},{1,0},{8,9},{9,8},{16,17},{17,16},{24,25},{25,24},{2,3},{3,2... | collective-permute-start | bytes 24584 | tf_op jit(solution)/shard_map/ppermute | solution.py:325
  38.4 3.7 %collective-permute-start.11 = (f32[16,128]{1,0:T(8,128)S(1)}, f32[16,128]{1,0:T(8,128)S(1)}, u32[]{:S(2)}, u32[]{:S(2)}) collective-permute-start(f32[16,128]{1,0:T(8,128)S(1)} %add.9), channel_id=1, source_target_pairs={{0,8},{1,9},{8,0},{9,1},{16,24},{17,25},{24,16},{25,17},{2,10},{3,... | collective-permute-start | bytes 24584 | tf_op jit(solution)/shard_map/ppermute | solution.py:325
  42.0 4.5 %collective-permute-start.12 = (f32[16,128]{1,0:T(8,128)S(1)}, f32[16,128]{1,0:T(8,128)S(1)}, u32[]{:S(2)}, u32[]{:S(2)}) collective-permute-start(f32[16,128]{1,0:T(8,128)S(1)} %add.10), channel_id=1, source_target_pairs={{0,16},{1,17},{8,24},{9,25},{16,0},{17,1},{24,8},{25,9},{2,18},{3,... | collective-permute-start | bytes 24584 | tf_op jit(solution)/shard_map/ppermute | solution.py:325

commit v3 on v2

--- a/solution.py
+++ b/solution.py
@@ -233,8 +233,8 @@
 def finish_kernel(
     plane_cells, sums, clark, similar, clark_model, similar_model, clark_corr, similar_corr
 ):
-    rows, width = sums.shape
-    table = sums[...] / plane_cells
+    _, rows, width = sums.shape
+    table = jnp.sum(sums[...], axis=0) / plane_cells
     lane = lane_index((rows, width))
     corr = jnp.zeros((rows, width), jnp.float32)
     for i in range(3):
@@ -319,11 +319,8 @@
     )
 
     group = spans * streams
-    step = 1
-    while step < group:
-        pairs = [(g, g ^ step) for g in range(group)]
-        sums = sums + lax.ppermute(sums, ("span", "stream"), pairs)
-        step *= 2
+    tables = jnp.broadcast_to(sums[None], (group, rows, width))
+    tables = lax.all_to_all(tables, ("span", "stream"), 0, 0)
     corr = jax.ShapeDtypeStruct((3, rows), jnp.float32)
     return pl.pallas_call(
         functools.partial(finish_kernel, float(layers * width * group)),
@@ -332,7 +329,7 @@
         out_specs=tuple(vmem(4)),
         compiler_params=pltpu.CompilerParams(vmem_limit_bytes=4 * 1024 * 1024),
         name="finish",
-    )(sums, clark, similar)
+    )(tables, clark, similar)
 
 
 def solution(mesh):

time: 47.9 us -> 47.1 us (0.983); the launches traced: 47.6 us -> 46.3 us
  blocking collectives: 0 us -> 10.6 us
  waiting for transfers between devices: 21 us -> 11.3 us
  starting transfers between devices: 17.3 us -> 15 us
    all_to_all x0 -> x1, blocking collectives: none -> 10.6 us  [shards(): tables = lax.all_to_all(tables, ('span', 'stream'), 0, 0)]
    ppermute x3 -> x0, waiting for transfers between devices: 9.67 us -> none  [shards(): sums = sums + lax.ppermute(sums, ('span', 'stream'), pairs)]
    ppermute x3 -> x0, starting transfers between devices: 2.23 us -> none  [shards(): sums = sums + lax.ppermute(sums, ('span', 'stream'), pairs)]
  transfers between devices with their start and end apart: 13 -> 10, of which waited for: 9 -> 6; matrix products, arithmetic and copies ran while one was open for 0% -> 0% of each run, Pallas kernels for 0% -> 0%
where the time goes in v3:
time: 47.1 us; the launch traced here: 46.3 us
  starting transfers between devices  15 us (32%)
  waiting for transfers between devices  11.3 us (24%)
  blocking collectives  10.6 us (23%)
  Pallas kernels  7.3 us (15%)
  local copies, waits for them, and re-layouts  1.24 us (3%)
  between operations  0.74 us (2%)
    all_to_all x1, blocking collectives, shards(): tables = lax.all_to_all(tables, ('span', 'stream'), 0, 0)  10.6 us
    ppermute x3, starting transfers between devices, pair_b(): lax.ppermute(value, 'wall', [(w, min(max((w + 1 ^ 1) - 1, 0), walls - 1))...  7.48 us
    pallas_call x1, Pallas kernels, shards(): pl.pallas_call(functools.partial(flux_kernel, walls), out_shape=(block, b...  5.13 us
    ppermute x2, waiting for transfers between devices, swap(): return lax.ppermute(value, 'stream', [(0, 1), (1, 0)])  4.94 us
    ppermute x3, waiting for transfers between devices, pair_b(): lax.ppermute(value, 'wall', [(w, min(max((w + 1 ^ 1) - 1, 0), walls - 1))...  3.97 us
    ppermute x2, starting transfers between devices, swap(): return lax.ppermute(value, 'stream', [(0, 1), (1, 0)])  3.05 us
    ppermute x1, starting transfers between devices, shards(): lax.ppermute(edges, 'span', [(p, (p - 1) % spans) for p in range(spans)])  2.25 us
    ppermute x1, starting transfers between devices, shards(): lax.ppermute(edges, 'span', [(p, (p + 1) % spans) for p in range(spans)])  1.63 us
  transfers between devices with their start and end apart: 10, of which 6 were waited for; matrix products, arithmetic and copies ran while one was open for 0% of the time, Pallas kernels for 0%

profile of v3, /device:TPU:4, one launch (start us, length us, event | category | flops | bytes accessed | tf_op | source)
XLA Modules:
  0.0 46.3 jit_solution(13546259504092136278)
XLA Ops:
  0.6 0.0 copy-start.2
  0.6 1.2 %edges.1 = f32[8,16,128]{2,1,0:T(8,128)S(1)} custom-call(f32[4,8,16,128]{3,2,1,0:T(8,128)} %own.3), custom_call_target="tpu_custom_call" | custom-call | tf_op jit(solution)/shard_map/edges/pallas_call | solution.py:278
  1.8 0.0 copy-start.1
  1.8 1.6 %collective-permute-start.6 = (f32[8,16,128]{2,1,0:T(8,128)S(1)}, f32[8,16,128]{2,1,0:T(8,128)S(1)}, u32[]{:S(2)}, u32[]{:S(2)}) collective-permute-start(f32[8,16,128]{2,1,0:T(8,128)S(1)} %edges.1), channel_id=1, source_target_pairs={{0,8},{8,16},{16,24},{24,0},{1,9},{9,17},{17,25},{25,1},{2,10},{10... | collective-permute-start | bytes 196616 | tf_op jit(solution)/shard_map/ppermute | solution.py:286
  3.5 2.2 %collective-permute-start.5 = (f32[8,16,128]{2,1,0:T(8,128)S(1)}, f32[8,16,128]{2,1,0:T(8,128)S(1)}, u32[]{:S(2)}, u32[]{:S(2)}) collective-permute-start(f32[8,16,128]{2,1,0:T(8,128)S(1)} %edges.1), channel_id=1, source_target_pairs={{0,24},{8,0},{16,8},{24,16},{1,25},{9,1},{17,9},{25,17},{2,26},{10... | collective-permute-start | bytes 196616 | tf_op jit(solution)/shard_map/ppermute | solution.py:287
  5.7 1.5 %collective-permute-start = (f32[4,8,16,128]{3,2,1,0:T(8,128)}, f32[4,8,16,128]{3,2,1,0:T(8,128)S(1)}, u32[]{:S(2)}, u32[]{:S(2)}) collective-permute-start(f32[4,8,16,128]{3,2,1,0:T(8,128)} %own.3), channel_id=1, source_target_pairs={{0,1},{1,0},{2,3},{3,2},{4,5},{5,4},{6,7},{7,6},{8,9},{9,8},{10,11... | collective-permute-start | bytes 786440 | tf_op jit(solution)/shard_map/ppermute | solution.py:268
  7.2 1.1 %collective-permute-done.6 = f32[8,16,128]{2,1,0:T(8,128)S(1)} collective-permute-done((f32[8,16,128]{2,1,0:T(8,128)S(1)}, f32[8,16,128]{2,1,0:T(8,128)S(1)}, u32[]{:S(2)}, u32[]{:S(2)}) %collective-permute-start.6) | collective-permute-done | bytes 65568 | tf_op jit(solution)/shard_map/ppermute | solution.py:286
  8.3 0.1 collective-permute-done.5
  8.4 1.6 %collective-permute-start.7 = (f32[8,16,128]{2,1,0:T(8,128)S(1)}, f32[8,16,128]{2,1,0:T(8,128)S(1)}, u32[]{:S(2)}, u32[]{:S(2)}) collective-permute-start(f32[8,16,128]{2,1,0:T(8,128)S(1)} %broadcast_select_fusion.s_own), channel_id=1, source_target_pairs={{0,1},{1,0},{2,3},{3,2},{4,5},{5,4},{6,7},{7,6},{8,9},{9,8},{10,11... | collective-permute-start | bytes 196616 | tf_op jit(solution)/shard_map/ppermute | solution.py:268
  10.0 4.9 %collective-permute-done.7.s_part = f32[8,16,128]{2,1,0:T(8,128)S(1)} collective-permute-done((f32[8,16,128]{2,1,0:T(8,128)S(1)}, f32[8,16,128]{2,1,0:T(8,128)S(1)}, u32[]{:S(2)}, u32[]{:S(2)}) %collective-permute-start.7) | collective-permute-done | bytes 65568 | tf_op jit(solution)/shard_map/ppermute | solution.py:268
  14.9 1.9 %collective-permute-start.9 = (f32[2,8,16,128]{3,2,1,0:T(8,128)S(1)}, f32[2,8,16,128]{3,2,1,0:T(8,128)S(1)}, u32[]{:S(2)}, u32[]{:S(2)}) collective-permute-start(f32[2,8,16,128]{3,2,1,0:T(8,128)S(1)} %pad_maximum_fusion), channel_id=1, source_target_pairs={{0,0},{2,4},{4,2},{6,6},{1,1},{3,5},{5,3},{7,7},{8,8},{10,12},{12,... | collective-permute-start | bytes 393224 | tf_op jit(solution)/shard_map/ppermute | solution.py:274
  16.9 3.6 %collective-permute-start.2 = (f32[4,8,16,128]{3,2,1,0:T(8,128)}, f32[4,8,16,128]{3,2,1,0:T(8,128)S(1)}, u32[]{:S(2)}, u32[]{:S(2)}) collective-permute-start(f32[4,8,16,128]{3,2,1,0:T(8,128)} %own.3), channel_id=1, source_target_pairs={{0,0},{2,4},{4,2},{6,6},{1,1},{3,5},{5,3},{7,7},{8,8},{10,12},{12,... | collective-permute-start | bytes 786440 | tf_op jit(solution)/shard_map/ppermute | solution.py:274
  20.5 0.1 collective-permute-start.1
  20.6 1.9 %collective-permute-start.4 = (f32[4,8,16,128]{3,2,1,0:T(8,128)S(1)}, f32[4,8,16,128]{3,2,1,0:T(8,128)S(1)}, u32[]{:S(2)}, u32[]{:S(2)}) collective-permute-start(f32[4,8,16,128]{3,2,1,0:T(8,128)S(1)} %collective-permute-done.part), channel_id=1, source_target_pairs={{0,0},{2,4},{4,2},{6,6},{1,1},{3,5},{5,3},{7,7},{8,8},{10,12},{12,... | collective-permute-start | bytes 786440 | tf_op jit(solution)/shard_map/ppermute | solution.py:274
  22.5 0.1 collective-permute-start.3
  22.6 0.5 %collective-permute-start.8 = (f32[2,8,16,128]{3,2,1,0:T(8,128)S(1)}, f32[2,8,16,128]{3,2,1,0:T(8,128)S(1)}, u32[]{:S(2)}, u32[]{:S(2)}) collective-permute-start(f32[2,8,16,128]{3,2,1,0:T(8,128)S(1)} %pad_maximum_fusion), channel_id=1, source_target_pairs={{0,2},{2,0},{4,6},{6,4},{1,3},{3,1},{5,7},{7,5},{8,10},{10,8},{12,... | collective-permute-start | bytes 393224 | tf_op jit(solution)/shard_map/ppermute | solution.py:271
  23.1 1.2 %collective-permute-done.8.a_strip = f32[2,8,16,128]{3,2,1,0:T(8,128)S(1)} collective-permute-done((f32[2,8,16,128]{3,2,1,0:T(8,128)S(1)}, f32[2,8,16,128]{3,2,1,0:T(8,128)S(1)}, u32[]{:S(2)}, u32[]{:S(2)}) %collective-permute-start.8) | collective-permute-done | bytes 131104 | tf_op jit(solution)/shard_map/ppermute | solution.py:271
  24.3 0.4 collective-permute-done.2.b_own
  24.8 3.5 %collective-permute-done.4.b_part = f32[4,8,16,128]{3,2,1,0:T(8,128)S(1)} collective-permute-done((f32[4,8,16,128]{3,2,1,0:T(8,128)S(1)}, f32[4,8,16,128]{3,2,1,0:T(8,128)S(1)}, u32[]{:S(2)}, u32[]{:S(2)}) %collective-permute-start.4) | collective-permute-done | bytes 262176 | tf_op jit(solution)/shard_map/ppermute | solution.py:274
  28.3 0.0 copy-start
  28.3 1.2 %copy-done = bf16[4,256,512]{2,1,0:T(8,128)(2,1)S(1)} copy-done((bf16[4,256,512]{2,1,0:T(8,128)(2,1)S(1)}, bf16[4,256,512]{2,1,0:T(8,128)(2,1)}, u32[]{:S(2)}) %copy-start) | copy-done | bytes 1048600
  29.5 5.1 %flux.1 = (f32[3,8,16,128]{3,2,1,0:T(8,128)S(1)}, f32[3,8,16,128]{3,2,1,0:T(8,128)S(1)}, f32[16,128]{1,0:T(8,128)S(1)}) custom-call(f32[4,8,16,128]{3,2,1,0:T(8,128)} %own.3, f32[4,8,16,128]{3,2,1,0:T(8,128)S(1)} %collective-permute-done.part, f32[4,8,16,128]{3,2,1,0:T(8,128)S(1)} %collective-permute-done.1.a_own, ...), custom_call_target="tpu_custom_call" | custom-call | tf_op jit(solution)/shard_map/flux/pallas_call | solution.py:299
  34.7 10.6 %all_to_all.5.sums = f32[8,16,128]{2,1,0:T(8,128)S(1)} all-to-all(f32[8,16,128]{2,1,0:T(8,128)S(1)} %broadcast_in_dim.2), channel_id=1, replica_groups=mesh['span'=4,'wall'=4,'stream'=2] {'span','stream'}, dimensions={0} | all-to-all | bytes 131072 | tf_op jit(solution)/shard_map/all_to_all | solution.py:323
  45.3 1.0 %finish.1 = (f32[3,8,16,128]{3,2,1,0:T(8,128)}, f32[3,8,16,128]{3,2,1,0:T(8,128)}, f32[3,16]{1,0:T(4,128)}, f32[3,16]{1,0:T(4,128)}) custom-call(f32[8,16,128]{2,1,0:T(8,128)S(1)} %all_to_all.5.sums, f32[3,8,16,128]{3,2,1,0:T(8,128)S(1)} %get-tuple-element.8.clark, f32[3,8,16,128]{3,2,1,0:T(8,128)S(1)} %get-tuple-element.9.similar), custom_call_target="tpu_custom_call" | custom-call | tf_op jit(solution)/shard_map/finish/pallas_call | solution.py:325
  (10 shorter events, 0.1 us)
Async XLA Ops:
  0.6 27.7 %copy-start.2 = (bf16[256,512]{1,0:T(8,128)(2,1)S(1)}, bf16[256,512]{1,0:T(8,128)(2,1)}, u32[]{:S(2)}) copy-start(bf16[256,512]{1,0:T(8,128)(2,1)} %constant.8.clone.plane_h) | copy-start | bytes 786436
  1.8 26.5 %copy-start.1 = (bf16[256,512]{1,0:T(8,128)(2,1)S(1)}, bf16[256,512]{1,0:T(8,128)(2,1)}, u32[]{:S(2)}) copy-start(bf16[256,512]{1,0:T(8,128)(2,1)} %constant.9.clone.plane_l) | copy-start | bytes 786436
  1.8 6.5 %collective-permute-start.6 = (f32[8,16,128]{2,1,0:T(8,128)S(1)}, f32[8,16,128]{2,1,0:T(8,128)S(1)}, u32[]{:S(2)}, u32[]{:S(2)}) collective-permute-start(f32[8,16,128]{2,1,0:T(8,128)S(1)} %edges.1), channel_id=1, source_target_pairs={{0,8},{8,16},{16,24},{24,0},{1,9},{9,17},{17,25},{25,1},{2,10},{10... | collective-permute-start | bytes 196616 | tf_op jit(solution)/shard_map/ppermute | solution.py:286
  3.5 5.0 %collective-permute-start.5 = (f32[8,16,128]{2,1,0:T(8,128)S(1)}, f32[8,16,128]{2,1,0:T(8,128)S(1)}, u32[]{:S(2)}, u32[]{:S(2)}) collective-permute-start(f32[8,16,128]{2,1,0:T(8,128)S(1)} %edges.1), channel_id=1, source_target_pairs={{0,24},{8,0},{16,8},{24,16},{1,25},{9,1},{17,9},{25,17},{2,26},{10... | collective-permute-start | bytes 196616 | tf_op jit(solution)/shard_map/ppermute | solution.py:287
  5.7 14.9 %collective-permute-start = (f32[4,8,16,128]{3,2,1,0:T(8,128)}, f32[4,8,16,128]{3,2,1,0:T(8,128)S(1)}, u32[]{:S(2)}, u32[]{:S(2)}) collective-permute-start(f32[4,8,16,128]{3,2,1,0:T(8,128)} %own.3), channel_id=1, source_target_pairs={{0,1},{1,0},{2,3},{3,2},{4,5},{5,4},{6,7},{7,6},{8,9},{9,8},{10,11... | collective-permute-start | bytes 786440 | tf_op jit(solution)/shard_map/ppermute | solution.py:268
  8.4 6.5 %collective-permute-start.7 = (f32[8,16,128]{2,1,0:T(8,128)S(1)}, f32[8,16,128]{2,1,0:T(8,128)S(1)}, u32[]{:S(2)}, u32[]{:S(2)}) collective-permute-start(f32[8,16,128]{2,1,0:T(8,128)S(1)} %broadcast_select_fusion.s_own), channel_id=1, source_target_pairs={{0,1},{1,0},{2,3},{3,2},{4,5},{5,4},{6,7},{7,6},{8,9},{9,8},{10,11... | collective-permute-start | bytes 196616 | tf_op jit(solution)/shard_map/ppermute | solution.py:268
  14.9 7.7 %collective-permute-start.9 = (f32[2,8,16,128]{3,2,1,0:T(8,128)S(1)}, f32[2,8,16,128]{3,2,1,0:T(8,128)S(1)}, u32[]{:S(2)}, u32[]{:S(2)}) collective-permute-start(f32[2,8,16,128]{3,2,1,0:T(8,128)S(1)} %pad_maximum_fusion), channel_id=1, source_target_pairs={{0,0},{2,4},{4,2},{6,6},{1,1},{3,5},{5,3},{7,7},{8,8},{10,12},{12,... | collective-permute-start | bytes 393224 | tf_op jit(solution)/shard_map/ppermute | solution.py:274
  16.9 7.9 %collective-permute-start.2 = (f32[4,8,16,128]{3,2,1,0:T(8,128)}, f32[4,8,16,128]{3,2,1,0:T(8,128)S(1)}, u32[]{:S(2)}, u32[]{:S(2)}) collective-permute-start(f32[4,8,16,128]{3,2,1,0:T(8,128)} %own.3), channel_id=1, source_target_pairs={{0,0},{2,4},{4,2},{6,6},{1,1},{3,5},{5,3},{7,7},{8,8},{10,12},{12,... | collective-permute-start | bytes 786440 | tf_op jit(solution)/shard_map/ppermute | solution.py:274
  20.5 4.3 %collective-permute-start.1 = (f32[4,8,16,128]{3,2,1,0:T(8,128)}, f32[4,8,16,128]{3,2,1,0:T(8,128)S(1)}, u32[]{:S(2)}, u32[]{:S(2)}) collective-permute-start(f32[4,8,16,128]{3,2,1,0:T(8,128)} %own.3), channel_id=1, source_target_pairs={{0,2},{2,0},{4,6},{6,4},{1,3},{3,1},{5,7},{7,5},{8,10},{10,8},{12,... | collective-permute-start | bytes 786440 | tf_op jit(solution)/shard_map/ppermute | solution.py:271
  20.6 7.7 %collective-permute-start.4 = (f32[4,8,16,128]{3,2,1,0:T(8,128)S(1)}, f32[4,8,16,128]{3,2,1,0:T(8,128)S(1)}, u32[]{:S(2)}, u32[]{:S(2)}) collective-permute-start(f32[4,8,16,128]{3,2,1,0:T(8,128)S(1)} %collective-permute-done.part), channel_id=1, source_target_pairs={{0,0},{2,4},{4,2},{6,6},{1,1},{3,5},{5,3},{7,7},{8,8},{10,12},{12,... | collective-permute-start | bytes 786440 | tf_op jit(solution)/shard_map/ppermute | solution.py:274
  22.5 5.8 %collective-permute-start.3 = (f32[4,8,16,128]{3,2,1,0:T(8,128)S(1)}, f32[4,8,16,128]{3,2,1,0:T(8,128)S(1)}, u32[]{:S(2)}, u32[]{:S(2)}) collective-permute-start(f32[4,8,16,128]{3,2,1,0:T(8,128)S(1)} %collective-permute-done.part), channel_id=1, source_target_pairs={{0,2},{2,0},{4,6},{6,4},{1,3},{3,1},{5,7},{7,5},{8,10},{10,8},{12,... | collective-permute-start | bytes 786440 | tf_op jit(solution)/shard_map/ppermute | solution.py:271
  22.6 1.7 %collective-permute-start.8 = (f32[2,8,16,128]{3,2,1,0:T(8,128)S(1)}, f32[2,8,16,128]{3,2,1,0:T(8,128)S(1)}, u32[]{:S(2)}, u32[]{:S(2)}) collective-permute-start(f32[2,8,16,128]{3,2,1,0:T(8,128)S(1)} %pad_maximum_fusion), channel_id=1, source_target_pairs={{0,2},{2,0},{4,6},{6,4},{1,3},{3,1},{5,7},{7,5},{8,10},{10,8},{12,... | collective-permute-start | bytes 393224 | tf_op jit(solution)/shard_map/ppermute | solution.py:271
  28.3 1.2 %copy-start = (bf16[4,256,512]{2,1,0:T(8,128)(2,1)S(1)}, bf16[4,256,512]{2,1,0:T(8,128)(2,1)}, u32[]{:S(2)}) copy-start(bf16[4,256,512]{2,1,0:T(8,128)(2,1)} %constant.10.clone.span_w) | copy-start | bytes 3145732

commit v4 on v3

--- a/solution.py
+++ b/solution.py
@@ -96,32 +96,26 @@
 
 
 def flux_kernel(
-    walls, own, part, a_own, b_own, a_part, b_part, s_own, s_part, a_strip, b_strip,
-    plane_h, plane_l, span_w, clark_ref, similar_ref, sums_ref,
+    walls, blocks, strips, plane_h, plane_l, span_w, clark_ref, similar_ref, sums_ref,
     raw, in_h, in_l, prod_h, prod_l, mean, mid_h, mid_l,
 ):
-    _, layers, rows, width = own.shape
+    _, _, layers, rows, width = blocks.shape
     both = 2 * layers
     cells = both * rows
     here = layers * rows
     me_s = lax.axis_index("stream")
     me_w = lax.axis_index("wall")
-    odd = lax.rem(me_w, 2)
     mine = pl.multiple_of(me_s * layers, layers)
-    other = pl.multiple_of((1 - me_s) * layers, layers)
-    row_a = pl.multiple_of((1 - odd) * (2 * rows), rows)
-    row_b = pl.multiple_of(odd * (2 * rows), rows)
-    at_end = (me_w == 0) | (me_w == walls - 1)
-    keep_b = jnp.where(at_end, 0.0, 1.0).astype(jnp.float32)
-
-    for where, blocks in ((mine, (own, a_own, b_own)), (other, (part, a_part, b_part))):
-        raw[:4, pl.ds(where, layers), rows : 2 * rows, :] = blocks[0][...]
-        raw[:4, pl.ds(where, layers), pl.ds(row_a, rows), :] = blocks[1][...]
-        raw[:4, pl.ds(where, layers), pl.ds(row_b, rows), :] = blocks[2][...] * keep_b
-    for k, where, block in ((0, mine, s_own), (1, other, s_part)):
-        raw[4, pl.ds(where, layers), rows : 2 * rows, :] = block[...]
-        raw[4, pl.ds(where, layers), pl.ds(row_a, rows), :] = a_strip[k]
-        raw[4, pl.ds(where, layers), pl.ds(row_b, rows), :] = b_strip[k] * keep_b
+
+    for block in range(3):
+        wall = me_w + block - 1
+        keep = jnp.where((wall >= 0) & (wall < walls), 1.0, 0.0).astype(jnp.float32)
+        wall = jnp.clip(wall, 0, walls - 1)
+        for k in range(2):
+            down = slice(block * rows, (block + 1) * rows)
+            along = slice(k * layers, (k + 1) * layers)
+            raw[:4, along, down, :] = blocks[2 * wall + k] * keep
+            raw[4, along, down, :] = strips[2 * wall + k] * keep
 
     for block in range(3):
         for t in range(5):
@@ -264,17 +258,6 @@
     streams = lax.axis_size("stream")
     cells = 2 * layers * rows
 
-    def swap(value):
-        return lax.ppermute(value, "stream", [(0, 1), (1, 0)])
-
-    def pair_a(value):
-        return lax.ppermute(value, "wall", [(w, w ^ 1) for w in range(walls)])
-
-    def pair_b(value):
-        return lax.ppermute(
-            value, "wall", [(w, min(max(((w + 1) ^ 1) - 1, 0), walls - 1)) for w in range(walls)]
-        )
-
     edges = pl.pallas_call(
         edge_kernel,
         out_shape=jax.ShapeDtypeStruct((layers, rows, width), jnp.float32),
@@ -285,13 +268,9 @@
     )(fields)
     before = lax.ppermute(edges, "span", [(p, (p + 1) % spans) for p in range(spans)])
     after = lax.ppermute(edges, "span", [(p, (p - 1) % spans) for p in range(spans)])
-    part = swap(fields)
-    a_own, b_own = pair_a(fields), pair_b(fields)
-    a_part, b_part = pair_a(part), pair_b(part)
+    blocks = lax.all_gather(fields, ("wall", "stream"))
     s_own = jnp.where(lane_index(edges.shape) < width // 2, after, before)
-    s_part = swap(s_own)
-    strips = jnp.stack([s_own, s_part])
-    a_strip, b_strip = pair_a(strips), pair_b(strips)
+    strips = lax.all_gather(s_own, ("wall", "stream"))
 
     plane_h, plane_l = plane_constants(2 * layers, rows)
     span_w = span_constants(width)
@@ -299,7 +278,7 @@
     clark, similar, sums = pl.pallas_call(
         functools.partial(flux_kernel, walls),
         out_shape=(block, block, jax.ShapeDtypeStruct((rows, width), jnp.float32)),
-        in_specs=vmem(13),
+        in_specs=vmem(5),
         out_specs=tuple(vmem(3)),
         scratch_shapes=[
             pltpu.VMEM((5, 2 * layers, 3 * rows, width), jnp.float32),
@@ -314,7 +293,7 @@
         compiler_params=pltpu.CompilerParams(vmem_limit_bytes=40 * 1024 * 1024),
         name="flux",
     )(
-        fields, part, a_own, b_own, a_part, b_part, s_own, s_part, a_strip, b_strip,
+        blocks, strips,
         jnp.asarray(plane_h), jnp.asarray(plane_l), jnp.asarray(span_w),
     )
 

time: 47.1 us -> 70.5 us (1.50)
  the two profiles are of different devices: /device:TPU:4 before, /device:TPU:0 now
where the time goes in v4:
time: 70.5 us; the launch traced here: 70.2 us
  blocking collectives  29.6 us (42%)
  between operations  14.1 us (20%)
  waiting for transfers between devices  10.2 us (14%)
  local copies, waits for them, and re-layouts  5.67 us (8%)
  Pallas kernels  5.33 us (8%)
  starting transfers between devices  5.2 us (7%)
    all_gather x1, blocking collectives, shards(): strips = lax.all_gather(s_own, ('wall', 'stream'))  17.8 us
    all_to_all x1, blocking collectives, shards(): tables = lax.all_to_all(tables, ('span', 'stream'), 0, 0)  11.9 us
    all_gather x1, waiting for transfers between devices, shards(): blocks = lax.all_gather(fields, ('wall', 'stream'))  6.69 us
    unnamed x10, local copies, waits for them, and re-layouts  5.66 us
    pallas_call x1, Pallas kernels, shards(): pl.pallas_call(functools.partial(flux_kernel, walls), out_shape=(block, b...  4.16 us
    ppermute x1, starting transfers between devices, shards(): lax.ppermute(edges, 'span', [(p, (p + 1) % spans) for p in range(spans)])  3.08 us
    ppermute x1, waiting for transfers between devices, shards(): lax.ppermute(edges, 'span', [(p, (p + 1) % spans) for p in range(spans)])  2.32 us
    ppermute x1, starting transfers between devices, shards(): lax.ppermute(edges, 'span', [(p, (p - 1) % spans) for p in range(spans)])  2.09 us
  transfers between devices with their start and end apart: 3, of which 3 were waited for; matrix products, arithmetic and copies ran while one was open for 0% of the time, Pallas kernels for 0%

profile of v4, /device:TPU:0, one launch (start us, length us, event | category | flops | bytes accessed | tf_op | source)
XLA Modules:
  0.0 70.2 jit_solution(11392873292049379750)
XLA Ops:
  7.2 0.0 all-gather.4.cloned.1.call-start
  7.2 0.7 all-gather.4.cloned.1.call-update
  7.9 0.0 copy-start.1
  7.9 0.9 %copy-done.1 = f32[4,8,16,128]{3,2,1,0:T(8,128)S(1)} copy-done((f32[4,8,16,128]{3,2,1,0:T(8,128)S(1)}, f32[4,8,16,128]{3,2,1,0:T(8,128)}, u32[]{:S(2)}) %copy-start.1) | copy-done | bytes 262168
  8.8 0.2 edges.1
  9.0 3.1 %collective-permute-start.1 = (f32[8,16,128]{2,1,0:T(8,128)S(1)}, f32[8,16,128]{2,1,0:T(8,128)S(1)}, u32[]{:S(2)}, u32[]{:S(2)}) collective-permute-start(f32[8,16,128]{2,1,0:T(8,128)S(1)} %edges.1), channel_id=1, source_target_pairs={{0,8},{8,16},{16,24},{24,0},{1,9},{9,17},{17,25},{25,1},{2,10},{10... | collective-permute-start | bytes 196616 | tf_op jit(solution)/shard_map/ppermute | solution.py:269
  12.1 2.1 %collective-permute-start = (f32[8,16,128]{2,1,0:T(8,128)S(1)}, f32[8,16,128]{2,1,0:T(8,128)S(1)}, u32[]{:S(2)}, u32[]{:S(2)}) collective-permute-start(f32[8,16,128]{2,1,0:T(8,128)S(1)} %edges.1), channel_id=1, source_target_pairs={{0,24},{8,0},{16,8},{24,16},{1,25},{9,1},{17,9},{25,17},{2,26},{10... | collective-permute-start | bytes 196616 | tf_op jit(solution)/shard_map/ppermute | solution.py:270
  14.2 2.3 %collective-permute-done.1 = f32[8,16,128]{2,1,0:T(8,128)S(1)} collective-permute-done((f32[8,16,128]{2,1,0:T(8,128)S(1)}, f32[8,16,128]{2,1,0:T(8,128)S(1)}, u32[]{:S(2)}, u32[]{:S(2)}) %collective-permute-start.1) | collective-permute-done | bytes 65568 | tf_op jit(solution)/shard_map/ppermute | solution.py:269
  16.5 0.5 collective-permute-done
  17.1 17.8 %all-gather.1 = f32[64,16,128]{2,1,0:T(8,128)S(1)} all-gather(f32[8,16,128]{2,1,0:T(8,128)S(1)} %broadcast_select_fusion), channel_id=3, replica_groups=mesh['span'=4,'wall'=4,'stream'=2] {'wall','stream'}, dimensions={0}, use_global_device_ids=true | all-gather | bytes 589824 | tf_op jit(solution)/shard_map/all_gather | solution.py:273
  34.9 6.7 %all-gather.4.cloned.1.call-done = f32[32,8,16,128]{3,2,1,0:T(8,128)} async-done(((f32[4,8,16,128]{3,2,1,0:T(8,128)}), f32[32,8,16,128]{3,2,1,0:T(8,128)}) %all-gather.4.cloned.1.call-update) | async-done | bytes 2097168 | tf_op jit(solution)/shard_map/all_gather | solution.py:271
  41.6 0.0 copy-start
  41.6 1.6 %copy-done = f32[32,8,16,128]{3,2,1,0:T(8,128)S(1)} copy-done((f32[32,8,16,128]{3,2,1,0:T(8,128)S(1)}, f32[32,8,16,128]{3,2,1,0:T(8,128)}, u32[]{:S(2)}) %copy-start) | copy-done | bytes 2097176
  43.2 0.0 copy-start.2
  43.2 1.2 %copy-done.2 = bf16[4,256,512]{2,1,0:T(8,128)(2,1)S(1)} copy-done((bf16[4,256,512]{2,1,0:T(8,128)(2,1)S(1)}, bf16[4,256,512]{2,1,0:T(8,128)(2,1)}, u32[]{:S(2)}) %copy-start.2) | copy-done | bytes 1048600
  44.4 0.0 copy-start.3
  44.4 0.9 %copy-done.3 = bf16[256,512]{1,0:T(8,128)(2,1)S(1)} copy-done((bf16[256,512]{1,0:T(8,128)(2,1)S(1)}, bf16[256,512]{1,0:T(8,128)(2,1)}, u32[]{:S(2)}) %copy-start.3) | copy-done | bytes 262168
  45.3 0.0 copy-start.4
  45.3 0.9 %copy-done.4 = bf16[256,512]{1,0:T(8,128)(2,1)S(1)} copy-done((bf16[256,512]{1,0:T(8,128)(2,1)S(1)}, bf16[256,512]{1,0:T(8,128)(2,1)}, u32[]{:S(2)}) %copy-start.4) | copy-done | bytes 262168
  46.3 4.2 %flux.1 = (f32[3,8,16,128]{3,2,1,0:T(8,128)S(1)}, f32[3,8,16,128]{3,2,1,0:T(8,128)S(1)}, f32[16,128]{1,0:T(8,128)S(1)}) custom-call(f32[8,4,8,16,128]{4,3,2,1,0:T(8,128)S(1)} %bitcast.2, f32[8,8,16,128]{3,2,1,0:T(8,128)S(1)} %bitcast.3, bf16[256,512]{1,0:T(8,128)(2,1)S(1)} %copy-done.4, bf16[256,512]{1,0:T(8,128)(2,1)S(1)} %copy-done.3, ...), custom_call_target="tpu_custom_call" | custom-call | tf_op jit(solution)/shard_map/flux/pallas_call | solution.py:278
  50.5 11.9 %all_to_all.5.sums = f32[8,16,128]{2,1,0:T(8,128)S(1)} all-to-all(f32[8,16,128]{2,1,0:T(8,128)S(1)} %broadcast_in_dim.2), channel_id=1, replica_groups=mesh['span'=4,'wall'=4,'stream'=2] {'span','stream'}, dimensions={0} | all-to-all | bytes 131072 | tf_op jit(solution)/shard_map/all_to_all | solution.py:302
  62.3 1.0 %finish.1 = (f32[3,8,16,128]{3,2,1,0:T(8,128)}, f32[3,8,16,128]{3,2,1,0:T(8,128)}, f32[3,16]{1,0:T(4,128)}, f32[3,16]{1,0:T(4,128)}) custom-call(f32[8,16,128]{2,1,0:T(8,128)S(1)} %all_to_all.5.sums, f32[3,8,16,128]{3,2,1,0:T(8,128)S(1)} %get-tuple-element.8.clark, f32[3,8,16,128]{3,2,1,0:T(8,128)S(1)} %get-tuple-element.9.similar), custom_call_target="tpu_custom_call" | custom-call | tf_op jit(solution)/shard_map/finish/pallas_call | solution.py:304
  (3 shorter events, 0.0 us)
Async XLA Ops:
  7.2 34.4 %all-gather.4.cloned.1.call-start = ((), (), s32[]{:S(2)}) async-start(), calls=%async_computation.1 | async-start | bytes 2359296 | tf_op jit(solution)/shard_map/all_gather | solution.py:271
  7.9 1.0 %copy-start.1 = (f32[4,8,16,128]{3,2,1,0:T(8,128)S(1)}, f32[4,8,16,128]{3,2,1,0:T(8,128)}, u32[]{:S(2)}) copy-start(f32[4,8,16,128]{3,2,1,0:T(8,128)} %own.1) | copy-start | bytes 786436
  9.0 7.5 %collective-permute-start.1 = (f32[8,16,128]{2,1,0:T(8,128)S(1)}, f32[8,16,128]{2,1,0:T(8,128)S(1)}, u32[]{:S(2)}, u32[]{:S(2)}) collective-permute-start(f32[8,16,128]{2,1,0:T(8,128)S(1)} %edges.1), channel_id=1, source_target_pairs={{0,8},{8,16},{16,24},{24,0},{1,9},{9,17},{17,25},{25,1},{2,10},{10... | collective-permute-start | bytes 196616 | tf_op jit(solution)/shard_map/ppermute | solution.py:269
  12.1 5.0 %collective-permute-start = (f32[8,16,128]{2,1,0:T(8,128)S(1)}, f32[8,16,128]{2,1,0:T(8,128)S(1)}, u32[]{:S(2)}, u32[]{:S(2)}) collective-permute-start(f32[8,16,128]{2,1,0:T(8,128)S(1)} %edges.1), channel_id=1, source_target_pairs={{0,24},{8,0},{16,8},{24,16},{1,25},{9,1},{17,9},{25,17},{2,26},{10... | collective-permute-start | bytes 196616 | tf_op jit(solution)/shard_map/ppermute | solution.py:270
  41.6 1.6 %copy-start = (f32[32,8,16,128]{3,2,1,0:T(8,128)S(1)}, f32[32,8,16,128]{3,2,1,0:T(8,128)}, u32[]{:S(2)}) copy-start(f32[32,8,16,128]{3,2,1,0:T(8,128)} %all-gather.4.cloned.1.call-done) | copy-start | bytes 6291460
  43.2 1.2 %copy-start.2 = (bf16[4,256,512]{2,1,0:T(8,128)(2,1)S(1)}, bf16[4,256,512]{2,1,0:T(8,128)(2,1)}, u32[]{:S(2)}) copy-start(bf16[4,256,512]{2,1,0:T(8,128)(2,1)} %constant.10.clone.span_w) | copy-start | bytes 3145732
  44.4 0.9 %copy-start.3 = (bf16[256,512]{1,0:T(8,128)(2,1)S(1)}, bf16[256,512]{1,0:T(8,128)(2,1)}, u32[]{:S(2)}) copy-start(bf16[256,512]{1,0:T(8,128)(2,1)} %constant.9.clone.plane_l) | copy-start | bytes 786436
  45.3 0.9 %copy-start.4 = (bf16[256,512]{1,0:T(8,128)(2,1)S(1)}, bf16[256,512]{1,0:T(8,128)(2,1)}, u32[]{:S(2)}) copy-start(bf16[256,512]{1,0:T(8,128)(2,1)} %constant.8.clone.plane_h) | copy-start | bytes 786436
Sparse Core Ops, SparseCore 0:
  9.9 31.6 all-gather.3

commit v5 on v3

v5 whole, which is shorter than its diff:
```python
import functools
import math

import jax
import jax.numpy as jnp
import ml_dtypes
import numpy as np
from jax import lax
from jax.experimental import pallas as pl
from jax.experimental.pallas import tpu as pltpu
from jax.sharding import PartitionSpec as P

raw_taps = [math.exp(-((k - 8) ** 2) / 18.0) for k in range(17)]
filter_taps = [value / sum(raw_taps) for value in raw_taps]
clark_coef = 9.0
small_eps = 1e-06

reach = 8
rim = 2 * reach


def split_constant(matrix):
    high = matrix.astype(ml_dtypes.bfloat16)
    low = (matrix - high.astype(np.float64)).astype(ml_dtypes.bfloat16)
    return high, low


def band(outs, ins, offset):
    matrix = np.zeros((outs, ins))
    for o in range(outs):
        for i in range(ins):
            k = i - o - offset + reach
            if 0 <= k <= 2 * reach:
                matrix[o, i] = filter_taps[k]
    return matrix


def plane_constants(layers, rows):
    stream = band(layers, layers, 0)
    wall = band(rows, 2 * rows, reach)
    blocks = [np.kron(stream, wall[:, :rows]), np.kron(stream, wall[:, rows:])]
    return split_constant(np.concatenate(blocks, axis=1))


def span_constants(width):
    circle = np.zeros((width, width))
    for o in range(width):
        for k in range(2 * reach + 1):
            circle[(o + k - reach) % width, o] = filter_taps[k]
    high, low = split_constant(circle)
    return np.block([[high, low], [high, np.zeros_like(low)]])


def halves(value):
    high = value.astype(jnp.bfloat16)
    return high, (value - high.astype(jnp.float32)).astype(jnp.bfloat16)


def dot(a, b):
    return lax.dot_general(a, b, (((1,), (0,)), ((), ())), preferred_element_type=jnp.float32)


def lane_index(shape):
    return lax.broadcasted_iota(jnp.int32, shape, len(shape) - 1)


def edge_kernel(own, to_partner_side, to_own_side):
    _, layers, rows, width = own.shape
    half = layers // 2
    lane = lane_index((half, rows, width))
    me_s = lax.axis_index("stream")
    sides = []
    for start in (0, width - rim):
        total = jnp.zeros((half, rows, width), jnp.float32)
        for k in range(2):
            for f in range(4):
                place = k * 64 + f * rim
                cells = pltpu.roll(own[f, k * half : (k + 1) * half], (place - start) % width, 2)
                total = jnp.where(lane // rim == place // rim, cells, total)
        sides.append(total)
    to_partner_side[...] = jnp.where(me_s == 0, sides[0], sides[1])
    to_own_side[...] = jnp.where(me_s == 0, sides[1], sides[0])


def merge_kernel(own, part, own_strip, part_strip, merged):
    _, layers, rows, width = own.shape
    half = layers // 2
    me_s = lax.axis_index("stream")
    start = jnp.where(me_s == 0, width - rim, 0)
    lane = lane_index((half, rows, width))
    beyond = lane // rim == start // rim
    for where, block, strip in ((me_s, own, own_strip), (1 - me_s, part, part_strip)):
        packed = strip[...]
        for k in range(2):
            for f in range(4):
                place = k * 64 + f * rim
                cells = pltpu.roll(packed, lax.rem(start - place + 2 * width, width), 2)
                layer = where * layers + k * half
                merged[f, pl.ds(layer, half)] = jnp.where(beyond, cells, block[f, k * half : (k + 1) * half])


def flux_kernel(
    walls, mid, a_block, b_block, plane_h, plane_l, span_w, keep_ref, send_ref, sums_ref,
    raw, in_h, in_l, prod_h, prod_l, mean, mid_h, mid_l, clark_all, similar_all,
):
    _, both, rows, width = mid.shape
    layers = both // 2
    cells = both * rows
    me_s = lax.axis_index("stream")
    me_w = lax.axis_index("wall")
    odd = lax.rem(me_w, 2)
    row_a = pl.multiple_of((1 - odd) * (2 * rows), rows)
    row_b = pl.multiple_of(odd * (2 * rows), rows)
    at_end = (me_w == 0) | (me_w == walls - 1)
    keep_b = jnp.where(at_end, 0.0, 1.0).astype(jnp.float32)

    raw[:, :, rows : 2 * rows, :] = mid[...]
    raw[:, :, pl.ds(row_a, rows), :] = a_block[...]
    raw[:, :, pl.ds(row_b, rows), :] = b_block[...] * keep_b

    def column(t):
        return slice(t * width, (t + 1) * width)

    for block in range(3):
        down = slice(block * cells, (block + 1) * cells)
        for t in range(4):
            value = raw[t, :, block * rows : (block + 1) * rows, :].reshape(cells, width)
            in_h[down, column(t)], in_l[down, column(t)] = halves(value)

    def planes_of(high, low):
        return dot(plane_h[...], high) + dot(plane_l[...], high) + dot(plane_h[...], low)

    def along_span_of(planes):
        high, low = halves(planes)
        tiles = planes.shape[1] // width
        parts = [jnp.concatenate([high[:, column(t)], low[:, column(t)]], axis=1) for t in range(tiles)]
        result = dot(jnp.concatenate(parts, axis=0), span_w[...])
        result = result[:, :width] + result[:, width:]
        return [result[t * cells : (t + 1) * cells].reshape(both, rows, width) for t in range(tiles)]

    for t in range(4):
        mean[t, 0] = jnp.zeros((2 * rows, width), jnp.float32)
        mean[t, both + 1] = jnp.zeros((2 * rows, width), jnp.float32)
    for half in range(2):
        span = slice(half * cells, (half + 2) * cells)
        planes = planes_of(in_h[span, :], in_l[span, :])
        row = lax.rem(lax.broadcasted_iota(jnp.int32, planes.shape, 0), rows)
        if half == 0:
            inside = (me_w > 0) | (row >= reach)
        else:
            inside = (me_w < walls - 1) | (row < rows - reach)
        planes = jnp.where(inside, planes, 0.0)
        for t, value in enumerate(along_span_of(planes)):
            mean[t, 1 : both + 1, half * rows : (half + 1) * rows, :] = value

    for half in range(2):
        span = slice(reach + half * rows, reach + (half + 1) * rows)
        down = slice(half * cells, (half + 1) * cells)
        temperature = raw[3, :, span, :].reshape(cells, width)
        for t in range(3):
            value = raw[t, :, span, :].reshape(cells, width) * temperature
            prod_h[down, column(t)], prod_l[down, column(t)] = halves(value)
    flux = along_span_of(planes_of(prod_h[...], prod_l[...]))

    for half in range(2):
        span = slice(half * rows, (half + 1) * rows)
        down = slice(half * cells, (half + 1) * cells)
        tiles = [mean[t, 1 : both + 1, span, :].reshape(cells, width) for t in range(4)]
        tiles += [tiles[i] * tiles[3] for i in range(3)]
        for t, value in enumerate(tiles):
            mid_h[down, column(t)], mid_l[down, column(t)] = halves(value)
    second = along_span_of(planes_of(mid_h[...], mid_l[...]))

    mid_rows = slice(reach, reach + rows)
    centre, along_span, along_wall, along_stream = [], [], [], []
    for f in range(4):
        here = mean[f, 1 : both + 1, mid_rows, :]
        centre.append(here)
        along_span.append((pltpu.roll(here, width - 1, 2) - pltpu.roll(here, 1, 2)) * 0.5)
        below = mean[f, 1 : both + 1, reach + 1 : reach + rows + 1, :]
        above = mean[f, 1 : both + 1, reach - 1 : reach + rows - 1, :]
        along_wall.append((below - above) * 0.5)
        along_stream.append((mean[f, 2 : both + 2, mid_rows, :] - mean[f, :both, mid_rows, :]) * 0.5)

    lane = lane_index((rows, width))
    useful = lane // (width // 2) == me_s
    table = jnp.zeros((rows, width), jnp.float32)
    for i in range(3):
        exact = flux[i] - centre[i] * centre[3]
        similar = second[4 + i] - second[i] * second[3]
        total = along_span[i] * along_span[3] + along_wall[i] * along_wall[3]
        clark = clark_coef * (total + along_stream[i] * along_stream[3])
        clark_all[i] = clark
        similar_all[i] = similar
        terms = (exact * clark, exact * similar, exact * exact, clark * clark, similar * similar)
        for q, term in enumerate(terms):
            value = jnp.where(useful, jnp.sum(term, axis=0), 0.0)
            table = jnp.where(lane == 3 * q + i, jnp.sum(value, axis=1, keepdims=True), table)
    sums_ref[...] = table

    first = lane_index((layers, rows, width)) < width // 2
    for i in range(3):
        keep_ref[i] = clark_all[i, pl.ds(me_s * layers, layers)]
        keep_ref[3 + i] = similar_all[i, pl.ds(me_s * layers, layers)]
        clark = clark_all[i, pl.ds((1 - me_s) * layers, layers)]
        similar = similar_all[i, pl.ds((1 - me_s) * layers, layers)]
        turn = me_s == 0
        clark = jnp.where(turn, clark, pltpu.roll(clark, width // 2, 2))
        similar = jnp.where(turn, pltpu.roll(similar, width // 2, 2), similar)
        send_ref[i] = jnp.where(first, clark, similar)


def finish_kernel(plane_cells, spans, *refs):
    tables = refs[:spans]
    keep, come, clark_model, similar_model, clark_corr, similar_corr, ordered = refs[spans:]
    _, layers, rows, width = keep.shape
    me_s = lax.axis_index("stream")
    me_p = lax.axis_index("span")
    for step, one in enumerate(tables):
        ordered[lax.rem(me_p - step + spans, spans)] = one[...]
    table = jnp.sum(ordered[...], axis=0) / plane_cells
    lane = lane_index((rows, width))
    useful = lane // (width // 2) == me_s
    corr = jnp.zeros((rows, width), jnp.float32)
    for i in range(3):
        cross_c, cross_s, power_e, power_c, power_s = (
            table[:, 3 * q + i : 3 * q + i + 1] for q in range(5)
        )
        packed = come[i]
        turned = pltpu.roll(packed, width // 2, 2)
        clark = jnp.where(useful[None], keep[i], jnp.where(me_s == 0, turned, packed))
        similar = jnp.where(useful[None], keep[3 + i], jnp.where(me_s == 0, packed, turned))
        clark_model[i] = clark / jnp.sqrt(power_c + small_eps)[None]
        similar_model[i] = similar / jnp.sqrt(power_s + small_eps)[None]
        value = cross_c / jnp.sqrt((power_e + small_eps) * (power_c + small_eps))
        corr = jnp.where(lane == i, value, corr)
        value = cross_s / jnp.sqrt((power_e + small_eps) * (power_s + small_eps))
        corr = jnp.where(lane == 8 + i, value, corr)
    square = jnp.concatenate([corr, jnp.zeros((width - rows, width), jnp.float32)], axis=0)
    turned = square.T
    clark_corr[...] = turned[:3, :rows]
    similar_corr[...] = turned[8:11, :rows]


def call(kernel, name, ins, outs, scratch=(), mib=4):
    return pl.pallas_call(
        kernel,
        out_shape=tuple(jax.ShapeDtypeStruct(shape, jnp.float32) for shape in outs),
        in_specs=[pl.BlockSpec(memory_space=pltpu.VMEM)] * len(ins),
        out_specs=tuple(pl.BlockSpec(memory_space=pltpu.VMEM) for _ in outs),
        scratch_shapes=[pltpu.VMEM(shape, dtype) for shape, dtype in scratch],
        compiler_params=pltpu.CompilerParams(vmem_limit_bytes=mib * 1024 * 1024),
        name=name,
    )(*ins)


def shards(fields):
    _, layers, rows, width = fields.shape
    spans = lax.axis_size("span")
    walls = lax.axis_size("wall")
    streams = lax.axis_size("stream")
    both = streams * layers
    cells = both * rows

    def swap(value):
        return lax.ppermute(value, "stream", [(0, 1), (1, 0)])

    def pair_a(value):
        return lax.ppermute(value, "wall", [(w, w ^ 1) for w in range(walls)])

    def pair_b(value):
        return lax.ppermute(
            value, "wall", [(w, min(max(((w + 1) ^ 1) - 1, 0), walls - 1)) for w in range(walls)]
        )

    def place(p, s):
        return (p % spans) * streams + s

    to_other, to_same = [], []
    for p in range(spans):
        to_other += [(place(p, 0), place(p - 1, 1)), (place(p, 1), place(p + 1, 0))]
        to_same += [(place(p, 1), place(p - 1, 1)), (place(p, 0), place(p + 1, 0))]

    strip = (layers // 2, rows, width)
    first, second = call(edge_kernel, "edges", (fields,), (strip, strip))
    part = swap(fields)
    part_strip = lax.ppermute(first, ("span", "stream"), to_other)
    own_strip = lax.ppermute(second, ("span", "stream"), to_same)
    (mid,) = call(merge_kernel, "merge", (fields, part, own_strip, part_strip), ((4, both, rows, width),))
    b_block, a_block = pair_b(mid), pair_a(mid)

    plane_h, plane_l = plane_constants(both, rows)
    single, brief = jnp.float32, jnp.bfloat16
    keep, send, sums = call(
        functools.partial(flux_kernel, walls),
        "flux",
        (mid, a_block, b_block, jnp.asarray(plane_h), jnp.asarray(plane_l), jnp.asarray(span_constants(width))),
        ((6, layers, rows, width), (3, layers, rows, width), (rows, width)),
        [
            ((4, both, 3 * rows, width), single),
            ((3 * cells, 4 * width), brief),
            ((3 * cells, 4 * width), brief),
            ((2 * cells, 3 * width), brief),
            ((2 * cells, 3 * width), brief),
            ((4, both + 2, 2 * rows, width), single),
            ((2 * cells, 7 * width), brief),
            ((2 * cells, 7 * width), brief),
            ((3, both, rows, width), single),
            ((3, both, rows, width), single),
        ],
        mib=32,
    )

    sums = sums + swap(sums)
    come = swap(send)
    tables = [sums]
    for step in range(1, spans):
        tables.append(lax.ppermute(sums, "span", [(p, (p + step) % spans) for p in range(spans)]))
    block, corr = (3, layers, rows, width), (3, rows)
    return call(
        functools.partial(finish_kernel, float(layers * width * spans * streams), spans),
        "finish",
        (*tables, keep, come),
        (block, block, corr, corr),
        [((spans, rows, width), single)],
    )


def solution(mesh):
    return jax.shard_map(
        shards,
        mesh=mesh,
        in_specs=(P(None, "stream", "wall", "span"),),
        out_specs=(
            P(None, "stream", "wall", "span"),
            P(None, "stream", "wall", "span"),
            P(None, "wall"),
            P(None, "wall"),
        ),
        check_vma=False,
    )
```

time: 47.1 us -> 40.7 us (0.86); the launches traced: 46.3 us -> 40.5 us
  blocking collectives: 10.6 us -> 0 us
  waiting for transfers between devices: 11.3 us -> 20.7 us
  starting transfers between devices: 15 us -> 12.5 us
  Pallas kernels: 7.3 us -> 5.65 us
    all_to_all x1 -> x0, blocking collectives: 10.6 us -> none  [shards(): tables = lax.all_to_all(tables, ('span', 'stream'), 0, 0)]
    ppermute x2 -> x5, waiting for transfers between devices: 1.22 us -> 8.44 us  [the longest x3 4.28 us: shards(): lax.ppermute(sums, 'span', [(p, (p + step) % spans) for p in range(spans)])]
    ppermute x3 -> x1, starting transfers between devices: 7.48 us -> 1.92 us  [pair_b(): lax.ppermute(value, 'wall', [(w, min(max((w + 1 ^ 1) - 1, 0), walls - 1))...]
    ppermute x3 -> x1, waiting for transfers between devices: 3.97 us -> 8.49 us  [pair_b(): lax.ppermute(value, 'wall', [(w, min(max((w + 1 ^ 1) - 1, 0), walls - 1))...]
    ppermute x2 -> x5, starting transfers between devices: 3.88 us -> 6.89 us  [the longest x3 2.81 us: shards(): lax.ppermute(sums, 'span', [(p, (p + step) % spans) for p in range(spans)])]
    pallas_call x3 -> x4, Pallas kernels: 7.3 us -> 5.65 us  [call(): pl.pallas_call(kernel, out_shape=tuple((jax.ShapeDtypeStruct(shape, jnp.f...]
    ppermute x3 -> x1, waiting for transfers between devices: 1.21 us -> 0.01 us  [pair_a(): return lax.ppermute(value, 'wall', [(w, w ^ 1) for w in range(walls)])]
    ppermute x2 -> x3, waiting for transfers between devices: 4.94 us -> 3.74 us  [swap(): return lax.ppermute(value, 'stream', [(0, 1), (1, 0)])]
  transfers between devices with their start and end apart: 10 -> 10, of which waited for: 6 -> 7; matrix products, arithmetic and copies ran while one was open for 0% -> 0% of each run, Pallas kernels for 0% -> 0%
where the time goes in v5:
time: 40.7 us; the launch traced here: 40.5 us
  waiting for transfers between devices  20.7 us (51%)
  starting transfers between devices  12.5 us (31%)
  Pallas kernels  5.65 us (14%)
  local copies, waits for them, and re-layouts  1 us (2%)
  between operations  0.69 us (2%)
    ppermute x1, waiting for transfers between devices, pair_b(): lax.ppermute(value, 'wall', [(w, min(max((w + 1 ^ 1) - 1, 0), walls - 1))...  8.49 us
    pallas_call x4, Pallas kernels, call(): pl.pallas_call(kernel, out_shape=tuple((jax.ShapeDtypeStruct(shape, jnp.f...  5.65 us
    ppermute x3, waiting for transfers between devices, shards(): lax.ppermute(sums, 'span', [(p, (p + step) % spans) for p in range(spans)])  4.28 us
    ppermute x3, waiting for transfers between devices, swap(): return lax.ppermute(value, 'stream', [(0, 1), (1, 0)])  3.74 us
    ppermute x3, starting transfers between devices, swap(): return lax.ppermute(value, 'stream', [(0, 1), (1, 0)])  3.65 us
    ppermute x3, starting transfers between devices, shards(): lax.ppermute(sums, 'span', [(p, (p + step) % spans) for p in range(spans)])  2.81 us
    ppermute x1, waiting for transfers between devices, shards(): part_strip = lax.ppermute(first, ('span', 'stream'), to_other)  2.45 us
    ppermute x1, starting transfers between devices, shards(): part_strip = lax.ppermute(first, ('span', 'stream'), to_other)  2.45 us
  transfers between devices with their start and end apart: 10, of which 7 were waited for; matrix products, arithmetic and copies ran while one was open for 0% of the time, Pallas kernels for 0%

profile of v5, /device:TPU:4, one launch (start us, length us, event | category | flops | bytes accessed | tf_op | source)
XLA Modules:
  0.0 40.5 jit_solution(3638161412177797028)
XLA Ops:
  0.6 1.6 %collective-permute-start = (f32[4,8,16,128]{3,2,1,0:T(8,128)}, f32[4,8,16,128]{3,2,1,0:T(8,128)S(1)}, u32[]{:S(2)}, u32[]{:S(2)}) collective-permute-start(f32[4,8,16,128]{3,2,1,0:T(8,128)} %own.3), channel_id=1, source_target_pairs={{0,1},{1,0},{2,3},{3,2},{4,5},{5,4},{6,7},{7,6},{8,9},{9,8},{10,11... | collective-permute-start | bytes 786440 | tf_op jit(solution)/shard_map/ppermute | solution.py:266
  2.2 1.0 %copy-done = f32[4,8,16,128]{3,2,1,0:T(8,128)S(1)} copy-done((f32[4,8,16,128]{3,2,1,0:T(8,128)S(1)}, f32[4,8,16,128]{3,2,1,0:T(8,128)}, u32[]{:S(2)}) %copy-start) | copy-done | bytes 262168
  3.2 0.2 edges.1
  3.4 1.6 %collective-permute-start.1 = (f32[4,16,128]{2,1,0:T(8,128)S(1)}, f32[4,16,128]{2,1,0:T(8,128)S(1)}, u32[]{:S(2)}, u32[]{:S(2)}) collective-permute-start(f32[4,16,128]{2,1,0:T(8,128)S(1)} %get-tuple-element.9), channel_id=1, source_target_pairs={{1,25},{0,8},{9,1},{8,16},{17,9},{16,24},{25,17},{24,0},{3,27},{2,... | collective-permute-start | bytes 98312 | tf_op jit(solution)/shard_map/ppermute | solution.py:288
  5.0 2.4 %collective-permute-start.2 = (f32[4,16,128]{2,1,0:T(8,128)S(1)}, f32[4,16,128]{2,1,0:T(8,128)S(1)}, u32[]{:S(2)}, u32[]{:S(2)}) collective-permute-start(f32[4,16,128]{2,1,0:T(8,128)S(1)} %get-tuple-element.10), channel_id=1, source_target_pairs={{0,25},{1,8},{8,1},{9,16},{16,9},{17,24},{24,17},{25,0},{2,27},{3,... | collective-permute-start | bytes 98312 | tf_op jit(solution)/shard_map/ppermute | solution.py:287
  7.4 1.7 %collective-permute-done.1.own_strip = f32[4,16,128]{2,1,0:T(8,128)S(1)} collective-permute-done((f32[4,16,128]{2,1,0:T(8,128)S(1)}, f32[4,16,128]{2,1,0:T(8,128)S(1)}, u32[]{:S(2)}, u32[]{:S(2)}) %collective-permute-start.1) | collective-permute-done | bytes 32800 | tf_op jit(solution)/shard_map/ppermute | solution.py:288
  9.2 2.5 %collective-permute-done.2.part_strip = f32[4,16,128]{2,1,0:T(8,128)S(1)} collective-permute-done((f32[4,16,128]{2,1,0:T(8,128)S(1)}, f32[4,16,128]{2,1,0:T(8,128)S(1)}, u32[]{:S(2)}, u32[]{:S(2)}) %collective-permute-start.2) | collective-permute-done | bytes 32800 | tf_op jit(solution)/shard_map/ppermute | solution.py:287
  11.6 0.0 collective-permute-done.part
  11.6 0.2 merge.1.mid
  11.8 1.9 %collective-permute-start.4 = (f32[4,16,16,128]{3,2,1,0:T(8,128)S(1)}, f32[4,16,16,128]{3,2,1,0:T(8,128)S(1)}, u32[]{:S(2)}, u32[]{:S(2)}) collective-permute-start(f32[4,16,16,128]{3,2,1,0:T(8,128)S(1)} %merge.1.mid), channel_id=1, source_target_pairs={{0,0},{2,4},{4,2},{6,6},{1,1},{3,5},{5,3},{7,7},{8,8},{10,12},{12,... | collective-permute-start | bytes 1572872 | tf_op jit(solution)/shard_map/ppermute | solution.py:272
  13.8 0.1 collective-permute-start.3
  13.8 8.5 %collective-permute-done.4.b_block = f32[4,16,16,128]{3,2,1,0:T(8,128)S(1)} collective-permute-done((f32[4,16,16,128]{3,2,1,0:T(8,128)S(1)}, f32[4,16,16,128]{3,2,1,0:T(8,128)S(1)}, u32[]{:S(2)}, u32[]{:S(2)}) %collective-permute-start.4) | collective-permute-done | bytes 524320 | tf_op jit(solution)/shard_map/ppermute | solution.py:272
  22.3 0.0 collective-permute-done.3.a_block
  22.3 4.2 %flux.1 = (f32[6,8,16,128]{3,2,1,0:T(8,128)S(1)}, f32[3,8,16,128]{3,2,1,0:T(8,128)S(1)}, f32[16,128]{1,0:T(8,128)S(1)}) custom-call(f32[4,16,16,128]{3,2,1,0:T(8,128)S(1)} %merge.1.mid, f32[4,16,16,128]{3,2,1,0:T(8,128)S(1)} %collective-permute-done.3.a_block, f32[4,16,16,128]{3,2,1,0:T(8,128)S(1)} %collective-permute-done.4.b_block, ...), custom_call_target="tpu_custom_call" | custom-call | tf_op jit(solution)/shard_map/flux/pallas_call | solution.py:246
  26.6 0.9 %collective-permute-start.9 = (f32[3,8,16,128]{3,2,1,0:T(8,128)S(1)}, f32[3,8,16,128]{3,2,1,0:T(8,128)S(1)}, u32[]{:S(2)}, u32[]{:S(2)}) collective-permute-start(f32[3,8,16,128]{3,2,1,0:T(8,128)S(1)} %get-tuple-element.13), channel_id=1, source_target_pairs={{0,1},{1,0},{2,3},{3,2},{4,5},{5,4},{6,7},{7,6},{8,9},{9,8},{10,11... | collective-permute-start | bytes 589832 | tf_op jit(solution)/shard_map/ppermute | solution.py:266
  27.4 1.2 %collective-permute-start.5 = (f32[16,128]{1,0:T(8,128)S(1)}, f32[16,128]{1,0:T(8,128)S(1)}, u32[]{:S(2)}, u32[]{:S(2)}) collective-permute-start(f32[16,128]{1,0:T(8,128)S(1)} %get-tuple-element.11), channel_id=1, source_target_pairs={{0,1},{1,0},{2,3},{3,2},{4,5},{5,4},{6,7},{7,6},{8,9},{9,8},{10,11... | collective-permute-start | bytes 24584 | tf_op jit(solution)/shard_map/ppermute | solution.py:266
  28.7 3.7 %collective-permute-done.5 = f32[16,128]{1,0:T(8,128)S(1)} collective-permute-done((f32[16,128]{1,0:T(8,128)S(1)}, f32[16,128]{1,0:T(8,128)S(1)}, u32[]{:S(2)}, u32[]{:S(2)}) %collective-permute-start.5) | collective-permute-done | bytes 8224 | tf_op jit(solution)/shard_map/ppermute | solution.py:266
  32.4 1.6 %collective-permute-start.8 = (f32[16,128]{1,0:T(8,128)S(1)}, f32[16,128]{1,0:T(8,128)S(1)}, u32[]{:S(2)}, u32[]{:S(2)}) collective-permute-start(f32[16,128]{1,0:T(8,128)S(1)} %add.3.refs_0_), channel_id=1, source_target_pairs={{0,24},{8,0},{16,8},{24,16},{1,25},{9,1},{17,9},{25,17},{2,26},{10... | collective-permute-start | bytes 24584 | tf_op jit(solution)/shard_map/ppermute | solution.py:318
  34.1 0.0 collective-permute-start.7
  34.1 1.2 %collective-permute-start.6 = (f32[16,128]{1,0:T(8,128)S(1)}, f32[16,128]{1,0:T(8,128)S(1)}, u32[]{:S(2)}, u32[]{:S(2)}) collective-permute-start(f32[16,128]{1,0:T(8,128)S(1)} %add.3.refs_0_), channel_id=1, source_target_pairs={{0,8},{8,16},{16,24},{24,0},{1,9},{9,17},{17,25},{25,1},{2,10},{10... | collective-permute-start | bytes 24584 | tf_op jit(solution)/shard_map/ppermute | solution.py:318
  35.2 0.8 %collective-permute-done.8.refs_3_ = f32[16,128]{1,0:T(8,128)S(1)} collective-permute-done((f32[16,128]{1,0:T(8,128)S(1)}, f32[16,128]{1,0:T(8,128)S(1)}, u32[]{:S(2)}, u32[]{:S(2)}) %collective-permute-start.8) | collective-permute-done | bytes 8224 | tf_op jit(solution)/shard_map/ppermute | solution.py:318
  36.1 2.5 %collective-permute-done.7.refs_2_ = f32[16,128]{1,0:T(8,128)S(1)} collective-permute-done((f32[16,128]{1,0:T(8,128)S(1)}, f32[16,128]{1,0:T(8,128)S(1)}, u32[]{:S(2)}, u32[]{:S(2)}) %collective-permute-start.7) | collective-permute-done | bytes 8224 | tf_op jit(solution)/shard_map/ppermute | solution.py:318
  38.6 0.9 %collective-permute-done.6.refs_1_ = f32[16,128]{1,0:T(8,128)S(1)} collective-permute-done((f32[16,128]{1,0:T(8,128)S(1)}, f32[16,128]{1,0:T(8,128)S(1)}, u32[]{:S(2)}, u32[]{:S(2)}) %collective-permute-start.6) | collective-permute-done | bytes 8224 | tf_op jit(solution)/shard_map/ppermute | solution.py:318
  39.5 1.0 %finish.1 = (f32[3,8,16,128]{3,2,1,0:T(8,128)}, f32[3,8,16,128]{3,2,1,0:T(8,128)}, f32[3,16]{1,0:T(4,128)}, f32[3,16]{1,0:T(4,128)}) custom-call(f32[16,128]{1,0:T(8,128)S(1)} %add.3.refs_0_, f32[16,128]{1,0:T(8,128)S(1)} %collective-permute-done.6.refs_1_, f32[16,128]{1,0:T(8,128)S(1)} %collective-permute-done.7.refs_2_, ...), custom_call_target="tpu_custom_call" | custom-call | tf_op jit(solution)/shard_map/finish/pallas_call | solution.py:246
  (11 shorter events, 0.0 us)
Async XLA Ops:
  0.6 11.0 %collective-permute-start = (f32[4,8,16,128]{3,2,1,0:T(8,128)}, f32[4,8,16,128]{3,2,1,0:T(8,128)S(1)}, u32[]{:S(2)}, u32[]{:S(2)}) collective-permute-start(f32[4,8,16,128]{3,2,1,0:T(8,128)} %own.3), channel_id=1, source_target_pairs={{0,1},{1,0},{2,3},{3,2},{4,5},{5,4},{6,7},{7,6},{8,9},{9,8},{10,11... | collective-permute-start | bytes 786440 | tf_op jit(solution)/shard_map/ppermute | solution.py:266
  2.2 1.0 %copy-start = (f32[4,8,16,128]{3,2,1,0:T(8,128)S(1)}, f32[4,8,16,128]{3,2,1,0:T(8,128)}, u32[]{:S(2)}) copy-start(f32[4,8,16,128]{3,2,1,0:T(8,128)} %own.3) | copy-start | bytes 786436
  3.2 8.4 %copy-start.1 = (f32[4,8,16,128]{3,2,1,0:T(8,128)S(1)}, f32[4,8,16,128]{3,2,1,0:T(8,128)}, u32[]{:S(2)}) copy-start(f32[4,8,16,128]{3,2,1,0:T(8,128)} %own.3) | copy-start | bytes 786436
  3.4 5.8 %collective-permute-start.1 = (f32[4,16,128]{2,1,0:T(8,128)S(1)}, f32[4,16,128]{2,1,0:T(8,128)S(1)}, u32[]{:S(2)}, u32[]{:S(2)}) collective-permute-start(f32[4,16,128]{2,1,0:T(8,128)S(1)} %get-tuple-element.9), channel_id=1, source_target_pairs={{1,25},{0,8},{9,1},{8,16},{17,9},{16,24},{25,17},{24,0},{3,27},{2,... | collective-permute-start | bytes 98312 | tf_op jit(solution)/shard_map/ppermute | solution.py:288
  5.0 17.3 %copy-start.2 = (bf16[256,512]{1,0:T(8,128)(2,1)S(1)}, bf16[256,512]{1,0:T(8,128)(2,1)}, u32[]{:S(2)}) copy-start(bf16[256,512]{1,0:T(8,128)(2,1)} %constant.7.clone.plane_l) | copy-start | bytes 786436
  5.0 17.3 %copy-start.3 = (bf16[256,512]{1,0:T(8,128)(2,1)S(1)}, bf16[256,512]{1,0:T(8,128)(2,1)}, u32[]{:S(2)}) copy-start(bf16[256,512]{1,0:T(8,128)(2,1)} %constant.6.clone.plane_h) | copy-start | bytes 786436
  5.0 17.3 %copy-start.4 = (bf16[256,256]{1,0:T(8,128)(2,1)S(1)}, bf16[256,256]{1,0:T(8,128)(2,1)}, u32[]{:S(2)}) copy-start(bf16[256,256]{1,0:T(8,128)(2,1)} %constant.8.clone.span_w) | copy-start | bytes 393220
  5.0 6.6 %collective-permute-start.2 = (f32[4,16,128]{2,1,0:T(8,128)S(1)}, f32[4,16,128]{2,1,0:T(8,128)S(1)}, u32[]{:S(2)}, u32[]{:S(2)}) collective-permute-start(f32[4,16,128]{2,1,0:T(8,128)S(1)} %get-tuple-element.10), channel_id=1, source_target_pairs={{0,25},{1,8},{8,1},{9,16},{16,9},{17,24},{24,17},{25,0},{2,27},{3,... | collective-permute-start | bytes 98312 | tf_op jit(solution)/shard_map/ppermute | solution.py:287
  11.8 10.5 %collective-permute-start.4 = (f32[4,16,16,128]{3,2,1,0:T(8,128)S(1)}, f32[4,16,16,128]{3,2,1,0:T(8,128)S(1)}, u32[]{:S(2)}, u32[]{:S(2)}) collective-permute-start(f32[4,16,16,128]{3,2,1,0:T(8,128)S(1)} %merge.1.mid), channel_id=1, source_target_pairs={{0,0},{2,4},{4,2},{6,6},{1,1},{3,5},{5,3},{7,7},{8,8},{10,12},{12,... | collective-permute-start | bytes 1572872 | tf_op jit(solution)/shard_map/ppermute | solution.py:272
  13.8 8.6 %collective-permute-start.3 = (f32[4,16,16,128]{3,2,1,0:T(8,128)S(1)}, f32[4,16,16,128]{3,2,1,0:T(8,128)S(1)}, u32[]{:S(2)}, u32[]{:S(2)}) collective-permute-start(f32[4,16,16,128]{3,2,1,0:T(8,128)S(1)} %merge.1.mid), channel_id=1, source_target_pairs={{0,2},{2,0},{4,6},{6,4},{1,3},{3,1},{5,7},{7,5},{8,10},{10,8},{12,... | collective-permute-start | bytes 1572872 | tf_op jit(solution)/shard_map/ppermute | solution.py:269
  26.6 12.9 %collective-permute-start.9 = (f32[3,8,16,128]{3,2,1,0:T(8,128)S(1)}, f32[3,8,16,128]{3,2,1,0:T(8,128)S(1)}, u32[]{:S(2)}, u32[]{:S(2)}) collective-permute-start(f32[3,8,16,128]{3,2,1,0:T(8,128)S(1)} %get-tuple-element.13), channel_id=1, source_target_pairs={{0,1},{1,0},{2,3},{3,2},{4,5},{5,4},{6,7},{7,6},{8,9},{9,8},{10,11... | collective-permute-start | bytes 589832 | tf_op jit(solution)/shard_map/ppermute | solution.py:266
  27.4 5.0 %collective-permute-start.5 = (f32[16,128]{1,0:T(8,128)S(1)}, f32[16,128]{1,0:T(8,128)S(1)}, u32[]{:S(2)}, u32[]{:S(2)}) collective-permute-start(f32[16,128]{1,0:T(8,128)S(1)} %get-tuple-element.11), channel_id=1, source_target_pairs={{0,1},{1,0},{2,3},{3,2},{4,5},{5,4},{6,7},{7,6},{8,9},{9,8},{10,11... | collective-permute-start | bytes 24584 | tf_op jit(solution)/shard_map/ppermute | solution.py:266
  32.4 3.7 %collective-permute-start.8 = (f32[16,128]{1,0:T(8,128)S(1)}, f32[16,128]{1,0:T(8,128)S(1)}, u32[]{:S(2)}, u32[]{:S(2)}) collective-permute-start(f32[16,128]{1,0:T(8,128)S(1)} %add.3.refs_0_), channel_id=1, source_target_pairs={{0,24},{8,0},{16,8},{24,16},{1,25},{9,1},{17,9},{25,17},{2,26},{10... | collective-permute-start | bytes 24584 | tf_op jit(solution)/shard_map/ppermute | solution.py:318
  34.1 4.5 %collective-permute-start.7 = (f32[16,128]{1,0:T(8,128)S(1)}, f32[16,128]{1,0:T(8,128)S(1)}, u32[]{:S(2)}, u32[]{:S(2)}) collective-permute-start(f32[16,128]{1,0:T(8,128)S(1)} %add.3.refs_0_), channel_id=1, source_target_pairs={{0,16},{8,24},{16,0},{24,8},{1,17},{9,25},{17,1},{25,9},{2,18},{10... | collective-permute-start | bytes 24584 | tf_op jit(solution)/shard_map/ppermute | solution.py:318
  34.1 5.4 %collective-permute-start.6 = (f32[16,128]{1,0:T(8,128)S(1)}, f32[16,128]{1,0:T(8,128)S(1)}, u32[]{:S(2)}, u32[]{:S(2)}) collective-permute-start(f32[16,128]{1,0:T(8,128)S(1)} %add.3.refs_0_), channel_id=1, source_target_pairs={{0,8},{8,16},{16,24},{24,0},{1,9},{9,17},{17,25},{25,1},{2,10},{10... | collective-permute-start | bytes 24584 | tf_op jit(solution)/shard_map/ppermute | solution.py:318

commit v6 on v5

--- a/solution.py
+++ b/solution.py
@@ -82,25 +82,32 @@
     to_own_side[...] = jnp.where(me_s == 0, sides[1], sides[0])
 
 
-def merge_kernel(own, part, own_strip, part_strip, merged):
+def unpack(packed, block, start):
+    _, layers, rows, width = block.shape
+    half = layers // 2
+    beyond = lane_index((half, rows, width)) // rim == start // rim
+    for f in range(4):
+        for k in range(2):
+            place = k * 64 + f * rim
+            cells = pltpu.roll(packed, lax.rem(start - place + 2 * width, width), 2)
+            yield f, k, jnp.where(beyond, cells, block[f, k * half : (k + 1) * half])
+
+
+def merge_kernel(own, part, own_strip, part_strip, merged, rest):
     _, layers, rows, width = own.shape
     half = layers // 2
     me_s = lax.axis_index("stream")
     start = jnp.where(me_s == 0, width - rim, 0)
-    lane = lane_index((half, rows, width))
-    beyond = lane // rim == start // rim
-    for where, block, strip in ((me_s, own, own_strip), (1 - me_s, part, part_strip)):
-        packed = strip[...]
-        for k in range(2):
-            for f in range(4):
-                place = k * 64 + f * rim
-                cells = pltpu.roll(packed, lax.rem(start - place + 2 * width, width), 2)
-                layer = where * layers + k * half
-                merged[f, pl.ds(layer, half)] = jnp.where(beyond, cells, block[f, k * half : (k + 1) * half])
+    for f, k, cells in unpack(own_strip[...], own, start):
+        merged[f, pl.ds(me_s * layers + k * half, half)] = cells
+    for f, k, cells in unpack(part_strip[...], part, start):
+        merged[f, pl.ds((1 - me_s) * layers + k * half, half)] = cells
+        rest[f * layers + k * half : f * layers + (k + 1) * half] = cells
+    rest[4 * layers :] = own_strip[...]
 
 
 def flux_kernel(
-    walls, mid, a_block, b_block, plane_h, plane_l, span_w, keep_ref, send_ref, sums_ref,
+    walls, mid, a_block, b_own, b_rest, plane_h, plane_l, span_w, keep_ref, send_ref, sums_ref,
     raw, in_h, in_l, prod_h, prod_l, mean, mid_h, mid_l, clark_all, similar_all,
 ):
     _, both, rows, width = mid.shape
@@ -116,7 +123,13 @@
 
     raw[:, :, rows : 2 * rows, :] = mid[...]
     raw[:, :, pl.ds(row_a, rows), :] = a_block[...]
-    raw[:, :, pl.ds(row_b, rows), :] = b_block[...] * keep_b
+    start = jnp.where(me_s == 0, width - rim, 0)
+    for f, k, value in unpack(b_rest[4 * layers :], b_own, start):
+        along = pl.ds(me_s * layers + k * (layers // 2), layers // 2)
+        raw[f, along, pl.ds(row_b, rows), :] = value * keep_b
+    for f in range(4):
+        value = b_rest[f * layers : (f + 1) * layers]
+        raw[f, pl.ds((1 - me_s) * layers, layers), pl.ds(row_b, rows), :] = value * keep_b
 
     def column(t):
         return slice(t * width, (t + 1) * width)
@@ -210,15 +223,12 @@
         send_ref[i] = jnp.where(first, clark, similar)
 
 
-def finish_kernel(plane_cells, spans, *refs):
-    tables = refs[:spans]
-    keep, come, clark_model, similar_model, clark_corr, similar_corr, ordered = refs[spans:]
+def finish_kernel(
+    plane_cells, tables, keep, come, clark_model, similar_model, clark_corr, similar_corr
+):
     _, layers, rows, width = keep.shape
     me_s = lax.axis_index("stream")
-    me_p = lax.axis_index("span")
-    for step, one in enumerate(tables):
-        ordered[lax.rem(me_p - step + spans, spans)] = one[...]
-    table = jnp.sum(ordered[...], axis=0) / plane_cells
+    table = jnp.sum(tables[...], axis=0) / plane_cells
     lane = lane_index((rows, width))
     useful = lane // (width // 2) == me_s
     corr = jnp.zeros((rows, width), jnp.float32)
@@ -286,15 +296,21 @@
     part = swap(fields)
     part_strip = lax.ppermute(first, ("span", "stream"), to_other)
     own_strip = lax.ppermute(second, ("span", "stream"), to_same)
-    (mid,) = call(merge_kernel, "merge", (fields, part, own_strip, part_strip), ((4, both, rows, width),))
-    b_block, a_block = pair_b(mid), pair_a(mid)
+    part, b_own = lax.optimization_barrier((part, pair_b(fields)))
+    mid, rest = call(
+        merge_kernel,
+        "merge",
+        (fields, part, own_strip, part_strip),
+        ((4, both, rows, width), (4 * layers + layers // 2, rows, width)),
+    )
+    b_rest, a_block = pair_b(rest), pair_a(mid)
 
     plane_h, plane_l = plane_constants(both, rows)
     single, brief = jnp.float32, jnp.bfloat16
     keep, send, sums = call(
         functools.partial(flux_kernel, walls),
         "flux",
-        (mid, a_block, b_block, jnp.asarray(plane_h), jnp.asarray(plane_l), jnp.asarray(span_constants(width))),
+        (mid, a_block, b_own, b_rest, jnp.asarray(plane_h), jnp.asarray(plane_l), jnp.asarray(span_constants(width))),
         ((6, layers, rows, width), (3, layers, rows, width), (rows, width)),
         [
             ((4, both, 3 * rows, width), single),
@@ -311,18 +327,16 @@
         mib=32,
     )
 
-    sums = sums + swap(sums)
+    other, send = lax.optimization_barrier((swap(sums), send))
     come = swap(send)
-    tables = [sums]
-    for step in range(1, spans):
-        tables.append(lax.ppermute(sums, "span", [(p, (p + step) % spans) for p in range(spans)]))
+    tables = jnp.broadcast_to((sums + other)[None], (spans, rows, width))
+    tables = lax.all_to_all(tables, "span", 0, 0)
     block, corr = (3, layers, rows, width), (3, rows)
     return call(
-        functools.partial(finish_kernel, float(layers * width * spans * streams), spans),
+        functools.partial(finish_kernel, float(layers * width * spans * streams)),
         "finish",
-        (*tables, keep, come),
+        (tables, keep, come),
         (block, block, corr, corr),
-        [((spans, rows, width), single)],
     )
 
 

time: 40.7 us -> 41.6 us (1.022)
  blocking collectives: 0 us -> 8.96 us
  waiting for transfers between devices: 20.7 us -> 12.9 us
  starting transfers between devices: 12.5 us -> 11.4 us
  local copies, waits for them, and re-layouts: 1 us -> 1.9 us
    all_to_all x0 -> x1, blocking collectives: none -> 8.96 us  [shards(): tables = lax.all_to_all(tables, 'span', 0, 0)]
    ppermute x3 -> x0, waiting for transfers between devices: 4.28 us -> none  [shards(): lax.ppermute(sums, 'span', [(p, (p + step) % spans) for p in range(spans)])]
    ppermute x3 -> x0, starting transfers between devices: 2.81 us -> none  [shards(): lax.ppermute(sums, 'span', [(p, (p + step) % spans) for p in range(spans)])]
    ppermute x1 -> x2, waiting for transfers between devices: 8.49 us -> 5.92 us  [pair_b(): lax.ppermute(value, 'wall', [(w, min(max((w + 1 ^ 1) - 1, 0), walls - 1))...]
    ppermute x1 -> x2, starting transfers between devices: 1.92 us -> 4.04 us  [pair_b(): lax.ppermute(value, 'wall', [(w, min(max((w + 1 ^ 1) - 1, 0), walls - 1))...]
    ppermute x1, waiting for transfers between devices: 1.71 us -> 0.61 us  [shards(): own_strip = lax.ppermute(second, ('span', 'stream'), to_same)]
    unnamed x10, local copies, waits for them, and re-layouts: 1 us -> 1.89 us
    ppermute x3, starting transfers between devices: 3.65 us -> 3.22 us  [swap(): return lax.ppermute(value, 'stream', [(0, 1), (1, 0)])]
  transfers between devices with their start and end apart: 10 -> 8, of which waited for: 7 -> 5; matrix products, arithmetic and copies ran while one was open for 0% -> 0% of each run, Pallas kernels for 0% -> 0%
where the time goes in v6:
time: 41.6 us; the launch traced here: 41.4 us
  waiting for transfers between devices  12.9 us (31%)
  starting transfers between devices  11.4 us (27%)
  blocking collectives  8.96 us (22%)
  Pallas kernels  5.46 us (13%)
  local copies, waits for them, and re-layouts  1.9 us (5%)
  between operations  0.69 us (2%)
    all_to_all x1, blocking collectives, shards(): tables = lax.all_to_all(tables, 'span', 0, 0)  8.96 us
    ppermute x2, waiting for transfers between devices, pair_b(): lax.ppermute(value, 'wall', [(w, min(max((w + 1 ^ 1) - 1, 0), walls - 1))...  5.92 us
    pallas_call x4, Pallas kernels, call(): pl.pallas_call(kernel, out_shape=tuple((jax.ShapeDtypeStruct(shape, jnp.f...  5.46 us
    ppermute x2, starting transfers between devices, pair_b(): lax.ppermute(value, 'wall', [(w, min(max((w + 1 ^ 1) - 1, 0), walls - 1))...  4.04 us
    ppermute x3, waiting for transfers between devices, swap(): return lax.ppermute(value, 'stream', [(0, 1), (1, 0)])  3.98 us
    ppermute x3, starting transfers between devices, swap(): return lax.ppermute(value, 'stream', [(0, 1), (1, 0)])  3.22 us
    ppermute x1, starting transfers between devices, shards(): part_strip = lax.ppermute(first, ('span', 'stream'), to_other)  2.45 us
    ppermute x1, waiting for transfers between devices, shards(): part_strip = lax.ppermute(first, ('span', 'stream'), to_other)  2.43 us
  transfers between devices with their start and end apart: 8, of which 5 were waited for; matrix products, arithmetic and copies ran while one was open for 0% of the time, Pallas kernels for 0%

profile of v6, /device:TPU:4, one launch (start us, length us, event | category | flops | bytes accessed | tf_op | source)
XLA Modules:
  0.0 41.4 jit_solution(9203441734430022419)
XLA Ops:
  0.6 1.9 %collective-permute-start.1 = (f32[4,8,16,128]{3,2,1,0:T(8,128)}, f32[4,8,16,128]{3,2,1,0:T(8,128)S(1)}, u32[]{:S(2)}, u32[]{:S(2)}) collective-permute-start(f32[4,8,16,128]{3,2,1,0:T(8,128)} %own.3), channel_id=1, source_target_pairs={{0,0},{2,4},{4,2},{6,6},{1,1},{3,5},{5,3},{7,7},{8,8},{10,12},{12,... | collective-permute-start | bytes 786440 | tf_op jit(solution)/shard_map/ppermute | solution.py:282
  2.6 1.6 %collective-permute-start = (f32[4,8,16,128]{3,2,1,0:T(8,128)}, f32[4,8,16,128]{3,2,1,0:T(8,128)S(1)}, u32[]{:S(2)}, u32[]{:S(2)}) collective-permute-start(f32[4,8,16,128]{3,2,1,0:T(8,128)} %own.3), channel_id=1, source_target_pairs={{0,1},{1,0},{2,3},{3,2},{4,5},{5,4},{6,7},{7,6},{8,9},{9,8},{10,11... | collective-permute-start | bytes 786440 | tf_op jit(solution)/shard_map/ppermute | solution.py:276
  4.1 1.0 %copy-done = f32[4,8,16,128]{3,2,1,0:T(8,128)S(1)} copy-done((f32[4,8,16,128]{3,2,1,0:T(8,128)S(1)}, f32[4,8,16,128]{3,2,1,0:T(8,128)}, u32[]{:S(2)}) %copy-start) | copy-done | bytes 262168
  5.1 0.2 edges.1
  5.3 1.6 %collective-permute-start.2 = (f32[4,16,128]{2,1,0:T(8,128)S(1)}, f32[4,16,128]{2,1,0:T(8,128)S(1)}, u32[]{:S(2)}, u32[]{:S(2)}) collective-permute-start(f32[4,16,128]{2,1,0:T(8,128)S(1)} %get-tuple-element.16), channel_id=1, source_target_pairs={{1,25},{0,8},{9,1},{8,16},{17,9},{16,24},{25,17},{24,0},{3,27},{2,... | collective-permute-start | bytes 98312 | tf_op jit(solution)/shard_map/ppermute | solution.py:298
  6.9 2.4 %collective-permute-start.3 = (f32[4,16,128]{2,1,0:T(8,128)S(1)}, f32[4,16,128]{2,1,0:T(8,128)S(1)}, u32[]{:S(2)}, u32[]{:S(2)}) collective-permute-start(f32[4,16,128]{2,1,0:T(8,128)S(1)} %get-tuple-element.17), channel_id=1, source_target_pairs={{0,25},{1,8},{8,1},{9,16},{16,9},{17,24},{24,17},{25,0},{2,27},{3,... | collective-permute-start | bytes 98312 | tf_op jit(solution)/shard_map/ppermute | solution.py:297
  9.4 0.0 collective-permute-done.1.b_own
  9.4 1.1 %collective-permute-done.part = f32[4,8,16,128]{3,2,1,0:T(8,128)S(1)} collective-permute-done((f32[4,8,16,128]{3,2,1,0:T(8,128)}, f32[4,8,16,128]{3,2,1,0:T(8,128)S(1)}, u32[]{:S(2)}, u32[]{:S(2)}) %collective-permute-start) | collective-permute-done | bytes 262176 | tf_op jit(solution)/shard_map/ppermute | solution.py:276
  10.5 0.6 %collective-permute-done.2.own_strip = f32[4,16,128]{2,1,0:T(8,128)S(1)} collective-permute-done((f32[4,16,128]{2,1,0:T(8,128)S(1)}, f32[4,16,128]{2,1,0:T(8,128)S(1)}, u32[]{:S(2)}, u32[]{:S(2)}) %collective-permute-start.2) | collective-permute-done | bytes 32800 | tf_op jit(solution)/shard_map/ppermute | solution.py:298
  11.1 2.4 %collective-permute-done.3.part_strip = f32[4,16,128]{2,1,0:T(8,128)S(1)} collective-permute-done((f32[4,16,128]{2,1,0:T(8,128)S(1)}, f32[4,16,128]{2,1,0:T(8,128)S(1)}, u32[]{:S(2)}, u32[]{:S(2)}) %collective-permute-start.3) | collective-permute-done | bytes 32800 | tf_op jit(solution)/shard_map/ppermute | solution.py:297
  13.5 0.2 merge.1
  13.8 0.1 collective-permute-start.4
  13.8 2.1 %collective-permute-start.5 = (f32[36,16,128]{2,1,0:T(8,128)S(1)}, f32[36,16,128]{2,1,0:T(8,128)S(1)}, u32[]{:S(2)}, u32[]{:S(2)}) collective-permute-start(f32[36,16,128]{2,1,0:T(8,128)S(1)} %get-tuple-element.20), channel_id=1, source_target_pairs={{0,0},{2,4},{4,2},{6,6},{1,1},{3,5},{5,3},{7,7},{8,8},{10,12},{12,... | collective-permute-start | bytes 884744 | tf_op jit(solution)/shard_map/ppermute | solution.py:282
  16.0 5.9 %collective-permute-done.5.b_rest = f32[36,16,128]{2,1,0:T(8,128)S(1)} collective-permute-done((f32[36,16,128]{2,1,0:T(8,128)S(1)}, f32[36,16,128]{2,1,0:T(8,128)S(1)}, u32[]{:S(2)}, u32[]{:S(2)}) %collective-permute-start.5) | collective-permute-done | bytes 294944 | tf_op jit(solution)/shard_map/ppermute | solution.py:282
  21.9 0.0 collective-permute-done.4.a_block
  21.9 0.0 copy-start.4
  21.9 0.9 %copy-done.4 = bf16[256,256]{1,0:T(8,128)(2,1)S(1)} copy-done((bf16[256,256]{1,0:T(8,128)(2,1)S(1)}, bf16[256,256]{1,0:T(8,128)(2,1)}, u32[]{:S(2)}) %copy-start.4) | copy-done | bytes 131096
  22.8 4.1 %flux.1 = (f32[6,8,16,128]{3,2,1,0:T(8,128)S(1)}, f32[3,8,16,128]{3,2,1,0:T(8,128)S(1)}, f32[16,128]{1,0:T(8,128)S(1)}) custom-call(f32[4,16,16,128]{3,2,1,0:T(8,128)S(1)} %get-tuple-element.18.mid, f32[4,16,16,128]{3,2,1,0:T(8,128)S(1)} %collective-permute-done.4.a_block, f32[4,8,16,128]{3,2,1,0:T(8,128)S(1)} %collective-permute-done.1.b_own, ...), custom_call_target="tpu_custom_call" | custom-call | tf_op jit(solution)/shard_map/flux/pallas_call | solution.py:256
  26.9 0.9 %collective-permute-start.6 = (f32[16,128]{1,0:T(8,128)S(1)}, f32[16,128]{1,0:T(8,128)S(1)}, u32[]{:S(2)}, u32[]{:S(2)}) collective-permute-start(f32[16,128]{1,0:T(8,128)S(1)} %get-tuple-element.21), channel_id=1, source_target_pairs={{0,1},{1,0},{2,3},{3,2},{4,5},{5,4},{6,7},{7,6},{8,9},{9,8},{10,11... | collective-permute-start | bytes 24584 | tf_op jit(solution)/shard_map/ppermute | solution.py:276
  27.7 2.9 %collective-permute-done.6 = f32[16,128]{1,0:T(8,128)S(1)} collective-permute-done((f32[16,128]{1,0:T(8,128)S(1)}, f32[16,128]{1,0:T(8,128)S(1)}, u32[]{:S(2)}, u32[]{:S(2)}) %collective-permute-start.6) | collective-permute-done | bytes 8224 | tf_op jit(solution)/shard_map/ppermute | solution.py:276
  30.6 0.8 %collective-permute-start.7 = (f32[3,8,16,128]{3,2,1,0:T(8,128)S(1)}, f32[3,8,16,128]{3,2,1,0:T(8,128)S(1)}, u32[]{:S(2)}, u32[]{:S(2)}) collective-permute-start(f32[3,8,16,128]{3,2,1,0:T(8,128)S(1)} %get-tuple-element.25), channel_id=1, source_target_pairs={{0,1},{1,0},{2,3},{3,2},{4,5},{5,4},{6,7},{7,6},{8,9},{9,8},{10,11... | collective-permute-start | bytes 589832 | tf_op jit(solution)/shard_map/ppermute | solution.py:276
  31.4 9.0 %all_to_all.5.tables = f32[4,16,128]{2,1,0:T(8,128)S(1)} all-to-all(f32[4,16,128]{2,1,0:T(8,128)S(1)} %broadcast_in_dim.2), channel_id=1, replica_groups=mesh['span'=4,'wall'=4,'stream'=2] {'span'}, dimensions={0} | all-to-all | bytes 65536 | tf_op jit(solution)/shard_map/all_to_all | solution.py:333
  40.3 0.0 collective-permute-done.7.come
  40.3 1.0 %finish.1 = (f32[3,8,16,128]{3,2,1,0:T(8,128)}, f32[3,8,16,128]{3,2,1,0:T(8,128)}, f32[3,16]{1,0:T(4,128)}, f32[3,16]{1,0:T(4,128)}) custom-call(f32[4,16,128]{2,1,0:T(8,128)S(1)} %all_to_all.5.tables, f32[6,8,16,128]{3,2,1,0:T(8,128)S(1)} %get-tuple-element.24.keep, f32[3,8,16,128]{3,2,1,0:T(8,128)S(1)} %collective-permute-done.7.come), custom_call_target="tpu_custom_call" | custom-call | tf_op jit(solution)/shard_map/finish/pallas_call | solution.py:256
  (9 shorter events, 0.0 us)
Async XLA Ops:
  0.6 8.7 %collective-permute-start.1 = (f32[4,8,16,128]{3,2,1,0:T(8,128)}, f32[4,8,16,128]{3,2,1,0:T(8,128)S(1)}, u32[]{:S(2)}, u32[]{:S(2)}) collective-permute-start(f32[4,8,16,128]{3,2,1,0:T(8,128)} %own.3), channel_id=1, source_target_pairs={{0,0},{2,4},{4,2},{6,6},{1,1},{3,5},{5,3},{7,7},{8,8},{10,12},{12,... | collective-permute-start | bytes 786440 | tf_op jit(solution)/shard_map/ppermute | solution.py:282
  2.6 7.9 %collective-permute-start = (f32[4,8,16,128]{3,2,1,0:T(8,128)}, f32[4,8,16,128]{3,2,1,0:T(8,128)S(1)}, u32[]{:S(2)}, u32[]{:S(2)}) collective-permute-start(f32[4,8,16,128]{3,2,1,0:T(8,128)} %own.3), channel_id=1, source_target_pairs={{0,1},{1,0},{2,3},{3,2},{4,5},{5,4},{6,7},{7,6},{8,9},{9,8},{10,11... | collective-permute-start | bytes 786440 | tf_op jit(solution)/shard_map/ppermute | solution.py:276
  4.1 1.0 %copy-start = (f32[4,8,16,128]{3,2,1,0:T(8,128)S(1)}, f32[4,8,16,128]{3,2,1,0:T(8,128)}, u32[]{:S(2)}) copy-start(f32[4,8,16,128]{3,2,1,0:T(8,128)} %own.3) | copy-start | bytes 786436
  5.1 8.4 %copy-start.1 = (f32[4,8,16,128]{3,2,1,0:T(8,128)S(1)}, f32[4,8,16,128]{3,2,1,0:T(8,128)}, u32[]{:S(2)}) copy-start(f32[4,8,16,128]{3,2,1,0:T(8,128)} %own.3) | copy-start | bytes 786436
  5.3 5.8 %collective-permute-start.2 = (f32[4,16,128]{2,1,0:T(8,128)S(1)}, f32[4,16,128]{2,1,0:T(8,128)S(1)}, u32[]{:S(2)}, u32[]{:S(2)}) collective-permute-start(f32[4,16,128]{2,1,0:T(8,128)S(1)} %get-tuple-element.16), channel_id=1, source_target_pairs={{1,25},{0,8},{9,1},{8,16},{17,9},{16,24},{25,17},{24,0},{3,27},{2,... | collective-permute-start | bytes 98312 | tf_op jit(solution)/shard_map/ppermute | solution.py:298
  6.9 15.0 %copy-start.2 = (bf16[256,512]{1,0:T(8,128)(2,1)S(1)}, bf16[256,512]{1,0:T(8,128)(2,1)}, u32[]{:S(2)}) copy-start(bf16[256,512]{1,0:T(8,128)(2,1)} %constant.7.clone.plane_l) | copy-start | bytes 786436
  6.9 15.0 %copy-start.3 = (bf16[256,512]{1,0:T(8,128)(2,1)S(1)}, bf16[256,512]{1,0:T(8,128)(2,1)}, u32[]{:S(2)}) copy-start(bf16[256,512]{1,0:T(8,128)(2,1)} %constant.6.clone.plane_h) | copy-start | bytes 786436
  6.9 6.6 %collective-permute-start.3 = (f32[4,16,128]{2,1,0:T(8,128)S(1)}, f32[4,16,128]{2,1,0:T(8,128)S(1)}, u32[]{:S(2)}, u32[]{:S(2)}) collective-permute-start(f32[4,16,128]{2,1,0:T(8,128)S(1)} %get-tuple-element.17), channel_id=1, source_target_pairs={{0,25},{1,8},{8,1},{9,16},{16,9},{17,24},{24,17},{25,0},{2,27},{3,... | collective-permute-start | bytes 98312 | tf_op jit(solution)/shard_map/ppermute | solution.py:297
  13.8 8.1 %collective-permute-start.4 = (f32[4,16,16,128]{3,2,1,0:T(8,128)S(1)}, f32[4,16,16,128]{3,2,1,0:T(8,128)S(1)}, u32[]{:S(2)}, u32[]{:S(2)}) collective-permute-start(f32[4,16,16,128]{3,2,1,0:T(8,128)S(1)} %get-tuple-element.18.mid), channel_id=1, source_target_pairs={{0,2},{2,0},{4,6},{6,4},{1,3},{3,1},{5,7},{7,5},{8,10},{10,8},{12,... | collective-permute-start | bytes 1572872 | tf_op jit(solution)/shard_map/ppermute | solution.py:279
  13.8 8.0 %collective-permute-start.5 = (f32[36,16,128]{2,1,0:T(8,128)S(1)}, f32[36,16,128]{2,1,0:T(8,128)S(1)}, u32[]{:S(2)}, u32[]{:S(2)}) collective-permute-start(f32[36,16,128]{2,1,0:T(8,128)S(1)} %get-tuple-element.20), channel_id=1, source_target_pairs={{0,0},{2,4},{4,2},{6,6},{1,1},{3,5},{5,3},{7,7},{8,8},{10,12},{12,... | collective-permute-start | bytes 884744 | tf_op jit(solution)/shard_map/ppermute | solution.py:282
  21.9 0.9 %copy-start.4 = (bf16[256,256]{1,0:T(8,128)(2,1)S(1)}, bf16[256,256]{1,0:T(8,128)(2,1)}, u32[]{:S(2)}) copy-start(bf16[256,256]{1,0:T(8,128)(2,1)} %constant.8.clone.span_w) | copy-start | bytes 393220
  26.9 3.7 %collective-permute-start.6 = (f32[16,128]{1,0:T(8,128)S(1)}, f32[16,128]{1,0:T(8,128)S(1)}, u32[]{:S(2)}, u32[]{:S(2)}) collective-permute-start(f32[16,128]{1,0:T(8,128)S(1)} %get-tuple-element.21), channel_id=1, source_target_pairs={{0,1},{1,0},{2,3},{3,2},{4,5},{5,4},{6,7},{7,6},{8,9},{9,8},{10,11... | collective-permute-start | bytes 24584 | tf_op jit(solution)/shard_map/ppermute | solution.py:276
  30.6 9.8 %collective-permute-start.7 = (f32[3,8,16,128]{3,2,1,0:T(8,128)S(1)}, f32[3,8,16,128]{3,2,1,0:T(8,128)S(1)}, u32[]{:S(2)}, u32[]{:S(2)}) collective-permute-start(f32[3,8,16,128]{3,2,1,0:T(8,128)S(1)} %get-tuple-element.25), channel_id=1, source_target_pairs={{0,1},{1,0},{2,3},{3,2},{4,5},{5,4},{6,7},{7,6},{8,9},{9,8},{10,11... | collective-permute-start | bytes 589832 | tf_op jit(solution)/shard_map/ppermute | solution.py:276

commit v7 on v6

--- a/solution.py
+++ b/solution.py
@@ -64,55 +64,88 @@
     return lax.broadcasted_iota(jnp.int32, shape, len(shape) - 1)
 
 
-def edge_kernel(own, to_partner_side, to_own_side):
-    _, layers, rows, width = own.shape
-    half = layers // 2
-    lane = lane_index((half, rows, width))
-    me_s = lax.axis_index("stream")
-    sides = []
-    for start in (0, width - rim):
-        total = jnp.zeros((half, rows, width), jnp.float32)
-        for k in range(2):
-            for f in range(4):
-                place = k * 64 + f * rim
-                cells = pltpu.roll(own[f, k * half : (k + 1) * half], (place - start) % width, 2)
-                total = jnp.where(lane // rim == place // rim, cells, total)
-        sides.append(total)
-    to_partner_side[...] = jnp.where(me_s == 0, sides[0], sides[1])
-    to_own_side[...] = jnp.where(me_s == 0, sides[1], sides[0])
-
-
-def unpack(packed, block, start):
+def unit_index(shape):
+    return lane_index(shape) // rim
+
+
+def pack_halves(block, half):
+    width = block.shape[-1]
+    in_place = lane_index(block.shape[1:]) // (width // 2) == half
+    for pair in range(2):
+        moved = pltpu.roll(block[2 * pair + 1], width // 2, 2)
+        yield pair, jnp.where(in_place, block[2 * pair], moved)
+
+
+def pack_strip(block, unit):
     _, layers, rows, width = block.shape
     half = layers // 2
-    beyond = lane_index((half, rows, width)) // rim == start // rim
-    for f in range(4):
-        for k in range(2):
-            place = k * 64 + f * rim
-            cells = pltpu.roll(packed, lax.rem(start - place + 2 * width, width), 2)
-            yield f, k, jnp.where(beyond, cells, block[f, k * half : (k + 1) * half])
-
-
-def merge_kernel(own, part, own_strip, part_strip, merged, rest):
+    units = unit_index((half, rows, width))
+    total = jnp.zeros((half, rows, width), jnp.float32)
+    for k in range(2):
+        for f in range(4):
+            step = 2 * f + k
+            cells = block[f, k * half : (k + 1) * half]
+            cells = pltpu.roll(cells, step * rim, 2) if step else cells
+            total = jnp.where(units == lax.rem(unit + step, width // rim), cells, total)
+    return total
+
+
+def strip_tile(inner, outer, me_s):
+    width = inner.shape[-1]
+    is_outer = lax.rem(unit_index(inner.shape), 2) == 1 - me_s
+    for k in range(2):
+        shift = (width - k * rim) % width
+        pieces = [pltpu.roll(strip, shift, 2) if k else strip for strip in (inner, outer)]
+        yield k, jnp.where(is_outer, pieces[1], pieces[0])
+
+
+def pack_kernel(own, to_partner, to_other, to_same):
+    _, layers, _, _ = own.shape
+    me_s = lax.axis_index("stream")
+    for pair, tile in pack_halves(own, 1 - me_s):
+        to_partner[pair * layers : (pair + 1) * layers] = tile
+    to_partner[2 * layers :] = pack_strip(own, 3 + me_s)
+    to_other[...] = pack_strip(own, 7 * me_s)
+    to_same[...] = pack_strip(own, 7 * (1 - me_s))
+
+
+def merge_kernel(own, part, own_strip, part_strip, packed):
     _, layers, rows, width = own.shape
     half = layers // 2
     me_s = lax.axis_index("stream")
-    start = jnp.where(me_s == 0, width - rim, 0)
-    for f, k, cells in unpack(own_strip[...], own, start):
-        merged[f, pl.ds(me_s * layers + k * half, half)] = cells
-    for f, k, cells in unpack(part_strip[...], part, start):
-        merged[f, pl.ds((1 - me_s) * layers + k * half, half)] = cells
-        rest[f * layers + k * half : f * layers + (k + 1) * half] = cells
-    rest[4 * layers :] = own_strip[...]
+    mine, other = me_s * layers, (1 - me_s) * layers
+    for pair, tile in pack_halves(own, me_s):
+        packed[pair, pl.ds(mine, layers)] = tile
+        packed[pair, pl.ds(other, layers)] = part[pair * layers : (pair + 1) * layers]
+    for k, tile in strip_tile(pack_strip(own, 4 - me_s), own_strip[...], me_s):
+        packed[2, pl.ds(mine + k * half, half)] = tile
+    for k, tile in strip_tile(part[2 * layers :], part_strip[...], me_s):
+        packed[2, pl.ds(other + k * half, half)] = tile
+
+
+def unpack(packed, me_s):
+    width = packed.shape[-1]
+    unit = unit_index(packed.shape[1:])
+    first = 4 * (1 - me_s)
+    in_strip = (unit == first) | (unit == first + 3)
+    for f in range(4):
+        cells = packed[f // 2]
+        cells = pltpu.roll(cells, width // 2, 2) if f % 2 else cells
+        strip = packed[2]
+        strip = pltpu.roll(strip, width - 2 * f * rim, 2) if f else strip
+        yield f, jnp.where(in_strip, strip, cells)
 
 
 def flux_kernel(
-    walls, mid, a_block, b_own, b_rest, plane_h, plane_l, span_w, keep_ref, send_ref, sums_ref,
+    walls, mid, a_block, b_block, weights, keep_ref, send_ref, sums_ref,
     raw, in_h, in_l, prod_h, prod_l, mean, mid_h, mid_l, clark_all, similar_all,
 ):
     _, both, rows, width = mid.shape
     layers = both // 2
     cells = both * rows
+    plane_h = weights.at[:cells]
+    plane_l = weights.at[cells : 2 * cells]
+    span_w = weights.at[2 * cells :, : 2 * width]
     me_s = lax.axis_index("stream")
     me_w = lax.axis_index("wall")
     odd = lax.rem(me_w, 2)
@@ -121,15 +154,12 @@
     at_end = (me_w == 0) | (me_w == walls - 1)
     keep_b = jnp.where(at_end, 0.0, 1.0).astype(jnp.float32)
 
-    raw[:, :, rows : 2 * rows, :] = mid[...]
-    raw[:, :, pl.ds(row_a, rows), :] = a_block[...]
-    start = jnp.where(me_s == 0, width - rim, 0)
-    for f, k, value in unpack(b_rest[4 * layers :], b_own, start):
-        along = pl.ds(me_s * layers + k * (layers // 2), layers // 2)
-        raw[f, along, pl.ds(row_b, rows), :] = value * keep_b
-    for f in range(4):
-        value = b_rest[f * layers : (f + 1) * layers]
-        raw[f, pl.ds((1 - me_s) * layers, layers), pl.ds(row_b, rows), :] = value * keep_b
+    for f, value in unpack(mid, me_s):
+        raw[f, :, rows : 2 * rows, :] = value
+    for f, value in unpack(a_block, me_s):
+        raw[f, :, pl.ds(row_a, rows), :] = value
+    for f, value in unpack(b_block, me_s):
+        raw[f, :, pl.ds(row_b, rows), :] = value * keep_b
 
     def column(t):
         return slice(t * width, (t + 1) * width)
@@ -292,25 +322,23 @@
         to_same += [(place(p, 1), place(p - 1, 1)), (place(p, 0), place(p + 1, 0))]
 
     strip = (layers // 2, rows, width)
-    first, second = call(edge_kernel, "edges", (fields,), (strip, strip))
-    part = swap(fields)
+    to_partner, first, second = call(
+        pack_kernel, "pack", (fields,), ((2 * layers + layers // 2, rows, width), strip, strip)
+    )
+    part = swap(to_partner)
     part_strip = lax.ppermute(first, ("span", "stream"), to_other)
     own_strip = lax.ppermute(second, ("span", "stream"), to_same)
-    part, b_own = lax.optimization_barrier((part, pair_b(fields)))
-    mid, rest = call(
-        merge_kernel,
-        "merge",
-        (fields, part, own_strip, part_strip),
-        ((4, both, rows, width), (4 * layers + layers // 2, rows, width)),
-    )
-    b_rest, a_block = pair_b(rest), pair_a(mid)
-
-    plane_h, plane_l = plane_constants(both, rows)
+    (mid,) = call(merge_kernel, "merge", (fields, part, own_strip, part_strip), ((3, both, rows, width),))
+    b_block, a_block = pair_b(mid), pair_a(mid)
+
+    weights = np.zeros((2 * cells + 2 * width, 2 * cells), ml_dtypes.bfloat16)
+    weights[:cells], weights[cells : 2 * cells] = plane_constants(both, rows)
+    weights[2 * cells :, : 2 * width] = span_constants(width)
     single, brief = jnp.float32, jnp.bfloat16
     keep, send, sums = call(
         functools.partial(flux_kernel, walls),
         "flux",
-        (mid, a_block, b_own, b_rest, jnp.asarray(plane_h), jnp.asarray(plane_l), jnp.asarray(span_constants(width))),
+        (mid, a_block, b_block, jnp.asarray(weights)),
         ((6, layers, rows, width), (3, layers, rows, width), (rows, width)),
         [
             ((4, both, 3 * rows, width), single),
@@ -327,13 +355,14 @@
         mib=32,
     )
 
-    other, send = lax.optimization_barrier((swap(sums), send))
     come = swap(send)
-    tables = jnp.broadcast_to((sums + other)[None], (spans, rows, width))
-    tables = lax.all_to_all(tables, "span", 0, 0)
+    group = spans * streams
+    tables = lax.all_to_all(
+        jnp.broadcast_to(sums[None], (group, rows, width)), ("span", "stream"), 0, 0
+    )
     block, corr = (3, layers, rows, width), (3, rows)
     return call(
-        functools.partial(finish_kernel, float(layers * width * spans * streams)),
+        functools.partial(finish_kernel, float(layers * width * group)),
         "finish",
         (tables, keep, come),
         (block, block, corr, corr),

time: 41.6 us -> 37.7 us (0.906)
  starting transfers between devices: 11.4 us -> 8.44 us
  waiting for transfers between devices: 12.9 us -> 11.3 us
  blocking collectives: 8.96 us -> 10.2 us
  local copies, waits for them, and re-layouts: 1.9 us -> 0.95 us
  Pallas kernels: 5.46 us -> 5.99 us
    ppermute x3 -> x2, waiting for transfers between devices: 3.98 us -> 0.01 us  [swap(): return lax.ppermute(value, 'stream', [(0, 1), (1, 0)])]
    ppermute x2 -> x1, starting transfers between devices: 4.04 us -> 1.92 us  [pair_b(): lax.ppermute(value, 'wall', [(w, min(max((w + 1 ^ 1) - 1, 0), walls - 1))...]
    all_to_all x1, blocking collectives: 8.96 us -> 10.2 us  [shards(): lax.all_to_all(jnp.broadcast_to(sums[None], (group, rows, width)), ('span...]
    ppermute x2 -> x1, waiting for transfers between devices: 5.92 us -> 7.09 us  [pair_b(): lax.ppermute(value, 'wall', [(w, min(max((w + 1 ^ 1) - 1, 0), walls - 1))...]
    ppermute x1, waiting for transfers between devices: 0.61 us -> 1.72 us  [shards(): own_strip = lax.ppermute(second, ('span', 'stream'), to_same)]
    unnamed x10 -> x4, local copies, waits for them, and re-layouts: 1.89 us -> 0.95 us
    ppermute x3 -> x2, starting transfers between devices: 3.22 us -> 2.43 us  [swap(): return lax.ppermute(value, 'stream', [(0, 1), (1, 0)])]
    pallas_call x4, Pallas kernels: 5.46 us -> 5.99 us  [call(): pl.pallas_call(kernel, out_shape=tuple((jax.ShapeDtypeStruct(shape, jnp.f...]
  transfers between devices with their start and end apart: 8 -> 6, of which waited for: 5 -> 3; matrix products, arithmetic and copies ran while one was open for 0% -> 0% of each run, Pallas kernels for 0% -> 0%
where the time goes in v7:
time: 37.7 us; the launch traced here: 37.5 us
  waiting for transfers between devices  11.3 us (30%)
  blocking collectives  10.2 us (27%)
  starting transfers between devices  8.44 us (22%)
  Pallas kernels  5.99 us (16%)
  local copies, waits for them, and re-layouts  0.95 us (3%)
  between operations  0.68 us (2%)
    all_to_all x1, blocking collectives, shards(): lax.all_to_all(jnp.broadcast_to(sums[None], (group, rows, width)), ('span...  10.2 us
    ppermute x1, waiting for transfers between devices, pair_b(): lax.ppermute(value, 'wall', [(w, min(max((w + 1 ^ 1) - 1, 0), walls - 1))...  7.09 us
    pallas_call x4, Pallas kernels, call(): pl.pallas_call(kernel, out_shape=tuple((jax.ShapeDtypeStruct(shape, jnp.f...  5.99 us
    ppermute x1, waiting for transfers between devices, shards(): part_strip = lax.ppermute(first, ('span', 'stream'), to_other)  2.45 us
    ppermute x1, starting transfers between devices, shards(): part_strip = lax.ppermute(first, ('span', 'stream'), to_other)  2.45 us
    ppermute x2, starting transfers between devices, swap(): return lax.ppermute(value, 'stream', [(0, 1), (1, 0)])  2.43 us
    ppermute x1, starting transfers between devices, pair_b(): lax.ppermute(value, 'wall', [(w, min(max((w + 1 ^ 1) - 1, 0), walls - 1))...  1.92 us
    ppermute x1, waiting for transfers between devices, shards(): own_strip = lax.ppermute(second, ('span', 'stream'), to_same)  1.72 us
  transfers between devices with their start and end apart: 6, of which 3 were waited for; matrix products, arithmetic and copies ran while one was open for 0% of the time, Pallas kernels for 0%

profile of v7, /device:TPU:4, one launch (start us, length us, event | category | flops | bytes accessed | tf_op | source)
XLA Modules:
  0.0 37.5 jit_solution(13565829754822451805)
XLA Ops:
  0.6 0.0 copy-start
  0.6 0.9 %copy-done = f32[4,8,16,128]{3,2,1,0:T(8,128)S(1)} copy-done((f32[4,8,16,128]{3,2,1,0:T(8,128)S(1)}, f32[4,8,16,128]{3,2,1,0:T(8,128)}, u32[]{:S(2)}) %copy-start) | copy-done | bytes 262168
  1.6 0.0 copy-start.1
  1.6 0.3 pack.1
  1.9 1.6 %collective-permute-start = (f32[20,16,128]{2,1,0:T(8,128)S(1)}, f32[20,16,128]{2,1,0:T(8,128)S(1)}, u32[]{:S(2)}, u32[]{:S(2)}) collective-permute-start(f32[20,16,128]{2,1,0:T(8,128)S(1)} %get-tuple-element.10), channel_id=1, source_target_pairs={{0,1},{1,0},{2,3},{3,2},{4,5},{5,4},{6,7},{7,6},{8,9},{9,8},{10,11... | collective-permute-start | bytes 491528 | tf_op jit(solution)/shard_map/ppermute | solution.py:306
  3.4 1.6 %collective-permute-start.1 = (f32[4,16,128]{2,1,0:T(8,128)S(1)}, f32[4,16,128]{2,1,0:T(8,128)S(1)}, u32[]{:S(2)}, u32[]{:S(2)}) collective-permute-start(f32[4,16,128]{2,1,0:T(8,128)S(1)} %get-tuple-element.11), channel_id=1, source_target_pairs={{1,25},{0,8},{9,1},{8,16},{17,9},{16,24},{25,17},{24,0},{3,27},{2,... | collective-permute-start | bytes 98312 | tf_op jit(solution)/shard_map/ppermute | solution.py:330
  5.0 2.4 %collective-permute-start.2 = (f32[4,16,128]{2,1,0:T(8,128)S(1)}, f32[4,16,128]{2,1,0:T(8,128)S(1)}, u32[]{:S(2)}, u32[]{:S(2)}) collective-permute-start(f32[4,16,128]{2,1,0:T(8,128)S(1)} %get-tuple-element.12), channel_id=1, source_target_pairs={{0,25},{1,8},{8,1},{9,16},{16,9},{17,24},{24,17},{25,0},{2,27},{3,... | collective-permute-start | bytes 98312 | tf_op jit(solution)/shard_map/ppermute | solution.py:329
  7.4 1.7 %collective-permute-done.1.own_strip = f32[4,16,128]{2,1,0:T(8,128)S(1)} collective-permute-done((f32[4,16,128]{2,1,0:T(8,128)S(1)}, f32[4,16,128]{2,1,0:T(8,128)S(1)}, u32[]{:S(2)}, u32[]{:S(2)}) %collective-permute-start.1) | collective-permute-done | bytes 32800 | tf_op jit(solution)/shard_map/ppermute | solution.py:330
  9.2 2.4 %collective-permute-done.2.part_strip = f32[4,16,128]{2,1,0:T(8,128)S(1)} collective-permute-done((f32[4,16,128]{2,1,0:T(8,128)S(1)}, f32[4,16,128]{2,1,0:T(8,128)S(1)}, u32[]{:S(2)}, u32[]{:S(2)}) %collective-permute-start.2) | collective-permute-done | bytes 32800 | tf_op jit(solution)/shard_map/ppermute | solution.py:329
  11.6 0.0 collective-permute-done.part
  11.6 0.2 merge.1.mid
  11.9 1.9 %collective-permute-start.4 = (f32[3,16,16,128]{3,2,1,0:T(8,128)S(1)}, f32[3,16,16,128]{3,2,1,0:T(8,128)S(1)}, u32[]{:S(2)}, u32[]{:S(2)}) collective-permute-start(f32[3,16,16,128]{3,2,1,0:T(8,128)S(1)} %merge.1.mid), channel_id=1, source_target_pairs={{0,0},{2,4},{4,2},{6,6},{1,1},{3,5},{5,3},{7,7},{8,8},{10,12},{12,... | collective-permute-start | bytes 1179656 | tf_op jit(solution)/shard_map/ppermute | solution.py:312
  13.8 0.1 collective-permute-start.3
  13.9 7.1 %collective-permute-done.4.b_block = f32[3,16,16,128]{3,2,1,0:T(8,128)S(1)} collective-permute-done((f32[3,16,16,128]{3,2,1,0:T(8,128)S(1)}, f32[3,16,16,128]{3,2,1,0:T(8,128)S(1)}, u32[]{:S(2)}, u32[]{:S(2)}) %collective-permute-start.4) | collective-permute-done | bytes 393248 | tf_op jit(solution)/shard_map/ppermute | solution.py:312
  21.0 0.0 collective-permute-done.3.a_block
  21.0 0.0 copy-done.1
  21.0 4.5 %flux.1 = (f32[6,8,16,128]{3,2,1,0:T(8,128)S(1)}, f32[3,8,16,128]{3,2,1,0:T(8,128)S(1)}, f32[16,128]{1,0:T(8,128)S(1)}) custom-call(f32[3,16,16,128]{3,2,1,0:T(8,128)S(1)} %merge.1.mid, f32[3,16,16,128]{3,2,1,0:T(8,128)S(1)} %collective-permute-done.3.a_block, f32[3,16,16,128]{3,2,1,0:T(8,128)S(1)} %collective-permute-done.4.b_block, ...), custom_call_target="tpu_custom_call" | custom-call | tf_op jit(solution)/shard_map/flux/pallas_call | solution.py:286
  25.4 0.9 %collective-permute-start.5 = (f32[3,8,16,128]{3,2,1,0:T(8,128)S(1)}, f32[3,8,16,128]{3,2,1,0:T(8,128)S(1)}, u32[]{:S(2)}, u32[]{:S(2)}) collective-permute-start(f32[3,8,16,128]{3,2,1,0:T(8,128)S(1)} %get-tuple-element.15), channel_id=1, source_target_pairs={{0,1},{1,0},{2,3},{3,2},{4,5},{5,4},{6,7},{7,6},{8,9},{9,8},{10,11... | collective-permute-start | bytes 589832 | tf_op jit(solution)/shard_map/ppermute | solution.py:306
  26.3 10.2 %all_to_all.5.tables = f32[8,16,128]{2,1,0:T(8,128)S(1)} all-to-all(f32[8,16,128]{2,1,0:T(8,128)S(1)} %broadcast_in_dim.2), channel_id=1, replica_groups=mesh['span'=4,'wall'=4,'stream'=2] {'span','stream'}, dimensions={0} | all-to-all | bytes 131072 | tf_op jit(solution)/shard_map/all_to_all | solution.py:360
  36.5 0.0 collective-permute-done.5.come
  36.5 1.0 %finish.1 = (f32[3,8,16,128]{3,2,1,0:T(8,128)}, f32[3,8,16,128]{3,2,1,0:T(8,128)}, f32[3,16]{1,0:T(4,128)}, f32[3,16]{1,0:T(4,128)}) custom-call(f32[8,16,128]{2,1,0:T(8,128)S(1)} %all_to_all.5.tables, f32[6,8,16,128]{3,2,1,0:T(8,128)S(1)} %get-tuple-element.14.keep, f32[3,8,16,128]{3,2,1,0:T(8,128)S(1)} %collective-permute-done.5.come), custom_call_target="tpu_custom_call" | custom-call | tf_op jit(solution)/shard_map/finish/pallas_call | solution.py:286
  (1 shorter events, 0.0 us)
Async XLA Ops:
  0.6 1.0 %copy-start = (f32[4,8,16,128]{3,2,1,0:T(8,128)S(1)}, f32[4,8,16,128]{3,2,1,0:T(8,128)}, u32[]{:S(2)}) copy-start(f32[4,8,16,128]{3,2,1,0:T(8,128)} %own.3) | copy-start | bytes 786436
  1.6 19.4 %copy-start.1 = (bf16[768,512]{1,0:T(8,128)(2,1)S(1)}, bf16[768,512]{1,0:T(8,128)(2,1)}, u32[]{:S(2)}) copy-start(bf16[768,512]{1,0:T(8,128)(2,1)} %constant.2.clone.weights) | copy-start | bytes 2359300
  1.9 9.7 %collective-permute-start = (f32[20,16,128]{2,1,0:T(8,128)S(1)}, f32[20,16,128]{2,1,0:T(8,128)S(1)}, u32[]{:S(2)}, u32[]{:S(2)}) collective-permute-start(f32[20,16,128]{2,1,0:T(8,128)S(1)} %get-tuple-element.10), channel_id=1, source_target_pairs={{0,1},{1,0},{2,3},{3,2},{4,5},{5,4},{6,7},{7,6},{8,9},{9,8},{10,11... | collective-permute-start | bytes 491528 | tf_op jit(solution)/shard_map/ppermute | solution.py:306
  3.4 5.7 %collective-permute-start.1 = (f32[4,16,128]{2,1,0:T(8,128)S(1)}, f32[4,16,128]{2,1,0:T(8,128)S(1)}, u32[]{:S(2)}, u32[]{:S(2)}) collective-permute-start(f32[4,16,128]{2,1,0:T(8,128)S(1)} %get-tuple-element.11), channel_id=1, source_target_pairs={{1,25},{0,8},{9,1},{8,16},{17,9},{16,24},{25,17},{24,0},{3,27},{2,... | collective-permute-start | bytes 98312 | tf_op jit(solution)/shard_map/ppermute | solution.py:330
  5.0 6.6 %collective-permute-start.2 = (f32[4,16,128]{2,1,0:T(8,128)S(1)}, f32[4,16,128]{2,1,0:T(8,128)S(1)}, u32[]{:S(2)}, u32[]{:S(2)}) collective-permute-start(f32[4,16,128]{2,1,0:T(8,128)S(1)} %get-tuple-element.12), channel_id=1, source_target_pairs={{0,25},{1,8},{8,1},{9,16},{16,9},{17,24},{24,17},{25,0},{2,27},{3,... | collective-permute-start | bytes 98312 | tf_op jit(solution)/shard_map/ppermute | solution.py:329
  11.9 9.1 %collective-permute-start.4 = (f32[3,16,16,128]{3,2,1,0:T(8,128)S(1)}, f32[3,16,16,128]{3,2,1,0:T(8,128)S(1)}, u32[]{:S(2)}, u32[]{:S(2)}) collective-permute-start(f32[3,16,16,128]{3,2,1,0:T(8,128)S(1)} %merge.1.mid), channel_id=1, source_target_pairs={{0,0},{2,4},{4,2},{6,6},{1,1},{3,5},{5,3},{7,7},{8,8},{10,12},{12,... | collective-permute-start | bytes 1179656 | tf_op jit(solution)/shard_map/ppermute | solution.py:312
  13.8 7.2 %collective-permute-start.3 = (f32[3,16,16,128]{3,2,1,0:T(8,128)S(1)}, f32[3,16,16,128]{3,2,1,0:T(8,128)S(1)}, u32[]{:S(2)}, u32[]{:S(2)}) collective-permute-start(f32[3,16,16,128]{3,2,1,0:T(8,128)S(1)} %merge.1.mid), channel_id=1, source_target_pairs={{0,2},{2,0},{4,6},{6,4},{1,3},{3,1},{5,7},{7,5},{8,10},{10,8},{12,... | collective-permute-start | bytes 1179656 | tf_op jit(solution)/shard_map/ppermute | solution.py:309
  25.4 11.1 %collective-permute-start.5 = (f32[3,8,16,128]{3,2,1,0:T(8,128)S(1)}, f32[3,8,16,128]{3,2,1,0:T(8,128)S(1)}, u32[]{:S(2)}, u32[]{:S(2)}) collective-permute-start(f32[3,8,16,128]{3,2,1,0:T(8,128)S(1)} %get-tuple-element.15), channel_id=1, source_target_pairs={{0,1},{1,0},{2,3},{3,2},{4,5},{5,4},{6,7},{7,6},{8,9},{9,8},{10,11... | collective-permute-start | bytes 589832 | tf_op jit(solution)/shard_map/ppermute | solution.py:306

commit v8 on v7

--- a/solution.py
+++ b/solution.py
@@ -109,39 +109,43 @@
     to_same[...] = pack_strip(own, 7 * (1 - me_s))
 
 
-def merge_kernel(own, part, own_strip, part_strip, packed):
-    _, layers, rows, width = own.shape
+def main_kernel(own, part, main):
+    _, layers, _, _ = own.shape
+    me_s = lax.axis_index("stream")
+    for pair, tile in pack_halves(own, me_s):
+        main[pair, pl.ds(me_s * layers, layers)] = tile
+        main[pair, pl.ds((1 - me_s) * layers, layers)] = part[pair * layers : (pair + 1) * layers]
+
+
+def rim_kernel(own, part, own_strip, part_strip, strips):
+    _, layers, _, _ = own.shape
     half = layers // 2
     me_s = lax.axis_index("stream")
-    mine, other = me_s * layers, (1 - me_s) * layers
-    for pair, tile in pack_halves(own, me_s):
-        packed[pair, pl.ds(mine, layers)] = tile
-        packed[pair, pl.ds(other, layers)] = part[pair * layers : (pair + 1) * layers]
     for k, tile in strip_tile(pack_strip(own, 4 - me_s), own_strip[...], me_s):
-        packed[2, pl.ds(mine + k * half, half)] = tile
+        strips[pl.ds(me_s * layers + k * half, half)] = tile
     for k, tile in strip_tile(part[2 * layers :], part_strip[...], me_s):
-        packed[2, pl.ds(other + k * half, half)] = tile
-
-
-def unpack(packed, me_s):
-    width = packed.shape[-1]
-    unit = unit_index(packed.shape[1:])
+        strips[pl.ds((1 - me_s) * layers + k * half, half)] = tile
+
+
+def unpack(main, strips, me_s):
+    width = strips.shape[-1]
+    unit = unit_index(strips.shape)
     first = 4 * (1 - me_s)
     in_strip = (unit == first) | (unit == first + 3)
     for f in range(4):
-        cells = packed[f // 2]
+        cells = main[f // 2]
         cells = pltpu.roll(cells, width // 2, 2) if f % 2 else cells
-        strip = packed[2]
+        strip = strips[...]
         strip = pltpu.roll(strip, width - 2 * f * rim, 2) if f else strip
         yield f, jnp.where(in_strip, strip, cells)
 
 
 def flux_kernel(
-    walls, mid, a_block, b_block, weights, keep_ref, send_ref, sums_ref,
+    walls, main, a_main, b_main, strips, a_strips, b_strips, weights, keep_ref, send_ref, sums_ref,
     raw, in_h, in_l, prod_h, prod_l, mean, mid_h, mid_l, clark_all, similar_all,
 ):
-    _, both, rows, width = mid.shape
-    layers = both // 2
+    _, layers, rows, width = keep_ref.shape
+    both = 2 * layers
     cells = both * rows
     plane_h = weights.at[:cells]
     plane_l = weights.at[cells : 2 * cells]
@@ -154,11 +158,11 @@
     at_end = (me_w == 0) | (me_w == walls - 1)
     keep_b = jnp.where(at_end, 0.0, 1.0).astype(jnp.float32)
 
-    for f, value in unpack(mid, me_s):
+    for f, value in unpack(main, strips, me_s):
         raw[f, :, rows : 2 * rows, :] = value
-    for f, value in unpack(a_block, me_s):
+    for f, value in unpack(a_main, a_strips, me_s):
         raw[f, :, pl.ds(row_a, rows), :] = value
-    for f, value in unpack(b_block, me_s):
+    for f, value in unpack(b_main, b_strips, me_s):
         raw[f, :, pl.ds(row_b, rows), :] = value * keep_b
 
     def column(t):
@@ -282,7 +286,8 @@
     similar_corr[...] = turned[8:11, :rows]
 
 
-def call(kernel, name, ins, outs, scratch=(), mib=4):
+def call(kernel, name, ins, outs, scratch=(), mib=4, hint=None):
+    cost = hint and pl.CostEstimate(flops=hint, bytes_accessed=hint // 100, transcendentals=0)
     return pl.pallas_call(
         kernel,
         out_shape=tuple(jax.ShapeDtypeStruct(shape, jnp.float32) for shape in outs),
@@ -290,6 +295,7 @@
         out_specs=tuple(pl.BlockSpec(memory_space=pltpu.VMEM) for _ in outs),
         scratch_shapes=[pltpu.VMEM(shape, dtype) for shape, dtype in scratch],
         compiler_params=pltpu.CompilerParams(vmem_limit_bytes=mib * 1024 * 1024),
+        cost_estimate=cost,
         name=name,
     )(*ins)
 
@@ -328,8 +334,10 @@
     part = swap(to_partner)
     part_strip = lax.ppermute(first, ("span", "stream"), to_other)
     own_strip = lax.ppermute(second, ("span", "stream"), to_same)
-    (mid,) = call(merge_kernel, "merge", (fields, part, own_strip, part_strip), ((3, both, rows, width),))
-    b_block, a_block = pair_b(mid), pair_a(mid)
+    (main,) = call(main_kernel, "main", (fields, part), ((2, both, rows, width),))
+    b_main, a_main = pair_b(main), pair_a(main)
+    (strips,) = call(rim_kernel, "strips", (fields, part, own_strip, part_strip), ((both, rows, width),), hint=2**35)
+    b_strips, a_strips = pair_b(strips), pair_a(strips)
 
     weights = np.zeros((2 * cells + 2 * width, 2 * cells), ml_dtypes.bfloat16)
     weights[:cells], weights[cells : 2 * cells] = plane_constants(both, rows)
@@ -338,7 +346,7 @@
     keep, send, sums = call(
         functools.partial(flux_kernel, walls),
         "flux",
-        (mid, a_block, b_block, jnp.asarray(weights)),
+        (main, a_main, b_main, strips, a_strips, b_strips, jnp.asarray(weights)),
         ((6, layers, rows, width), (3, layers, rows, width), (rows, width)),
         [
             ((4, both, 3 * rows, width), single),

time: 37.7 us -> 37 us (0.981)
  waiting for transfers between devices: 11.3 us -> 5.93 us
  starting transfers between devices: 8.44 us -> 10.8 us
  blocking collectives: 10.2 us -> 12 us
    ppermute x1 -> x2, waiting for transfers between devices: 7.09 us -> 4.02 us  [pair_b(): lax.ppermute(value, 'wall', [(w, min(max((w + 1 ^ 1) - 1, 0), walls - 1))...]
    ppermute x1 -> x2, starting transfers between devices: 1.92 us -> 4.23 us  [pair_b(): lax.ppermute(value, 'wall', [(w, min(max((w + 1 ^ 1) - 1, 0), walls - 1))...]
    all_to_all x1, blocking collectives: 10.2 us -> 12 us  [shards(): lax.all_to_all(jnp.broadcast_to(sums[None], (group, rows, width)), ('span...]
    ppermute x1, waiting for transfers between devices: 1.72 us -> 0.01 us  [shards(): own_strip = lax.ppermute(second, ('span', 'stream'), to_same)]
    ppermute x1, waiting for transfers between devices: 2.45 us -> 1.47 us  [shards(): part_strip = lax.ppermute(first, ('span', 'stream'), to_other)]
    ppermute x2, waiting for transfers between devices: 0.01 us -> 0.43 us  [swap(): return lax.ppermute(value, 'stream', [(0, 1), (1, 0)])]
    pallas_call x4 -> x5, Pallas kernels: 5.99 us -> 6.05 us  [call(): pl.pallas_call(kernel, out_shape=tuple((jax.ShapeDtypeStruct(shape, jnp.f...]
  transfers between devices with their start and end apart: 6 -> 8, of which waited for: 3 -> 3; matrix products, arithmetic and copies ran while one was open for 0% -> 0% of each run, Pallas kernels for 0% -> 1%
where the time goes in v8:
time: 37 us; the launch traced here: 36.5 us
  blocking collectives  12 us (32%)
  starting transfers between devices  10.8 us (29%)
  Pallas kernels  6.05 us (16%)
  waiting for transfers between devices  5.93 us (16%)
  local copies, waits for them, and re-layouts  0.96 us (3%)
  between operations  0.73 us (2%)
    all_to_all x1, blocking collectives, shards(): lax.all_to_all(jnp.broadcast_to(sums[None], (group, rows, width)), ('span...  12 us
    pallas_call x5, Pallas kernels, call(): pl.pallas_call(kernel, out_shape=tuple((jax.ShapeDtypeStruct(shape, jnp.f...  6.05 us
    ppermute x2, starting transfers between devices, pair_b(): lax.ppermute(value, 'wall', [(w, min(max((w + 1 ^ 1) - 1, 0), walls - 1))...  4.23 us
    ppermute x2, waiting for transfers between devices, pair_b(): lax.ppermute(value, 'wall', [(w, min(max((w + 1 ^ 1) - 1, 0), walls - 1))...  4.02 us
    ppermute x1, starting transfers between devices, shards(): part_strip = lax.ppermute(first, ('span', 'stream'), to_other)  2.45 us
    ppermute x2, starting transfers between devices, swap(): return lax.ppermute(value, 'stream', [(0, 1), (1, 0)])  2.42 us
    ppermute x1, starting transfers between devices, shards(): own_strip = lax.ppermute(second, ('span', 'stream'), to_same)  1.58 us
    ppermute x1, waiting for transfers between devices, shards(): part_strip = lax.ppermute(first, ('span', 'stream'), to_other)  1.47 us
  transfers between devices with their start and end apart: 8, of which 3 were waited for; matrix products, arithmetic and copies ran while one was open for 0% of the time, Pallas kernels for 1%

profile of v8, /device:TPU:4, one launch (start us, length us, event | category | flops | bytes accessed | tf_op | source)
XLA Modules:
  0.0 36.5 jit_solution(3032136235764699775)
XLA Ops:
  0.6 0.9 %copy-done = f32[4,8,16,128]{3,2,1,0:T(8,128)S(1)} copy-done((f32[4,8,16,128]{3,2,1,0:T(8,128)S(1)}, f32[4,8,16,128]{3,2,1,0:T(8,128)}, u32[]{:S(2)}) %copy-start) | copy-done | bytes 262168
  1.6 0.3 pack.1
  1.9 1.6 %collective-permute-start = (f32[20,16,128]{2,1,0:T(8,128)S(1)}, f32[20,16,128]{2,1,0:T(8,128)S(1)}, u32[]{:S(2)}, u32[]{:S(2)}) collective-permute-start(f32[20,16,128]{2,1,0:T(8,128)S(1)} %get-tuple-element.10), channel_id=1, source_target_pairs={{0,1},{1,0},{2,3},{3,2},{4,5},{5,4},{6,7},{7,6},{8,9},{9,8},{10,11... | collective-permute-start | bytes 491528 | tf_op jit(solution)/shard_map/ppermute | solution.py:312
  3.4 1.6 %collective-permute-start.3 = (f32[4,16,128]{2,1,0:T(8,128)S(1)}, f32[4,16,128]{2,1,0:T(8,128)S(1)}, u32[]{:S(2)}, u32[]{:S(2)}) collective-permute-start(f32[4,16,128]{2,1,0:T(8,128)S(1)} %get-tuple-element.11), channel_id=1, source_target_pairs={{1,25},{0,8},{9,1},{8,16},{17,9},{16,24},{25,17},{24,0},{3,27},{2,... | collective-permute-start | bytes 98312 | tf_op jit(solution)/shard_map/ppermute | solution.py:336
  5.0 2.4 %collective-permute-start.4 = (f32[4,16,128]{2,1,0:T(8,128)S(1)}, f32[4,16,128]{2,1,0:T(8,128)S(1)}, u32[]{:S(2)}, u32[]{:S(2)}) collective-permute-start(f32[4,16,128]{2,1,0:T(8,128)S(1)} %get-tuple-element.12), channel_id=1, source_target_pairs={{0,25},{1,8},{8,1},{9,16},{16,9},{17,24},{24,17},{25,0},{2,27},{3,... | collective-permute-start | bytes 98312 | tf_op jit(solution)/shard_map/ppermute | solution.py:335
  7.4 0.4 %collective-permute-done.part = f32[20,16,128]{2,1,0:T(8,128)S(1)} collective-permute-done((f32[20,16,128]{2,1,0:T(8,128)S(1)}, f32[20,16,128]{2,1,0:T(8,128)S(1)}, u32[]{:S(2)}, u32[]{:S(2)}) %collective-permute-start) | collective-permute-done | bytes 163872 | tf_op jit(solution)/shard_map/ppermute | solution.py:312
  7.9 0.1 main.1
  8.0 0.0 copy-start.1
  8.0 2.1 %collective-permute-start.2 = (f32[2,16,16,128]{3,2,1,0:T(8,128)S(1)}, f32[2,16,16,128]{3,2,1,0:T(8,128)S(1)}, u32[]{:S(2)}, u32[]{:S(2)}) collective-permute-start(f32[2,16,16,128]{3,2,1,0:T(8,128)S(1)} %main.1), channel_id=1, source_target_pairs={{0,0},{2,4},{4,2},{6,6},{1,1},{3,5},{5,3},{7,7},{8,8},{10,12},{12,... | collective-permute-start | bytes 786440 | tf_op jit(solution)/shard_map/ppermute | solution.py:318
  10.0 0.1 collective-permute-start.1
  10.1 0.0 collective-permute-done.3.own_strip
  10.1 1.5 %collective-permute-done.4.part_strip = f32[4,16,128]{2,1,0:T(8,128)S(1)} collective-permute-done((f32[4,16,128]{2,1,0:T(8,128)S(1)}, f32[4,16,128]{2,1,0:T(8,128)S(1)}, u32[]{:S(2)}, u32[]{:S(2)}) %collective-permute-start.4) | collective-permute-done | bytes 32800 | tf_op jit(solution)/shard_map/ppermute | solution.py:335
  11.6 0.2 strips.1
  11.8 2.2 %collective-permute-start.6 = (f32[16,16,128]{2,1,0:T(8,128)S(1)}, f32[16,16,128]{2,1,0:T(8,128)S(1)}, u32[]{:S(2)}, u32[]{:S(2)}) collective-permute-start(f32[16,16,128]{2,1,0:T(8,128)S(1)} %strips.1), channel_id=1, source_target_pairs={{0,0},{2,4},{4,2},{6,6},{1,1},{3,5},{5,3},{7,7},{8,8},{10,12},{12,... | collective-permute-start | bytes 393224 | tf_op jit(solution)/shard_map/ppermute | solution.py:318
  14.0 0.1 collective-permute-start.5
  14.1 4.0 %collective-permute-done.6.b_strips = f32[16,16,128]{2,1,0:T(8,128)S(1)} collective-permute-done((f32[16,16,128]{2,1,0:T(8,128)S(1)}, f32[16,16,128]{2,1,0:T(8,128)S(1)}, u32[]{:S(2)}, u32[]{:S(2)}) %collective-permute-start.6) | collective-permute-done | bytes 131104 | tf_op jit(solution)/shard_map/ppermute | solution.py:318
  18.1 0.0 collective-permute-done.5.a_strips
  18.1 0.0 collective-permute-done.2.b_main
  18.1 0.0 collective-permute-done.1.a_main
  18.1 4.4 %flux.1 = (f32[6,8,16,128]{3,2,1,0:T(8,128)S(1)}, f32[3,8,16,128]{3,2,1,0:T(8,128)S(1)}, f32[16,128]{1,0:T(8,128)S(1)}) custom-call(f32[2,16,16,128]{3,2,1,0:T(8,128)S(1)} %main.1, f32[2,16,16,128]{3,2,1,0:T(8,128)S(1)} %collective-permute-done.1.a_main, f32[2,16,16,128]{3,2,1,0:T(8,128)S(1)} %collective-permute-done.2.b_main, f32[16,16,128]{2,1,0:T(8,128)S(1)} %strips.1, ...), custom_call_target="tpu_custom_call" | custom-call | tf_op jit(solution)/shard_map/flux/pallas_call | solution.py:291
  22.6 0.9 %collective-permute-start.7 = (f32[3,8,16,128]{3,2,1,0:T(8,128)S(1)}, f32[3,8,16,128]{3,2,1,0:T(8,128)S(1)}, u32[]{:S(2)}, u32[]{:S(2)}) collective-permute-start(f32[3,8,16,128]{3,2,1,0:T(8,128)S(1)} %get-tuple-element.15), channel_id=1, source_target_pairs={{0,1},{1,0},{2,3},{3,2},{4,5},{5,4},{6,7},{7,6},{8,9},{9,8},{10,11... | collective-permute-start | bytes 589832 | tf_op jit(solution)/shard_map/ppermute | solution.py:312
  23.5 12.0 %all_to_all.5.tables = f32[8,16,128]{2,1,0:T(8,128)S(1)} all-to-all(f32[8,16,128]{2,1,0:T(8,128)S(1)} %broadcast_in_dim.2), channel_id=1, replica_groups=mesh['span'=4,'wall'=4,'stream'=2] {'span','stream'}, dimensions={0} | all-to-all | bytes 131072 | tf_op jit(solution)/shard_map/all_to_all | solution.py:368
  35.5 0.0 collective-permute-done.7.come
  35.5 1.0 %finish.1 = (f32[3,8,16,128]{3,2,1,0:T(8,128)}, f32[3,8,16,128]{3,2,1,0:T(8,128)}, f32[3,16]{1,0:T(4,128)}, f32[3,16]{1,0:T(4,128)}) custom-call(f32[8,16,128]{2,1,0:T(8,128)S(1)} %all_to_all.5.tables, f32[6,8,16,128]{3,2,1,0:T(8,128)S(1)} %get-tuple-element.14.keep, f32[3,8,16,128]{3,2,1,0:T(8,128)S(1)} %collective-permute-done.7.come), custom_call_target="tpu_custom_call" | custom-call | tf_op jit(solution)/shard_map/finish/pallas_call | solution.py:291
  (3 shorter events, 0.0 us)
Async XLA Ops:
  0.6 1.0 %copy-start = (f32[4,8,16,128]{3,2,1,0:T(8,128)S(1)}, f32[4,8,16,128]{3,2,1,0:T(8,128)}, u32[]{:S(2)}) copy-start(f32[4,8,16,128]{3,2,1,0:T(8,128)} %own.5) | copy-start | bytes 786436
  1.9 6.0 %collective-permute-start = (f32[20,16,128]{2,1,0:T(8,128)S(1)}, f32[20,16,128]{2,1,0:T(8,128)S(1)}, u32[]{:S(2)}, u32[]{:S(2)}) collective-permute-start(f32[20,16,128]{2,1,0:T(8,128)S(1)} %get-tuple-element.10), channel_id=1, source_target_pairs={{0,1},{1,0},{2,3},{3,2},{4,5},{5,4},{6,7},{7,6},{8,9},{9,8},{10,11... | collective-permute-start | bytes 491528 | tf_op jit(solution)/shard_map/ppermute | solution.py:312
  3.4 6.7 %collective-permute-start.3 = (f32[4,16,128]{2,1,0:T(8,128)S(1)}, f32[4,16,128]{2,1,0:T(8,128)S(1)}, u32[]{:S(2)}, u32[]{:S(2)}) collective-permute-start(f32[4,16,128]{2,1,0:T(8,128)S(1)} %get-tuple-element.11), channel_id=1, source_target_pairs={{1,25},{0,8},{9,1},{8,16},{17,9},{16,24},{25,17},{24,0},{3,27},{2,... | collective-permute-start | bytes 98312 | tf_op jit(solution)/shard_map/ppermute | solution.py:336
  5.0 6.6 %collective-permute-start.4 = (f32[4,16,128]{2,1,0:T(8,128)S(1)}, f32[4,16,128]{2,1,0:T(8,128)S(1)}, u32[]{:S(2)}, u32[]{:S(2)}) collective-permute-start(f32[4,16,128]{2,1,0:T(8,128)S(1)} %get-tuple-element.12), channel_id=1, source_target_pairs={{0,25},{1,8},{8,1},{9,16},{16,9},{17,24},{24,17},{25,0},{2,27},{3,... | collective-permute-start | bytes 98312 | tf_op jit(solution)/shard_map/ppermute | solution.py:335
  8.0 10.2 %copy-start.1 = (bf16[768,512]{1,0:T(8,128)(2,1)S(1)}, bf16[768,512]{1,0:T(8,128)(2,1)}, u32[]{:S(2)}) copy-start(bf16[768,512]{1,0:T(8,128)(2,1)} %constant.2.clone.weights) | copy-start | bytes 2359300
  8.0 10.1 %collective-permute-start.2 = (f32[2,16,16,128]{3,2,1,0:T(8,128)S(1)}, f32[2,16,16,128]{3,2,1,0:T(8,128)S(1)}, u32[]{:S(2)}, u32[]{:S(2)}) collective-permute-start(f32[2,16,16,128]{3,2,1,0:T(8,128)S(1)} %main.1), channel_id=1, source_target_pairs={{0,0},{2,4},{4,2},{6,6},{1,1},{3,5},{5,3},{7,7},{8,8},{10,12},{12,... | collective-permute-start | bytes 786440 | tf_op jit(solution)/shard_map/ppermute | solution.py:318
  10.0 8.1 %collective-permute-start.1 = (f32[2,16,16,128]{3,2,1,0:T(8,128)S(1)}, f32[2,16,16,128]{3,2,1,0:T(8,128)S(1)}, u32[]{:S(2)}, u32[]{:S(2)}) collective-permute-start(f32[2,16,16,128]{3,2,1,0:T(8,128)S(1)} %main.1), channel_id=1, source_target_pairs={{0,2},{2,0},{4,6},{6,4},{1,3},{3,1},{5,7},{7,5},{8,10},{10,8},{12,... | collective-permute-start | bytes 786440 | tf_op jit(solution)/shard_map/ppermute | solution.py:315
  11.8 6.3 %collective-permute-start.6 = (f32[16,16,128]{2,1,0:T(8,128)S(1)}, f32[16,16,128]{2,1,0:T(8,128)S(1)}, u32[]{:S(2)}, u32[]{:S(2)}) collective-permute-start(f32[16,16,128]{2,1,0:T(8,128)S(1)} %strips.1), channel_id=1, source_target_pairs={{0,0},{2,4},{4,2},{6,6},{1,1},{3,5},{5,3},{7,7},{8,8},{10,12},{12,... | collective-permute-start | bytes 393224 | tf_op jit(solution)/shard_map/ppermute | solution.py:318
  14.0 4.1 %collective-permute-start.5 = (f32[16,16,128]{2,1,0:T(8,128)S(1)}, f32[16,16,128]{2,1,0:T(8,128)S(1)}, u32[]{:S(2)}, u32[]{:S(2)}) collective-permute-start(f32[16,16,128]{2,1,0:T(8,128)S(1)} %strips.1), channel_id=1, source_target_pairs={{0,2},{2,0},{4,6},{6,4},{1,3},{3,1},{5,7},{7,5},{8,10},{10,8},{12,... | collective-permute-start | bytes 393224 | tf_op jit(solution)/shard_map/ppermute | solution.py:315
  22.6 12.9 %collective-permute-start.7 = (f32[3,8,16,128]{3,2,1,0:T(8,128)S(1)}, f32[3,8,16,128]{3,2,1,0:T(8,128)S(1)}, u32[]{:S(2)}, u32[]{:S(2)}) collective-permute-start(f32[3,8,16,128]{3,2,1,0:T(8,128)S(1)} %get-tuple-element.15), channel_id=1, source_target_pairs={{0,1},{1,0},{2,3},{3,2},{4,5},{5,4},{6,7},{7,6},{8,9},{9,8},{10,11... | collective-permute-start | bytes 589832 | tf_op jit(solution)/shard_map/ppermute | solution.py:312

commit v9 on v8

--- a/solution.py
+++ b/solution.py
@@ -258,11 +258,11 @@
 
 
 def finish_kernel(
-    plane_cells, tables, keep, come, clark_model, similar_model, clark_corr, similar_corr
+    plane_cells, sums, keep, come, clark_model, similar_model, clark_corr, similar_corr
 ):
     _, layers, rows, width = keep.shape
     me_s = lax.axis_index("stream")
-    table = jnp.sum(tables[...], axis=0) / plane_cells
+    table = sums[...] / plane_cells
     lane = lane_index((rows, width))
     useful = lane // (width // 2) == me_s
     corr = jnp.zeros((rows, width), jnp.float32)
@@ -363,16 +363,23 @@
         mib=32,
     )
 
+    group = spans * streams
+
+    def exchange(value, step):
+        return lax.ppermute(value, ("span", "stream"), [(g, g ^ step) for g in range(group)])
+
+    sums = (sums + exchange(sums, 1)) + (exchange(sums, 2) + exchange(sums, 3))
+    sums, send = lax.optimization_barrier((sums, send))
     come = swap(send)
-    group = spans * streams
-    tables = lax.all_to_all(
-        jnp.broadcast_to(sums[None], (group, rows, width)), ("span", "stream"), 0, 0
-    )
+    step = 4
+    while step < group:
+        sums = sums + exchange(sums, step)
+        step *= 2
     block, corr = (3, layers, rows, width), (3, rows)
     return call(
         functools.partial(finish_kernel, float(layers * width * group)),
         "finish",
-        (tables, keep, come),
+        (sums, keep, come),
         (block, block, corr, corr),
     )
 

time: 37 us -> 36.9 us (level)
  the two profiles are of different devices: /device:TPU:4 before, /device:TPU:0 now
where the time goes in v9:
time: 36.9 us; the launch traced here: 36.7 us
  starting transfers between devices  20.7 us (56%)
  waiting for transfers between devices  8.29 us (22%)
  Pallas kernels  6.04 us (16%)
  local copies, waits for them, and re-layouts  0.95 us (3%)
  between operations  0.7 us (2%)
    pallas_call x5, Pallas kernels, call(): pl.pallas_call(kernel, out_shape=tuple((jax.ShapeDtypeStruct(shape, jnp.f...  6.04 us
    ppermute x2, starting transfers between devices, pair_a(): return lax.ppermute(value, 'wall', [(w, w ^ 1) for w in range(walls)])  5.99 us
    ppermute x4, waiting for transfers between devices, exchange(): lax.ppermute(value, ('span', 'stream'), [(g, g ^ step) for g in range(gro...  5.53 us
    ppermute x4, starting transfers between devices, exchange(): lax.ppermute(value, ('span', 'stream'), [(g, g ^ step) for g in range(gro...  5.01 us
    ppermute x2, starting transfers between devices, swap(): return lax.ppermute(value, 'stream', [(0, 1), (1, 0)])  4.23 us
    ppermute x1, starting transfers between devices, shards(): part_strip = lax.ppermute(first, ('span', 'stream'), to_other)  2.45 us
    ppermute x2, waiting for transfers between devices, swap(): return lax.ppermute(value, 'stream', [(0, 1), (1, 0)])  1.76 us
    ppermute x1, starting transfers between devices, shards(): own_strip = lax.ppermute(second, ('span', 'stream'), to_same)  1.58 us
  transfers between devices with their start and end apart: 12, of which 7 were waited for; matrix products, arithmetic and copies ran while one was open for 0% of the time, Pallas kernels for 1%

profile of v9, /device:TPU:0, one launch (start us, length us, event | category | flops | bytes accessed | tf_op | source)
XLA Modules:
  0.0 36.7 jit_solution(9708616051084655934)
XLA Ops:
  0.6 0.9 %copy-done = f32[4,8,16,128]{3,2,1,0:T(8,128)S(1)} copy-done((f32[4,8,16,128]{3,2,1,0:T(8,128)S(1)}, f32[4,8,16,128]{3,2,1,0:T(8,128)}, u32[]{:S(2)}) %copy-start) | copy-done | bytes 262168
  1.6 0.3 pack.1
  1.9 3.0 %collective-permute-start = (f32[20,16,128]{2,1,0:T(8,128)S(1)}, f32[20,16,128]{2,1,0:T(8,128)S(1)}, u32[]{:S(2)}, u32[]{:S(2)}) collective-permute-start(f32[20,16,128]{2,1,0:T(8,128)S(1)} %get-tuple-element.12), channel_id=1, source_target_pairs={{0,1},{1,0},{2,3},{3,2},{4,5},{5,4},{6,7},{7,6},{8,9},{9,8},{10,11... | collective-permute-start | bytes 491528 | tf_op jit(solution)/shard_map/ppermute | solution.py:312
  4.9 1.6 %collective-permute-start.3 = (f32[4,16,128]{2,1,0:T(8,128)S(1)}, f32[4,16,128]{2,1,0:T(8,128)S(1)}, u32[]{:S(2)}, u32[]{:S(2)}) collective-permute-start(f32[4,16,128]{2,1,0:T(8,128)S(1)} %get-tuple-element.13), channel_id=1, source_target_pairs={{1,25},{0,8},{9,1},{8,16},{17,9},{16,24},{25,17},{24,0},{3,27},{2,... | collective-permute-start | bytes 98312 | tf_op jit(solution)/shard_map/ppermute | solution.py:336
  6.4 2.4 %collective-permute-start.4 = (f32[4,16,128]{2,1,0:T(8,128)S(1)}, f32[4,16,128]{2,1,0:T(8,128)S(1)}, u32[]{:S(2)}, u32[]{:S(2)}) collective-permute-start(f32[4,16,128]{2,1,0:T(8,128)S(1)} %get-tuple-element.14), channel_id=1, source_target_pairs={{0,25},{1,8},{8,1},{9,16},{16,9},{17,24},{24,17},{25,0},{2,27},{3,... | collective-permute-start | bytes 98312 | tf_op jit(solution)/shard_map/ppermute | solution.py:335
  8.9 0.2 collective-permute-done.part
  9.2 0.8 %collective-permute-start.2 = (f32[2,16,16,128]{3,2,1,0:T(8,128)S(1)}, f32[2,16,16,128]{3,2,1,0:T(8,128)S(1)}, u32[]{:S(2)}, u32[]{:S(2)}) collective-permute-start(f32[2,16,16,128]{3,2,1,0:T(8,128)S(1)} %main.1), channel_id=1, source_target_pairs={{0,0},{2,4},{4,2},{6,6},{1,1},{3,5},{5,3},{7,7},{8,8},{10,12},{12,... | collective-permute-start | bytes 786440 | tf_op jit(solution)/shard_map/ppermute | solution.py:318
  10.0 3.2 %collective-permute-start.1 = (f32[2,16,16,128]{3,2,1,0:T(8,128)S(1)}, f32[2,16,16,128]{3,2,1,0:T(8,128)S(1)}, u32[]{:S(2)}, u32[]{:S(2)}) collective-permute-start(f32[2,16,16,128]{3,2,1,0:T(8,128)S(1)} %main.1), channel_id=1, source_target_pairs={{0,2},{2,0},{4,6},{6,4},{1,3},{3,1},{5,7},{7,5},{8,10},{10,8},{12,... | collective-permute-start | bytes 786440 | tf_op jit(solution)/shard_map/ppermute | solution.py:315
  13.2 0.2 strips.1
  13.4 0.7 %collective-permute-start.6 = (f32[16,16,128]{2,1,0:T(8,128)S(1)}, f32[16,16,128]{2,1,0:T(8,128)S(1)}, u32[]{:S(2)}, u32[]{:S(2)}) collective-permute-start(f32[16,16,128]{2,1,0:T(8,128)S(1)} %strips.1), channel_id=1, source_target_pairs={{0,0},{2,4},{4,2},{6,6},{1,1},{3,5},{5,3},{7,7},{8,8},{10,12},{12,... | collective-permute-start | bytes 393224 | tf_op jit(solution)/shard_map/ppermute | solution.py:318
  14.1 2.8 %collective-permute-start.5 = (f32[16,16,128]{2,1,0:T(8,128)S(1)}, f32[16,16,128]{2,1,0:T(8,128)S(1)}, u32[]{:S(2)}, u32[]{:S(2)}) collective-permute-start(f32[16,16,128]{2,1,0:T(8,128)S(1)} %strips.1), channel_id=1, source_target_pairs={{0,2},{2,0},{4,6},{6,4},{1,3},{3,1},{5,7},{7,5},{8,10},{10,8},{12,... | collective-permute-start | bytes 393224 | tf_op jit(solution)/shard_map/ppermute | solution.py:315
  16.9 1.0 %collective-permute-done.5.a_strips = f32[16,16,128]{2,1,0:T(8,128)S(1)} collective-permute-done((f32[16,16,128]{2,1,0:T(8,128)S(1)}, f32[16,16,128]{2,1,0:T(8,128)S(1)}, u32[]{:S(2)}, u32[]{:S(2)}) %collective-permute-start.5) | collective-permute-done | bytes 131104 | tf_op jit(solution)/shard_map/ppermute | solution.py:315
  17.9 4.4 %flux.1 = (f32[6,8,16,128]{3,2,1,0:T(8,128)S(1)}, f32[3,8,16,128]{3,2,1,0:T(8,128)S(1)}, f32[16,128]{1,0:T(8,128)S(1)}) custom-call(f32[2,16,16,128]{3,2,1,0:T(8,128)S(1)} %main.1, f32[2,16,16,128]{3,2,1,0:T(8,128)S(1)} %collective-permute-done.1.a_main, f32[2,16,16,128]{3,2,1,0:T(8,128)S(1)} %collective-permute-done.2.b_main, f32[16,16,128]{2,1,0:T(8,128)S(1)} %strips.1, ...), custom_call_target="tpu_custom_call" | custom-call | tf_op jit(solution)/shard_map/flux/pallas_call | solution.py:291
  22.3 1.8 %collective-permute-start.9 = (f32[16,128]{1,0:T(8,128)S(1)}, f32[16,128]{1,0:T(8,128)S(1)}, u32[]{:S(2)}, u32[]{:S(2)}) collective-permute-start(f32[16,128]{1,0:T(8,128)S(1)} %get-tuple-element.15), channel_id=1, source_target_pairs={{0,9},{1,8},{8,1},{9,0},{16,25},{17,24},{24,17},{25,16},{2,11},{3,... | collective-permute-start | bytes 24584 | tf_op jit(solution)/shard_map/ppermute | solution.py:369
  24.2 0.5 %collective-permute-start.8 = (f32[16,128]{1,0:T(8,128)S(1)}, f32[16,128]{1,0:T(8,128)S(1)}, u32[]{:S(2)}, u32[]{:S(2)}) collective-permute-start(f32[16,128]{1,0:T(8,128)S(1)} %get-tuple-element.15), channel_id=1, source_target_pairs={{0,8},{1,9},{8,0},{9,1},{16,24},{17,25},{24,16},{25,17},{2,10},{3,... | collective-permute-start | bytes 24584 | tf_op jit(solution)/shard_map/ppermute | solution.py:369
  24.7 1.2 %collective-permute-start.7 = (f32[16,128]{1,0:T(8,128)S(1)}, f32[16,128]{1,0:T(8,128)S(1)}, u32[]{:S(2)}, u32[]{:S(2)}) collective-permute-start(f32[16,128]{1,0:T(8,128)S(1)} %get-tuple-element.15), channel_id=1, source_target_pairs={{0,1},{1,0},{8,9},{9,8},{16,17},{17,16},{24,25},{25,24},{2,3},{3,2... | collective-permute-start | bytes 24584 | tf_op jit(solution)/shard_map/ppermute | solution.py:369
  25.9 1.1 %collective-permute-done.9 = f32[16,128]{1,0:T(8,128)S(1)} collective-permute-done((f32[16,128]{1,0:T(8,128)S(1)}, f32[16,128]{1,0:T(8,128)S(1)}, u32[]{:S(2)}, u32[]{:S(2)}) %collective-permute-start.9) | collective-permute-done | bytes 8224 | tf_op jit(solution)/shard_map/ppermute | solution.py:369
  27.0 0.9 %collective-permute-done.8 = f32[16,128]{1,0:T(8,128)S(1)} collective-permute-done((f32[16,128]{1,0:T(8,128)S(1)}, f32[16,128]{1,0:T(8,128)S(1)}, u32[]{:S(2)}, u32[]{:S(2)}) %collective-permute-start.8) | collective-permute-done | bytes 8224 | tf_op jit(solution)/shard_map/ppermute | solution.py:369
  27.9 0.4 %collective-permute-done.7 = f32[16,128]{1,0:T(8,128)S(1)} collective-permute-done((f32[16,128]{1,0:T(8,128)S(1)}, f32[16,128]{1,0:T(8,128)S(1)}, u32[]{:S(2)}, u32[]{:S(2)}) %collective-permute-start.7) | collective-permute-done | bytes 8224 | tf_op jit(solution)/shard_map/ppermute | solution.py:369
  28.3 1.2 %collective-permute-start.11 = (f32[3,8,16,128]{3,2,1,0:T(8,128)S(1)}, f32[3,8,16,128]{3,2,1,0:T(8,128)S(1)}, u32[]{:S(2)}, u32[]{:S(2)}) collective-permute-start(f32[3,8,16,128]{3,2,1,0:T(8,128)S(1)} %get-tuple-element.19), channel_id=1, source_target_pairs={{0,1},{1,0},{2,3},{3,2},{4,5},{5,4},{6,7},{7,6},{8,9},{9,8},{10,11... | collective-permute-start | bytes 589832 | tf_op jit(solution)/shard_map/ppermute | solution.py:312
  29.5 1.5 %collective-permute-start.10 = (f32[16,128]{1,0:T(8,128)S(1)}, f32[16,128]{1,0:T(8,128)S(1)}, u32[]{:S(2)}, u32[]{:S(2)}) collective-permute-start(f32[16,128]{1,0:T(8,128)S(1)} %add_add_fusion), channel_id=1, source_target_pairs={{0,16},{1,17},{8,24},{9,25},{16,0},{17,1},{24,8},{25,9},{2,18},{3,... | collective-permute-start | bytes 24584 | tf_op jit(solution)/shard_map/ppermute | solution.py:369
  31.0 3.1 %collective-permute-done.10 = f32[16,128]{1,0:T(8,128)S(1)} collective-permute-done((f32[16,128]{1,0:T(8,128)S(1)}, f32[16,128]{1,0:T(8,128)S(1)}, u32[]{:S(2)}, u32[]{:S(2)}) %collective-permute-start.10) | collective-permute-done | bytes 8224 | tf_op jit(solution)/shard_map/ppermute | solution.py:369
  34.1 1.6 %collective-permute-done.11.come = f32[3,8,16,128]{3,2,1,0:T(8,128)S(1)} collective-permute-done((f32[3,8,16,128]{3,2,1,0:T(8,128)S(1)}, f32[3,8,16,128]{3,2,1,0:T(8,128)S(1)}, u32[]{:S(2)}, u32[]{:S(2)}) %collective-permute-start.11) | collective-permute-done | bytes 196640 | tf_op jit(solution)/shard_map/ppermute | solution.py:312
  35.7 1.0 %finish.1 = (f32[3,8,16,128]{3,2,1,0:T(8,128)}, f32[3,8,16,128]{3,2,1,0:T(8,128)}, f32[3,16]{1,0:T(4,128)}, f32[3,16]{1,0:T(4,128)}) custom-call(f32[16,128]{1,0:T(8,128)S(1)} %add.15.sums, f32[6,8,16,128]{3,2,1,0:T(8,128)S(1)} %get-tuple-element.18.keep, f32[3,8,16,128]{3,2,1,0:T(8,128)S(1)} %collective-permute-done.11.come), custom_call_target="tpu_custom_call" | custom-call | tf_op jit(solution)/shard_map/finish/pallas_call | solution.py:291
  (11 shorter events, 0.1 us)
Async XLA Ops:
  0.6 1.0 %copy-start = (f32[4,8,16,128]{3,2,1,0:T(8,128)S(1)}, f32[4,8,16,128]{3,2,1,0:T(8,128)}, u32[]{:S(2)}) copy-start(f32[4,8,16,128]{3,2,1,0:T(8,128)} %own.5) | copy-start | bytes 786436
  1.9 7.2 %collective-permute-start = (f32[20,16,128]{2,1,0:T(8,128)S(1)}, f32[20,16,128]{2,1,0:T(8,128)S(1)}, u32[]{:S(2)}, u32[]{:S(2)}) collective-permute-start(f32[20,16,128]{2,1,0:T(8,128)S(1)} %get-tuple-element.12), channel_id=1, source_target_pairs={{0,1},{1,0},{2,3},{3,2},{4,5},{5,4},{6,7},{7,6},{8,9},{9,8},{10,11... | collective-permute-start | bytes 491528 | tf_op jit(solution)/shard_map/ppermute | solution.py:312
  4.9 8.3 %collective-permute-start.3 = (f32[4,16,128]{2,1,0:T(8,128)S(1)}, f32[4,16,128]{2,1,0:T(8,128)S(1)}, u32[]{:S(2)}, u32[]{:S(2)}) collective-permute-start(f32[4,16,128]{2,1,0:T(8,128)S(1)} %get-tuple-element.13), channel_id=1, source_target_pairs={{1,25},{0,8},{9,1},{8,16},{17,9},{16,24},{25,17},{24,0},{3,27},{2,... | collective-permute-start | bytes 98312 | tf_op jit(solution)/shard_map/ppermute | solution.py:336
  6.4 6.7 %collective-permute-start.4 = (f32[4,16,128]{2,1,0:T(8,128)S(1)}, f32[4,16,128]{2,1,0:T(8,128)S(1)}, u32[]{:S(2)}, u32[]{:S(2)}) collective-permute-start(f32[4,16,128]{2,1,0:T(8,128)S(1)} %get-tuple-element.14), channel_id=1, source_target_pairs={{0,25},{1,8},{8,1},{9,16},{16,9},{17,24},{24,17},{25,0},{2,27},{3,... | collective-permute-start | bytes 98312 | tf_op jit(solution)/shard_map/ppermute | solution.py:335
  9.2 8.7 %copy-start.1 = (bf16[768,512]{1,0:T(8,128)(2,1)S(1)}, bf16[768,512]{1,0:T(8,128)(2,1)}, u32[]{:S(2)}) copy-start(bf16[768,512]{1,0:T(8,128)(2,1)} %constant.2.clone.weights) | copy-start | bytes 2359300
  9.2 8.7 %collective-permute-start.2 = (f32[2,16,16,128]{3,2,1,0:T(8,128)S(1)}, f32[2,16,16,128]{3,2,1,0:T(8,128)S(1)}, u32[]{:S(2)}, u32[]{:S(2)}) collective-permute-start(f32[2,16,16,128]{3,2,1,0:T(8,128)S(1)} %main.1), channel_id=1, source_target_pairs={{0,0},{2,4},{4,2},{6,6},{1,1},{3,5},{5,3},{7,7},{8,8},{10,12},{12,... | collective-permute-start | bytes 786440 | tf_op jit(solution)/shard_map/ppermute | solution.py:318
  10.0 7.9 %collective-permute-start.1 = (f32[2,16,16,128]{3,2,1,0:T(8,128)S(1)}, f32[2,16,16,128]{3,2,1,0:T(8,128)S(1)}, u32[]{:S(2)}, u32[]{:S(2)}) collective-permute-start(f32[2,16,16,128]{3,2,1,0:T(8,128)S(1)} %main.1), channel_id=1, source_target_pairs={{0,2},{2,0},{4,6},{6,4},{1,3},{3,1},{5,7},{7,5},{8,10},{10,8},{12,... | collective-permute-start | bytes 786440 | tf_op jit(solution)/shard_map/ppermute | solution.py:315
  13.4 3.5 %collective-permute-start.6 = (f32[16,16,128]{2,1,0:T(8,128)S(1)}, f32[16,16,128]{2,1,0:T(8,128)S(1)}, u32[]{:S(2)}, u32[]{:S(2)}) collective-permute-start(f32[16,16,128]{2,1,0:T(8,128)S(1)} %strips.1), channel_id=1, source_target_pairs={{0,0},{2,4},{4,2},{6,6},{1,1},{3,5},{5,3},{7,7},{8,8},{10,12},{12,... | collective-permute-start | bytes 393224 | tf_op jit(solution)/shard_map/ppermute | solution.py:318
  14.1 3.8 %collective-permute-start.5 = (f32[16,16,128]{2,1,0:T(8,128)S(1)}, f32[16,16,128]{2,1,0:T(8,128)S(1)}, u32[]{:S(2)}, u32[]{:S(2)}) collective-permute-start(f32[16,16,128]{2,1,0:T(8,128)S(1)} %strips.1), channel_id=1, source_target_pairs={{0,2},{2,0},{4,6},{6,4},{1,3},{3,1},{5,7},{7,5},{8,10},{10,8},{12,... | collective-permute-start | bytes 393224 | tf_op jit(solution)/shard_map/ppermute | solution.py:315
  22.3 4.6 %collective-permute-start.9 = (f32[16,128]{1,0:T(8,128)S(1)}, f32[16,128]{1,0:T(8,128)S(1)}, u32[]{:S(2)}, u32[]{:S(2)}) collective-permute-start(f32[16,128]{1,0:T(8,128)S(1)} %get-tuple-element.15), channel_id=1, source_target_pairs={{0,9},{1,8},{8,1},{9,0},{16,25},{17,24},{24,17},{25,16},{2,11},{3,... | collective-permute-start | bytes 24584 | tf_op jit(solution)/shard_map/ppermute | solution.py:369
  24.2 3.7 %collective-permute-start.8 = (f32[16,128]{1,0:T(8,128)S(1)}, f32[16,128]{1,0:T(8,128)S(1)}, u32[]{:S(2)}, u32[]{:S(2)}) collective-permute-start(f32[16,128]{1,0:T(8,128)S(1)} %get-tuple-element.15), channel_id=1, source_target_pairs={{0,8},{1,9},{8,0},{9,1},{16,24},{17,25},{24,16},{25,17},{2,10},{3,... | collective-permute-start | bytes 24584 | tf_op jit(solution)/shard_map/ppermute | solution.py:369
  24.7 3.7 %collective-permute-start.7 = (f32[16,128]{1,0:T(8,128)S(1)}, f32[16,128]{1,0:T(8,128)S(1)}, u32[]{:S(2)}, u32[]{:S(2)}) collective-permute-start(f32[16,128]{1,0:T(8,128)S(1)} %get-tuple-element.15), channel_id=1, source_target_pairs={{0,1},{1,0},{8,9},{9,8},{16,17},{17,16},{24,25},{25,24},{2,3},{3,2... | collective-permute-start | bytes 24584 | tf_op jit(solution)/shard_map/ppermute | solution.py:369
  28.3 7.4 %collective-permute-start.11 = (f32[3,8,16,128]{3,2,1,0:T(8,128)S(1)}, f32[3,8,16,128]{3,2,1,0:T(8,128)S(1)}, u32[]{:S(2)}, u32[]{:S(2)}) collective-permute-start(f32[3,8,16,128]{3,2,1,0:T(8,128)S(1)} %get-tuple-element.19), channel_id=1, source_target_pairs={{0,1},{1,0},{2,3},{3,2},{4,5},{5,4},{6,7},{7,6},{8,9},{9,8},{10,11... | collective-permute-start | bytes 589832 | tf_op jit(solution)/shard_map/ppermute | solution.py:312
  29.5 4.6 %collective-permute-start.10 = (f32[16,128]{1,0:T(8,128)S(1)}, f32[16,128]{1,0:T(8,128)S(1)}, u32[]{:S(2)}, u32[]{:S(2)}) collective-permute-start(f32[16,128]{1,0:T(8,128)S(1)} %add_add_fusion), channel_id=1, source_target_pairs={{0,16},{1,17},{8,24},{9,25},{16,0},{17,1},{24,8},{25,9},{2,18},{3,... | collective-permute-start | bytes 24584 | tf_op jit(solution)/shard_map/ppermute | solution.py:369

commit v10 on v8

--- a/solution.py
+++ b/solution.py
@@ -38,7 +38,10 @@
 def plane_constants(layers, rows):
     stream = band(layers, layers, 0)
     wall = band(rows, 2 * rows, reach)
-    blocks = [np.kron(stream, wall[:, :rows]), np.kron(stream, wall[:, rows:])]
+    near = np.arange(reach, reach + rows)
+    far = np.setdiff1d(np.arange(2 * rows), near)
+    parts = [np.arange(rows), np.arange(rows, 2 * rows), near, far]
+    blocks = [np.kron(stream, wall[:, part]) for part in parts]
     return split_constant(np.concatenate(blocks, axis=1))
 
 
@@ -140,42 +143,51 @@
         yield f, jnp.where(in_strip, strip, cells)
 
 
+def column(t, width=128):
+    return slice(t * width, (t + 1) * width)
+
+
+def planes_of(weights, part, high, low):
+    cells = weights.shape[1] // 4
+    plane_h = weights[:cells, part.start * cells : part.stop * cells]
+    plane_l = weights[cells : 2 * cells, part.start * cells : part.stop * cells]
+    return dot(plane_h, high) + dot(plane_l, high) + dot(plane_h, low)
+
+
+def centre_kernel(main, strips, weights, centre, upper, lower, products, in_h, in_l, prod_h, prod_l):
+    _, both, rows, width = main.shape
+    cells = both * rows
+    me_s = lax.axis_index("stream")
+    for f, value in unpack(main, strips, me_s):
+        centre[f] = value
+        in_h[:, column(f)], in_l[:, column(f)] = halves(value.reshape(cells, width))
+    for i in range(3):
+        value = (centre[i] * centre[3]).reshape(cells, width)
+        prod_h[:, column(i)], prod_l[:, column(i)] = halves(value)
+    upper[...] = planes_of(weights, slice(1, 2), in_h[...], in_l[...])
+    lower[...] = planes_of(weights, slice(0, 1), in_h[...], in_l[...])
+    products[...] = planes_of(weights, slice(2, 3), prod_h[...], prod_l[...])
+
+
 def flux_kernel(
-    walls, main, a_main, b_main, strips, a_strips, b_strips, weights, keep_ref, send_ref, sums_ref,
+    walls, a_main, b_main, a_strips, b_strips, centre_raw, upper, lower, products, weights,
+    keep_ref, send_ref, sums_ref,
     raw, in_h, in_l, prod_h, prod_l, mean, mid_h, mid_l, clark_all, similar_all,
 ):
     _, layers, rows, width = keep_ref.shape
     both = 2 * layers
     cells = both * rows
-    plane_h = weights.at[:cells]
-    plane_l = weights.at[cells : 2 * cells]
     span_w = weights.at[2 * cells :, : 2 * width]
     me_s = lax.axis_index("stream")
     me_w = lax.axis_index("wall")
     odd = lax.rem(me_w, 2)
-    row_a = pl.multiple_of((1 - odd) * (2 * rows), rows)
-    row_b = pl.multiple_of(odd * (2 * rows), rows)
     at_end = (me_w == 0) | (me_w == walls - 1)
     keep_b = jnp.where(at_end, 0.0, 1.0).astype(jnp.float32)
 
-    for f, value in unpack(main, strips, me_s):
-        raw[f, :, rows : 2 * rows, :] = value
     for f, value in unpack(a_main, a_strips, me_s):
-        raw[f, :, pl.ds(row_a, rows), :] = value
+        raw[1 - odd, f] = value
     for f, value in unpack(b_main, b_strips, me_s):
-        raw[f, :, pl.ds(row_b, rows), :] = value * keep_b
-
-    def column(t):
-        return slice(t * width, (t + 1) * width)
-
-    for block in range(3):
-        down = slice(block * cells, (block + 1) * cells)
-        for t in range(4):
-            value = raw[t, :, block * rows : (block + 1) * rows, :].reshape(cells, width)
-            in_h[down, column(t)], in_l[down, column(t)] = halves(value)
-
-    def planes_of(high, low):
-        return dot(plane_h[...], high) + dot(plane_l[...], high) + dot(plane_h[...], low)
+        raw[odd, f] = value * keep_b
 
     def along_span_of(planes):
         high, low = halves(planes)
@@ -188,9 +200,10 @@
     for t in range(4):
         mean[t, 0] = jnp.zeros((2 * rows, width), jnp.float32)
         mean[t, both + 1] = jnp.zeros((2 * rows, width), jnp.float32)
-    for half in range(2):
-        span = slice(half * cells, (half + 2) * cells)
-        planes = planes_of(in_h[span, :], in_l[span, :])
+    for half, partial in enumerate((upper, lower)):
+        for f in range(4):
+            in_h[:, column(f)], in_l[:, column(f)] = halves(raw[half, f].reshape(cells, width))
+        planes = partial[...] + planes_of(weights, slice(half, half + 1), in_h[...], in_l[...])
         row = lax.rem(lax.broadcasted_iota(jnp.int32, planes.shape, 0), rows)
         if half == 0:
             inside = (me_w > 0) | (row >= reach)
@@ -200,14 +213,14 @@
         for t, value in enumerate(along_span_of(planes)):
             mean[t, 1 : both + 1, half * rows : (half + 1) * rows, :] = value
 
-    for half in range(2):
-        span = slice(reach + half * rows, reach + (half + 1) * rows)
-        down = slice(half * cells, (half + 1) * cells)
-        temperature = raw[3, :, span, :].reshape(cells, width)
-        for t in range(3):
-            value = raw[t, :, span, :].reshape(cells, width) * temperature
-            prod_h[down, column(t)], prod_l[down, column(t)] = halves(value)
-    flux = along_span_of(planes_of(prod_h[...], prod_l[...]))
+    def around(f):
+        return jnp.concatenate([raw[0, f, :, rows - reach :, :], raw[1, f, :, :reach, :]], axis=1)
+
+    temperature = around(3)
+    for i in range(3):
+        value = (around(i) * temperature).reshape(cells, width)
+        prod_h[:, column(i)], prod_l[:, column(i)] = halves(value)
+    flux = along_span_of(products[...] + planes_of(weights, slice(3, 4), prod_h[...], prod_l[...]))
 
     for half in range(2):
         span = slice(half * rows, (half + 1) * rows)
@@ -216,7 +229,7 @@
         tiles += [tiles[i] * tiles[3] for i in range(3)]
         for t, value in enumerate(tiles):
             mid_h[down, column(t)], mid_l[down, column(t)] = halves(value)
-    second = along_span_of(planes_of(mid_h[...], mid_l[...]))
+    second = along_span_of(planes_of(weights, slice(0, 2), mid_h[...], mid_l[...]))
 
     mid_rows = slice(reach, reach + rows)
     centre, along_span, along_wall, along_stream = [], [], [], []
@@ -258,11 +271,11 @@
 
 
 def finish_kernel(
-    plane_cells, tables, keep, come, clark_model, similar_model, clark_corr, similar_corr
+    plane_cells, sums, keep, come, clark_model, similar_model, clark_corr, similar_corr
 ):
     _, layers, rows, width = keep.shape
     me_s = lax.axis_index("stream")
-    table = jnp.sum(tables[...], axis=0) / plane_cells
+    table = sums[...] / plane_cells
     lane = lane_index((rows, width))
     useful = lane // (width // 2) == me_s
     corr = jnp.zeros((rows, width), jnp.float32)
@@ -339,40 +352,64 @@
     (strips,) = call(rim_kernel, "strips", (fields, part, own_strip, part_strip), ((both, rows, width),), hint=2**35)
     b_strips, a_strips = pair_b(strips), pair_a(strips)
 
-    weights = np.zeros((2 * cells + 2 * width, 2 * cells), ml_dtypes.bfloat16)
-    weights[:cells], weights[cells : 2 * cells] = plane_constants(both, rows)
-    weights[2 * cells :, : 2 * width] = span_constants(width)
+    matrices = np.zeros((2 * cells + 2 * width, 4 * cells), ml_dtypes.bfloat16)
+    matrices[:cells], matrices[cells : 2 * cells] = plane_constants(both, rows)
+    matrices[2 * cells :, : 2 * width] = span_constants(width)
+    weights = jnp.asarray(matrices)
     single, brief = jnp.float32, jnp.bfloat16
+    partial = call(
+        centre_kernel,
+        "centre",
+        (main, strips, weights),
+        ((4, both, rows, width), (cells, 4 * width), (cells, 4 * width), (cells, 3 * width)),
+        [
+            ((cells, 4 * width), brief),
+            ((cells, 4 * width), brief),
+            ((cells, 3 * width), brief),
+            ((cells, 3 * width), brief),
+        ],
+        mib=16,
+        hint=2**31,
+    )
     keep, send, sums = call(
         functools.partial(flux_kernel, walls),
         "flux",
-        (main, a_main, b_main, strips, a_strips, b_strips, jnp.asarray(weights)),
+        (a_main, b_main, a_strips, b_strips, *partial, weights),
         ((6, layers, rows, width), (3, layers, rows, width), (rows, width)),
         [
-            ((4, both, 3 * rows, width), single),
-            ((3 * cells, 4 * width), brief),
-            ((3 * cells, 4 * width), brief),
-            ((2 * cells, 3 * width), brief),
-            ((2 * cells, 3 * width), brief),
+            ((2, 4, both, rows, width), single),
+            ((cells, 4 * width), brief),
+            ((cells, 4 * width), brief),
+            ((cells, 3 * width), brief),
+            ((cells, 3 * width), brief),
             ((4, both + 2, 2 * rows, width), single),
             ((2 * cells, 7 * width), brief),
             ((2 * cells, 7 * width), brief),
             ((3, both, rows, width), single),
             ((3, both, rows, width), single),
         ],
-        mib=32,
+        mib=24,
     )
 
     come = swap(send)
-    group = spans * streams
-    tables = lax.all_to_all(
-        jnp.broadcast_to(sums[None], (group, rows, width)), ("span", "stream"), 0, 0
-    )
+
+    def from_span(value, step):
+        return lax.ppermute(value, "span", [(p, p ^ step) for p in range(spans)])
+
+    step = 1
+    while step < spans:
+        if 2 * step < spans:
+            far = from_span(sums, 3 * step) + from_span(sums, 2 * step)
+            sums = (sums + from_span(sums, step)) + far
+        else:
+            sums = sums + from_span(sums, step)
+        step *= 4
+    sums = sums + swap(sums)
     block, corr = (3, layers, rows, width), (3, rows)
     return call(
-        functools.partial(finish_kernel, float(layers * width * group)),
+        functools.partial(finish_kernel, float(layers * width * spans * streams)),
         "finish",
-        (tables, keep, come),
+        (sums, keep, come),
         (block, block, corr, corr),
     )
 

time: 37 us -> 34.5 us (0.932)
  the two profiles are of different devices: /device:TPU:4 before, /device:TPU:6 now
where the time goes in v10:
time: 34.5 us; the launch traced here: 34.3 us
  starting transfers between devices  15.1 us (44%)
  waiting for transfers between devices  11.3 us (33%)
  Pallas kernels  6.14 us (18%)
  local copies, waits for them, and re-layouts  0.95 us (3%)
  between operations  0.75 us (2%)
    pallas_call x6, Pallas kernels, call(): pl.pallas_call(kernel, out_shape=tuple((jax.ShapeDtypeStruct(shape, jnp.f...  6.14 us
    ppermute x3, waiting for transfers between devices, swap(): return lax.ppermute(value, 'stream', [(0, 1), (1, 0)])  4.96 us
    ppermute x2, starting transfers between devices, pair_b(): lax.ppermute(value, 'wall', [(w, min(max((w + 1 ^ 1) - 1, 0), walls - 1))...  4.96 us
    ppermute x3, starting transfers between devices, from_span(): return lax.ppermute(value, 'span', [(p, p ^ step) for p in range(spans)])  4.54 us
    ppermute x1, starting transfers between devices, shards(): own_strip = lax.ppermute(second, ('span', 'stream'), to_same)  3.6 us
    ppermute x3, waiting for transfers between devices, from_span(): return lax.ppermute(value, 'span', [(p, p ^ step) for p in range(spans)])  3.36 us
    ppermute x2, waiting for transfers between devices, pair_b(): lax.ppermute(value, 'wall', [(w, min(max((w + 1 ^ 1) - 1, 0), walls - 1))...  2.23 us
    ppermute x3, starting transfers between devices, swap(): return lax.ppermute(value, 'stream', [(0, 1), (1, 0)])  1.41 us
  transfers between devices with their start and end apart: 12, of which 5 were waited for; matrix products, arithmetic and copies ran while one was open for 0% of the time, Pallas kernels for 4%

profile of v10, /device:TPU:6, one launch (start us, length us, event | category | flops | bytes accessed | tf_op | source)
XLA Modules:
  0.0 34.3 jit_solution(6136827499221554788)
XLA Ops:
  0.6 0.9 %copy-done.1 = f32[4,8,16,128]{3,2,1,0:T(8,128)S(1)} copy-done((f32[4,8,16,128]{3,2,1,0:T(8,128)S(1)}, f32[4,8,16,128]{3,2,1,0:T(8,128)}, u32[]{:S(2)}) %copy-start.1) | copy-done | bytes 262168
  1.6 0.3 pack.1
  1.9 0.6 %collective-permute-start = (f32[20,16,128]{2,1,0:T(8,128)S(1)}, f32[20,16,128]{2,1,0:T(8,128)S(1)}, u32[]{:S(2)}, u32[]{:S(2)}) collective-permute-start(f32[20,16,128]{2,1,0:T(8,128)S(1)} %get-tuple-element.14), channel_id=1, source_target_pairs={{0,1},{1,0},{2,3},{3,2},{4,5},{5,4},{6,7},{7,6},{8,9},{9,8},{10,11... | collective-permute-start | bytes 491528 | tf_op jit(solution)/shard_map/ppermute | solution.py:325
  2.5 3.6 %collective-permute-start.3 = (f32[4,16,128]{2,1,0:T(8,128)S(1)}, f32[4,16,128]{2,1,0:T(8,128)S(1)}, u32[]{:S(2)}, u32[]{:S(2)}) collective-permute-start(f32[4,16,128]{2,1,0:T(8,128)S(1)} %get-tuple-element.15), channel_id=1, source_target_pairs={{1,25},{0,8},{9,1},{8,16},{17,9},{16,24},{25,17},{24,0},{3,27},{2,... | collective-permute-start | bytes 98312 | tf_op jit(solution)/shard_map/ppermute | solution.py:349
  6.1 0.5 %collective-permute-start.4 = (f32[4,16,128]{2,1,0:T(8,128)S(1)}, f32[4,16,128]{2,1,0:T(8,128)S(1)}, u32[]{:S(2)}, u32[]{:S(2)}) collective-permute-start(f32[4,16,128]{2,1,0:T(8,128)S(1)} %get-tuple-element.16), channel_id=1, source_target_pairs={{0,25},{1,8},{8,1},{9,16},{16,9},{17,24},{24,17},{25,0},{2,27},{3,... | collective-permute-start | bytes 98312 | tf_op jit(solution)/shard_map/ppermute | solution.py:348
  6.5 1.3 %collective-permute-done.part = f32[20,16,128]{2,1,0:T(8,128)S(1)} collective-permute-done((f32[20,16,128]{2,1,0:T(8,128)S(1)}, f32[20,16,128]{2,1,0:T(8,128)S(1)}, u32[]{:S(2)}, u32[]{:S(2)}) %collective-permute-start) | collective-permute-done | bytes 163872 | tf_op jit(solution)/shard_map/ppermute | solution.py:325
  7.9 0.1 main.1
  8.0 0.0 copy-start
  8.0 2.1 %collective-permute-start.2 = (f32[2,16,16,128]{3,2,1,0:T(8,128)S(1)}, f32[2,16,16,128]{3,2,1,0:T(8,128)S(1)}, u32[]{:S(2)}, u32[]{:S(2)}) collective-permute-start(f32[2,16,16,128]{3,2,1,0:T(8,128)S(1)} %main.1), channel_id=1, source_target_pairs={{0,0},{2,4},{4,2},{6,6},{1,1},{3,5},{5,3},{7,7},{8,8},{10,12},{12,... | collective-permute-start | bytes 786440 | tf_op jit(solution)/shard_map/ppermute | solution.py:331
  10.0 0.1 collective-permute-start.1
  10.1 0.7 %collective-permute-done.4.part_strip = f32[4,16,128]{2,1,0:T(8,128)S(1)} collective-permute-done((f32[4,16,128]{2,1,0:T(8,128)S(1)}, f32[4,16,128]{2,1,0:T(8,128)S(1)}, u32[]{:S(2)}, u32[]{:S(2)}) %collective-permute-start.4) | collective-permute-done | bytes 32800 | tf_op jit(solution)/shard_map/ppermute | solution.py:348
  10.9 0.2 strips.1
  11.1 2.9 %collective-permute-start.6 = (f32[16,16,128]{2,1,0:T(8,128)S(1)}, f32[16,16,128]{2,1,0:T(8,128)S(1)}, u32[]{:S(2)}, u32[]{:S(2)}) collective-permute-start(f32[16,16,128]{2,1,0:T(8,128)S(1)} %strips.1), channel_id=1, source_target_pairs={{0,0},{2,4},{4,2},{6,6},{1,1},{3,5},{5,3},{7,7},{8,8},{10,12},{12,... | collective-permute-start | bytes 393224 | tf_op jit(solution)/shard_map/ppermute | solution.py:331
  14.0 0.1 collective-permute-start.5
  14.1 1.0 %centre.1 = (f32[4,16,16,128]{3,2,1,0:T(8,128)S(1)}, f32[256,512]{1,0:T(8,128)S(1)}, f32[256,512]{1,0:T(8,128)S(1)}, f32[256,384]{1,0:T(8,128)S(1)}) custom-call(f32[2,16,16,128]{3,2,1,0:T(8,128)S(1)} %main.1, f32[16,16,128]{2,1,0:T(8,128)S(1)} %strips.1, bf16[768,1024]{1,0:T(8,128)(2,1)S(1)} %copy-done), custom_call_target="tpu_custom_call" | custom-call | flops 2147483648 | bytes 21474836 | tf_op jit(solution)/shard_map/centre/pallas_call | solution.py:304
  15.2 2.2 %collective-permute-done.6.b_strips = f32[16,16,128]{2,1,0:T(8,128)S(1)} collective-permute-done((f32[16,16,128]{2,1,0:T(8,128)S(1)}, f32[16,16,128]{2,1,0:T(8,128)S(1)}, u32[]{:S(2)}, u32[]{:S(2)}) %collective-permute-start.6) | collective-permute-done | bytes 131104 | tf_op jit(solution)/shard_map/ppermute | solution.py:331
  17.4 3.5 %flux.1 = (f32[6,8,16,128]{3,2,1,0:T(8,128)S(1)}, f32[3,8,16,128]{3,2,1,0:T(8,128)S(1)}, f32[16,128]{1,0:T(8,128)S(1)}) custom-call(f32[2,16,16,128]{3,2,1,0:T(8,128)S(1)} %collective-permute-done.1.a_main, f32[2,16,16,128]{3,2,1,0:T(8,128)S(1)} %collective-permute-done.2.b_main, f32[16,16,128]{2,1,0:T(8,128)S(1)} %collective-permute-done.5.a_strips, ...), custom_call_target="tpu_custom_call" | custom-call | tf_op jit(solution)/shard_map/flux/pallas_call | solution.py:304
  20.9 3.2 %collective-permute-start.9 = (f32[16,128]{1,0:T(8,128)S(1)}, f32[16,128]{1,0:T(8,128)S(1)}, u32[]{:S(2)}, u32[]{:S(2)}) collective-permute-start(f32[16,128]{1,0:T(8,128)S(1)} %get-tuple-element.21), channel_id=1, source_target_pairs={{0,16},{8,24},{16,0},{24,8},{1,17},{9,25},{17,1},{25,9},{2,18},{10... | collective-permute-start | bytes 24584 | tf_op jit(solution)/shard_map/ppermute | solution.py:397
  24.1 1.3 %collective-permute-start.8 = (f32[16,128]{1,0:T(8,128)S(1)}, f32[16,128]{1,0:T(8,128)S(1)}, u32[]{:S(2)}, u32[]{:S(2)}) collective-permute-start(f32[16,128]{1,0:T(8,128)S(1)} %get-tuple-element.21), channel_id=1, source_target_pairs={{0,24},{8,16},{16,8},{24,0},{1,25},{9,17},{17,9},{25,1},{2,26},{10... | collective-permute-start | bytes 24584 | tf_op jit(solution)/shard_map/ppermute | solution.py:397
  25.4 0.7 %collective-permute-start.11 = (f32[3,8,16,128]{3,2,1,0:T(8,128)S(1)}, f32[3,8,16,128]{3,2,1,0:T(8,128)S(1)}, u32[]{:S(2)}, u32[]{:S(2)}) collective-permute-start(f32[3,8,16,128]{3,2,1,0:T(8,128)S(1)} %get-tuple-element.23), channel_id=1, source_target_pairs={{0,1},{1,0},{2,3},{3,2},{4,5},{5,4},{6,7},{7,6},{8,9},{9,8},{10,11... | collective-permute-start | bytes 589832 | tf_op jit(solution)/shard_map/ppermute | solution.py:325
  26.2 3.4 %collective-permute-done.8 = f32[16,128]{1,0:T(8,128)S(1)} collective-permute-done((f32[16,128]{1,0:T(8,128)S(1)}, f32[16,128]{1,0:T(8,128)S(1)}, u32[]{:S(2)}, u32[]{:S(2)}) %collective-permute-start.8) | collective-permute-done | bytes 8224 | tf_op jit(solution)/shard_map/ppermute | solution.py:397
  29.5 0.1 collective-permute-start.10
  29.6 3.6 %collective-permute-done.10 = f32[16,128]{1,0:T(8,128)S(1)} collective-permute-done((f32[16,128]{1,0:T(8,128)S(1)}, f32[16,128]{1,0:T(8,128)S(1)}, u32[]{:S(2)}, u32[]{:S(2)}) %collective-permute-start.10) | collective-permute-done | bytes 8224 | tf_op jit(solution)/shard_map/ppermute | solution.py:325
  33.3 1.0 %finish.1 = (f32[3,8,16,128]{3,2,1,0:T(8,128)}, f32[3,8,16,128]{3,2,1,0:T(8,128)}, f32[3,16]{1,0:T(4,128)}, f32[3,16]{1,0:T(4,128)}) custom-call(f32[16,128]{1,0:T(8,128)S(1)} %add.15.sums, f32[6,8,16,128]{3,2,1,0:T(8,128)S(1)} %get-tuple-element.22.keep, f32[3,8,16,128]{3,2,1,0:T(8,128)S(1)} %collective-permute-done.11.come), custom_call_target="tpu_custom_call" | custom-call | tf_op jit(solution)/shard_map/finish/pallas_call | solution.py:304
  (12 shorter events, 0.0 us)
Async XLA Ops:
  0.6 1.0 %copy-start.1 = (f32[4,8,16,128]{3,2,1,0:T(8,128)S(1)}, f32[4,8,16,128]{3,2,1,0:T(8,128)}, u32[]{:S(2)}) copy-start(f32[4,8,16,128]{3,2,1,0:T(8,128)} %own.5) | copy-start | bytes 786436
  1.9 6.0 %collective-permute-start = (f32[20,16,128]{2,1,0:T(8,128)S(1)}, f32[20,16,128]{2,1,0:T(8,128)S(1)}, u32[]{:S(2)}, u32[]{:S(2)}) collective-permute-start(f32[20,16,128]{2,1,0:T(8,128)S(1)} %get-tuple-element.14), channel_id=1, source_target_pairs={{0,1},{1,0},{2,3},{3,2},{4,5},{5,4},{6,7},{7,6},{8,9},{9,8},{10,11... | collective-permute-start | bytes 491528 | tf_op jit(solution)/shard_map/ppermute | solution.py:325
  2.5 7.7 %collective-permute-start.3 = (f32[4,16,128]{2,1,0:T(8,128)S(1)}, f32[4,16,128]{2,1,0:T(8,128)S(1)}, u32[]{:S(2)}, u32[]{:S(2)}) collective-permute-start(f32[4,16,128]{2,1,0:T(8,128)S(1)} %get-tuple-element.15), channel_id=1, source_target_pairs={{1,25},{0,8},{9,1},{8,16},{17,9},{16,24},{25,17},{24,0},{3,27},{2,... | collective-permute-start | bytes 98312 | tf_op jit(solution)/shard_map/ppermute | solution.py:349
  6.1 4.8 %collective-permute-start.4 = (f32[4,16,128]{2,1,0:T(8,128)S(1)}, f32[4,16,128]{2,1,0:T(8,128)S(1)}, u32[]{:S(2)}, u32[]{:S(2)}) collective-permute-start(f32[4,16,128]{2,1,0:T(8,128)S(1)} %get-tuple-element.16), channel_id=1, source_target_pairs={{0,25},{1,8},{8,1},{9,16},{16,9},{17,24},{24,17},{25,0},{2,27},{3,... | collective-permute-start | bytes 98312 | tf_op jit(solution)/shard_map/ppermute | solution.py:348
  8.0 6.1 %copy-start = (bf16[768,1024]{1,0:T(8,128)(2,1)S(1)}, bf16[768,1024]{1,0:T(8,128)(2,1)}, u32[]{:S(2)}) copy-start(bf16[768,1024]{1,0:T(8,128)(2,1)} %constant.2.clone.weights) | copy-start | bytes 4718596
  8.0 9.4 %collective-permute-start.2 = (f32[2,16,16,128]{3,2,1,0:T(8,128)S(1)}, f32[2,16,16,128]{3,2,1,0:T(8,128)S(1)}, u32[]{:S(2)}, u32[]{:S(2)}) collective-permute-start(f32[2,16,16,128]{3,2,1,0:T(8,128)S(1)} %main.1), channel_id=1, source_target_pairs={{0,0},{2,4},{4,2},{6,6},{1,1},{3,5},{5,3},{7,7},{8,8},{10,12},{12,... | collective-permute-start | bytes 786440 | tf_op jit(solution)/shard_map/ppermute | solution.py:331
  10.0 7.3 %collective-permute-start.1 = (f32[2,16,16,128]{3,2,1,0:T(8,128)S(1)}, f32[2,16,16,128]{3,2,1,0:T(8,128)S(1)}, u32[]{:S(2)}, u32[]{:S(2)}) collective-permute-start(f32[2,16,16,128]{3,2,1,0:T(8,128)S(1)} %main.1), channel_id=1, source_target_pairs={{0,2},{2,0},{4,6},{6,4},{1,3},{3,1},{5,7},{7,5},{8,10},{10,8},{12,... | collective-permute-start | bytes 786440 | tf_op jit(solution)/shard_map/ppermute | solution.py:328
  11.1 6.3 %collective-permute-start.6 = (f32[16,16,128]{2,1,0:T(8,128)S(1)}, f32[16,16,128]{2,1,0:T(8,128)S(1)}, u32[]{:S(2)}, u32[]{:S(2)}) collective-permute-start(f32[16,16,128]{2,1,0:T(8,128)S(1)} %strips.1), channel_id=1, source_target_pairs={{0,0},{2,4},{4,2},{6,6},{1,1},{3,5},{5,3},{7,7},{8,8},{10,12},{12,... | collective-permute-start | bytes 393224 | tf_op jit(solution)/shard_map/ppermute | solution.py:331
  14.0 3.4 %collective-permute-start.5 = (f32[16,16,128]{2,1,0:T(8,128)S(1)}, f32[16,16,128]{2,1,0:T(8,128)S(1)}, u32[]{:S(2)}, u32[]{:S(2)}) collective-permute-start(f32[16,16,128]{2,1,0:T(8,128)S(1)} %strips.1), channel_id=1, source_target_pairs={{0,2},{2,0},{4,6},{6,4},{1,3},{3,1},{5,7},{7,5},{8,10},{10,8},{12,... | collective-permute-start | bytes 393224 | tf_op jit(solution)/shard_map/ppermute | solution.py:328
  20.9 5.3 %collective-permute-start.9 = (f32[16,128]{1,0:T(8,128)S(1)}, f32[16,128]{1,0:T(8,128)S(1)}, u32[]{:S(2)}, u32[]{:S(2)}) collective-permute-start(f32[16,128]{1,0:T(8,128)S(1)} %get-tuple-element.21), channel_id=1, source_target_pairs={{0,16},{8,24},{16,0},{24,8},{1,17},{9,25},{17,1},{25,9},{2,18},{10... | collective-permute-start | bytes 24584 | tf_op jit(solution)/shard_map/ppermute | solution.py:397
  24.1 5.4 %collective-permute-start.8 = (f32[16,128]{1,0:T(8,128)S(1)}, f32[16,128]{1,0:T(8,128)S(1)}, u32[]{:S(2)}, u32[]{:S(2)}) collective-permute-start(f32[16,128]{1,0:T(8,128)S(1)} %get-tuple-element.21), channel_id=1, source_target_pairs={{0,24},{8,16},{16,8},{24,0},{1,25},{9,17},{17,9},{25,1},{2,26},{10... | collective-permute-start | bytes 24584 | tf_op jit(solution)/shard_map/ppermute | solution.py:397
  25.4 4.1 %collective-permute-start.7 = (f32[16,128]{1,0:T(8,128)S(1)}, f32[16,128]{1,0:T(8,128)S(1)}, u32[]{:S(2)}, u32[]{:S(2)}) collective-permute-start(f32[16,128]{1,0:T(8,128)S(1)} %get-tuple-element.21), channel_id=1, source_target_pairs={{0,8},{8,0},{16,24},{24,16},{1,9},{9,1},{17,25},{25,17},{2,10},{10... | collective-permute-start | bytes 24584 | tf_op jit(solution)/shard_map/ppermute | solution.py:397
  25.4 7.8 %collective-permute-start.11 = (f32[3,8,16,128]{3,2,1,0:T(8,128)S(1)}, f32[3,8,16,128]{3,2,1,0:T(8,128)S(1)}, u32[]{:S(2)}, u32[]{:S(2)}) collective-permute-start(f32[3,8,16,128]{3,2,1,0:T(8,128)S(1)} %get-tuple-element.23), channel_id=1, source_target_pairs={{0,1},{1,0},{2,3},{3,2},{4,5},{5,4},{6,7},{7,6},{8,9},{9,8},{10,11... | collective-permute-start | bytes 589832 | tf_op jit(solution)/shard_map/ppermute | solution.py:325
  29.5 3.7 %collective-permute-start.10 = (f32[16,128]{1,0:T(8,128)S(1)}, f32[16,128]{1,0:T(8,128)S(1)}, u32[]{:S(2)}, u32[]{:S(2)}) collective-permute-start(f32[16,128]{1,0:T(8,128)S(1)} %add_add_fusion), channel_id=1, source_target_pairs={{0,1},{1,0},{2,3},{3,2},{4,5},{5,4},{6,7},{7,6},{8,9},{9,8},{10,11... | collective-permute-start | bytes 24584 | tf_op jit(solution)/shard_map/ppermute | solution.py:325

commit v11 on v10

--- a/solution.py
+++ b/solution.py
@@ -112,35 +112,43 @@
     to_same[...] = pack_strip(own, 7 * (1 - me_s))
 
 
-def main_kernel(own, part, main):
+def main_kernel(own, part, packed):
     _, layers, _, _ = own.shape
-    me_s = lax.axis_index("stream")
-    for pair, tile in pack_halves(own, me_s):
-        main[pair, pl.ds(me_s * layers, layers)] = tile
-        main[pair, pl.ds((1 - me_s) * layers, layers)] = part[pair * layers : (pair + 1) * layers]
-
-
-def rim_kernel(own, part, own_strip, part_strip, strips):
-    _, layers, _, _ = own.shape
+    both = 2 * layers
     half = layers // 2
     me_s = lax.axis_index("stream")
-    for k, tile in strip_tile(pack_strip(own, 4 - me_s), own_strip[...], me_s):
-        strips[pl.ds(me_s * layers + k * half, half)] = tile
-    for k, tile in strip_tile(part[2 * layers :], part_strip[...], me_s):
-        strips[pl.ds((1 - me_s) * layers + k * half, half)] = tile
-
-
-def unpack(main, strips, me_s):
-    width = strips.shape[-1]
-    unit = unit_index(strips.shape)
+    mine, other = me_s * layers, (1 - me_s) * layers
+    for pair, tile in pack_halves(own, me_s):
+        packed[pl.ds(pair * both + mine, layers)] = tile
+        packed[pl.ds(pair * both + other, layers)] = part[pair * layers : (pair + 1) * layers]
+    packed[pl.ds(2 * both + me_s * half, half)] = pack_strip(own, 4 - me_s)
+    packed[pl.ds(2 * both + (1 - me_s) * half, half)] = part[2 * layers :]
+
+
+def outer_kernel(own_strip, part_strip, outer):
+    half = own_strip.shape[0]
+    me_s = lax.axis_index("stream")
+    outer[pl.ds(me_s * half, half)] = own_strip[...]
+    outer[pl.ds((1 - me_s) * half, half)] = part_strip[...]
+
+
+def unpack(packed, outer, me_s):
+    layers, rows, width = outer.shape
+    both = 2 * layers
+    half = layers // 2
+    unit = unit_index((half, rows, width))
     first = 4 * (1 - me_s)
     in_strip = (unit == first) | (unit == first + 3)
-    for f in range(4):
-        cells = main[f // 2]
-        cells = pltpu.roll(cells, width // 2, 2) if f % 2 else cells
-        strip = strips[...]
-        strip = pltpu.roll(strip, width - 2 * f * rim, 2) if f else strip
-        yield f, jnp.where(in_strip, strip, cells)
+    for s in range(2):
+        inner = packed[2 * both + s * half : 2 * both + (s + 1) * half]
+        for k, strip in strip_tile(inner, outer[s * half : (s + 1) * half], me_s):
+            layer = s * layers + k * half
+            for f in range(4):
+                start = f // 2 * both + layer
+                cells = packed[start : start + half]
+                cells = pltpu.roll(cells, width // 2, 2) if f % 2 else cells
+                moved = pltpu.roll(strip, width - 2 * f * rim, 2) if f else strip
+                yield f, slice(layer, layer + half), jnp.where(in_strip, moved, cells)
 
 
 def column(t, width=128):
@@ -149,28 +157,43 @@
 
 def planes_of(weights, part, high, low):
     cells = weights.shape[1] // 4
-    plane_h = weights[:cells, part.start * cells : part.stop * cells]
-    plane_l = weights[cells : 2 * cells, part.start * cells : part.stop * cells]
+    if part is None:
+        along = slice(0, 2 * cells)
+    else:
+        along = pl.ds(part * cells if isinstance(part, int) else pl.multiple_of(part * cells, cells), cells)
+    plane_h, plane_l = weights[:cells, along], weights[cells : 2 * cells, along]
     return dot(plane_h, high) + dot(plane_l, high) + dot(plane_h, low)
 
 
-def centre_kernel(main, strips, weights, centre, upper, lower, products, in_h, in_l, prod_h, prod_l):
-    _, both, rows, width = main.shape
-    cells = both * rows
-    me_s = lax.axis_index("stream")
-    for f, value in unpack(main, strips, me_s):
-        centre[f] = value
-        in_h[:, column(f)], in_l[:, column(f)] = halves(value.reshape(cells, width))
+def bring(packed, outer, raw, high, low, keep=None):
+    rows, width = packed.shape[1:]
+    for f, along, value in unpack(packed, outer, lax.axis_index("stream")):
+        value = value if keep is None else value * keep
+        raw[f, along] = value
+        down = slice(along.start * rows, along.stop * rows)
+        high[down, column(f)], low[down, column(f)] = halves(value.reshape(-1, width))
+
+
+def centre_kernel(main, outer, weights, upper, lower, products, centre, in_h, in_l, prod_h, prod_l):
+    cells, width = in_h.shape[0], main.shape[-1]
+    bring(main, outer, centre, in_h, in_l)
     for i in range(3):
         value = (centre[i] * centre[3]).reshape(cells, width)
         prod_h[:, column(i)], prod_l[:, column(i)] = halves(value)
-    upper[...] = planes_of(weights, slice(1, 2), in_h[...], in_l[...])
-    lower[...] = planes_of(weights, slice(0, 1), in_h[...], in_l[...])
-    products[...] = planes_of(weights, slice(2, 3), prod_h[...], prod_l[...])
+    upper[...] = planes_of(weights, 1, in_h[...], in_l[...])
+    lower[...] = planes_of(weights, 0, in_h[...], in_l[...])
+    products[...] = planes_of(weights, 2, prod_h[...], prod_l[...])
+
+
+def mate_kernel(main, outer, upper, lower, weights, raw, partial, in_h, in_l):
+    odd = lax.rem(lax.axis_index("wall"), 2)
+    bring(main, outer, raw, in_h, in_l)
+    base = jnp.where(odd == 1, upper[...], lower[...])
+    partial[...] = base + planes_of(weights, 1 - odd, in_h[...], in_l[...])
 
 
 def flux_kernel(
-    walls, a_main, b_main, a_strips, b_strips, centre_raw, upper, lower, products, weights,
+    walls, b_main, b_outer, a_raw, a_partial, upper, lower, products, weights,
     keep_ref, send_ref, sums_ref,
     raw, in_h, in_l, prod_h, prod_l, mean, mid_h, mid_l, clark_all, similar_all,
 ):
@@ -184,10 +207,7 @@
     at_end = (me_w == 0) | (me_w == walls - 1)
     keep_b = jnp.where(at_end, 0.0, 1.0).astype(jnp.float32)
 
-    for f, value in unpack(a_main, a_strips, me_s):
-        raw[1 - odd, f] = value
-    for f, value in unpack(b_main, b_strips, me_s):
-        raw[odd, f] = value * keep_b
+    bring(b_main, b_outer, raw, in_h, in_l, keep_b)
 
     def along_span_of(planes):
         high, low = halves(planes)
@@ -200,10 +220,11 @@
     for t in range(4):
         mean[t, 0] = jnp.zeros((2 * rows, width), jnp.float32)
         mean[t, both + 1] = jnp.zeros((2 * rows, width), jnp.float32)
-    for half, partial in enumerate((upper, lower)):
-        for f in range(4):
-            in_h[:, column(f)], in_l[:, column(f)] = halves(raw[half, f].reshape(cells, width))
-        planes = partial[...] + planes_of(weights, slice(half, half + 1), in_h[...], in_l[...])
+    from_b = planes_of(weights, odd, in_h[...], in_l[...])
+    from_b += jnp.where(odd == 0, upper[...], lower[...])
+    from_a = a_partial[...]
+    for half in range(2):
+        planes = jnp.where(odd == half, from_b, from_a)
         row = lax.rem(lax.broadcasted_iota(jnp.int32, planes.shape, 0), rows)
         if half == 0:
             inside = (me_w > 0) | (row >= reach)
@@ -214,13 +235,15 @@
             mean[t, 1 : both + 1, half * rows : (half + 1) * rows, :] = value
 
     def around(f):
-        return jnp.concatenate([raw[0, f, :, rows - reach :, :], raw[1, f, :, :reach, :]], axis=1)
+        above = jnp.where(odd == 0, raw[f, :, rows - reach :, :], a_raw[f, :, rows - reach :, :])
+        below = jnp.where(odd == 1, raw[f, :, :reach, :], a_raw[f, :, :reach, :])
+        return jnp.concatenate([above, below], axis=1)
 
     temperature = around(3)
     for i in range(3):
         value = (around(i) * temperature).reshape(cells, width)
         prod_h[:, column(i)], prod_l[:, column(i)] = halves(value)
-    flux = along_span_of(products[...] + planes_of(weights, slice(3, 4), prod_h[...], prod_l[...]))
+    flux = along_span_of(products[...] + planes_of(weights, 3, prod_h[...], prod_l[...]))
 
     for half in range(2):
         span = slice(half * rows, (half + 1) * rows)
@@ -229,7 +252,7 @@
         tiles += [tiles[i] * tiles[3] for i in range(3)]
         for t, value in enumerate(tiles):
             mid_h[down, column(t)], mid_l[down, column(t)] = halves(value)
-    second = along_span_of(planes_of(weights, slice(0, 2), mid_h[...], mid_l[...]))
+    second = along_span_of(planes_of(weights, None, mid_h[...], mid_l[...]))
 
     mid_rows = slice(reach, reach + rows)
     centre, along_span, along_wall, along_stream = [], [], [], []
@@ -300,7 +323,7 @@
 
 
 def call(kernel, name, ins, outs, scratch=(), mib=4, hint=None):
-    cost = hint and pl.CostEstimate(flops=hint, bytes_accessed=hint // 100, transcendentals=0)
+    cost = hint and pl.CostEstimate(flops=hint, bytes_accessed=0, transcendentals=0)
     return pl.pallas_call(
         kernel,
         out_shape=tuple(jax.ShapeDtypeStruct(shape, jnp.float32) for shape in outs),
@@ -347,37 +370,43 @@
     part = swap(to_partner)
     part_strip = lax.ppermute(first, ("span", "stream"), to_other)
     own_strip = lax.ppermute(second, ("span", "stream"), to_same)
-    (main,) = call(main_kernel, "main", (fields, part), ((2, both, rows, width),))
+    (main,) = call(main_kernel, "main", (fields, part), ((2 * both + layers, rows, width),))
     b_main, a_main = pair_b(main), pair_a(main)
-    (strips,) = call(rim_kernel, "strips", (fields, part, own_strip, part_strip), ((both, rows, width),), hint=2**35)
-    b_strips, a_strips = pair_b(strips), pair_a(strips)
+    (outer,) = call(outer_kernel, "outer", (own_strip, part_strip), ((layers, rows, width),), hint=2**35)
+    b_outer, a_outer = pair_b(outer), pair_a(outer)
 
     matrices = np.zeros((2 * cells + 2 * width, 4 * cells), ml_dtypes.bfloat16)
     matrices[:cells], matrices[cells : 2 * cells] = plane_constants(both, rows)
     matrices[2 * cells :, : 2 * width] = span_constants(width)
     weights = jnp.asarray(matrices)
     single, brief = jnp.float32, jnp.bfloat16
-    partial = call(
+    block = (4, both, rows, width)
+    pieces = [((cells, 4 * width), brief), ((cells, 4 * width), brief)]
+    upper, lower, products = call(
         centre_kernel,
         "centre",
-        (main, strips, weights),
-        ((4, both, rows, width), (cells, 4 * width), (cells, 4 * width), (cells, 3 * width)),
-        [
-            ((cells, 4 * width), brief),
-            ((cells, 4 * width), brief),
-            ((cells, 3 * width), brief),
-            ((cells, 3 * width), brief),
-        ],
+        (main, outer, weights),
+        ((cells, 4 * width), (cells, 4 * width), (cells, 3 * width)),
+        [(block, single), *pieces, ((cells, 3 * width), brief), ((cells, 3 * width), brief)],
         mib=16,
-        hint=2**31,
+        hint=2**29,
+    )
+    a_raw, a_partial = call(
+        mate_kernel,
+        "mate",
+        (a_main, a_outer, upper, lower, weights),
+        (block, (cells, 4 * width)),
+        pieces,
+        mib=16,
+        hint=2**29,
     )
     keep, send, sums = call(
         functools.partial(flux_kernel, walls),
         "flux",
-        (a_main, b_main, a_strips, b_strips, *partial, weights),
+        (b_main, b_outer, a_raw, a_partial, upper, lower, products, weights),
         ((6, layers, rows, width), (3, layers, rows, width), (rows, width)),
         [
-            ((2, 4, both, rows, width), single),
+            (block, single),
             ((cells, 4 * width), brief),
             ((cells, 4 * width), brief),
             ((cells, 3 * width), brief),
@@ -398,11 +427,13 @@
 
     step = 1
     while step < spans:
+        near = from_span(sums, step)
         if 2 * step < spans:
-            far = from_span(sums, 3 * step) + from_span(sums, 2 * step)
-            sums = (sums + from_span(sums, step)) + far
+            far = [from_span(sums, 2 * step), from_span(sums, 3 * step)]
+            near, far, come = lax.optimization_barrier((near, far, come))
+            sums = (sums + near) + (far[0] + far[1])
         else:
-            sums = sums + from_span(sums, step)
+            sums = sums + near
         step *= 4
     sums = sums + swap(sums)
     block, corr = (3, layers, rows, width), (3, rows)

time: 34.5 us -> 35.4 us (1.026)
  the two profiles are of different devices: /device:TPU:6 before, /device:TPU:4 now
where the time goes in v11:
time: 35.4 us; the launch traced here: 35.3 us
  starting transfers between devices  17.5 us (49%)
  waiting for transfers between devices  9.75 us (28%)
  Pallas kernels  6.28 us (18%)
  local copies, waits for them, and re-layouts  0.95 us (3%)
  between operations  0.75 us (2%)
    pallas_call x7, Pallas kernels, call(): pl.pallas_call(kernel, out_shape=tuple((jax.ShapeDtypeStruct(shape, jnp.f...  6.28 us
    ppermute x2, starting transfers between devices, pair_b(): lax.ppermute(value, 'wall', [(w, min(max((w + 1 ^ 1) - 1, 0), walls - 1))...  4.76 us
    ppermute x3, starting transfers between devices, from_span(): return lax.ppermute(value, 'span', [(p, p ^ step) for p in range(spans)])  4.52 us
    ppermute x3, starting transfers between devices, swap(): return lax.ppermute(value, 'stream', [(0, 1), (1, 0)])  4.06 us
    ppermute x3, waiting for transfers between devices, from_span(): return lax.ppermute(value, 'span', [(p, p ^ step) for p in range(spans)])  3.98 us
    ppermute x3, waiting for transfers between devices, swap(): return lax.ppermute(value, 'stream', [(0, 1), (1, 0)])  3.21 us
    ppermute x1, starting transfers between devices, shards(): part_strip = lax.ppermute(first, ('span', 'stream'), to_other)  2.45 us
    ppermute x1, starting transfers between devices, shards(): own_strip = lax.ppermute(second, ('span', 'stream'), to_same)  1.58 us
  transfers between devices with their start and end apart: 12, of which 6 were waited for; matrix products, arithmetic and copies ran while one was open for 0% of the time, Pallas kernels for 5%

profile of v11, /device:TPU:4, one launch (start us, length us, event | category | flops | bytes accessed | tf_op | source)
XLA Modules:
  0.0 35.3 jit_solution(18263775596486683100)
XLA Ops:
  0.6 0.9 %copy-done.1 = f32[4,8,16,128]{3,2,1,0:T(8,128)S(1)} copy-done((f32[4,8,16,128]{3,2,1,0:T(8,128)S(1)}, f32[4,8,16,128]{3,2,1,0:T(8,128)}, u32[]{:S(2)}) %copy-start.1) | copy-done | bytes 262168
  1.6 0.3 pack.1
  1.9 1.6 %collective-permute-start = (f32[20,16,128]{2,1,0:T(8,128)S(1)}, f32[20,16,128]{2,1,0:T(8,128)S(1)}, u32[]{:S(2)}, u32[]{:S(2)}) collective-permute-start(f32[20,16,128]{2,1,0:T(8,128)S(1)} %get-tuple-element.19), channel_id=1, source_target_pairs={{0,1},{1,0},{2,3},{3,2},{4,5},{5,4},{6,7},{7,6},{8,9},{9,8},{10,11... | collective-permute-start | bytes 491528 | tf_op jit(solution)/shard_map/ppermute | solution.py:348
  3.4 1.6 %collective-permute-start.2 = (f32[4,16,128]{2,1,0:T(8,128)S(1)}, f32[4,16,128]{2,1,0:T(8,128)S(1)}, u32[]{:S(2)}, u32[]{:S(2)}) collective-permute-start(f32[4,16,128]{2,1,0:T(8,128)S(1)} %get-tuple-element.20), channel_id=1, source_target_pairs={{1,25},{0,8},{9,1},{8,16},{17,9},{16,24},{25,17},{24,0},{3,27},{2,... | collective-permute-start | bytes 98312 | tf_op jit(solution)/shard_map/ppermute | solution.py:372
  5.0 2.4 %collective-permute-start.3 = (f32[4,16,128]{2,1,0:T(8,128)S(1)}, f32[4,16,128]{2,1,0:T(8,128)S(1)}, u32[]{:S(2)}, u32[]{:S(2)}) collective-permute-start(f32[4,16,128]{2,1,0:T(8,128)S(1)} %get-tuple-element.21), channel_id=1, source_target_pairs={{0,25},{1,8},{8,1},{9,16},{16,9},{17,24},{24,17},{25,0},{2,27},{3,... | collective-permute-start | bytes 98312 | tf_op jit(solution)/shard_map/ppermute | solution.py:371
  7.4 0.4 %collective-permute-done.part = f32[20,16,128]{2,1,0:T(8,128)S(1)} collective-permute-done((f32[20,16,128]{2,1,0:T(8,128)S(1)}, f32[20,16,128]{2,1,0:T(8,128)S(1)}, u32[]{:S(2)}, u32[]{:S(2)}) %collective-permute-start) | collective-permute-done | bytes 163872 | tf_op jit(solution)/shard_map/ppermute | solution.py:348
  7.9 0.2 main.1
  8.0 0.1 collective-permute-start.5
  8.1 2.3 %collective-permute-start.1 = (f32[40,16,128]{2,1,0:T(8,128)S(1)}, f32[40,16,128]{2,1,0:T(8,128)S(1)}, u32[]{:S(2)}, u32[]{:S(2)}) collective-permute-start(f32[40,16,128]{2,1,0:T(8,128)S(1)} %main.1), channel_id=1, source_target_pairs={{0,0},{2,4},{4,2},{6,6},{1,1},{3,5},{5,3},{7,7},{8,8},{10,12},{12,... | collective-permute-start | bytes 983048 | tf_op jit(solution)/shard_map/ppermute | solution.py:354
  10.4 1.2 %collective-permute-done.3.part_strip = f32[4,16,128]{2,1,0:T(8,128)S(1)} collective-permute-done((f32[4,16,128]{2,1,0:T(8,128)S(1)}, f32[4,16,128]{2,1,0:T(8,128)S(1)}, u32[]{:S(2)}, u32[]{:S(2)}) %collective-permute-start.3) | collective-permute-done | bytes 32800 | tf_op jit(solution)/shard_map/ppermute | solution.py:371
  11.6 0.1 collective-permute-start.6
  11.7 2.5 %collective-permute-start.4 = (f32[8,16,128]{2,1,0:T(8,128)S(1)}, f32[8,16,128]{2,1,0:T(8,128)S(1)}, u32[]{:S(2)}, u32[]{:S(2)}) collective-permute-start(f32[8,16,128]{2,1,0:T(8,128)S(1)} %outer.1), channel_id=1, source_target_pairs={{0,0},{2,4},{4,2},{6,6},{1,1},{3,5},{5,3},{7,7},{8,8},{10,12},{12,... | collective-permute-start | bytes 196616 | tf_op jit(solution)/shard_map/ppermute | solution.py:354
  14.2 1.1 %centre.1 = (f32[256,512]{1,0:T(8,128)S(1)}, f32[256,512]{1,0:T(8,128)S(1)}, f32[256,384]{1,0:T(8,128)S(1)}) custom-call(f32[40,16,128]{2,1,0:T(8,128)S(1)} %main.1, f32[8,16,128]{2,1,0:T(8,128)S(1)} %outer.1, bf16[768,1024]{1,0:T(8,128)(2,1)S(1)} %copy-done), custom_call_target="tpu_custom_call" | custom-call | flops 536870912 | tf_op jit(solution)/shard_map/centre/pallas_call | solution.py:327
  15.3 0.7 %mate.1 = (f32[4,16,16,128]{3,2,1,0:T(8,128)S(1)}, f32[256,512]{1,0:T(8,128)S(1)}) custom-call(f32[40,16,128]{2,1,0:T(8,128)S(1)} %collective-permute-done.5.main, f32[8,16,128]{2,1,0:T(8,128)S(1)} %collective-permute-done.6.outer, f32[256,512]{1,0:T(8,128)S(1)} %get-tuple-element.22.upper, f32[256,512]{1,0:T(8,128)S(1)} %get-tuple-element.23.lower, ...), custom_call_target="tpu_custom_call" | custom-call | flops 536870912 | tf_op jit(solution)/shard_map/mate/pallas_call | solution.py:327
  16.0 1.3 %collective-permute-done.4.b_outer = f32[8,16,128]{2,1,0:T(8,128)S(1)} collective-permute-done((f32[8,16,128]{2,1,0:T(8,128)S(1)}, f32[8,16,128]{2,1,0:T(8,128)S(1)}, u32[]{:S(2)}, u32[]{:S(2)}) %collective-permute-start.4) | collective-permute-done | bytes 65568 | tf_op jit(solution)/shard_map/ppermute | solution.py:354
  17.4 3.1 %flux.1 = (f32[6,8,16,128]{3,2,1,0:T(8,128)S(1)}, f32[3,8,16,128]{3,2,1,0:T(8,128)S(1)}, f32[16,128]{1,0:T(8,128)S(1)}) custom-call(f32[40,16,128]{2,1,0:T(8,128)S(1)} %collective-permute-done.1.b_main, f32[8,16,128]{2,1,0:T(8,128)S(1)} %collective-permute-done.4.b_outer, f32[4,16,16,128]{3,2,1,0:T(8,128)S(1)} %get-tuple-element.24.a_raw, ...), custom_call_target="tpu_custom_call" | custom-call | tf_op jit(solution)/shard_map/flux/pallas_call | solution.py:327
  20.4 1.6 %collective-permute-start.10 = (f32[3,8,16,128]{3,2,1,0:T(8,128)S(1)}, f32[3,8,16,128]{3,2,1,0:T(8,128)S(1)}, u32[]{:S(2)}, u32[]{:S(2)}) collective-permute-start(f32[3,8,16,128]{3,2,1,0:T(8,128)S(1)} %get-tuple-element.28), channel_id=1, source_target_pairs={{0,1},{1,0},{2,3},{3,2},{4,5},{5,4},{6,7},{7,6},{8,9},{9,8},{10,11... | collective-permute-start | bytes 589832 | tf_op jit(solution)/shard_map/ppermute | solution.py:348
  22.0 4.0 %collective-permute-start.9 = (f32[16,128]{1,0:T(8,128)S(1)}, f32[16,128]{1,0:T(8,128)S(1)}, u32[]{:S(2)}, u32[]{:S(2)}) collective-permute-start(f32[16,128]{1,0:T(8,128)S(1)} %get-tuple-element.27), channel_id=1, source_target_pairs={{0,24},{8,16},{16,8},{24,0},{1,25},{9,17},{17,9},{25,1},{2,26},{10... | collective-permute-start | bytes 24584 | tf_op jit(solution)/shard_map/ppermute | solution.py:426
  26.0 0.6 %collective-permute-start.7 = (f32[16,128]{1,0:T(8,128)S(1)}, f32[16,128]{1,0:T(8,128)S(1)}, u32[]{:S(2)}, u32[]{:S(2)}) collective-permute-start(f32[16,128]{1,0:T(8,128)S(1)} %get-tuple-element.27), channel_id=1, source_target_pairs={{0,8},{8,0},{16,24},{24,16},{1,9},{9,1},{17,25},{25,17},{2,10},{10... | collective-permute-start | bytes 24584 | tf_op jit(solution)/shard_map/ppermute | solution.py:426
  26.5 1.1 %collective-permute-done.9 = f32[16,128]{1,0:T(8,128)S(1)} collective-permute-done((f32[16,128]{1,0:T(8,128)S(1)}, f32[16,128]{1,0:T(8,128)S(1)}, u32[]{:S(2)}, u32[]{:S(2)}) %collective-permute-start.9) | collective-permute-done | bytes 8224 | tf_op jit(solution)/shard_map/ppermute | solution.py:426
  27.6 2.9 %collective-permute-done.8 = f32[16,128]{1,0:T(8,128)S(1)} collective-permute-done((f32[16,128]{1,0:T(8,128)S(1)}, f32[16,128]{1,0:T(8,128)S(1)}, u32[]{:S(2)}, u32[]{:S(2)}) %collective-permute-start.8) | collective-permute-done | bytes 8224 | tf_op jit(solution)/shard_map/ppermute | solution.py:426
  30.5 0.9 %collective-permute-start.11 = (f32[16,128]{1,0:T(8,128)S(1)}, f32[16,128]{1,0:T(8,128)S(1)}, u32[]{:S(2)}, u32[]{:S(2)}) collective-permute-start(f32[16,128]{1,0:T(8,128)S(1)} %add_add_fusion), channel_id=1, source_target_pairs={{0,1},{1,0},{2,3},{3,2},{4,5},{5,4},{6,7},{7,6},{8,9},{9,8},{10,11... | collective-permute-start | bytes 24584 | tf_op jit(solution)/shard_map/ppermute | solution.py:348
  31.5 2.8 %collective-permute-done.11 = f32[16,128]{1,0:T(8,128)S(1)} collective-permute-done((f32[16,128]{1,0:T(8,128)S(1)}, f32[16,128]{1,0:T(8,128)S(1)}, u32[]{:S(2)}, u32[]{:S(2)}) %collective-permute-start.11) | collective-permute-done | bytes 8224 | tf_op jit(solution)/shard_map/ppermute | solution.py:348
  34.2 1.0 %finish.1 = (f32[3,8,16,128]{3,2,1,0:T(8,128)}, f32[3,8,16,128]{3,2,1,0:T(8,128)}, f32[3,16]{1,0:T(4,128)}, f32[3,16]{1,0:T(4,128)}) custom-call(f32[16,128]{1,0:T(8,128)S(1)} %add.15.sums, f32[6,8,16,128]{3,2,1,0:T(8,128)S(1)} %get-tuple-element.32.keep, f32[3,8,16,128]{3,2,1,0:T(8,128)S(1)} %collective-permute-done.10.come), custom_call_target="tpu_custom_call" | custom-call | tf_op jit(solution)/shard_map/finish/pallas_call | solution.py:327
  (13 shorter events, 0.0 us)
Async XLA Ops:
  0.6 1.0 %copy-start.1 = (f32[4,8,16,128]{3,2,1,0:T(8,128)S(1)}, f32[4,8,16,128]{3,2,1,0:T(8,128)}, u32[]{:S(2)}) copy-start(f32[4,8,16,128]{3,2,1,0:T(8,128)} %own.3) | copy-start | bytes 786436
  1.9 6.0 %collective-permute-start = (f32[20,16,128]{2,1,0:T(8,128)S(1)}, f32[20,16,128]{2,1,0:T(8,128)S(1)}, u32[]{:S(2)}, u32[]{:S(2)}) collective-permute-start(f32[20,16,128]{2,1,0:T(8,128)S(1)} %get-tuple-element.19), channel_id=1, source_target_pairs={{0,1},{1,0},{2,3},{3,2},{4,5},{5,4},{6,7},{7,6},{8,9},{9,8},{10,11... | collective-permute-start | bytes 491528 | tf_op jit(solution)/shard_map/ppermute | solution.py:348
  3.4 7.0 %collective-permute-start.2 = (f32[4,16,128]{2,1,0:T(8,128)S(1)}, f32[4,16,128]{2,1,0:T(8,128)S(1)}, u32[]{:S(2)}, u32[]{:S(2)}) collective-permute-start(f32[4,16,128]{2,1,0:T(8,128)S(1)} %get-tuple-element.20), channel_id=1, source_target_pairs={{1,25},{0,8},{9,1},{8,16},{17,9},{16,24},{25,17},{24,0},{3,27},{2,... | collective-permute-start | bytes 98312 | tf_op jit(solution)/shard_map/ppermute | solution.py:372
  5.0 6.6 %collective-permute-start.3 = (f32[4,16,128]{2,1,0:T(8,128)S(1)}, f32[4,16,128]{2,1,0:T(8,128)S(1)}, u32[]{:S(2)}, u32[]{:S(2)}) collective-permute-start(f32[4,16,128]{2,1,0:T(8,128)S(1)} %get-tuple-element.21), channel_id=1, source_target_pairs={{0,25},{1,8},{8,1},{9,16},{16,9},{17,24},{24,17},{25,0},{2,27},{3,... | collective-permute-start | bytes 98312 | tf_op jit(solution)/shard_map/ppermute | solution.py:371
  8.0 6.2 %copy-start = (bf16[768,1024]{1,0:T(8,128)(2,1)S(1)}, bf16[768,1024]{1,0:T(8,128)(2,1)}, u32[]{:S(2)}) copy-start(bf16[768,1024]{1,0:T(8,128)(2,1)} %constant.2.clone.weights) | copy-start | bytes 4718596
  8.0 7.3 %collective-permute-start.5 = (f32[40,16,128]{2,1,0:T(8,128)S(1)}, f32[40,16,128]{2,1,0:T(8,128)S(1)}, u32[]{:S(2)}, u32[]{:S(2)}) collective-permute-start(f32[40,16,128]{2,1,0:T(8,128)S(1)} %main.1), channel_id=1, source_target_pairs={{0,2},{2,0},{4,6},{6,4},{1,3},{3,1},{5,7},{7,5},{8,10},{10,8},{12,... | collective-permute-start | bytes 983048 | tf_op jit(solution)/shard_map/ppermute | solution.py:351
  8.1 9.2 %collective-permute-start.1 = (f32[40,16,128]{2,1,0:T(8,128)S(1)}, f32[40,16,128]{2,1,0:T(8,128)S(1)}, u32[]{:S(2)}, u32[]{:S(2)}) collective-permute-start(f32[40,16,128]{2,1,0:T(8,128)S(1)} %main.1), channel_id=1, source_target_pairs={{0,0},{2,4},{4,2},{6,6},{1,1},{3,5},{5,3},{7,7},{8,8},{10,12},{12,... | collective-permute-start | bytes 983048 | tf_op jit(solution)/shard_map/ppermute | solution.py:354
  11.6 3.7 %collective-permute-start.6 = (f32[8,16,128]{2,1,0:T(8,128)S(1)}, f32[8,16,128]{2,1,0:T(8,128)S(1)}, u32[]{:S(2)}, u32[]{:S(2)}) collective-permute-start(f32[8,16,128]{2,1,0:T(8,128)S(1)} %outer.1), channel_id=1, source_target_pairs={{0,2},{2,0},{4,6},{6,4},{1,3},{3,1},{5,7},{7,5},{8,10},{10,8},{12,... | collective-permute-start | bytes 196616 | tf_op jit(solution)/shard_map/ppermute | solution.py:351
  11.7 5.7 %collective-permute-start.4 = (f32[8,16,128]{2,1,0:T(8,128)S(1)}, f32[8,16,128]{2,1,0:T(8,128)S(1)}, u32[]{:S(2)}, u32[]{:S(2)}) collective-permute-start(f32[8,16,128]{2,1,0:T(8,128)S(1)} %outer.1), channel_id=1, source_target_pairs={{0,0},{2,4},{4,2},{6,6},{1,1},{3,5},{5,3},{7,7},{8,8},{10,12},{12,... | collective-permute-start | bytes 196616 | tf_op jit(solution)/shard_map/ppermute | solution.py:354
  20.4 10.1 %collective-permute-start.10 = (f32[3,8,16,128]{3,2,1,0:T(8,128)S(1)}, f32[3,8,16,128]{3,2,1,0:T(8,128)S(1)}, u32[]{:S(2)}, u32[]{:S(2)}) collective-permute-start(f32[3,8,16,128]{3,2,1,0:T(8,128)S(1)} %get-tuple-element.28), channel_id=1, source_target_pairs={{0,1},{1,0},{2,3},{3,2},{4,5},{5,4},{6,7},{7,6},{8,9},{9,8},{10,11... | collective-permute-start | bytes 589832 | tf_op jit(solution)/shard_map/ppermute | solution.py:348
  22.0 5.6 %collective-permute-start.9 = (f32[16,128]{1,0:T(8,128)S(1)}, f32[16,128]{1,0:T(8,128)S(1)}, u32[]{:S(2)}, u32[]{:S(2)}) collective-permute-start(f32[16,128]{1,0:T(8,128)S(1)} %get-tuple-element.27), channel_id=1, source_target_pairs={{0,24},{8,16},{16,8},{24,0},{1,25},{9,17},{17,9},{25,1},{2,26},{10... | collective-permute-start | bytes 24584 | tf_op jit(solution)/shard_map/ppermute | solution.py:426
  26.0 4.5 %collective-permute-start.8 = (f32[16,128]{1,0:T(8,128)S(1)}, f32[16,128]{1,0:T(8,128)S(1)}, u32[]{:S(2)}, u32[]{:S(2)}) collective-permute-start(f32[16,128]{1,0:T(8,128)S(1)} %get-tuple-element.27), channel_id=1, source_target_pairs={{0,16},{8,24},{16,0},{24,8},{1,17},{9,25},{17,1},{25,9},{2,18},{10... | collective-permute-start | bytes 24584 | tf_op jit(solution)/shard_map/ppermute | solution.py:426
  26.0 4.5 %collective-permute-start.7 = (f32[16,128]{1,0:T(8,128)S(1)}, f32[16,128]{1,0:T(8,128)S(1)}, u32[]{:S(2)}, u32[]{:S(2)}) collective-permute-start(f32[16,128]{1,0:T(8,128)S(1)} %get-tuple-element.27), channel_id=1, source_target_pairs={{0,8},{8,0},{16,24},{24,16},{1,9},{9,1},{17,25},{25,17},{2,10},{10... | collective-permute-start | bytes 24584 | tf_op jit(solution)/shard_map/ppermute | solution.py:426
  30.5 3.7 %collective-permute-start.11 = (f32[16,128]{1,0:T(8,128)S(1)}, f32[16,128]{1,0:T(8,128)S(1)}, u32[]{:S(2)}, u32[]{:S(2)}) collective-permute-start(f32[16,128]{1,0:T(8,128)S(1)} %add_add_fusion), channel_id=1, source_target_pairs={{0,1},{1,0},{2,3},{3,2},{4,5},{5,4},{6,7},{7,6},{8,9},{9,8},{10,11... | collective-permute-start | bytes 24584 | tf_op jit(solution)/shard_map/ppermute | solution.py:348

commit v12 on v11

--- a/solution.py
+++ b/solution.py
@@ -102,53 +102,39 @@
         yield k, jnp.where(is_outer, pieces[1], pieces[0])
 
 
-def pack_kernel(own, to_partner, to_other, to_same):
+def pack_kernel(own, to_partner, to_mine, to_other, to_same):
     _, layers, _, _ = own.shape
     me_s = lax.axis_index("stream")
-    for pair, tile in pack_halves(own, 1 - me_s):
-        to_partner[pair * layers : (pair + 1) * layers] = tile
-    to_partner[2 * layers :] = pack_strip(own, 3 + me_s)
+    for message, half in ((to_partner, 1 - me_s), (to_mine, me_s)):
+        for pair, tile in pack_halves(own, half):
+            message[pair * layers : (pair + 1) * layers] = tile
+        message[2 * layers :] = pack_strip(own, 4 - half)
     to_other[...] = pack_strip(own, 7 * me_s)
     to_same[...] = pack_strip(own, 7 * (1 - me_s))
 
 
-def main_kernel(own, part, packed):
-    _, layers, _, _ = own.shape
-    both = 2 * layers
-    half = layers // 2
-    me_s = lax.axis_index("stream")
-    mine, other = me_s * layers, (1 - me_s) * layers
-    for pair, tile in pack_halves(own, me_s):
-        packed[pl.ds(pair * both + mine, layers)] = tile
-        packed[pl.ds(pair * both + other, layers)] = part[pair * layers : (pair + 1) * layers]
-    packed[pl.ds(2 * both + me_s * half, half)] = pack_strip(own, 4 - me_s)
-    packed[pl.ds(2 * both + (1 - me_s) * half, half)] = part[2 * layers :]
-
-
 def outer_kernel(own_strip, part_strip, outer):
     half = own_strip.shape[0]
-    me_s = lax.axis_index("stream")
-    outer[pl.ds(me_s * half, half)] = own_strip[...]
-    outer[pl.ds((1 - me_s) * half, half)] = part_strip[...]
-
-
-def unpack(packed, outer, me_s):
+    outer[:half] = own_strip[...]
+    outer[half:] = part_strip[...]
+
+
+def unpack(mine, part, outer, me_s):
     layers, rows, width = outer.shape
-    both = 2 * layers
     half = layers // 2
     unit = unit_index((half, rows, width))
     first = 4 * (1 - me_s)
     in_strip = (unit == first) | (unit == first + 3)
-    for s in range(2):
-        inner = packed[2 * both + s * half : 2 * both + (s + 1) * half]
-        for k, strip in strip_tile(inner, outer[s * half : (s + 1) * half], me_s):
-            layer = s * layers + k * half
+    for which, packed in enumerate((mine, part)):
+        far = outer[which * half : (which + 1) * half]
+        for k, strip in strip_tile(packed[2 * layers :], far, me_s):
+            layer = (me_s if which == 0 else 1 - me_s) * layers + k * half
             for f in range(4):
-                start = f // 2 * both + layer
+                start = f // 2 * layers + k * half
                 cells = packed[start : start + half]
                 cells = pltpu.roll(cells, width // 2, 2) if f % 2 else cells
                 moved = pltpu.roll(strip, width - 2 * f * rim, 2) if f else strip
-                yield f, slice(layer, layer + half), jnp.where(in_strip, moved, cells)
+                yield f, layer, jnp.where(in_strip, moved, cells)
 
 
 def column(t, width=128):
@@ -165,18 +151,21 @@
     return dot(plane_h, high) + dot(plane_l, high) + dot(plane_h, low)
 
 
-def bring(packed, outer, raw, high, low, keep=None):
-    rows, width = packed.shape[1:]
-    for f, along, value in unpack(packed, outer, lax.axis_index("stream")):
+def bring(mine, part, outer, raw, high, low, keep=None):
+    rows, width = outer.shape[1:]
+    for f, layer, value in unpack(mine, part, outer, lax.axis_index("stream")):
+        count = value.shape[0]
         value = value if keep is None else value * keep
-        raw[f, along] = value
-        down = slice(along.start * rows, along.stop * rows)
+        raw[f, pl.ds(layer, count)] = value
+        down = pl.ds(pl.multiple_of(layer * rows, count * rows), count * rows)
         high[down, column(f)], low[down, column(f)] = halves(value.reshape(-1, width))
 
 
-def centre_kernel(main, outer, weights, upper, lower, products, centre, in_h, in_l, prod_h, prod_l):
-    cells, width = in_h.shape[0], main.shape[-1]
-    bring(main, outer, centre, in_h, in_l)
+def centre_kernel(
+    mine, part, outer, weights, upper, lower, products, centre, in_h, in_l, prod_h, prod_l
+):
+    cells, width = in_h.shape[0], outer.shape[-1]
+    bring(mine, part, outer, centre, in_h, in_l)
     for i in range(3):
         value = (centre[i] * centre[3]).reshape(cells, width)
         prod_h[:, column(i)], prod_l[:, column(i)] = halves(value)
@@ -185,15 +174,15 @@
     products[...] = planes_of(weights, 2, prod_h[...], prod_l[...])
 
 
-def mate_kernel(main, outer, upper, lower, weights, raw, partial, in_h, in_l):
+def mate_kernel(mine, part, outer, upper, lower, weights, raw, partial, in_h, in_l):
     odd = lax.rem(lax.axis_index("wall"), 2)
-    bring(main, outer, raw, in_h, in_l)
+    bring(mine, part, outer, raw, in_h, in_l)
     base = jnp.where(odd == 1, upper[...], lower[...])
     partial[...] = base + planes_of(weights, 1 - odd, in_h[...], in_l[...])
 
 
 def flux_kernel(
-    walls, b_main, b_outer, a_raw, a_partial, upper, lower, products, weights,
+    walls, b_mine, b_part, b_outer, a_raw, a_partial, upper, lower, products, weights,
     keep_ref, send_ref, sums_ref,
     raw, in_h, in_l, prod_h, prod_l, mean, mid_h, mid_l, clark_all, similar_all,
 ):
@@ -207,7 +196,7 @@
     at_end = (me_w == 0) | (me_w == walls - 1)
     keep_b = jnp.where(at_end, 0.0, 1.0).astype(jnp.float32)
 
-    bring(b_main, b_outer, raw, in_h, in_l, keep_b)
+    bring(b_mine, b_part, b_outer, raw, in_h, in_l, keep_b)
 
     def along_span_of(planes):
         high, low = halves(planes)
@@ -363,15 +352,15 @@
         to_other += [(place(p, 0), place(p - 1, 1)), (place(p, 1), place(p + 1, 0))]
         to_same += [(place(p, 1), place(p - 1, 1)), (place(p, 0), place(p + 1, 0))]
 
-    strip = (layers // 2, rows, width)
-    to_partner, first, second = call(
-        pack_kernel, "pack", (fields,), ((2 * layers + layers // 2, rows, width), strip, strip)
+    message, strip = (2 * layers + layers // 2, rows, width), (layers // 2, rows, width)
+    to_partner, mine, first, second = call(
+        pack_kernel, "pack", (fields,), (message, message, strip, strip)
     )
     part = swap(to_partner)
     part_strip = lax.ppermute(first, ("span", "stream"), to_other)
     own_strip = lax.ppermute(second, ("span", "stream"), to_same)
-    (main,) = call(main_kernel, "main", (fields, part), ((2 * both + layers, rows, width),))
-    b_main, a_main = pair_b(main), pair_a(main)
+    part, b_mine, a_mine = lax.optimization_barrier((part, pair_b(mine), pair_a(mine)))
+    b_part, a_part = pair_b(part), pair_a(part)
     (outer,) = call(outer_kernel, "outer", (own_strip, part_strip), ((layers, rows, width),), hint=2**35)
     b_outer, a_outer = pair_b(outer), pair_a(outer)
 
@@ -385,7 +374,7 @@
     upper, lower, products = call(
         centre_kernel,
         "centre",
-        (main, outer, weights),
+        (mine, part, outer, weights),
         ((cells, 4 * width), (cells, 4 * width), (cells, 3 * width)),
         [(block, single), *pieces, ((cells, 3 * width), brief), ((cells, 3 * width), brief)],
         mib=16,
@@ -394,7 +383,7 @@
     a_raw, a_partial = call(
         mate_kernel,
         "mate",
-        (a_main, a_outer, upper, lower, weights),
+        (a_mine, a_part, a_outer, upper, lower, weights),
         (block, (cells, 4 * width)),
         pieces,
         mib=16,
@@ -403,7 +392,7 @@
     keep, send, sums = call(
         functools.partial(flux_kernel, walls),
         "flux",
-        (b_main, b_outer, a_raw, a_partial, upper, lower, products, weights),
+        (b_mine, b_part, b_outer, a_raw, a_partial, upper, lower, products, weights),
         ((6, layers, rows, width), (3, layers, rows, width), (rows, width)),
         [
             (block, single),
@@ -427,13 +416,11 @@
 
     step = 1
     while step < spans:
-        near = from_span(sums, step)
         if 2 * step < spans:
-            far = [from_span(sums, 2 * step), from_span(sums, 3 * step)]
-            near, far, come = lax.optimization_barrier((near, far, come))
-            sums = (sums + near) + (far[0] + far[1])
+            far = from_span(sums, 3 * step) + from_span(sums, 2 * step)
+            sums = (sums + from_span(sums, step)) + far
         else:
-            sums = sums + near
+            sums = sums + from_span(sums, step)
         step *= 4
     sums = sums + swap(sums)
     block, corr = (3, layers, rows, width), (3, rows)

time: 35.4 us -> 34.6 us (0.977)
  waiting for transfers between devices: 9.75 us -> 9.01 us
    ppermute x2 -> x3, starting transfers between devices: 4.76 us -> 6.91 us  [pair_b(): lax.ppermute(value, 'wall', [(w, min(max((w + 1 ^ 1) - 1, 0), walls - 1))...]
    ppermute x3, waiting for transfers between devices: 3.98 us -> 2.33 us  [from_span(): return lax.ppermute(value, 'span', [(p, p ^ step) for p in range(spans)])]
    ppermute x3, starting transfers between devices: 4.06 us -> 2.9 us  [swap(): return lax.ppermute(value, 'stream', [(0, 1), (1, 0)])]
    ppermute x3, starting transfers between devices: 4.52 us -> 3.55 us  [from_span(): return lax.ppermute(value, 'span', [(p, p ^ step) for p in range(spans)])]
    ppermute x2 -> x3, waiting for transfers between devices: 1.34 us -> 1.92 us  [pair_b(): lax.ppermute(value, 'wall', [(w, min(max((w + 1 ^ 1) - 1, 0), walls - 1))...]
    ppermute x1, waiting for transfers between devices: 1.21 us -> 1.58 us  [shards(): part_strip = lax.ppermute(first, ('span', 'stream'), to_other)]
    pallas_call x7 -> x6, Pallas kernels: 6.28 us -> 6.19 us  [call(): pl.pallas_call(kernel, out_shape=tuple((jax.ShapeDtypeStruct(shape, jnp.f...]
  transfers between devices with their start and end apart: 12 -> 14, of which waited for: 6 -> 5; matrix products, arithmetic and copies ran while one was open for 0% -> 0% of each run, Pallas kernels for 5% -> 5%
where the time goes in v12:
time: 34.6 us; the launch traced here: 34.4 us
  starting transfers between devices  17.5 us (51%)
  waiting for transfers between devices  9.01 us (26%)
  Pallas kernels  6.19 us (18%)
  local copies, waits for them, and re-layouts  0.95 us (3%)
  between operations  0.74 us (2%)
    ppermute x3, starting transfers between devices, pair_b(): lax.ppermute(value, 'wall', [(w, min(max((w + 1 ^ 1) - 1, 0), walls - 1))...  6.91 us
    pallas_call x6, Pallas kernels, call(): pl.pallas_call(kernel, out_shape=tuple((jax.ShapeDtypeStruct(shape, jnp.f...  6.19 us
    ppermute x3, starting transfers between devices, from_span(): return lax.ppermute(value, 'span', [(p, p ^ step) for p in range(spans)])  3.55 us
    ppermute x3, waiting for transfers between devices, swap(): return lax.ppermute(value, 'stream', [(0, 1), (1, 0)])  3.18 us
    ppermute x3, starting transfers between devices, swap(): return lax.ppermute(value, 'stream', [(0, 1), (1, 0)])  2.9 us
    ppermute x1, starting transfers between devices, shards(): part_strip = lax.ppermute(first, ('span', 'stream'), to_other)  2.45 us
    ppermute x3, waiting for transfers between devices, from_span(): return lax.ppermute(value, 'span', [(p, p ^ step) for p in range(spans)])  2.33 us
    ppermute x3, waiting for transfers between devices, pair_b(): lax.ppermute(value, 'wall', [(w, min(max((w + 1 ^ 1) - 1, 0), walls - 1))...  1.92 us
  transfers between devices with their start and end apart: 14, of which 5 were waited for; matrix products, arithmetic and copies ran while one was open for 0% of the time, Pallas kernels for 5%

profile of v12, /device:TPU:4, one launch (start us, length us, event | category | flops | bytes accessed | tf_op | source)
XLA Modules:
  0.0 34.4 jit_solution(18404301679109897533)
XLA Ops:
  0.6 0.9 %copy-done.1 = f32[4,8,16,128]{3,2,1,0:T(8,128)S(1)} copy-done((f32[4,8,16,128]{3,2,1,0:T(8,128)S(1)}, f32[4,8,16,128]{3,2,1,0:T(8,128)}, u32[]{:S(2)}) %copy-start.1) | copy-done | bytes 262168
  1.6 0.4 %pack.1 = (f32[20,16,128]{2,1,0:T(8,128)S(1)}, f32[20,16,128]{2,1,0:T(8,128)S(1)}, f32[4,16,128]{2,1,0:T(8,128)S(1)}, f32[4,16,128]{2,1,0:T(8,128)S(1)}) custom-call(f32[4,8,16,128]{3,2,1,0:T(8,128)S(1)} %copy-done.1), custom_call_target="tpu_custom_call" | custom-call | tf_op jit(solution)/shard_map/pack/pallas_call | solution.py:316
  2.0 1.6 %collective-permute-start = (f32[20,16,128]{2,1,0:T(8,128)S(1)}, f32[20,16,128]{2,1,0:T(8,128)S(1)}, u32[]{:S(2)}, u32[]{:S(2)}) collective-permute-start(f32[20,16,128]{2,1,0:T(8,128)S(1)} %get-tuple-element.19), channel_id=1, source_target_pairs={{0,1},{1,0},{2,3},{3,2},{4,5},{5,4},{6,7},{7,6},{8,9},{9,8},{10,11... | collective-permute-start | bytes 491528 | tf_op jit(solution)/shard_map/ppermute | solution.py:337
  3.5 2.5 %collective-permute-start.1 = (f32[20,16,128]{2,1,0:T(8,128)S(1)}, f32[20,16,128]{2,1,0:T(8,128)S(1)}, u32[]{:S(2)}, u32[]{:S(2)}) collective-permute-start(f32[20,16,128]{2,1,0:T(8,128)S(1)} %get-tuple-element.20.mine), channel_id=1, source_target_pairs={{0,0},{2,4},{4,2},{6,6},{1,1},{3,5},{5,3},{7,7},{8,8},{10,12},{12,... | collective-permute-start | bytes 491528 | tf_op jit(solution)/shard_map/ppermute | solution.py:343
  6.0 1.6 %collective-permute-start.4 = (f32[4,16,128]{2,1,0:T(8,128)S(1)}, f32[4,16,128]{2,1,0:T(8,128)S(1)}, u32[]{:S(2)}, u32[]{:S(2)}) collective-permute-start(f32[4,16,128]{2,1,0:T(8,128)S(1)} %get-tuple-element.23), channel_id=1, source_target_pairs={{1,25},{0,8},{9,1},{8,16},{17,9},{16,24},{25,17},{24,0},{3,27},{2,... | collective-permute-start | bytes 98312 | tf_op jit(solution)/shard_map/ppermute | solution.py:361
  7.7 2.4 %collective-permute-start.5 = (f32[4,16,128]{2,1,0:T(8,128)S(1)}, f32[4,16,128]{2,1,0:T(8,128)S(1)}, u32[]{:S(2)}, u32[]{:S(2)}) collective-permute-start(f32[4,16,128]{2,1,0:T(8,128)S(1)} %get-tuple-element.24), channel_id=1, source_target_pairs={{0,25},{1,8},{8,1},{9,16},{16,9},{17,24},{24,17},{25,0},{2,27},{3,... | collective-permute-start | bytes 98312 | tf_op jit(solution)/shard_map/ppermute | solution.py:360
  10.1 0.0 collective-permute-done.1.b_mine
  10.1 0.1 collective-permute-start.7
  10.2 2.5 %collective-permute-start.3 = (f32[20,16,128]{2,1,0:T(8,128)S(1)}, f32[20,16,128]{2,1,0:T(8,128)S(1)}, u32[]{:S(2)}, u32[]{:S(2)}) collective-permute-start(f32[20,16,128]{2,1,0:T(8,128)S(1)} %collective-permute-done.part), channel_id=1, source_target_pairs={{0,0},{2,4},{4,2},{6,6},{1,1},{3,5},{5,3},{7,7},{8,8},{10,12},{12,... | collective-permute-start | bytes 491528 | tf_op jit(solution)/shard_map/ppermute | solution.py:343
  12.7 1.6 %collective-permute-done.5.part_strip = f32[4,16,128]{2,1,0:T(8,128)S(1)} collective-permute-done((f32[4,16,128]{2,1,0:T(8,128)S(1)}, f32[4,16,128]{2,1,0:T(8,128)S(1)}, u32[]{:S(2)}, u32[]{:S(2)}) %collective-permute-start.5) | collective-permute-done | bytes 32800 | tf_op jit(solution)/shard_map/ppermute | solution.py:360
  14.3 1.9 %collective-permute-start.6 = (f32[8,16,128]{2,1,0:T(8,128)S(1)}, f32[8,16,128]{2,1,0:T(8,128)S(1)}, u32[]{:S(2)}, u32[]{:S(2)}) collective-permute-start(f32[8,16,128]{2,1,0:T(8,128)S(1)} %outer.1), channel_id=1, source_target_pairs={{0,0},{2,4},{4,2},{6,6},{1,1},{3,5},{5,3},{7,7},{8,8},{10,12},{12,... | collective-permute-start | bytes 196616 | tf_op jit(solution)/shard_map/ppermute | solution.py:343
  16.2 1.1 %centre.1 = (f32[256,512]{1,0:T(8,128)S(1)}, f32[256,512]{1,0:T(8,128)S(1)}, f32[256,384]{1,0:T(8,128)S(1)}) custom-call(f32[20,16,128]{2,1,0:T(8,128)S(1)} %get-tuple-element.20.mine, f32[20,16,128]{2,1,0:T(8,128)S(1)} %collective-permute-done.part, f32[8,16,128]{2,1,0:T(8,128)S(1)} %outer.1, bf16[768,1024]{1,0:T(8,128)(2,1)S(1)} %copy-done), custom_call_target="tpu_custom_call" | custom-call | flops 536870912 | tf_op jit(solution)/shard_map/centre/pallas_call | solution.py:316
  17.3 0.6 %mate.1 = (f32[4,16,16,128]{3,2,1,0:T(8,128)S(1)}, f32[256,512]{1,0:T(8,128)S(1)}) custom-call(f32[20,16,128]{2,1,0:T(8,128)S(1)} %collective-permute-done.2.mine, f32[20,16,128]{2,1,0:T(8,128)S(1)} %collective-permute-done.7.part, f32[8,16,128]{2,1,0:T(8,128)S(1)} %collective-permute-done.8.outer, f32[256,512]{1,0:T(8,128)S(1)} %get-tuple-element.26.upper, ...), custom_call_target="tpu_custom_call" | custom-call | flops 536870912 | tf_op jit(solution)/shard_map/mate/pallas_call | solution.py:316
  18.0 1.9 %collective-permute-done.6.b_outer = f32[8,16,128]{2,1,0:T(8,128)S(1)} collective-permute-done((f32[8,16,128]{2,1,0:T(8,128)S(1)}, f32[8,16,128]{2,1,0:T(8,128)S(1)}, u32[]{:S(2)}, u32[]{:S(2)}) %collective-permute-start.6) | collective-permute-done | bytes 65568 | tf_op jit(solution)/shard_map/ppermute | solution.py:343
  19.9 3.1 %flux.1 = (f32[6,8,16,128]{3,2,1,0:T(8,128)S(1)}, f32[3,8,16,128]{3,2,1,0:T(8,128)S(1)}, f32[16,128]{1,0:T(8,128)S(1)}) custom-call(f32[20,16,128]{2,1,0:T(8,128)S(1)} %collective-permute-done.1.b_mine, f32[20,16,128]{2,1,0:T(8,128)S(1)} %collective-permute-done.3.b_part, f32[8,16,128]{2,1,0:T(8,128)S(1)} %collective-permute-done.6.b_outer, ...), custom_call_target="tpu_custom_call" | custom-call | tf_op jit(solution)/shard_map/flux/pallas_call | solution.py:316
  23.0 1.2 %collective-permute-start.11 = (f32[16,128]{1,0:T(8,128)S(1)}, f32[16,128]{1,0:T(8,128)S(1)}, u32[]{:S(2)}, u32[]{:S(2)}) collective-permute-start(f32[16,128]{1,0:T(8,128)S(1)} %get-tuple-element.31), channel_id=1, source_target_pairs={{0,16},{8,24},{16,0},{24,8},{1,17},{9,25},{17,1},{25,9},{2,18},{10... | collective-permute-start | bytes 24584 | tf_op jit(solution)/shard_map/ppermute | solution.py:415
  24.2 1.3 %collective-permute-start.10 = (f32[16,128]{1,0:T(8,128)S(1)}, f32[16,128]{1,0:T(8,128)S(1)}, u32[]{:S(2)}, u32[]{:S(2)}) collective-permute-start(f32[16,128]{1,0:T(8,128)S(1)} %get-tuple-element.31), channel_id=1, source_target_pairs={{0,24},{8,16},{16,8},{24,0},{1,25},{9,17},{17,9},{25,1},{2,26},{10... | collective-permute-start | bytes 24584 | tf_op jit(solution)/shard_map/ppermute | solution.py:415
  25.6 1.0 %collective-permute-start.9 = (f32[16,128]{1,0:T(8,128)S(1)}, f32[16,128]{1,0:T(8,128)S(1)}, u32[]{:S(2)}, u32[]{:S(2)}) collective-permute-start(f32[16,128]{1,0:T(8,128)S(1)} %get-tuple-element.31), channel_id=1, source_target_pairs={{0,8},{8,0},{16,24},{24,16},{1,9},{9,1},{17,25},{25,17},{2,10},{10... | collective-permute-start | bytes 24584 | tf_op jit(solution)/shard_map/ppermute | solution.py:415
  26.5 0.8 %collective-permute-start.13 = (f32[3,8,16,128]{3,2,1,0:T(8,128)S(1)}, f32[3,8,16,128]{3,2,1,0:T(8,128)S(1)}, u32[]{:S(2)}, u32[]{:S(2)}) collective-permute-start(f32[3,8,16,128]{3,2,1,0:T(8,128)S(1)} %get-tuple-element.33), channel_id=1, source_target_pairs={{0,1},{1,0},{2,3},{3,2},{4,5},{5,4},{6,7},{7,6},{8,9},{9,8},{10,11... | collective-permute-start | bytes 589832 | tf_op jit(solution)/shard_map/ppermute | solution.py:337
  27.3 0.3 collective-permute-done.11
  27.6 2.1 %collective-permute-done.10 = f32[16,128]{1,0:T(8,128)S(1)} collective-permute-done((f32[16,128]{1,0:T(8,128)S(1)}, f32[16,128]{1,0:T(8,128)S(1)}, u32[]{:S(2)}, u32[]{:S(2)}) %collective-permute-start.10) | collective-permute-done | bytes 8224 | tf_op jit(solution)/shard_map/ppermute | solution.py:415
  29.7 0.5 %collective-permute-start.12 = (f32[16,128]{1,0:T(8,128)S(1)}, f32[16,128]{1,0:T(8,128)S(1)}, u32[]{:S(2)}, u32[]{:S(2)}) collective-permute-start(f32[16,128]{1,0:T(8,128)S(1)} %add_add_fusion), channel_id=1, source_target_pairs={{0,1},{1,0},{2,3},{3,2},{4,5},{5,4},{6,7},{7,6},{8,9},{9,8},{10,11... | collective-permute-start | bytes 24584 | tf_op jit(solution)/shard_map/ppermute | solution.py:337
  30.2 3.2 %collective-permute-done.12 = f32[16,128]{1,0:T(8,128)S(1)} collective-permute-done((f32[16,128]{1,0:T(8,128)S(1)}, f32[16,128]{1,0:T(8,128)S(1)}, u32[]{:S(2)}, u32[]{:S(2)}) %collective-permute-start.12) | collective-permute-done | bytes 8224 | tf_op jit(solution)/shard_map/ppermute | solution.py:337
  33.4 1.0 %finish.1 = (f32[3,8,16,128]{3,2,1,0:T(8,128)}, f32[3,8,16,128]{3,2,1,0:T(8,128)}, f32[3,16]{1,0:T(4,128)}, f32[3,16]{1,0:T(4,128)}) custom-call(f32[16,128]{1,0:T(8,128)S(1)} %add.15.sums, f32[6,8,16,128]{3,2,1,0:T(8,128)S(1)} %get-tuple-element.32.keep, f32[3,8,16,128]{3,2,1,0:T(8,128)S(1)} %collective-permute-done.13.come), custom_call_target="tpu_custom_call" | custom-call | tf_op jit(solution)/shard_map/finish/pallas_call | solution.py:316
  (16 shorter events, 0.0 us)
Async XLA Ops:
  0.6 1.0 %copy-start.1 = (f32[4,8,16,128]{3,2,1,0:T(8,128)S(1)}, f32[4,8,16,128]{3,2,1,0:T(8,128)}, u32[]{:S(2)}) copy-start(f32[4,8,16,128]{3,2,1,0:T(8,128)} %own.1) | copy-start | bytes 786436
  2.0 8.2 %collective-permute-start = (f32[20,16,128]{2,1,0:T(8,128)S(1)}, f32[20,16,128]{2,1,0:T(8,128)S(1)}, u32[]{:S(2)}, u32[]{:S(2)}) collective-permute-start(f32[20,16,128]{2,1,0:T(8,128)S(1)} %get-tuple-element.19), channel_id=1, source_target_pairs={{0,1},{1,0},{2,3},{3,2},{4,5},{5,4},{6,7},{7,6},{8,9},{9,8},{10,11... | collective-permute-start | bytes 491528 | tf_op jit(solution)/shard_map/ppermute | solution.py:337
  3.5 6.6 %collective-permute-start.2 = (f32[20,16,128]{2,1,0:T(8,128)S(1)}, f32[20,16,128]{2,1,0:T(8,128)S(1)}, u32[]{:S(2)}, u32[]{:S(2)}) collective-permute-start(f32[20,16,128]{2,1,0:T(8,128)S(1)} %get-tuple-element.20.mine), channel_id=1, source_target_pairs={{0,2},{2,0},{4,6},{6,4},{1,3},{3,1},{5,7},{7,5},{8,10},{10,8},{12,... | collective-permute-start | bytes 491528 | tf_op jit(solution)/shard_map/ppermute | solution.py:340
  3.5 6.6 %collective-permute-start.1 = (f32[20,16,128]{2,1,0:T(8,128)S(1)}, f32[20,16,128]{2,1,0:T(8,128)S(1)}, u32[]{:S(2)}, u32[]{:S(2)}) collective-permute-start(f32[20,16,128]{2,1,0:T(8,128)S(1)} %get-tuple-element.20.mine), channel_id=1, source_target_pairs={{0,0},{2,4},{4,2},{6,6},{1,1},{3,5},{5,3},{7,7},{8,8},{10,12},{12,... | collective-permute-start | bytes 491528 | tf_op jit(solution)/shard_map/ppermute | solution.py:343
  6.0 6.7 %collective-permute-start.4 = (f32[4,16,128]{2,1,0:T(8,128)S(1)}, f32[4,16,128]{2,1,0:T(8,128)S(1)}, u32[]{:S(2)}, u32[]{:S(2)}) collective-permute-start(f32[4,16,128]{2,1,0:T(8,128)S(1)} %get-tuple-element.23), channel_id=1, source_target_pairs={{1,25},{0,8},{9,1},{8,16},{17,9},{16,24},{25,17},{24,0},{3,27},{2,... | collective-permute-start | bytes 98312 | tf_op jit(solution)/shard_map/ppermute | solution.py:361
  7.7 8.6 %copy-start = (bf16[768,1024]{1,0:T(8,128)(2,1)S(1)}, bf16[768,1024]{1,0:T(8,128)(2,1)}, u32[]{:S(2)}) copy-start(bf16[768,1024]{1,0:T(8,128)(2,1)} %constant.2.clone.weights) | copy-start | bytes 4718596
  7.7 6.6 %collective-permute-start.5 = (f32[4,16,128]{2,1,0:T(8,128)S(1)}, f32[4,16,128]{2,1,0:T(8,128)S(1)}, u32[]{:S(2)}, u32[]{:S(2)}) collective-permute-start(f32[4,16,128]{2,1,0:T(8,128)S(1)} %get-tuple-element.24), channel_id=1, source_target_pairs={{0,25},{1,8},{8,1},{9,16},{16,9},{17,24},{24,17},{25,0},{2,27},{3,... | collective-permute-start | bytes 98312 | tf_op jit(solution)/shard_map/ppermute | solution.py:360
  10.1 7.2 %collective-permute-start.7 = (f32[20,16,128]{2,1,0:T(8,128)S(1)}, f32[20,16,128]{2,1,0:T(8,128)S(1)}, u32[]{:S(2)}, u32[]{:S(2)}) collective-permute-start(f32[20,16,128]{2,1,0:T(8,128)S(1)} %collective-permute-done.part), channel_id=1, source_target_pairs={{0,2},{2,0},{4,6},{6,4},{1,3},{3,1},{5,7},{7,5},{8,10},{10,8},{12,... | collective-permute-start | bytes 491528 | tf_op jit(solution)/shard_map/ppermute | solution.py:340
  10.2 9.7 %collective-permute-start.3 = (f32[20,16,128]{2,1,0:T(8,128)S(1)}, f32[20,16,128]{2,1,0:T(8,128)S(1)}, u32[]{:S(2)}, u32[]{:S(2)}) collective-permute-start(f32[20,16,128]{2,1,0:T(8,128)S(1)} %collective-permute-done.part), channel_id=1, source_target_pairs={{0,0},{2,4},{4,2},{6,6},{1,1},{3,5},{5,3},{7,7},{8,8},{10,12},{12,... | collective-permute-start | bytes 491528 | tf_op jit(solution)/shard_map/ppermute | solution.py:343
  14.3 3.0 %collective-permute-start.8 = (f32[8,16,128]{2,1,0:T(8,128)S(1)}, f32[8,16,128]{2,1,0:T(8,128)S(1)}, u32[]{:S(2)}, u32[]{:S(2)}) collective-permute-start(f32[8,16,128]{2,1,0:T(8,128)S(1)} %outer.1), channel_id=1, source_target_pairs={{0,2},{2,0},{4,6},{6,4},{1,3},{3,1},{5,7},{7,5},{8,10},{10,8},{12,... | collective-permute-start | bytes 196616 | tf_op jit(solution)/shard_map/ppermute | solution.py:340
  14.3 5.6 %collective-permute-start.6 = (f32[8,16,128]{2,1,0:T(8,128)S(1)}, f32[8,16,128]{2,1,0:T(8,128)S(1)}, u32[]{:S(2)}, u32[]{:S(2)}) collective-permute-start(f32[8,16,128]{2,1,0:T(8,128)S(1)} %outer.1), channel_id=1, source_target_pairs={{0,0},{2,4},{4,2},{6,6},{1,1},{3,5},{5,3},{7,7},{8,8},{10,12},{12,... | collective-permute-start | bytes 196616 | tf_op jit(solution)/shard_map/ppermute | solution.py:343
  23.0 4.6 %collective-permute-start.11 = (f32[16,128]{1,0:T(8,128)S(1)}, f32[16,128]{1,0:T(8,128)S(1)}, u32[]{:S(2)}, u32[]{:S(2)}) collective-permute-start(f32[16,128]{1,0:T(8,128)S(1)} %get-tuple-element.31), channel_id=1, source_target_pairs={{0,16},{8,24},{16,0},{24,8},{1,17},{9,25},{17,1},{25,9},{2,18},{10... | collective-permute-start | bytes 24584 | tf_op jit(solution)/shard_map/ppermute | solution.py:415
  24.2 5.4 %collective-permute-start.10 = (f32[16,128]{1,0:T(8,128)S(1)}, f32[16,128]{1,0:T(8,128)S(1)}, u32[]{:S(2)}, u32[]{:S(2)}) collective-permute-start(f32[16,128]{1,0:T(8,128)S(1)} %get-tuple-element.31), channel_id=1, source_target_pairs={{0,24},{8,16},{16,8},{24,0},{1,25},{9,17},{17,9},{25,1},{2,26},{10... | collective-permute-start | bytes 24584 | tf_op jit(solution)/shard_map/ppermute | solution.py:415
  25.6 4.1 %collective-permute-start.9 = (f32[16,128]{1,0:T(8,128)S(1)}, f32[16,128]{1,0:T(8,128)S(1)}, u32[]{:S(2)}, u32[]{:S(2)}) collective-permute-start(f32[16,128]{1,0:T(8,128)S(1)} %get-tuple-element.31), channel_id=1, source_target_pairs={{0,8},{8,0},{16,24},{24,16},{1,9},{9,1},{17,25},{25,17},{2,10},{10... | collective-permute-start | bytes 24584 | tf_op jit(solution)/shard_map/ppermute | solution.py:415
  26.5 6.9 %collective-permute-start.13 = (f32[3,8,16,128]{3,2,1,0:T(8,128)S(1)}, f32[3,8,16,128]{3,2,1,0:T(8,128)S(1)}, u32[]{:S(2)}, u32[]{:S(2)}) collective-permute-start(f32[3,8,16,128]{3,2,1,0:T(8,128)S(1)} %get-tuple-element.33), channel_id=1, source_target_pairs={{0,1},{1,0},{2,3},{3,2},{4,5},{5,4},{6,7},{7,6},{8,9},{9,8},{10,11... | collective-permute-start | bytes 589832 | tf_op jit(solution)/shard_map/ppermute | solution.py:337
  29.7 3.7 %collective-permute-start.12 = (f32[16,128]{1,0:T(8,128)S(1)}, f32[16,128]{1,0:T(8,128)S(1)}, u32[]{:S(2)}, u32[]{:S(2)}) collective-permute-start(f32[16,128]{1,0:T(8,128)S(1)} %add_add_fusion), channel_id=1, source_target_pairs={{0,1},{1,0},{2,3},{3,2},{4,5},{5,4},{6,7},{7,6},{8,9},{9,8},{10,11... | collective-permute-start | bytes 24584 | tf_op jit(solution)/shard_map/ppermute | solution.py:337

commit v13 on v12

--- a/solution.py
+++ b/solution.py
@@ -102,32 +102,38 @@
         yield k, jnp.where(is_outer, pieces[1], pieces[0])
 
 
-def pack_kernel(own, to_partner, to_mine, to_other, to_same):
+def pack_kernel(own, to_partner, tiles, to_other, to_same):
     _, layers, _, _ = own.shape
     me_s = lax.axis_index("stream")
-    for message, half in ((to_partner, 1 - me_s), (to_mine, me_s)):
+    for message, half in ((to_partner, 1 - me_s), (tiles, me_s)):
         for pair, tile in pack_halves(own, half):
             message[pair * layers : (pair + 1) * layers] = tile
-        message[2 * layers :] = pack_strip(own, 4 - half)
+    to_partner[2 * layers :] = pack_strip(own, 3 + me_s)
     to_other[...] = pack_strip(own, 7 * me_s)
     to_same[...] = pack_strip(own, 7 * (1 - me_s))
 
 
-def outer_kernel(own_strip, part_strip, outer):
-    half = own_strip.shape[0]
-    outer[:half] = own_strip[...]
-    outer[half:] = part_strip[...]
-
-
-def unpack(mine, part, outer, me_s):
-    layers, rows, width = outer.shape
-    half = layers // 2
+def join_kernel(own, tiles, part, own_strip, part_strip, whole, rest):
+    count, half = tiles.shape[0], own_strip.shape[0]
+    inner = pack_strip(own, 4 - lax.axis_index("stream"))
+    whole[:count] = tiles[...]
+    for message, start in ((whole, count), (rest, 0)):
+        start += count + half
+        message[start - count - half : start] = part[...]
+        message[start : start + half] = inner
+        message[start + half : start + 2 * half] = own_strip[...]
+        message[start + 2 * half :] = part_strip[...]
+
+
+def unpack(tiles, rest, me_s):
+    count, rows, width = tiles.shape
+    layers, half = count // 2, count // 4
     unit = unit_index((half, rows, width))
     first = 4 * (1 - me_s)
     in_strip = (unit == first) | (unit == first + 3)
-    for which, packed in enumerate((mine, part)):
-        far = outer[which * half : (which + 1) * half]
-        for k, strip in strip_tile(packed[2 * layers :], far, me_s):
+    strips = [rest[count + i * half : count + (i + 1) * half] for i in range(4)]
+    for which, packed, near, far in ((0, tiles, strips[1], strips[2]), (1, rest, strips[0], strips[3])):
+        for k, strip in strip_tile(near, far, me_s):
             layer = (me_s if which == 0 else 1 - me_s) * layers + k * half
             for f in range(4):
                 start = f // 2 * layers + k * half
@@ -151,9 +157,9 @@
     return dot(plane_h, high) + dot(plane_l, high) + dot(plane_h, low)
 
 
-def bring(mine, part, outer, raw, high, low, keep=None):
-    rows, width = outer.shape[1:]
-    for f, layer, value in unpack(mine, part, outer, lax.axis_index("stream")):
+def bring(tiles, rest, raw, high, low, keep=None):
+    rows, width = tiles.shape[1:]
+    for f, layer, value in unpack(tiles, rest, lax.axis_index("stream")):
         count = value.shape[0]
         value = value if keep is None else value * keep
         raw[f, pl.ds(layer, count)] = value
@@ -162,10 +168,10 @@
 
 
 def centre_kernel(
-    mine, part, outer, weights, upper, lower, products, centre, in_h, in_l, prod_h, prod_l
+    tiles, rest, weights, upper, lower, products, centre, in_h, in_l, prod_h, prod_l
 ):
-    cells, width = in_h.shape[0], outer.shape[-1]
-    bring(mine, part, outer, centre, in_h, in_l)
+    cells, width = in_h.shape[0], tiles.shape[-1]
+    bring(tiles, rest, centre, in_h, in_l)
     for i in range(3):
         value = (centre[i] * centre[3]).reshape(cells, width)
         prod_h[:, column(i)], prod_l[:, column(i)] = halves(value)
@@ -174,15 +180,16 @@
     products[...] = planes_of(weights, 2, prod_h[...], prod_l[...])
 
 
-def mate_kernel(mine, part, outer, upper, lower, weights, raw, partial, in_h, in_l):
+def mate_kernel(whole, upper, lower, weights, raw, partial, in_h, in_l):
     odd = lax.rem(lax.axis_index("wall"), 2)
-    bring(mine, part, outer, raw, in_h, in_l)
+    count = raw.shape[1]
+    bring(whole.at[:count], whole.at[count:], raw, in_h, in_l)
     base = jnp.where(odd == 1, upper[...], lower[...])
     partial[...] = base + planes_of(weights, 1 - odd, in_h[...], in_l[...])
 
 
 def flux_kernel(
-    walls, b_mine, b_part, b_outer, a_raw, a_partial, upper, lower, products, weights,
+    walls, b_tiles, b_rest, a_raw, a_partial, upper, lower, products, weights,
     keep_ref, send_ref, sums_ref,
     raw, in_h, in_l, prod_h, prod_l, mean, mid_h, mid_l, clark_all, similar_all,
 ):
@@ -196,7 +203,7 @@
     at_end = (me_w == 0) | (me_w == walls - 1)
     keep_b = jnp.where(at_end, 0.0, 1.0).astype(jnp.float32)
 
-    bring(b_mine, b_part, b_outer, raw, in_h, in_l, keep_b)
+    bring(b_tiles, b_rest, raw, in_h, in_l, keep_b)
 
     def along_span_of(planes):
         high, low = halves(planes)
@@ -352,17 +359,22 @@
         to_other += [(place(p, 0), place(p - 1, 1)), (place(p, 1), place(p + 1, 0))]
         to_same += [(place(p, 1), place(p - 1, 1)), (place(p, 0), place(p + 1, 0))]
 
-    message, strip = (2 * layers + layers // 2, rows, width), (layers // 2, rows, width)
-    to_partner, mine, first, second = call(
-        pack_kernel, "pack", (fields,), (message, message, strip, strip)
+    message, strip = (both + layers // 2, rows, width), (layers // 2, rows, width)
+    to_partner, own_tiles, first, second = call(
+        pack_kernel, "pack", (fields,), (message, (both, rows, width), strip, strip)
     )
     part = swap(to_partner)
     part_strip = lax.ppermute(first, ("span", "stream"), to_other)
     own_strip = lax.ppermute(second, ("span", "stream"), to_same)
-    part, b_mine, a_mine = lax.optimization_barrier((part, pair_b(mine), pair_a(mine)))
-    b_part, a_part = pair_b(part), pair_a(part)
-    (outer,) = call(outer_kernel, "outer", (own_strip, part_strip), ((layers, rows, width),), hint=2**35)
-    b_outer, a_outer = pair_b(outer), pair_a(outer)
+    tiles, b_tiles = lax.optimization_barrier((own_tiles, pair_b(own_tiles)))
+    whole, rest = call(
+        join_kernel,
+        "join",
+        (fields, own_tiles, part, own_strip, part_strip),
+        ((2 * both + 2 * layers, rows, width), (both + 2 * layers, rows, width)),
+        hint=2**35,
+    )
+    b_rest, a_whole = pair_b(rest), pair_a(whole)
 
     matrices = np.zeros((2 * cells + 2 * width, 4 * cells), ml_dtypes.bfloat16)
     matrices[:cells], matrices[cells : 2 * cells] = plane_constants(both, rows)
@@ -374,16 +386,16 @@
     upper, lower, products = call(
         centre_kernel,
         "centre",
-        (mine, part, outer, weights),
+        (tiles, rest, weights),
         ((cells, 4 * width), (cells, 4 * width), (cells, 3 * width)),
         [(block, single), *pieces, ((cells, 3 * width), brief), ((cells, 3 * width), brief)],
         mib=16,
-        hint=2**29,
+        hint=2**35,
     )
     a_raw, a_partial = call(
         mate_kernel,
         "mate",
-        (a_mine, a_part, a_outer, upper, lower, weights),
+        (a_whole, upper, lower, weights),
         (block, (cells, 4 * width)),
         pieces,
         mib=16,
@@ -392,7 +404,7 @@
     keep, send, sums = call(
         functools.partial(flux_kernel, walls),
         "flux",
-        (b_mine, b_part, b_outer, a_raw, a_partial, upper, lower, products, weights),
+        (b_tiles, b_rest, a_raw, a_partial, upper, lower, products, weights),
         ((6, layers, rows, width), (3, layers, rows, width), (rows, width)),
         [
             (block, single),

time: 34.6 us -> 36.2 us (1.046); the launches traced: 34.4 us -> 35.6 us
  waiting for transfers between devices: 9.01 us -> 12.9 us
  starting transfers between devices: 17.5 us -> 14.7 us
    ppermute x3 -> x2, starting transfers between devices: 6.91 us -> 4.12 us  [pair_b(): lax.ppermute(value, 'wall', [(w, min(max((w + 1 ^ 1) - 1, 0), walls - 1))...]
    ppermute x1, waiting for transfers between devices: 0.01 us -> 1.41 us  [shards(): own_strip = lax.ppermute(second, ('span', 'stream'), to_same)]
    ppermute x3 -> x2, waiting for transfers between devices: 1.92 us -> 3.32 us  [pair_b(): lax.ppermute(value, 'wall', [(w, min(max((w + 1 ^ 1) - 1, 0), walls - 1))...]
    ppermute x1, waiting for transfers between devices: 1.58 us -> 2.48 us  [shards(): part_strip = lax.ppermute(first, ('span', 'stream'), to_other)]
    ppermute x3 -> x1, waiting for transfers between devices: 0.01 us -> 0.61 us  [pair_a(): return lax.ppermute(value, 'wall', [(w, w ^ 1) for w in range(walls)])]
    ppermute x3, waiting for transfers between devices: 2.33 us -> 1.95 us  [from_span(): return lax.ppermute(value, 'span', [(p, p ^ step) for p in range(spans)])]
  transfers between devices with their start and end apart: 14 -> 11, of which waited for: 5 -> 8; matrix products, arithmetic and copies ran while one was open for 0% -> 0% of each run, Pallas kernels for 5% -> 5%
where the time goes in v13:
time: 36.2 us; the launch traced here: 35.6 us
  starting transfers between devices  14.7 us (41%)
  waiting for transfers between devices  12.9 us (36%)
  Pallas kernels  6.26 us (17%)
  local copies, waits for them, and re-layouts  0.95 us (3%)
  between operations  0.71 us (2%)
    pallas_call x6, Pallas kernels, call(): pl.pallas_call(kernel, out_shape=tuple((jax.ShapeDtypeStruct(shape, jnp.f...  6.26 us
    ppermute x2, starting transfers between devices, pair_b(): lax.ppermute(value, 'wall', [(w, min(max((w + 1 ^ 1) - 1, 0), walls - 1))...  4.12 us
    ppermute x3, starting transfers between devices, from_span(): return lax.ppermute(value, 'span', [(p, p ^ step) for p in range(spans)])  3.55 us
    ppermute x2, waiting for transfers between devices, pair_b(): lax.ppermute(value, 'wall', [(w, min(max((w + 1 ^ 1) - 1, 0), walls - 1))...  3.32 us
    ppermute x3, waiting for transfers between devices, swap(): return lax.ppermute(value, 'stream', [(0, 1), (1, 0)])  3.19 us
    ppermute x3, starting transfers between devices, swap(): return lax.ppermute(value, 'stream', [(0, 1), (1, 0)])  2.88 us
    ppermute x1, waiting for transfers between devices, shards(): part_strip = lax.ppermute(first, ('span', 'stream'), to_other)  2.48 us
    ppermute x1, starting transfers between devices, shards(): part_strip = lax.ppermute(first, ('span', 'stream'), to_other)  2.45 us
  transfers between devices with their start and end apart: 11, of which 8 were waited for; matrix products, arithmetic and copies ran while one was open for 0% of the time, Pallas kernels for 5%

profile of v13, /device:TPU:4, one launch (start us, length us, event | category | flops | bytes accessed | tf_op | source)
XLA Modules:
  0.0 35.6 jit_solution(12572928948612743221)
XLA Ops:
  0.6 0.9 %copy-done.1 = f32[4,8,16,128]{3,2,1,0:T(8,128)S(1)} copy-done((f32[4,8,16,128]{3,2,1,0:T(8,128)S(1)}, f32[4,8,16,128]{3,2,1,0:T(8,128)}, u32[]{:S(2)}) %copy-start.1) | copy-done | bytes 262168
  1.6 0.3 pack.1
  1.9 1.6 %collective-permute-start.1 = (f32[20,16,128]{2,1,0:T(8,128)S(1)}, f32[20,16,128]{2,1,0:T(8,128)S(1)}, u32[]{:S(2)}, u32[]{:S(2)}) collective-permute-start(f32[20,16,128]{2,1,0:T(8,128)S(1)} %get-tuple-element.22), channel_id=1, source_target_pairs={{0,1},{1,0},{2,3},{3,2},{4,5},{5,4},{6,7},{7,6},{8,9},{9,8},{10,11... | collective-permute-start | bytes 491528 | tf_op jit(solution)/shard_map/ppermute | solution.py:344
  3.5 1.9 %collective-permute-start = (f32[16,16,128]{2,1,0:T(8,128)S(1)}, f32[16,16,128]{2,1,0:T(8,128)S(1)}, u32[]{:S(2)}, u32[]{:S(2)}) collective-permute-start(f32[16,16,128]{2,1,0:T(8,128)S(1)} %get-tuple-element.27.tiles), channel_id=1, source_target_pairs={{0,0},{2,4},{4,2},{6,6},{1,1},{3,5},{5,3},{7,7},{8,8},{10,12},{12,... | collective-permute-start | bytes 393224 | tf_op jit(solution)/shard_map/ppermute | solution.py:350
  5.4 1.6 %collective-permute-start.2 = (f32[4,16,128]{2,1,0:T(8,128)S(1)}, f32[4,16,128]{2,1,0:T(8,128)S(1)}, u32[]{:S(2)}, u32[]{:S(2)}) collective-permute-start(f32[4,16,128]{2,1,0:T(8,128)S(1)} %get-tuple-element.23), channel_id=1, source_target_pairs={{1,25},{0,8},{9,1},{8,16},{17,9},{16,24},{25,17},{24,0},{3,27},{2,... | collective-permute-start | bytes 98312 | tf_op jit(solution)/shard_map/ppermute | solution.py:368
  7.0 2.4 %collective-permute-start.3 = (f32[4,16,128]{2,1,0:T(8,128)S(1)}, f32[4,16,128]{2,1,0:T(8,128)S(1)}, u32[]{:S(2)}, u32[]{:S(2)}) collective-permute-start(f32[4,16,128]{2,1,0:T(8,128)S(1)} %get-tuple-element.24), channel_id=1, source_target_pairs={{0,25},{1,8},{8,1},{9,16},{16,9},{17,24},{24,17},{25,0},{2,27},{3,... | collective-permute-start | bytes 98312 | tf_op jit(solution)/shard_map/ppermute | solution.py:367
  9.4 0.3 collective-permute-done.b_tiles
  9.7 1.4 %collective-permute-done.2.own_strip = f32[4,16,128]{2,1,0:T(8,128)S(1)} collective-permute-done((f32[4,16,128]{2,1,0:T(8,128)S(1)}, f32[4,16,128]{2,1,0:T(8,128)S(1)}, u32[]{:S(2)}, u32[]{:S(2)}) %collective-permute-start.2) | collective-permute-done | bytes 32800 | tf_op jit(solution)/shard_map/ppermute | solution.py:368
  11.1 2.5 %collective-permute-done.3.part_strip = f32[4,16,128]{2,1,0:T(8,128)S(1)} collective-permute-done((f32[4,16,128]{2,1,0:T(8,128)S(1)}, f32[4,16,128]{2,1,0:T(8,128)S(1)}, u32[]{:S(2)}, u32[]{:S(2)}) %collective-permute-start.3) | collective-permute-done | bytes 32800 | tf_op jit(solution)/shard_map/ppermute | solution.py:367
  13.7 2.2 %collective-permute-start.4 = (f32[32,16,128]{2,1,0:T(8,128)S(1)}, f32[32,16,128]{2,1,0:T(8,128)S(1)}, u32[]{:S(2)}, u32[]{:S(2)}) collective-permute-start(f32[32,16,128]{2,1,0:T(8,128)S(1)} %get-tuple-element.25.rest), channel_id=1, source_target_pairs={{0,0},{2,4},{4,2},{6,6},{1,1},{3,5},{5,3},{7,7},{8,8},{10,12},{12,... | collective-permute-start | bytes 786440 | tf_op jit(solution)/shard_map/ppermute | solution.py:350
  16.1 1.1 %centre.1 = (f32[256,512]{1,0:T(8,128)S(1)}, f32[256,512]{1,0:T(8,128)S(1)}, f32[256,384]{1,0:T(8,128)S(1)}) custom-call(f32[16,16,128]{2,1,0:T(8,128)S(1)} %get-tuple-element.27.tiles, f32[32,16,128]{2,1,0:T(8,128)S(1)} %get-tuple-element.25.rest, bf16[768,1024]{1,0:T(8,128)(2,1)S(1)} %copy-done), custom_call_target="tpu_custom_call" | custom-call | flops 34359738368 | tf_op jit(solution)/shard_map/centre/pallas_call | solution.py:323
  17.1 0.6 %collective-permute-done.5.whole = f32[48,16,128]{2,1,0:T(8,128)S(1)} collective-permute-done((f32[48,16,128]{2,1,0:T(8,128)S(1)}, f32[48,16,128]{2,1,0:T(8,128)S(1)}, u32[]{:S(2)}, u32[]{:S(2)}) %collective-permute-start.5) | collective-permute-done | bytes 393248 | tf_op jit(solution)/shard_map/ppermute | solution.py:347
  17.8 0.6 %mate.1 = (f32[4,16,16,128]{3,2,1,0:T(8,128)S(1)}, f32[256,512]{1,0:T(8,128)S(1)}) custom-call(f32[48,16,128]{2,1,0:T(8,128)S(1)} %collective-permute-done.5.whole, f32[256,512]{1,0:T(8,128)S(1)} %get-tuple-element.28.upper, f32[256,512]{1,0:T(8,128)S(1)} %get-tuple-element.29.lower, bf16[768,1024]{1,0:T(8,128)(2,1)S(1)} %copy-done), custom_call_target="tpu_custom_call" | custom-call | flops 536870912 | tf_op jit(solution)/shard_map/mate/pallas_call | solution.py:323
  18.4 3.0 %collective-permute-done.4.b_rest = f32[32,16,128]{2,1,0:T(8,128)S(1)} collective-permute-done((f32[32,16,128]{2,1,0:T(8,128)S(1)}, f32[32,16,128]{2,1,0:T(8,128)S(1)}, u32[]{:S(2)}, u32[]{:S(2)}) %collective-permute-start.4) | collective-permute-done | bytes 262176 | tf_op jit(solution)/shard_map/ppermute | solution.py:350
  21.4 3.1 %flux.1 = (f32[6,8,16,128]{3,2,1,0:T(8,128)S(1)}, f32[3,8,16,128]{3,2,1,0:T(8,128)S(1)}, f32[16,128]{1,0:T(8,128)S(1)}) custom-call(f32[16,16,128]{2,1,0:T(8,128)S(1)} %collective-permute-done.b_tiles, f32[32,16,128]{2,1,0:T(8,128)S(1)} %collective-permute-done.4.b_rest, f32[4,16,16,128]{3,2,1,0:T(8,128)S(1)} %get-tuple-element.30.a_raw, ...), custom_call_target="tpu_custom_call" | custom-call | tf_op jit(solution)/shard_map/flux/pallas_call | solution.py:323
  24.5 0.8 %collective-permute-start.8 = (f32[16,128]{1,0:T(8,128)S(1)}, f32[16,128]{1,0:T(8,128)S(1)}, u32[]{:S(2)}, u32[]{:S(2)}) collective-permute-start(f32[16,128]{1,0:T(8,128)S(1)} %get-tuple-element.33), channel_id=1, source_target_pairs={{0,16},{8,24},{16,0},{24,8},{1,17},{9,25},{17,1},{25,9},{2,18},{10... | collective-permute-start | bytes 24584 | tf_op jit(solution)/shard_map/ppermute | solution.py:427
  25.4 1.3 %collective-permute-start.7 = (f32[16,128]{1,0:T(8,128)S(1)}, f32[16,128]{1,0:T(8,128)S(1)}, u32[]{:S(2)}, u32[]{:S(2)}) collective-permute-start(f32[16,128]{1,0:T(8,128)S(1)} %get-tuple-element.33), channel_id=1, source_target_pairs={{0,24},{8,16},{16,8},{24,0},{1,25},{9,17},{17,9},{25,1},{2,26},{10... | collective-permute-start | bytes 24584 | tf_op jit(solution)/shard_map/ppermute | solution.py:427
  26.7 1.4 %collective-permute-start.6 = (f32[16,128]{1,0:T(8,128)S(1)}, f32[16,128]{1,0:T(8,128)S(1)}, u32[]{:S(2)}, u32[]{:S(2)}) collective-permute-start(f32[16,128]{1,0:T(8,128)S(1)} %get-tuple-element.33), channel_id=1, source_target_pairs={{0,8},{8,0},{16,24},{24,16},{1,9},{9,1},{17,25},{25,17},{2,10},{10... | collective-permute-start | bytes 24584 | tf_op jit(solution)/shard_map/ppermute | solution.py:427
  28.1 0.8 %collective-permute-start.10 = (f32[3,8,16,128]{3,2,1,0:T(8,128)S(1)}, f32[3,8,16,128]{3,2,1,0:T(8,128)S(1)}, u32[]{:S(2)}, u32[]{:S(2)}) collective-permute-start(f32[3,8,16,128]{3,2,1,0:T(8,128)S(1)} %get-tuple-element.35), channel_id=1, source_target_pairs={{0,1},{1,0},{2,3},{3,2},{4,5},{5,4},{6,7},{7,6},{8,9},{9,8},{10,11... | collective-permute-start | bytes 589832 | tf_op jit(solution)/shard_map/ppermute | solution.py:344
  28.9 0.3 collective-permute-done.8
  29.2 1.7 %collective-permute-done.7 = f32[16,128]{1,0:T(8,128)S(1)} collective-permute-done((f32[16,128]{1,0:T(8,128)S(1)}, f32[16,128]{1,0:T(8,128)S(1)}, u32[]{:S(2)}, u32[]{:S(2)}) %collective-permute-start.7) | collective-permute-done | bytes 8224 | tf_op jit(solution)/shard_map/ppermute | solution.py:427
  30.8 0.5 %collective-permute-start.9 = (f32[16,128]{1,0:T(8,128)S(1)}, f32[16,128]{1,0:T(8,128)S(1)}, u32[]{:S(2)}, u32[]{:S(2)}) collective-permute-start(f32[16,128]{1,0:T(8,128)S(1)} %add_add_fusion), channel_id=1, source_target_pairs={{0,1},{1,0},{2,3},{3,2},{4,5},{5,4},{6,7},{7,6},{8,9},{9,8},{10,11... | collective-permute-start | bytes 24584 | tf_op jit(solution)/shard_map/ppermute | solution.py:344
  31.4 3.2 %collective-permute-done.9 = f32[16,128]{1,0:T(8,128)S(1)} collective-permute-done((f32[16,128]{1,0:T(8,128)S(1)}, f32[16,128]{1,0:T(8,128)S(1)}, u32[]{:S(2)}, u32[]{:S(2)}) %collective-permute-start.9) | collective-permute-done | bytes 8224 | tf_op jit(solution)/shard_map/ppermute | solution.py:344
  34.6 1.0 %finish.1 = (f32[3,8,16,128]{3,2,1,0:T(8,128)}, f32[3,8,16,128]{3,2,1,0:T(8,128)}, f32[3,16]{1,0:T(4,128)}, f32[3,16]{1,0:T(4,128)}) custom-call(f32[16,128]{1,0:T(8,128)S(1)} %add.15.sums, f32[6,8,16,128]{3,2,1,0:T(8,128)S(1)} %get-tuple-element.34.keep, f32[3,8,16,128]{3,2,1,0:T(8,128)S(1)} %collective-permute-done.10.come), custom_call_target="tpu_custom_call" | custom-call | tf_op jit(solution)/shard_map/finish/pallas_call | solution.py:323
  (10 shorter events, 0.2 us)
Async XLA Ops:
  0.6 1.0 %copy-start.1 = (f32[4,8,16,128]{3,2,1,0:T(8,128)S(1)}, f32[4,8,16,128]{3,2,1,0:T(8,128)}, u32[]{:S(2)}) copy-start(f32[4,8,16,128]{3,2,1,0:T(8,128)} %own.3) | copy-start | bytes 786436
  1.9 11.7 %collective-permute-start.1 = (f32[20,16,128]{2,1,0:T(8,128)S(1)}, f32[20,16,128]{2,1,0:T(8,128)S(1)}, u32[]{:S(2)}, u32[]{:S(2)}) collective-permute-start(f32[20,16,128]{2,1,0:T(8,128)S(1)} %get-tuple-element.22), channel_id=1, source_target_pairs={{0,1},{1,0},{2,3},{3,2},{4,5},{5,4},{6,7},{7,6},{8,9},{9,8},{10,11... | collective-permute-start | bytes 491528 | tf_op jit(solution)/shard_map/ppermute | solution.py:344
  3.5 6.3 %collective-permute-start = (f32[16,16,128]{2,1,0:T(8,128)S(1)}, f32[16,16,128]{2,1,0:T(8,128)S(1)}, u32[]{:S(2)}, u32[]{:S(2)}) collective-permute-start(f32[16,16,128]{2,1,0:T(8,128)S(1)} %get-tuple-element.27.tiles), channel_id=1, source_target_pairs={{0,0},{2,4},{4,2},{6,6},{1,1},{3,5},{5,3},{7,7},{8,8},{10,12},{12,... | collective-permute-start | bytes 393224 | tf_op jit(solution)/shard_map/ppermute | solution.py:350
  5.4 5.8 %collective-permute-start.2 = (f32[4,16,128]{2,1,0:T(8,128)S(1)}, f32[4,16,128]{2,1,0:T(8,128)S(1)}, u32[]{:S(2)}, u32[]{:S(2)}) collective-permute-start(f32[4,16,128]{2,1,0:T(8,128)S(1)} %get-tuple-element.23), channel_id=1, source_target_pairs={{1,25},{0,8},{9,1},{8,16},{17,9},{16,24},{25,17},{24,0},{3,27},{2,... | collective-permute-start | bytes 98312 | tf_op jit(solution)/shard_map/ppermute | solution.py:368
  7.0 9.0 %copy-start = (bf16[768,1024]{1,0:T(8,128)(2,1)S(1)}, bf16[768,1024]{1,0:T(8,128)(2,1)}, u32[]{:S(2)}) copy-start(bf16[768,1024]{1,0:T(8,128)(2,1)} %constant.2.clone.weights) | copy-start | bytes 4718596
  7.0 6.6 %collective-permute-start.3 = (f32[4,16,128]{2,1,0:T(8,128)S(1)}, f32[4,16,128]{2,1,0:T(8,128)S(1)}, u32[]{:S(2)}, u32[]{:S(2)}) collective-permute-start(f32[4,16,128]{2,1,0:T(8,128)S(1)} %get-tuple-element.24), channel_id=1, source_target_pairs={{0,25},{1,8},{8,1},{9,16},{16,9},{17,24},{24,17},{25,0},{2,27},{3,... | collective-permute-start | bytes 98312 | tf_op jit(solution)/shard_map/ppermute | solution.py:367
  13.7 7.7 %collective-permute-start.4 = (f32[32,16,128]{2,1,0:T(8,128)S(1)}, f32[32,16,128]{2,1,0:T(8,128)S(1)}, u32[]{:S(2)}, u32[]{:S(2)}) collective-permute-start(f32[32,16,128]{2,1,0:T(8,128)S(1)} %get-tuple-element.25.rest), channel_id=1, source_target_pairs={{0,0},{2,4},{4,2},{6,6},{1,1},{3,5},{5,3},{7,7},{8,8},{10,12},{12,... | collective-permute-start | bytes 786440 | tf_op jit(solution)/shard_map/ppermute | solution.py:350
  16.0 1.8 %collective-permute-start.5 = (f32[48,16,128]{2,1,0:T(8,128)S(1)}, f32[48,16,128]{2,1,0:T(8,128)S(1)}, u32[]{:S(2)}, u32[]{:S(2)}) collective-permute-start(f32[48,16,128]{2,1,0:T(8,128)S(1)} %get-tuple-element.26), channel_id=1, source_target_pairs={{0,2},{2,0},{4,6},{6,4},{1,3},{3,1},{5,7},{7,5},{8,10},{10,8},{12,... | collective-permute-start | bytes 1179656 | tf_op jit(solution)/shard_map/ppermute | solution.py:347
  24.5 4.6 %collective-permute-start.8 = (f32[16,128]{1,0:T(8,128)S(1)}, f32[16,128]{1,0:T(8,128)S(1)}, u32[]{:S(2)}, u32[]{:S(2)}) collective-permute-start(f32[16,128]{1,0:T(8,128)S(1)} %get-tuple-element.33), channel_id=1, source_target_pairs={{0,16},{8,24},{16,0},{24,8},{1,17},{9,25},{17,1},{25,9},{2,18},{10... | collective-permute-start | bytes 24584 | tf_op jit(solution)/shard_map/ppermute | solution.py:427
  25.4 5.4 %collective-permute-start.7 = (f32[16,128]{1,0:T(8,128)S(1)}, f32[16,128]{1,0:T(8,128)S(1)}, u32[]{:S(2)}, u32[]{:S(2)}) collective-permute-start(f32[16,128]{1,0:T(8,128)S(1)} %get-tuple-element.33), channel_id=1, source_target_pairs={{0,24},{8,16},{16,8},{24,0},{1,25},{9,17},{17,9},{25,1},{2,26},{10... | collective-permute-start | bytes 24584 | tf_op jit(solution)/shard_map/ppermute | solution.py:427
  26.7 4.1 %collective-permute-start.6 = (f32[16,128]{1,0:T(8,128)S(1)}, f32[16,128]{1,0:T(8,128)S(1)}, u32[]{:S(2)}, u32[]{:S(2)}) collective-permute-start(f32[16,128]{1,0:T(8,128)S(1)} %get-tuple-element.33), channel_id=1, source_target_pairs={{0,8},{8,0},{16,24},{24,16},{1,9},{9,1},{17,25},{25,17},{2,10},{10... | collective-permute-start | bytes 24584 | tf_op jit(solution)/shard_map/ppermute | solution.py:427
  28.1 6.5 %collective-permute-start.10 = (f32[3,8,16,128]{3,2,1,0:T(8,128)S(1)}, f32[3,8,16,128]{3,2,1,0:T(8,128)S(1)}, u32[]{:S(2)}, u32[]{:S(2)}) collective-permute-start(f32[3,8,16,128]{3,2,1,0:T(8,128)S(1)} %get-tuple-element.35), channel_id=1, source_target_pairs={{0,1},{1,0},{2,3},{3,2},{4,5},{5,4},{6,7},{7,6},{8,9},{9,8},{10,11... | collective-permute-start | bytes 589832 | tf_op jit(solution)/shard_map/ppermute | solution.py:344
  30.8 3.7 %collective-permute-start.9 = (f32[16,128]{1,0:T(8,128)S(1)}, f32[16,128]{1,0:T(8,128)S(1)}, u32[]{:S(2)}, u32[]{:S(2)}) collective-permute-start(f32[16,128]{1,0:T(8,128)S(1)} %add_add_fusion), channel_id=1, source_target_pairs={{0,1},{1,0},{2,3},{3,2},{4,5},{5,4},{6,7},{7,6},{8,9},{9,8},{10,11... | collective-permute-start | bytes 24584 | tf_op jit(solution)/shard_map/ppermute | solution.py:344

commit v14 on v11

--- a/solution.py
+++ b/solution.py
@@ -157,10 +157,7 @@
 
 def planes_of(weights, part, high, low):
     cells = weights.shape[1] // 4
-    if part is None:
-        along = slice(0, 2 * cells)
-    else:
-        along = pl.ds(part * cells if isinstance(part, int) else pl.multiple_of(part * cells, cells), cells)
+    along = pl.ds(part * cells if isinstance(part, int) else pl.multiple_of(part * cells, cells), cells)
     plane_h, plane_l = weights[:cells, along], weights[cells : 2 * cells, along]
     return dot(plane_h, high) + dot(plane_l, high) + dot(plane_h, low)
 
@@ -185,22 +182,48 @@
     products[...] = planes_of(weights, 2, prod_h[...], prod_l[...])
 
 
-def mate_kernel(main, outer, upper, lower, weights, raw, partial, in_h, in_l):
+def span_pass(weights, planes, both):
+    cells = planes.shape[0]
+    rows = cells // both
+    width = 128
+    span_w = weights[2 * cells :, : 2 * width]
+    high, low = halves(planes)
+    tiles = planes.shape[1] // width
+    parts = [jnp.concatenate([high[:, column(t)], low[:, column(t)]], axis=1) for t in range(tiles)]
+    result = dot(jnp.concatenate(parts, axis=0), span_w)
+    result = result[:, :width] + result[:, width:]
+    return [result[t * cells : (t + 1) * cells].reshape(both, rows, width) for t in range(tiles)]
+
+
+def second_input(means, high, low):
+    tiles = means + [means[i] * means[3] for i in range(3)]
+    for t, value in enumerate(tiles):
+        high[:, column(t)], low[:, column(t)] = halves(value.reshape(-1, value.shape[-1]))
+
+
+def mate_kernel(
+    main, outer, upper, lower, weights, raw, mean, second, in_h, in_l, mid_h, mid_l
+):
+    both = raw.shape[1]
     odd = lax.rem(lax.axis_index("wall"), 2)
     bring(main, outer, raw, in_h, in_l)
-    base = jnp.where(odd == 1, upper[...], lower[...])
-    partial[...] = base + planes_of(weights, 1 - odd, in_h[...], in_l[...])
+    planes = jnp.where(odd == 1, upper[...], lower[...])
+    planes = planes + planes_of(weights, 1 - odd, in_h[...], in_l[...])
+    means = span_pass(weights, planes, both)
+    for t, value in enumerate(means):
+        mean[t] = value
+    second_input(means, mid_h, mid_l)
+    second[...] = planes_of(weights, 1 - odd, mid_h[...], mid_l[...])
 
 
 def flux_kernel(
-    walls, b_main, b_outer, a_raw, a_partial, upper, lower, products, weights,
+    walls, b_main, b_outer, a_raw, a_mean, a_second, upper, lower, products, weights,
     keep_ref, send_ref, sums_ref,
     raw, in_h, in_l, prod_h, prod_l, mean, mid_h, mid_l, clark_all, similar_all,
 ):
     _, layers, rows, width = keep_ref.shape
     both = 2 * layers
     cells = both * rows
-    span_w = weights.at[2 * cells :, : 2 * width]
     me_s = lax.axis_index("stream")
     me_w = lax.axis_index("wall")
     odd = lax.rem(me_w, 2)
@@ -209,30 +232,22 @@
 
     bring(b_main, b_outer, raw, in_h, in_l, keep_b)
 
-    def along_span_of(planes):
-        high, low = halves(planes)
-        tiles = planes.shape[1] // width
-        parts = [jnp.concatenate([high[:, column(t)], low[:, column(t)]], axis=1) for t in range(tiles)]
-        result = dot(jnp.concatenate(parts, axis=0), span_w[...])
-        result = result[:, :width] + result[:, width:]
-        return [result[t * cells : (t + 1) * cells].reshape(both, rows, width) for t in range(tiles)]
-
     for t in range(4):
         mean[t, 0] = jnp.zeros((2 * rows, width), jnp.float32)
         mean[t, both + 1] = jnp.zeros((2 * rows, width), jnp.float32)
-    from_b = planes_of(weights, odd, in_h[...], in_l[...])
-    from_b += jnp.where(odd == 0, upper[...], lower[...])
-    from_a = a_partial[...]
-    for half in range(2):
-        planes = jnp.where(odd == half, from_b, from_a)
-        row = lax.rem(lax.broadcasted_iota(jnp.int32, planes.shape, 0), rows)
-        if half == 0:
-            inside = (me_w > 0) | (row >= reach)
-        else:
-            inside = (me_w < walls - 1) | (row < rows - reach)
-        planes = jnp.where(inside, planes, 0.0)
-        for t, value in enumerate(along_span_of(planes)):
-            mean[t, 1 : both + 1, half * rows : (half + 1) * rows, :] = value
+    planes = jnp.where(odd == 0, upper[...], lower[...])
+    planes = planes + planes_of(weights, odd, in_h[...], in_l[...])
+    row = lax.rem(lax.broadcasted_iota(jnp.int32, planes.shape, 0), rows)
+    inside = (row < reach) == (odd == 1)
+    planes = jnp.where(jnp.logical_or(inside, jnp.logical_not(at_end)), planes, 0.0)
+    means = span_pass(weights, planes, both)
+    rows_b = pl.ds(pl.multiple_of(odd * rows, rows), rows)
+    rows_a = pl.ds(pl.multiple_of((1 - odd) * rows, rows), rows)
+    for t, value in enumerate(means):
+        mean[t, 1 : both + 1, rows_b, :] = value
+        mean[t, 1 : both + 1, rows_a, :] = a_mean[t]
+    second_input(means, mid_h, mid_l)
+    second = span_pass(weights, a_second[...] + planes_of(weights, odd, mid_h[...], mid_l[...]), both)
 
     def around(f):
         above = jnp.where(odd == 0, raw[f, :, rows - reach :, :], a_raw[f, :, rows - reach :, :])
@@ -243,16 +258,7 @@
     for i in range(3):
         value = (around(i) * temperature).reshape(cells, width)
         prod_h[:, column(i)], prod_l[:, column(i)] = halves(value)
-    flux = along_span_of(products[...] + planes_of(weights, 3, prod_h[...], prod_l[...]))
-
-    for half in range(2):
-        span = slice(half * rows, (half + 1) * rows)
-        down = slice(half * cells, (half + 1) * cells)
-        tiles = [mean[t, 1 : both + 1, span, :].reshape(cells, width) for t in range(4)]
-        tiles += [tiles[i] * tiles[3] for i in range(3)]
-        for t, value in enumerate(tiles):
-            mid_h[down, column(t)], mid_l[down, column(t)] = halves(value)
-    second = along_span_of(planes_of(weights, None, mid_h[...], mid_l[...]))
+    flux = span_pass(weights, products[...] + planes_of(weights, 3, prod_h[...], prod_l[...]), both)
 
     mid_rows = slice(reach, reach + rows)
     centre, along_span, along_wall, along_stream = [], [], [], []
@@ -371,9 +377,9 @@
     part_strip = lax.ppermute(first, ("span", "stream"), to_other)
     own_strip = lax.ppermute(second, ("span", "stream"), to_same)
     (main,) = call(main_kernel, "main", (fields, part), ((2 * both + layers, rows, width),))
-    b_main, a_main = pair_b(main), pair_a(main)
+    a_main, b_main = pair_a(main), pair_b(main)
     (outer,) = call(outer_kernel, "outer", (own_strip, part_strip), ((layers, rows, width),), hint=2**35)
-    b_outer, a_outer = pair_b(outer), pair_a(outer)
+    a_outer, b_outer = pair_a(outer), pair_b(outer)
 
     matrices = np.zeros((2 * cells + 2 * width, 4 * cells), ml_dtypes.bfloat16)
     matrices[:cells], matrices[cells : 2 * cells] = plane_constants(both, rows)
@@ -391,19 +397,19 @@
         mib=16,
         hint=2**29,
     )
-    a_raw, a_partial = call(
+    a_raw, a_mean, a_second = call(
         mate_kernel,
         "mate",
         (a_main, a_outer, upper, lower, weights),
-        (block, (cells, 4 * width)),
-        pieces,
+        (block, block, (cells, 7 * width)),
+        [*pieces, ((cells, 7 * width), brief), ((cells, 7 * width), brief)],
         mib=16,
         hint=2**29,
     )
     keep, send, sums = call(
         functools.partial(flux_kernel, walls),
         "flux",
-        (b_main, b_outer, a_raw, a_partial, upper, lower, products, weights),
+        (b_main, b_outer, a_raw, a_mean, a_second, upper, lower, products, weights),
         ((6, layers, rows, width), (3, layers, rows, width), (rows, width)),
         [
             (block, single),
@@ -412,8 +418,8 @@
             ((cells, 3 * width), brief),
             ((cells, 3 * width), brief),
             ((4, both + 2, 2 * rows, width), single),
-            ((2 * cells, 7 * width), brief),
-            ((2 * cells, 7 * width), brief),
+            ((cells, 7 * width), brief),
+            ((cells, 7 * width), brief),
             ((3, both, rows, width), single),
             ((3, both, rows, width), single),
         ],
@@ -427,13 +433,11 @@
 
     step = 1
     while step < spans:
-        near = from_span(sums, step)
         if 2 * step < spans:
-            far = [from_span(sums, 2 * step), from_span(sums, 3 * step)]
-            near, far, come = lax.optimization_barrier((near, far, come))
-            sums = (sums + near) + (far[0] + far[1])
+            far = from_span(sums, 3 * step) + from_span(sums, 2 * step)
+            sums = (sums + from_span(sums, step)) + far
         else:
-            sums = sums + near
+            sums = sums + from_span(sums, step)
         step *= 4
     sums = sums + swap(sums)
     block, corr = (3, layers, rows, width), (3, rows)

time: 35.4 us -> 34.2 us (0.966)
  the two profiles are of different devices: /device:TPU:4 before, /device:TPU:6 now
where the time goes in v14:
time: 34.2 us; the launch traced here: 34 us
  starting transfers between devices  15.8 us (46%)
  waiting for transfers between devices  8.93 us (26%)
  Pallas kernels  7.55 us (22%)
  local copies, waits for them, and re-layouts  0.95 us (3%)
  between operations  0.76 us (2%)
    pallas_call x7, Pallas kernels, call(): pl.pallas_call(kernel, out_shape=tuple((jax.ShapeDtypeStruct(shape, jnp.f...  7.55 us
    ppermute x2, starting transfers between devices, pair_b(): lax.ppermute(value, 'wall', [(w, min(max((w + 1 ^ 1) - 1, 0), walls - 1))...  5.48 us
    ppermute x3, waiting for transfers between devices, swap(): return lax.ppermute(value, 'stream', [(0, 1), (1, 0)])  4.96 us
    ppermute x3, starting transfers between devices, from_span(): return lax.ppermute(value, 'span', [(p, p ^ step) for p in range(spans)])  4.7 us
    ppermute x1, starting transfers between devices, shards(): own_strip = lax.ppermute(second, ('span', 'stream'), to_same)  3.6 us
    ppermute x3, waiting for transfers between devices, from_span(): return lax.ppermute(value, 'span', [(p, p ^ step) for p in range(spans)])  3.35 us
    ppermute x3, starting transfers between devices, swap(): return lax.ppermute(value, 'stream', [(0, 1), (1, 0)])  1.42 us
    unnamed x4, local copies, waits for them, and re-layouts  0.95 us
  transfers between devices with their start and end apart: 12, of which 5 were waited for; matrix products, arithmetic and copies ran while one was open for 0% of the time, Pallas kernels for 9%

profile of v14, /device:TPU:6, one launch (start us, length us, event | category | flops | bytes accessed | tf_op | source)
XLA Modules:
  0.0 34.0 jit_solution(1675032180086620902)
XLA Ops:
  0.6 0.9 %copy-done.1 = f32[4,8,16,128]{3,2,1,0:T(8,128)S(1)} copy-done((f32[4,8,16,128]{3,2,1,0:T(8,128)S(1)}, f32[4,8,16,128]{3,2,1,0:T(8,128)}, u32[]{:S(2)}) %copy-start.1) | copy-done | bytes 262168
  1.6 0.3 pack.1
  1.9 0.6 %collective-permute-start = (f32[20,16,128]{2,1,0:T(8,128)S(1)}, f32[20,16,128]{2,1,0:T(8,128)S(1)}, u32[]{:S(2)}, u32[]{:S(2)}) collective-permute-start(f32[20,16,128]{2,1,0:T(8,128)S(1)} %get-tuple-element.16), channel_id=1, source_target_pairs={{0,1},{1,0},{2,3},{3,2},{4,5},{5,4},{6,7},{7,6},{8,9},{9,8},{10,11... | collective-permute-start | bytes 491528 | tf_op jit(solution)/shard_map/ppermute | solution.py:354
  2.5 3.6 %collective-permute-start.2 = (f32[4,16,128]{2,1,0:T(8,128)S(1)}, f32[4,16,128]{2,1,0:T(8,128)S(1)}, u32[]{:S(2)}, u32[]{:S(2)}) collective-permute-start(f32[4,16,128]{2,1,0:T(8,128)S(1)} %get-tuple-element.17), channel_id=1, source_target_pairs={{1,25},{0,8},{9,1},{8,16},{17,9},{16,24},{25,17},{24,0},{3,27},{2,... | collective-permute-start | bytes 98312 | tf_op jit(solution)/shard_map/ppermute | solution.py:378
  6.1 0.5 %collective-permute-start.3 = (f32[4,16,128]{2,1,0:T(8,128)S(1)}, f32[4,16,128]{2,1,0:T(8,128)S(1)}, u32[]{:S(2)}, u32[]{:S(2)}) collective-permute-start(f32[4,16,128]{2,1,0:T(8,128)S(1)} %get-tuple-element.18), channel_id=1, source_target_pairs={{0,25},{1,8},{8,1},{9,16},{16,9},{17,24},{24,17},{25,0},{2,27},{3,... | collective-permute-start | bytes 98312 | tf_op jit(solution)/shard_map/ppermute | solution.py:377
  6.5 1.3 %collective-permute-done.part = f32[20,16,128]{2,1,0:T(8,128)S(1)} collective-permute-done((f32[20,16,128]{2,1,0:T(8,128)S(1)}, f32[20,16,128]{2,1,0:T(8,128)S(1)}, u32[]{:S(2)}, u32[]{:S(2)}) %collective-permute-start) | collective-permute-done | bytes 163872 | tf_op jit(solution)/shard_map/ppermute | solution.py:354
  7.9 0.2 main.1
  8.0 0.0 copy-start
  8.0 0.1 collective-permute-start.5
  8.1 2.5 %collective-permute-start.1 = (f32[40,16,128]{2,1,0:T(8,128)S(1)}, f32[40,16,128]{2,1,0:T(8,128)S(1)}, u32[]{:S(2)}, u32[]{:S(2)}) collective-permute-start(f32[40,16,128]{2,1,0:T(8,128)S(1)} %main.1), channel_id=1, source_target_pairs={{0,0},{2,4},{4,2},{6,6},{1,1},{3,5},{5,3},{7,7},{8,8},{10,12},{12,... | collective-permute-start | bytes 983048 | tf_op jit(solution)/shard_map/ppermute | solution.py:360
  10.6 0.2 collective-permute-done.3.part_strip
  10.9 0.1 collective-permute-start.6
  11.0 3.0 %collective-permute-start.4 = (f32[8,16,128]{2,1,0:T(8,128)S(1)}, f32[8,16,128]{2,1,0:T(8,128)S(1)}, u32[]{:S(2)}, u32[]{:S(2)}) collective-permute-start(f32[8,16,128]{2,1,0:T(8,128)S(1)} %outer.1), channel_id=1, source_target_pairs={{0,0},{2,4},{4,2},{6,6},{1,1},{3,5},{5,3},{7,7},{8,8},{10,12},{12,... | collective-permute-start | bytes 196616 | tf_op jit(solution)/shard_map/ppermute | solution.py:360
  14.0 1.1 %centre.1 = (f32[256,512]{1,0:T(8,128)S(1)}, f32[256,512]{1,0:T(8,128)S(1)}, f32[256,384]{1,0:T(8,128)S(1)}) custom-call(f32[40,16,128]{2,1,0:T(8,128)S(1)} %main.1, f32[8,16,128]{2,1,0:T(8,128)S(1)} %outer.1, bf16[768,1024]{1,0:T(8,128)(2,1)S(1)} %copy-done), custom_call_target="tpu_custom_call" | custom-call | flops 536870912 | tf_op jit(solution)/shard_map/centre/pallas_call | solution.py:333
  15.1 1.9 %mate.1 = (f32[4,16,16,128]{3,2,1,0:T(8,128)S(1)}, f32[4,16,16,128]{3,2,1,0:T(8,128)S(1)}, f32[256,896]{1,0:T(8,128)S(1)}) custom-call(f32[40,16,128]{2,1,0:T(8,128)S(1)} %collective-permute-done.5.main, f32[8,16,128]{2,1,0:T(8,128)S(1)} %collective-permute-done.6.outer, f32[256,512]{1,0:T(8,128)S(1)} %get-tuple-element.19.upper, ...), custom_call_target="tpu_custom_call" | custom-call | flops 536870912 | tf_op jit(solution)/shard_map/mate/pallas_call | solution.py:333
  17.0 0.4 %collective-permute-done.4.b_outer = f32[8,16,128]{2,1,0:T(8,128)S(1)} collective-permute-done((f32[8,16,128]{2,1,0:T(8,128)S(1)}, f32[8,16,128]{2,1,0:T(8,128)S(1)}, u32[]{:S(2)}, u32[]{:S(2)}) %collective-permute-start.4) | collective-permute-done | bytes 65568 | tf_op jit(solution)/shard_map/ppermute | solution.py:360
  17.4 3.1 %flux.1 = (f32[6,8,16,128]{3,2,1,0:T(8,128)S(1)}, f32[3,8,16,128]{3,2,1,0:T(8,128)S(1)}, f32[16,128]{1,0:T(8,128)S(1)}) custom-call(f32[40,16,128]{2,1,0:T(8,128)S(1)} %collective-permute-done.1.b_main, f32[8,16,128]{2,1,0:T(8,128)S(1)} %collective-permute-done.4.b_outer, f32[4,16,16,128]{3,2,1,0:T(8,128)S(1)} %get-tuple-element.21.a_raw, ...), custom_call_target="tpu_custom_call" | custom-call | tf_op jit(solution)/shard_map/flux/pallas_call | solution.py:333
  20.5 3.4 %collective-permute-start.9 = (f32[16,128]{1,0:T(8,128)S(1)}, f32[16,128]{1,0:T(8,128)S(1)}, u32[]{:S(2)}, u32[]{:S(2)}) collective-permute-start(f32[16,128]{1,0:T(8,128)S(1)} %get-tuple-element.25), channel_id=1, source_target_pairs={{0,16},{8,24},{16,0},{24,8},{1,17},{9,25},{17,1},{25,9},{2,18},{10... | collective-permute-start | bytes 24584 | tf_op jit(solution)/shard_map/ppermute | solution.py:432
  23.8 1.3 %collective-permute-start.8 = (f32[16,128]{1,0:T(8,128)S(1)}, f32[16,128]{1,0:T(8,128)S(1)}, u32[]{:S(2)}, u32[]{:S(2)}) collective-permute-start(f32[16,128]{1,0:T(8,128)S(1)} %get-tuple-element.25), channel_id=1, source_target_pairs={{0,24},{8,16},{16,8},{24,0},{1,25},{9,17},{17,9},{25,1},{2,26},{10... | collective-permute-start | bytes 24584 | tf_op jit(solution)/shard_map/ppermute | solution.py:432
  25.2 0.8 %collective-permute-start.11 = (f32[3,8,16,128]{3,2,1,0:T(8,128)S(1)}, f32[3,8,16,128]{3,2,1,0:T(8,128)S(1)}, u32[]{:S(2)}, u32[]{:S(2)}) collective-permute-start(f32[3,8,16,128]{3,2,1,0:T(8,128)S(1)} %get-tuple-element.27), channel_id=1, source_target_pairs={{0,1},{1,0},{2,3},{3,2},{4,5},{5,4},{6,7},{7,6},{8,9},{9,8},{10,11... | collective-permute-start | bytes 589832 | tf_op jit(solution)/shard_map/ppermute | solution.py:354
  25.9 3.3 %collective-permute-done.8 = f32[16,128]{1,0:T(8,128)S(1)} collective-permute-done((f32[16,128]{1,0:T(8,128)S(1)}, f32[16,128]{1,0:T(8,128)S(1)}, u32[]{:S(2)}, u32[]{:S(2)}) %collective-permute-start.8) | collective-permute-done | bytes 8224 | tf_op jit(solution)/shard_map/ppermute | solution.py:432
  29.3 0.1 collective-permute-start.10
  29.4 3.6 %collective-permute-done.10 = f32[16,128]{1,0:T(8,128)S(1)} collective-permute-done((f32[16,128]{1,0:T(8,128)S(1)}, f32[16,128]{1,0:T(8,128)S(1)}, u32[]{:S(2)}, u32[]{:S(2)}) %collective-permute-start.10) | collective-permute-done | bytes 8224 | tf_op jit(solution)/shard_map/ppermute | solution.py:354
  33.0 1.0 %finish.1 = (f32[3,8,16,128]{3,2,1,0:T(8,128)}, f32[3,8,16,128]{3,2,1,0:T(8,128)}, f32[3,16]{1,0:T(4,128)}, f32[3,16]{1,0:T(4,128)}) custom-call(f32[16,128]{1,0:T(8,128)S(1)} %add.15.sums, f32[6,8,16,128]{3,2,1,0:T(8,128)S(1)} %get-tuple-element.26.keep, f32[3,8,16,128]{3,2,1,0:T(8,128)S(1)} %collective-permute-done.11.come), custom_call_target="tpu_custom_call" | custom-call | tf_op jit(solution)/shard_map/finish/pallas_call | solution.py:333
  (13 shorter events, 0.0 us)
Async XLA Ops:
  0.6 1.0 %copy-start.1 = (f32[4,8,16,128]{3,2,1,0:T(8,128)S(1)}, f32[4,8,16,128]{3,2,1,0:T(8,128)}, u32[]{:S(2)}) copy-start(f32[4,8,16,128]{3,2,1,0:T(8,128)} %own.3) | copy-start | bytes 786436
  1.9 6.0 %collective-permute-start = (f32[20,16,128]{2,1,0:T(8,128)S(1)}, f32[20,16,128]{2,1,0:T(8,128)S(1)}, u32[]{:S(2)}, u32[]{:S(2)}) collective-permute-start(f32[20,16,128]{2,1,0:T(8,128)S(1)} %get-tuple-element.16), channel_id=1, source_target_pairs={{0,1},{1,0},{2,3},{3,2},{4,5},{5,4},{6,7},{7,6},{8,9},{9,8},{10,11... | collective-permute-start | bytes 491528 | tf_op jit(solution)/shard_map/ppermute | solution.py:354
  2.5 8.2 %collective-permute-start.2 = (f32[4,16,128]{2,1,0:T(8,128)S(1)}, f32[4,16,128]{2,1,0:T(8,128)S(1)}, u32[]{:S(2)}, u32[]{:S(2)}) collective-permute-start(f32[4,16,128]{2,1,0:T(8,128)S(1)} %get-tuple-element.17), channel_id=1, source_target_pairs={{1,25},{0,8},{9,1},{8,16},{17,9},{16,24},{25,17},{24,0},{3,27},{2,... | collective-permute-start | bytes 98312 | tf_op jit(solution)/shard_map/ppermute | solution.py:378
  6.1 4.8 %collective-permute-start.3 = (f32[4,16,128]{2,1,0:T(8,128)S(1)}, f32[4,16,128]{2,1,0:T(8,128)S(1)}, u32[]{:S(2)}, u32[]{:S(2)}) collective-permute-start(f32[4,16,128]{2,1,0:T(8,128)S(1)} %get-tuple-element.18), channel_id=1, source_target_pairs={{0,25},{1,8},{8,1},{9,16},{16,9},{17,24},{24,17},{25,0},{2,27},{3,... | collective-permute-start | bytes 98312 | tf_op jit(solution)/shard_map/ppermute | solution.py:377
  8.0 5.9 %copy-start = (bf16[768,1024]{1,0:T(8,128)(2,1)S(1)}, bf16[768,1024]{1,0:T(8,128)(2,1)}, u32[]{:S(2)}) copy-start(bf16[768,1024]{1,0:T(8,128)(2,1)} %constant.2.clone.weights) | copy-start | bytes 4718596
  8.0 7.0 %collective-permute-start.5 = (f32[40,16,128]{2,1,0:T(8,128)S(1)}, f32[40,16,128]{2,1,0:T(8,128)S(1)}, u32[]{:S(2)}, u32[]{:S(2)}) collective-permute-start(f32[40,16,128]{2,1,0:T(8,128)S(1)} %main.1), channel_id=1, source_target_pairs={{0,2},{2,0},{4,6},{6,4},{1,3},{3,1},{5,7},{7,5},{8,10},{10,8},{12,... | collective-permute-start | bytes 983048 | tf_op jit(solution)/shard_map/ppermute | solution.py:357
  8.1 9.2 %collective-permute-start.1 = (f32[40,16,128]{2,1,0:T(8,128)S(1)}, f32[40,16,128]{2,1,0:T(8,128)S(1)}, u32[]{:S(2)}, u32[]{:S(2)}) collective-permute-start(f32[40,16,128]{2,1,0:T(8,128)S(1)} %main.1), channel_id=1, source_target_pairs={{0,0},{2,4},{4,2},{6,6},{1,1},{3,5},{5,3},{7,7},{8,8},{10,12},{12,... | collective-permute-start | bytes 983048 | tf_op jit(solution)/shard_map/ppermute | solution.py:360
  10.9 4.2 %collective-permute-start.6 = (f32[8,16,128]{2,1,0:T(8,128)S(1)}, f32[8,16,128]{2,1,0:T(8,128)S(1)}, u32[]{:S(2)}, u32[]{:S(2)}) collective-permute-start(f32[8,16,128]{2,1,0:T(8,128)S(1)} %outer.1), channel_id=1, source_target_pairs={{0,2},{2,0},{4,6},{6,4},{1,3},{3,1},{5,7},{7,5},{8,10},{10,8},{12,... | collective-permute-start | bytes 196616 | tf_op jit(solution)/shard_map/ppermute | solution.py:357
  11.0 6.4 %collective-permute-start.4 = (f32[8,16,128]{2,1,0:T(8,128)S(1)}, f32[8,16,128]{2,1,0:T(8,128)S(1)}, u32[]{:S(2)}, u32[]{:S(2)}) collective-permute-start(f32[8,16,128]{2,1,0:T(8,128)S(1)} %outer.1), channel_id=1, source_target_pairs={{0,0},{2,4},{4,2},{6,6},{1,1},{3,5},{5,3},{7,7},{8,8},{10,12},{12,... | collective-permute-start | bytes 196616 | tf_op jit(solution)/shard_map/ppermute | solution.py:360
  20.5 5.5 %collective-permute-start.9 = (f32[16,128]{1,0:T(8,128)S(1)}, f32[16,128]{1,0:T(8,128)S(1)}, u32[]{:S(2)}, u32[]{:S(2)}) collective-permute-start(f32[16,128]{1,0:T(8,128)S(1)} %get-tuple-element.25), channel_id=1, source_target_pairs={{0,16},{8,24},{16,0},{24,8},{1,17},{9,25},{17,1},{25,9},{2,18},{10... | collective-permute-start | bytes 24584 | tf_op jit(solution)/shard_map/ppermute | solution.py:432
  23.8 5.4 %collective-permute-start.8 = (f32[16,128]{1,0:T(8,128)S(1)}, f32[16,128]{1,0:T(8,128)S(1)}, u32[]{:S(2)}, u32[]{:S(2)}) collective-permute-start(f32[16,128]{1,0:T(8,128)S(1)} %get-tuple-element.25), channel_id=1, source_target_pairs={{0,24},{8,16},{16,8},{24,0},{1,25},{9,17},{17,9},{25,1},{2,26},{10... | collective-permute-start | bytes 24584 | tf_op jit(solution)/shard_map/ppermute | solution.py:432
  25.2 4.1 %collective-permute-start.7 = (f32[16,128]{1,0:T(8,128)S(1)}, f32[16,128]{1,0:T(8,128)S(1)}, u32[]{:S(2)}, u32[]{:S(2)}) collective-permute-start(f32[16,128]{1,0:T(8,128)S(1)} %get-tuple-element.25), channel_id=1, source_target_pairs={{0,8},{8,0},{16,24},{24,16},{1,9},{9,1},{17,25},{25,17},{2,10},{10... | collective-permute-start | bytes 24584 | tf_op jit(solution)/shard_map/ppermute | solution.py:432
  25.2 7.8 %collective-permute-start.11 = (f32[3,8,16,128]{3,2,1,0:T(8,128)S(1)}, f32[3,8,16,128]{3,2,1,0:T(8,128)S(1)}, u32[]{:S(2)}, u32[]{:S(2)}) collective-permute-start(f32[3,8,16,128]{3,2,1,0:T(8,128)S(1)} %get-tuple-element.27), channel_id=1, source_target_pairs={{0,1},{1,0},{2,3},{3,2},{4,5},{5,4},{6,7},{7,6},{8,9},{9,8},{10,11... | collective-permute-start | bytes 589832 | tf_op jit(solution)/shard_map/ppermute | solution.py:354
  29.3 3.7 %collective-permute-start.10 = (f32[16,128]{1,0:T(8,128)S(1)}, f32[16,128]{1,0:T(8,128)S(1)}, u32[]{:S(2)}, u32[]{:S(2)}) collective-permute-start(f32[16,128]{1,0:T(8,128)S(1)} %add_add_fusion), channel_id=1, source_target_pairs={{0,1},{1,0},{2,3},{3,2},{4,5},{5,4},{6,7},{7,6},{8,9},{9,8},{10,11... | collective-permute-start | bytes 24584 | tf_op jit(solution)/shard_map/ppermute | solution.py:354

commit v15 on v14

--- a/solution.py
+++ b/solution.py
@@ -102,53 +102,45 @@
         yield k, jnp.where(is_outer, pieces[1], pieces[0])
 
 
-def pack_kernel(own, to_partner, to_other, to_same):
+def pack_kernel(own, to_partner, to_mine, to_other, to_same):
     _, layers, _, _ = own.shape
     me_s = lax.axis_index("stream")
-    for pair, tile in pack_halves(own, 1 - me_s):
-        to_partner[pair * layers : (pair + 1) * layers] = tile
-    to_partner[2 * layers :] = pack_strip(own, 3 + me_s)
+    for message, half in ((to_partner, 1 - me_s), (to_mine, me_s)):
+        for pair, tile in pack_halves(own, half):
+            message[pair * layers : (pair + 1) * layers] = tile
+        message[2 * layers :] = pack_strip(own, 4 - half)
     to_other[...] = pack_strip(own, 7 * me_s)
     to_same[...] = pack_strip(own, 7 * (1 - me_s))
 
 
-def main_kernel(own, part, packed):
-    _, layers, _, _ = own.shape
-    both = 2 * layers
-    half = layers // 2
-    me_s = lax.axis_index("stream")
-    mine, other = me_s * layers, (1 - me_s) * layers
-    for pair, tile in pack_halves(own, me_s):
-        packed[pl.ds(pair * both + mine, layers)] = tile
-        packed[pl.ds(pair * both + other, layers)] = part[pair * layers : (pair + 1) * layers]
-    packed[pl.ds(2 * both + me_s * half, half)] = pack_strip(own, 4 - me_s)
-    packed[pl.ds(2 * both + (1 - me_s) * half, half)] = part[2 * layers :]
-
-
 def outer_kernel(own_strip, part_strip, outer):
     half = own_strip.shape[0]
-    me_s = lax.axis_index("stream")
-    outer[pl.ds(me_s * half, half)] = own_strip[...]
-    outer[pl.ds((1 - me_s) * half, half)] = part_strip[...]
-
-
-def unpack(packed, outer, me_s):
+    outer[:half] = own_strip[...]
+    outer[half:] = part_strip[...]
+
+
+def join_kernel(mine, part, whole):
+    count = mine.shape[0]
+    whole[:count] = mine[...]
+    whole[count:] = part[...]
+
+
+def unpack(mine, part, outer, me_s):
     layers, rows, width = outer.shape
-    both = 2 * layers
     half = layers // 2
     unit = unit_index((half, rows, width))
     first = 4 * (1 - me_s)
     in_strip = (unit == first) | (unit == first + 3)
-    for s in range(2):
-        inner = packed[2 * both + s * half : 2 * both + (s + 1) * half]
-        for k, strip in strip_tile(inner, outer[s * half : (s + 1) * half], me_s):
-            layer = s * layers + k * half
+    for which, packed in enumerate((mine, part)):
+        far = outer[which * half : (which + 1) * half]
+        for k, strip in strip_tile(packed[2 * layers :], far, me_s):
+            layer = (me_s if which == 0 else 1 - me_s) * layers + k * half
             for f in range(4):
-                start = f // 2 * both + layer
+                start = f // 2 * layers + k * half
                 cells = packed[start : start + half]
                 cells = pltpu.roll(cells, width // 2, 2) if f % 2 else cells
                 moved = pltpu.roll(strip, width - 2 * f * rim, 2) if f else strip
-                yield f, slice(layer, layer + half), jnp.where(in_strip, moved, cells)
+                yield f, layer, jnp.where(in_strip, moved, cells)
 
 
 def column(t, width=128):
@@ -162,18 +154,19 @@
     return dot(plane_h, high) + dot(plane_l, high) + dot(plane_h, low)
 
 
-def bring(packed, outer, raw, high, low, keep=None):
-    rows, width = packed.shape[1:]
-    for f, along, value in unpack(packed, outer, lax.axis_index("stream")):
+def bring(mine, part, outer, raw, high, low, keep=None):
+    rows, width = outer.shape[1:]
+    for f, layer, value in unpack(mine, part, outer, lax.axis_index("stream")):
+        count = value.shape[0]
         value = value if keep is None else value * keep
-        raw[f, along] = value
-        down = slice(along.start * rows, along.stop * rows)
+        raw[f, pl.ds(layer, count)] = value
+        down = pl.ds(pl.multiple_of(layer * rows, count * rows), count * rows)
         high[down, column(f)], low[down, column(f)] = halves(value.reshape(-1, width))
 
 
-def centre_kernel(main, outer, weights, upper, lower, products, centre, in_h, in_l, prod_h, prod_l):
-    cells, width = in_h.shape[0], main.shape[-1]
-    bring(main, outer, centre, in_h, in_l)
+def centre_kernel(mine, part, outer, weights, upper, lower, products, centre, in_h, in_l, prod_h, prod_l):
+    cells, width = in_h.shape[0], outer.shape[-1]
+    bring(mine, part, outer, centre, in_h, in_l)
     for i in range(3):
         value = (centre[i] * centre[3]).reshape(cells, width)
         prod_h[:, column(i)], prod_l[:, column(i)] = halves(value)
@@ -202,11 +195,12 @@
 
 
 def mate_kernel(
-    main, outer, upper, lower, weights, raw, mean, second, in_h, in_l, mid_h, mid_l
+    whole, outer, upper, lower, weights, raw, mean, second, in_h, in_l, mid_h, mid_l
 ):
     both = raw.shape[1]
     odd = lax.rem(lax.axis_index("wall"), 2)
-    bring(main, outer, raw, in_h, in_l)
+    count = whole.shape[0] // 2
+    bring(whole.at[:count], whole.at[count:], outer, raw, in_h, in_l)
     planes = jnp.where(odd == 1, upper[...], lower[...])
     planes = planes + planes_of(weights, 1 - odd, in_h[...], in_l[...])
     means = span_pass(weights, planes, both)
@@ -217,7 +211,7 @@
 
 
 def flux_kernel(
-    walls, b_main, b_outer, a_raw, a_mean, a_second, upper, lower, products, weights,
+    walls, b_mine, b_part, b_outer, a_raw, a_mean, a_second, upper, lower, products, weights,
     keep_ref, send_ref, sums_ref,
     raw, in_h, in_l, prod_h, prod_l, mean, mid_h, mid_l, clark_all, similar_all,
 ):
@@ -230,7 +224,7 @@
     at_end = (me_w == 0) | (me_w == walls - 1)
     keep_b = jnp.where(at_end, 0.0, 1.0).astype(jnp.float32)
 
-    bring(b_main, b_outer, raw, in_h, in_l, keep_b)
+    bring(b_mine, b_part, b_outer, raw, in_h, in_l, keep_b)
 
     for t in range(4):
         mean[t, 0] = jnp.zeros((2 * rows, width), jnp.float32)
@@ -369,15 +363,16 @@
         to_other += [(place(p, 0), place(p - 1, 1)), (place(p, 1), place(p + 1, 0))]
         to_same += [(place(p, 1), place(p - 1, 1)), (place(p, 0), place(p + 1, 0))]
 
-    strip = (layers // 2, rows, width)
-    to_partner, first, second = call(
-        pack_kernel, "pack", (fields,), ((2 * layers + layers // 2, rows, width), strip, strip)
+    message, strip = (2 * layers + layers // 2, rows, width), (layers // 2, rows, width)
+    to_partner, mine, first, second = call(
+        pack_kernel, "pack", (fields,), (message, message, strip, strip)
     )
     part = swap(to_partner)
     part_strip = lax.ppermute(first, ("span", "stream"), to_other)
     own_strip = lax.ppermute(second, ("span", "stream"), to_same)
-    (main,) = call(main_kernel, "main", (fields, part), ((2 * both + layers, rows, width),))
-    a_main, b_main = pair_a(main), pair_b(main)
+    (whole,) = call(join_kernel, "join", (mine, part), ((2 * message[0], rows, width),))
+    a_whole, b_part = pair_a(whole), pair_b(part)
+    mine_now, b_mine = lax.optimization_barrier((mine, pair_b(mine)))
     (outer,) = call(outer_kernel, "outer", (own_strip, part_strip), ((layers, rows, width),), hint=2**35)
     a_outer, b_outer = pair_a(outer), pair_b(outer)
 
@@ -391,7 +386,7 @@
     upper, lower, products = call(
         centre_kernel,
         "centre",
-        (main, outer, weights),
+        (mine_now, part, outer, weights),
         ((cells, 4 * width), (cells, 4 * width), (cells, 3 * width)),
         [(block, single), *pieces, ((cells, 3 * width), brief), ((cells, 3 * width), brief)],
         mib=16,
@@ -400,7 +395,7 @@
     a_raw, a_mean, a_second = call(
         mate_kernel,
         "mate",
-        (a_main, a_outer, upper, lower, weights),
+        (a_whole, a_outer, upper, lower, weights),
         (block, block, (cells, 7 * width)),
         [*pieces, ((cells, 7 * width), brief), ((cells, 7 * width), brief)],
         mib=16,
@@ -409,7 +404,7 @@
     keep, send, sums = call(
         functools.partial(flux_kernel, walls),
         "flux",
-        (b_main, b_outer, a_raw, a_mean, a_second, upper, lower, products, weights),
+        (b_mine, b_part, b_outer, a_raw, a_mean, a_second, upper, lower, products, weights),
         ((6, layers, rows, width), (3, layers, rows, width), (rows, width)),
         [
             (block, single),

time: 34.2 us -> 34.6 us (1.012)
  the two profiles are of different devices: /device:TPU:6 before, /device:TPU:4 now
where the time goes in v15:
time: 34.6 us; the launch traced here: 34.4 us
  starting transfers between devices  18.6 us (54%)
  Pallas kernels  7.39 us (21%)
  waiting for transfers between devices  6.73 us (19%)
  local copies, waits for them, and re-layouts  0.95 us (3%)
  between operations  0.79 us (2%)
    ppermute x3, starting transfers between devices, pair_b(): lax.ppermute(value, 'wall', [(w, min(max((w + 1 ^ 1) - 1, 0), walls - 1))...  7.6 us
    pallas_call x7, Pallas kernels, call(): pl.pallas_call(kernel, out_shape=tuple((jax.ShapeDtypeStruct(shape, jnp.f...  7.39 us
    ppermute x3, starting transfers between devices, from_span(): return lax.ppermute(value, 'span', [(p, p ^ step) for p in range(spans)])  4.01 us
    ppermute x3, waiting for transfers between devices, swap(): return lax.ppermute(value, 'stream', [(0, 1), (1, 0)])  3.03 us
    ppermute x3, waiting for transfers between devices, from_span(): return lax.ppermute(value, 'span', [(p, p ^ step) for p in range(spans)])  3.03 us
    ppermute x3, starting transfers between devices, swap(): return lax.ppermute(value, 'stream', [(0, 1), (1, 0)])  2.8 us
    ppermute x1, starting transfers between devices, shards(): part_strip = lax.ppermute(first, ('span', 'stream'), to_other)  2.45 us
    ppermute x1, starting transfers between devices, shards(): own_strip = lax.ppermute(second, ('span', 'stream'), to_same)  1.58 us
  transfers between devices with their start and end apart: 13, of which 4 were waited for; matrix products, arithmetic and copies ran while one was open for 0% of the time, Pallas kernels for 9%

profile of v15, /device:TPU:4, one launch (start us, length us, event | category | flops | bytes accessed | tf_op | source)
XLA Modules:
  0.0 34.4 jit_solution(9812397359832786560)
XLA Ops:
  0.6 0.9 %copy-done.1 = f32[4,8,16,128]{3,2,1,0:T(8,128)S(1)} copy-done((f32[4,8,16,128]{3,2,1,0:T(8,128)S(1)}, f32[4,8,16,128]{3,2,1,0:T(8,128)}, u32[]{:S(2)}) %copy-start.1) | copy-done | bytes 262168
  1.6 0.4 %pack.1 = (f32[20,16,128]{2,1,0:T(8,128)S(1)}, f32[20,16,128]{2,1,0:T(8,128)S(1)}, f32[4,16,128]{2,1,0:T(8,128)S(1)}, f32[4,16,128]{2,1,0:T(8,128)S(1)}) custom-call(f32[4,8,16,128]{3,2,1,0:T(8,128)S(1)} %copy-done.1), custom_call_target="tpu_custom_call" | custom-call | tf_op jit(solution)/shard_map/pack/pallas_call | solution.py:327
  2.0 1.6 %collective-permute-start.1 = (f32[20,16,128]{2,1,0:T(8,128)S(1)}, f32[20,16,128]{2,1,0:T(8,128)S(1)}, u32[]{:S(2)}, u32[]{:S(2)}) collective-permute-start(f32[20,16,128]{2,1,0:T(8,128)S(1)} %get-tuple-element.21), channel_id=1, source_target_pairs={{0,1},{1,0},{2,3},{3,2},{4,5},{5,4},{6,7},{7,6},{8,9},{9,8},{10,11... | collective-permute-start | bytes 491528 | tf_op jit(solution)/shard_map/ppermute | solution.py:348
  3.5 1.6 %collective-permute-start.3 = (f32[4,16,128]{2,1,0:T(8,128)S(1)}, f32[4,16,128]{2,1,0:T(8,128)S(1)}, u32[]{:S(2)}, u32[]{:S(2)}) collective-permute-start(f32[4,16,128]{2,1,0:T(8,128)S(1)} %get-tuple-element.22), channel_id=1, source_target_pairs={{1,25},{0,8},{9,1},{8,16},{17,9},{16,24},{25,17},{24,0},{3,27},{2,... | collective-permute-start | bytes 98312 | tf_op jit(solution)/shard_map/ppermute | solution.py:372
  5.1 2.4 %collective-permute-start.4 = (f32[4,16,128]{2,1,0:T(8,128)S(1)}, f32[4,16,128]{2,1,0:T(8,128)S(1)}, u32[]{:S(2)}, u32[]{:S(2)}) collective-permute-start(f32[4,16,128]{2,1,0:T(8,128)S(1)} %get-tuple-element.23), channel_id=1, source_target_pairs={{0,25},{1,8},{8,1},{9,16},{16,9},{17,24},{24,17},{25,0},{2,27},{3,... | collective-permute-start | bytes 98312 | tf_op jit(solution)/shard_map/ppermute | solution.py:371
  7.5 1.9 %collective-permute-start = (f32[20,16,128]{2,1,0:T(8,128)S(1)}, f32[20,16,128]{2,1,0:T(8,128)S(1)}, u32[]{:S(2)}, u32[]{:S(2)}) collective-permute-start(f32[20,16,128]{2,1,0:T(8,128)S(1)} %get-tuple-element.24.mine), channel_id=1, source_target_pairs={{0,0},{2,4},{4,2},{6,6},{1,1},{3,5},{5,3},{7,7},{8,8},{10,12},{12,... | collective-permute-start | bytes 491528 | tf_op jit(solution)/shard_map/ppermute | solution.py:354
  9.5 0.0 collective-permute-done.1.part
  9.5 0.0 copy-start
  9.5 0.1 collective-permute-start.6
  9.6 3.8 %collective-permute-start.2 = (f32[20,16,128]{2,1,0:T(8,128)S(1)}, f32[20,16,128]{2,1,0:T(8,128)S(1)}, u32[]{:S(2)}, u32[]{:S(2)}) collective-permute-start(f32[20,16,128]{2,1,0:T(8,128)S(1)} %collective-permute-done.1.part), channel_id=1, source_target_pairs={{0,0},{2,4},{4,2},{6,6},{1,1},{3,5},{5,3},{7,7},{8,8},{10,12},{12,... | collective-permute-start | bytes 491528 | tf_op jit(solution)/shard_map/ppermute | solution.py:354
  13.4 0.1 collective-permute-start.7
  13.5 1.9 %collective-permute-start.5 = (f32[8,16,128]{2,1,0:T(8,128)S(1)}, f32[8,16,128]{2,1,0:T(8,128)S(1)}, u32[]{:S(2)}, u32[]{:S(2)}) collective-permute-start(f32[8,16,128]{2,1,0:T(8,128)S(1)} %outer.1), channel_id=1, source_target_pairs={{0,0},{2,4},{4,2},{6,6},{1,1},{3,5},{5,3},{7,7},{8,8},{10,12},{12,... | collective-permute-start | bytes 196616 | tf_op jit(solution)/shard_map/ppermute | solution.py:354
  15.4 1.1 %centre.1 = (f32[256,512]{1,0:T(8,128)S(1)}, f32[256,512]{1,0:T(8,128)S(1)}, f32[256,384]{1,0:T(8,128)S(1)}) custom-call(f32[20,16,128]{2,1,0:T(8,128)S(1)} %get-tuple-element.24.mine, f32[20,16,128]{2,1,0:T(8,128)S(1)} %collective-permute-done.1.part, f32[8,16,128]{2,1,0:T(8,128)S(1)} %outer.1, bf16[768,1024]{1,0:T(8,128)(2,1)S(1)} %copy-done), custom_call_target="tpu_custom_call" | custom-call | flops 536870912 | tf_op jit(solution)/shard_map/centre/pallas_call | solution.py:327
  16.5 1.9 %mate.1 = (f32[4,16,16,128]{3,2,1,0:T(8,128)S(1)}, f32[4,16,16,128]{3,2,1,0:T(8,128)S(1)}, f32[256,896]{1,0:T(8,128)S(1)}) custom-call(f32[40,16,128]{2,1,0:T(8,128)S(1)} %collective-permute-done.6.whole, f32[8,16,128]{2,1,0:T(8,128)S(1)} %collective-permute-done.7.outer, f32[256,512]{1,0:T(8,128)S(1)} %get-tuple-element.25.upper, ...), custom_call_target="tpu_custom_call" | custom-call | flops 536870912 | tf_op jit(solution)/shard_map/mate/pallas_call | solution.py:327
  18.4 0.7 %collective-permute-done.5.b_outer = f32[8,16,128]{2,1,0:T(8,128)S(1)} collective-permute-done((f32[8,16,128]{2,1,0:T(8,128)S(1)}, f32[8,16,128]{2,1,0:T(8,128)S(1)}, u32[]{:S(2)}, u32[]{:S(2)}) %collective-permute-start.5) | collective-permute-done | bytes 65568 | tf_op jit(solution)/shard_map/ppermute | solution.py:354
  19.1 3.0 %flux.1 = (f32[6,8,16,128]{3,2,1,0:T(8,128)S(1)}, f32[3,8,16,128]{3,2,1,0:T(8,128)S(1)}, f32[16,128]{1,0:T(8,128)S(1)}) custom-call(f32[20,16,128]{2,1,0:T(8,128)S(1)} %collective-permute-done.b_mine, f32[20,16,128]{2,1,0:T(8,128)S(1)} %collective-permute-done.2.b_part, f32[8,16,128]{2,1,0:T(8,128)S(1)} %collective-permute-done.5.b_outer, ...), custom_call_target="tpu_custom_call" | custom-call | tf_op jit(solution)/shard_map/flux/pallas_call | solution.py:327
  22.1 0.5 %collective-permute-start.10 = (f32[16,128]{1,0:T(8,128)S(1)}, f32[16,128]{1,0:T(8,128)S(1)}, u32[]{:S(2)}, u32[]{:S(2)}) collective-permute-start(f32[16,128]{1,0:T(8,128)S(1)} %get-tuple-element.31), channel_id=1, source_target_pairs={{0,16},{8,24},{16,0},{24,8},{1,17},{9,25},{17,1},{25,9},{2,18},{10... | collective-permute-start | bytes 24584 | tf_op jit(solution)/shard_map/ppermute | solution.py:427
  22.6 3.5 %collective-permute-start.9 = (f32[16,128]{1,0:T(8,128)S(1)}, f32[16,128]{1,0:T(8,128)S(1)}, u32[]{:S(2)}, u32[]{:S(2)}) collective-permute-start(f32[16,128]{1,0:T(8,128)S(1)} %get-tuple-element.31), channel_id=1, source_target_pairs={{0,24},{8,16},{16,8},{24,0},{1,25},{9,17},{17,9},{25,1},{2,26},{10... | collective-permute-start | bytes 24584 | tf_op jit(solution)/shard_map/ppermute | solution.py:427
  26.1 0.6 %collective-permute-start.12 = (f32[3,8,16,128]{3,2,1,0:T(8,128)S(1)}, f32[3,8,16,128]{3,2,1,0:T(8,128)S(1)}, u32[]{:S(2)}, u32[]{:S(2)}) collective-permute-start(f32[3,8,16,128]{3,2,1,0:T(8,128)S(1)} %get-tuple-element.33), channel_id=1, source_target_pairs={{0,1},{1,0},{2,3},{3,2},{4,5},{5,4},{6,7},{7,6},{8,9},{9,8},{10,11... | collective-permute-start | bytes 589832 | tf_op jit(solution)/shard_map/ppermute | solution.py:348
  26.7 1.3 %collective-permute-done.9 = f32[16,128]{1,0:T(8,128)S(1)} collective-permute-done((f32[16,128]{1,0:T(8,128)S(1)}, f32[16,128]{1,0:T(8,128)S(1)}, u32[]{:S(2)}, u32[]{:S(2)}) %collective-permute-start.9) | collective-permute-done | bytes 8224 | tf_op jit(solution)/shard_map/ppermute | solution.py:427
  28.1 1.7 %collective-permute-done.8 = f32[16,128]{1,0:T(8,128)S(1)} collective-permute-done((f32[16,128]{1,0:T(8,128)S(1)}, f32[16,128]{1,0:T(8,128)S(1)}, u32[]{:S(2)}, u32[]{:S(2)}) %collective-permute-start.8) | collective-permute-done | bytes 8224 | tf_op jit(solution)/shard_map/ppermute | solution.py:427
  29.8 0.6 %collective-permute-start.11 = (f32[16,128]{1,0:T(8,128)S(1)}, f32[16,128]{1,0:T(8,128)S(1)}, u32[]{:S(2)}, u32[]{:S(2)}) collective-permute-start(f32[16,128]{1,0:T(8,128)S(1)} %add_add_fusion), channel_id=1, source_target_pairs={{0,1},{1,0},{2,3},{3,2},{4,5},{5,4},{6,7},{7,6},{8,9},{9,8},{10,11... | collective-permute-start | bytes 24584 | tf_op jit(solution)/shard_map/ppermute | solution.py:348
  30.4 3.0 %collective-permute-done.11 = f32[16,128]{1,0:T(8,128)S(1)} collective-permute-done((f32[16,128]{1,0:T(8,128)S(1)}, f32[16,128]{1,0:T(8,128)S(1)}, u32[]{:S(2)}, u32[]{:S(2)}) %collective-permute-start.11) | collective-permute-done | bytes 8224 | tf_op jit(solution)/shard_map/ppermute | solution.py:348
  33.4 1.0 %finish.1 = (f32[3,8,16,128]{3,2,1,0:T(8,128)}, f32[3,8,16,128]{3,2,1,0:T(8,128)}, f32[3,16]{1,0:T(4,128)}, f32[3,16]{1,0:T(4,128)}) custom-call(f32[16,128]{1,0:T(8,128)S(1)} %add.15.sums, f32[6,8,16,128]{3,2,1,0:T(8,128)S(1)} %get-tuple-element.32.keep, f32[3,8,16,128]{3,2,1,0:T(8,128)S(1)} %collective-permute-done.12.come), custom_call_target="tpu_custom_call" | custom-call | tf_op jit(solution)/shard_map/finish/pallas_call | solution.py:327
  (15 shorter events, 0.1 us)
Async XLA Ops:
  0.6 1.0 %copy-start.1 = (f32[4,8,16,128]{3,2,1,0:T(8,128)S(1)}, f32[4,8,16,128]{3,2,1,0:T(8,128)}, u32[]{:S(2)}) copy-start(f32[4,8,16,128]{3,2,1,0:T(8,128)} %own.1) | copy-start | bytes 786436
  2.0 7.5 %collective-permute-start.1 = (f32[20,16,128]{2,1,0:T(8,128)S(1)}, f32[20,16,128]{2,1,0:T(8,128)S(1)}, u32[]{:S(2)}, u32[]{:S(2)}) collective-permute-start(f32[20,16,128]{2,1,0:T(8,128)S(1)} %get-tuple-element.21), channel_id=1, source_target_pairs={{0,1},{1,0},{2,3},{3,2},{4,5},{5,4},{6,7},{7,6},{8,9},{9,8},{10,11... | collective-permute-start | bytes 491528 | tf_op jit(solution)/shard_map/ppermute | solution.py:348
  3.5 9.9 %collective-permute-start.3 = (f32[4,16,128]{2,1,0:T(8,128)S(1)}, f32[4,16,128]{2,1,0:T(8,128)S(1)}, u32[]{:S(2)}, u32[]{:S(2)}) collective-permute-start(f32[4,16,128]{2,1,0:T(8,128)S(1)} %get-tuple-element.22), channel_id=1, source_target_pairs={{1,25},{0,8},{9,1},{8,16},{17,9},{16,24},{25,17},{24,0},{3,27},{2,... | collective-permute-start | bytes 98312 | tf_op jit(solution)/shard_map/ppermute | solution.py:372
  5.1 8.3 %collective-permute-start.4 = (f32[4,16,128]{2,1,0:T(8,128)S(1)}, f32[4,16,128]{2,1,0:T(8,128)S(1)}, u32[]{:S(2)}, u32[]{:S(2)}) collective-permute-start(f32[4,16,128]{2,1,0:T(8,128)S(1)} %get-tuple-element.23), channel_id=1, source_target_pairs={{0,25},{1,8},{8,1},{9,16},{16,9},{17,24},{24,17},{25,0},{2,27},{3,... | collective-permute-start | bytes 98312 | tf_op jit(solution)/shard_map/ppermute | solution.py:371
  7.5 7.9 %collective-permute-start = (f32[20,16,128]{2,1,0:T(8,128)S(1)}, f32[20,16,128]{2,1,0:T(8,128)S(1)}, u32[]{:S(2)}, u32[]{:S(2)}) collective-permute-start(f32[20,16,128]{2,1,0:T(8,128)S(1)} %get-tuple-element.24.mine), channel_id=1, source_target_pairs={{0,0},{2,4},{4,2},{6,6},{1,1},{3,5},{5,3},{7,7},{8,8},{10,12},{12,... | collective-permute-start | bytes 491528 | tf_op jit(solution)/shard_map/ppermute | solution.py:354
  9.5 5.9 %copy-start = (bf16[768,1024]{1,0:T(8,128)(2,1)S(1)}, bf16[768,1024]{1,0:T(8,128)(2,1)}, u32[]{:S(2)}) copy-start(bf16[768,1024]{1,0:T(8,128)(2,1)} %constant.2.clone.weights) | copy-start | bytes 4718596
  9.5 7.0 %collective-permute-start.6 = (f32[40,16,128]{2,1,0:T(8,128)S(1)}, f32[40,16,128]{2,1,0:T(8,128)S(1)}, u32[]{:S(2)}, u32[]{:S(2)}) collective-permute-start(f32[40,16,128]{2,1,0:T(8,128)S(1)} %join.1), channel_id=1, source_target_pairs={{0,2},{2,0},{4,6},{6,4},{1,3},{3,1},{5,7},{7,5},{8,10},{10,8},{12,... | collective-permute-start | bytes 983048 | tf_op jit(solution)/shard_map/ppermute | solution.py:351
  9.6 9.5 %collective-permute-start.2 = (f32[20,16,128]{2,1,0:T(8,128)S(1)}, f32[20,16,128]{2,1,0:T(8,128)S(1)}, u32[]{:S(2)}, u32[]{:S(2)}) collective-permute-start(f32[20,16,128]{2,1,0:T(8,128)S(1)} %collective-permute-done.1.part), channel_id=1, source_target_pairs={{0,0},{2,4},{4,2},{6,6},{1,1},{3,5},{5,3},{7,7},{8,8},{10,12},{12,... | collective-permute-start | bytes 491528 | tf_op jit(solution)/shard_map/ppermute | solution.py:354
  13.4 3.1 %collective-permute-start.7 = (f32[8,16,128]{2,1,0:T(8,128)S(1)}, f32[8,16,128]{2,1,0:T(8,128)S(1)}, u32[]{:S(2)}, u32[]{:S(2)}) collective-permute-start(f32[8,16,128]{2,1,0:T(8,128)S(1)} %outer.1), channel_id=1, source_target_pairs={{0,2},{2,0},{4,6},{6,4},{1,3},{3,1},{5,7},{7,5},{8,10},{10,8},{12,... | collective-permute-start | bytes 196616 | tf_op jit(solution)/shard_map/ppermute | solution.py:351
  13.5 5.6 %collective-permute-start.5 = (f32[8,16,128]{2,1,0:T(8,128)S(1)}, f32[8,16,128]{2,1,0:T(8,128)S(1)}, u32[]{:S(2)}, u32[]{:S(2)}) collective-permute-start(f32[8,16,128]{2,1,0:T(8,128)S(1)} %outer.1), channel_id=1, source_target_pairs={{0,0},{2,4},{4,2},{6,6},{1,1},{3,5},{5,3},{7,7},{8,8},{10,12},{12,... | collective-permute-start | bytes 196616 | tf_op jit(solution)/shard_map/ppermute | solution.py:354
  22.1 4.6 %collective-permute-start.10 = (f32[16,128]{1,0:T(8,128)S(1)}, f32[16,128]{1,0:T(8,128)S(1)}, u32[]{:S(2)}, u32[]{:S(2)}) collective-permute-start(f32[16,128]{1,0:T(8,128)S(1)} %get-tuple-element.31), channel_id=1, source_target_pairs={{0,16},{8,24},{16,0},{24,8},{1,17},{9,25},{17,1},{25,9},{2,18},{10... | collective-permute-start | bytes 24584 | tf_op jit(solution)/shard_map/ppermute | solution.py:427
  22.6 5.4 %collective-permute-start.9 = (f32[16,128]{1,0:T(8,128)S(1)}, f32[16,128]{1,0:T(8,128)S(1)}, u32[]{:S(2)}, u32[]{:S(2)}) collective-permute-start(f32[16,128]{1,0:T(8,128)S(1)} %get-tuple-element.31), channel_id=1, source_target_pairs={{0,24},{8,16},{16,8},{24,0},{1,25},{9,17},{17,9},{25,1},{2,26},{10... | collective-permute-start | bytes 24584 | tf_op jit(solution)/shard_map/ppermute | solution.py:427
  26.1 3.7 %collective-permute-start.8 = (f32[16,128]{1,0:T(8,128)S(1)}, f32[16,128]{1,0:T(8,128)S(1)}, u32[]{:S(2)}, u32[]{:S(2)}) collective-permute-start(f32[16,128]{1,0:T(8,128)S(1)} %get-tuple-element.31), channel_id=1, source_target_pairs={{0,8},{8,0},{16,24},{24,16},{1,9},{9,1},{17,25},{25,17},{2,10},{10... | collective-permute-start | bytes 24584 | tf_op jit(solution)/shard_map/ppermute | solution.py:427
  26.1 7.3 %collective-permute-start.12 = (f32[3,8,16,128]{3,2,1,0:T(8,128)S(1)}, f32[3,8,16,128]{3,2,1,0:T(8,128)S(1)}, u32[]{:S(2)}, u32[]{:S(2)}) collective-permute-start(f32[3,8,16,128]{3,2,1,0:T(8,128)S(1)} %get-tuple-element.33), channel_id=1, source_target_pairs={{0,1},{1,0},{2,3},{3,2},{4,5},{5,4},{6,7},{7,6},{8,9},{9,8},{10,11... | collective-permute-start | bytes 589832 | tf_op jit(solution)/shard_map/ppermute | solution.py:348
  29.8 3.7 %collective-permute-start.11 = (f32[16,128]{1,0:T(8,128)S(1)}, f32[16,128]{1,0:T(8,128)S(1)}, u32[]{:S(2)}, u32[]{:S(2)}) collective-permute-start(f32[16,128]{1,0:T(8,128)S(1)} %add_add_fusion), channel_id=1, source_target_pairs={{0,1},{1,0},{2,3},{3,2},{4,5},{5,4},{6,7},{7,6},{8,9},{9,8},{10,11... | collective-permute-start | bytes 24584 | tf_op jit(solution)/shard_map/ppermute | solution.py:348

commit v16 on v15

--- a/solution.py
+++ b/solution.py
@@ -113,10 +113,12 @@
     to_same[...] = pack_strip(own, 7 * (1 - me_s))
 
 
-def outer_kernel(own_strip, part_strip, outer):
-    half = own_strip.shape[0]
+def rest_kernel(part, own_strip, part_strip, rest, outer):
+    count, half = part.shape[0], own_strip.shape[0]
     outer[:half] = own_strip[...]
     outer[half:] = part_strip[...]
+    rest[:count] = part[...]
+    rest[count:] = outer[...]
 
 
 def join_kernel(mine, part, whole):
@@ -211,7 +213,7 @@
 
 
 def flux_kernel(
-    walls, b_mine, b_part, b_outer, a_raw, a_mean, a_second, upper, lower, products, weights,
+    walls, b_mine, b_rest, a_raw, a_mean, a_second, upper, lower, products, weights,
     keep_ref, send_ref, sums_ref,
     raw, in_h, in_l, prod_h, prod_l, mean, mid_h, mid_l, clark_all, similar_all,
 ):
@@ -224,7 +226,8 @@
     at_end = (me_w == 0) | (me_w == walls - 1)
     keep_b = jnp.where(at_end, 0.0, 1.0).astype(jnp.float32)
 
-    bring(b_mine, b_part, b_outer, raw, in_h, in_l, keep_b)
+    count = b_mine.shape[0]
+    bring(b_mine, b_rest.at[:count], b_rest.at[count:], raw, in_h, in_l, keep_b)
 
     for t in range(4):
         mean[t, 0] = jnp.zeros((2 * rows, width), jnp.float32)
@@ -371,10 +374,16 @@
     part_strip = lax.ppermute(first, ("span", "stream"), to_other)
     own_strip = lax.ppermute(second, ("span", "stream"), to_same)
     (whole,) = call(join_kernel, "join", (mine, part), ((2 * message[0], rows, width),))
-    a_whole, b_part = pair_a(whole), pair_b(part)
+    a_whole = pair_a(whole)
     mine_now, b_mine = lax.optimization_barrier((mine, pair_b(mine)))
-    (outer,) = call(outer_kernel, "outer", (own_strip, part_strip), ((layers, rows, width),), hint=2**35)
-    a_outer, b_outer = pair_a(outer), pair_b(outer)
+    rest, outer = call(
+        rest_kernel,
+        "rest",
+        (part, own_strip, part_strip),
+        ((message[0] + layers, rows, width), (layers, rows, width)),
+        hint=2**35,
+    )
+    b_rest, a_outer = pair_b(rest), pair_a(outer)
 
     matrices = np.zeros((2 * cells + 2 * width, 4 * cells), ml_dtypes.bfloat16)
     matrices[:cells], matrices[cells : 2 * cells] = plane_constants(both, rows)
@@ -404,7 +413,7 @@
     keep, send, sums = call(
         functools.partial(flux_kernel, walls),
         "flux",
-        (b_mine, b_part, b_outer, a_raw, a_mean, a_second, upper, lower, products, weights),
+        (b_mine, b_rest, a_raw, a_mean, a_second, upper, lower, products, weights),
         ((6, layers, rows, width), (3, layers, rows, width), (rows, width)),
         [
             (block, single),

time: 34.6 us -> 34.8 us (level)
  the two profiles are of different devices: /device:TPU:4 before, /device:TPU:0 now
where the time goes in v16:
time: 34.8 us; the launch traced here: 34.7 us
  starting transfers between devices  19.3 us (55%)
  Pallas kernels  7.41 us (21%)
  waiting for transfers between devices  6.21 us (18%)
  local copies, waits for them, and re-layouts  0.95 us (3%)
  between operations  0.74 us (2%)
    pallas_call x7, Pallas kernels, call(): pl.pallas_call(kernel, out_shape=tuple((jax.ShapeDtypeStruct(shape, jnp.f...  7.41 us
    ppermute x2, starting transfers between devices, pair_a(): return lax.ppermute(value, 'wall', [(w, w ^ 1) for w in range(walls)])  5.87 us
    ppermute x3, starting transfers between devices, swap(): return lax.ppermute(value, 'stream', [(0, 1), (1, 0)])  4.56 us
    ppermute x3, waiting for transfers between devices, swap(): return lax.ppermute(value, 'stream', [(0, 1), (1, 0)])  3.73 us
    ppermute x3, starting transfers between devices, from_span(): return lax.ppermute(value, 'span', [(p, p ^ step) for p in range(spans)])  3.55 us
    ppermute x1, starting transfers between devices, shards(): part_strip = lax.ppermute(first, ('span', 'stream'), to_other)  2.45 us
    ppermute x3, waiting for transfers between devices, from_span(): return lax.ppermute(value, 'span', [(p, p ^ step) for p in range(spans)])  1.96 us
    ppermute x1, starting transfers between devices, shards(): own_strip = lax.ppermute(second, ('span', 'stream'), to_same)  1.58 us
  transfers between devices with their start and end apart: 12, of which 4 were waited for; matrix products, arithmetic and copies ran while one was open for 0% of the time, Pallas kernels for 9%

profile of v16, /device:TPU:0, one launch (start us, length us, event | category | flops | bytes accessed | tf_op | source)
XLA Modules:
  0.0 34.7 jit_solution(7855800478967612701)
XLA Ops:
  0.6 0.9 %copy-done.1 = f32[4,8,16,128]{3,2,1,0:T(8,128)S(1)} copy-done((f32[4,8,16,128]{3,2,1,0:T(8,128)S(1)}, f32[4,8,16,128]{3,2,1,0:T(8,128)}, u32[]{:S(2)}) %copy-start.1) | copy-done | bytes 262168
  1.6 0.4 %pack.1 = (f32[20,16,128]{2,1,0:T(8,128)S(1)}, f32[20,16,128]{2,1,0:T(8,128)S(1)}, f32[4,16,128]{2,1,0:T(8,128)S(1)}, f32[4,16,128]{2,1,0:T(8,128)S(1)}) custom-call(f32[4,8,16,128]{3,2,1,0:T(8,128)S(1)} %copy-done.1), custom_call_target="tpu_custom_call" | custom-call | tf_op jit(solution)/shard_map/pack/pallas_call | solution.py:330
  2.0 3.0 %collective-permute-start.1 = (f32[20,16,128]{2,1,0:T(8,128)S(1)}, f32[20,16,128]{2,1,0:T(8,128)S(1)}, u32[]{:S(2)}, u32[]{:S(2)}) collective-permute-start(f32[20,16,128]{2,1,0:T(8,128)S(1)} %get-tuple-element.23), channel_id=1, source_target_pairs={{0,1},{1,0},{2,3},{3,2},{4,5},{5,4},{6,7},{7,6},{8,9},{9,8},{10,11... | collective-permute-start | bytes 491528 | tf_op jit(solution)/shard_map/ppermute | solution.py:351
  5.0 1.6 %collective-permute-start.2 = (f32[4,16,128]{2,1,0:T(8,128)S(1)}, f32[4,16,128]{2,1,0:T(8,128)S(1)}, u32[]{:S(2)}, u32[]{:S(2)}) collective-permute-start(f32[4,16,128]{2,1,0:T(8,128)S(1)} %get-tuple-element.24), channel_id=1, source_target_pairs={{1,25},{0,8},{9,1},{8,16},{17,9},{16,24},{25,17},{24,0},{3,27},{2,... | collective-permute-start | bytes 98312 | tf_op jit(solution)/shard_map/ppermute | solution.py:375
  6.5 2.4 %collective-permute-start.3 = (f32[4,16,128]{2,1,0:T(8,128)S(1)}, f32[4,16,128]{2,1,0:T(8,128)S(1)}, u32[]{:S(2)}, u32[]{:S(2)}) collective-permute-start(f32[4,16,128]{2,1,0:T(8,128)S(1)} %get-tuple-element.25), channel_id=1, source_target_pairs={{0,25},{1,8},{8,1},{9,16},{16,9},{17,24},{24,17},{25,0},{2,27},{3,... | collective-permute-start | bytes 98312 | tf_op jit(solution)/shard_map/ppermute | solution.py:374
  9.0 0.7 %collective-permute-start = (f32[20,16,128]{2,1,0:T(8,128)S(1)}, f32[20,16,128]{2,1,0:T(8,128)S(1)}, u32[]{:S(2)}, u32[]{:S(2)}) collective-permute-start(f32[20,16,128]{2,1,0:T(8,128)S(1)} %get-tuple-element.28.mine), channel_id=1, source_target_pairs={{0,0},{2,4},{4,2},{6,6},{1,1},{3,5},{5,3},{7,7},{8,8},{10,12},{12,... | collective-permute-start | bytes 491528 | tf_op jit(solution)/shard_map/ppermute | solution.py:357
  9.7 0.0 copy-start
  9.7 2.9 %collective-permute-start.5 = (f32[40,16,128]{2,1,0:T(8,128)S(1)}, f32[40,16,128]{2,1,0:T(8,128)S(1)}, u32[]{:S(2)}, u32[]{:S(2)}) collective-permute-start(f32[40,16,128]{2,1,0:T(8,128)S(1)} %join.1), channel_id=1, source_target_pairs={{0,2},{2,0},{4,6},{6,4},{1,3},{3,1},{5,7},{7,5},{8,10},{10,8},{12,... | collective-permute-start | bytes 983048 | tf_op jit(solution)/shard_map/ppermute | solution.py:354
  12.6 0.0 collective-permute-done.2.own_strip
  12.6 0.5 %collective-permute-done.3.part_strip = f32[4,16,128]{2,1,0:T(8,128)S(1)} collective-permute-done((f32[4,16,128]{2,1,0:T(8,128)S(1)}, f32[4,16,128]{2,1,0:T(8,128)S(1)}, u32[]{:S(2)}, u32[]{:S(2)}) %collective-permute-start.3) | collective-permute-done | bytes 32800 | tf_op jit(solution)/shard_map/ppermute | solution.py:374
  13.2 0.7 %collective-permute-start.4 = (f32[28,16,128]{2,1,0:T(8,128)S(1)}, f32[28,16,128]{2,1,0:T(8,128)S(1)}, u32[]{:S(2)}, u32[]{:S(2)}) collective-permute-start(f32[28,16,128]{2,1,0:T(8,128)S(1)} %get-tuple-element.26), channel_id=1, source_target_pairs={{0,0},{2,4},{4,2},{6,6},{1,1},{3,5},{5,3},{7,7},{8,8},{10,12},{12,... | collective-permute-start | bytes 688136 | tf_op jit(solution)/shard_map/ppermute | solution.py:357
  13.9 2.9 %collective-permute-start.6 = (f32[8,16,128]{2,1,0:T(8,128)S(1)}, f32[8,16,128]{2,1,0:T(8,128)S(1)}, u32[]{:S(2)}, u32[]{:S(2)}) collective-permute-start(f32[8,16,128]{2,1,0:T(8,128)S(1)} %get-tuple-element.27.outer), channel_id=1, source_target_pairs={{0,2},{2,0},{4,6},{6,4},{1,3},{3,1},{5,7},{7,5},{8,10},{10,8},{12,... | collective-permute-start | bytes 196616 | tf_op jit(solution)/shard_map/ppermute | solution.py:354
  16.8 1.1 %centre.1 = (f32[256,512]{1,0:T(8,128)S(1)}, f32[256,512]{1,0:T(8,128)S(1)}, f32[256,384]{1,0:T(8,128)S(1)}) custom-call(f32[20,16,128]{2,1,0:T(8,128)S(1)} %get-tuple-element.28.mine, f32[20,16,128]{2,1,0:T(8,128)S(1)} %collective-permute-done.1.part, f32[8,16,128]{2,1,0:T(8,128)S(1)} %get-tuple-element.27.outer, bf16[768,1024]{1,0:T(8,128)(2,1)S(1)} %copy-done), custom_call_target="tpu_custom_call" | custom-call | flops 536870912 | tf_op jit(solution)/shard_map/centre/pallas_call | solution.py:330
  17.9 1.9 %mate.1 = (f32[4,16,16,128]{3,2,1,0:T(8,128)S(1)}, f32[4,16,16,128]{3,2,1,0:T(8,128)S(1)}, f32[256,896]{1,0:T(8,128)S(1)}) custom-call(f32[40,16,128]{2,1,0:T(8,128)S(1)} %collective-permute-done.5.whole, f32[8,16,128]{2,1,0:T(8,128)S(1)} %collective-permute-done.6.outer, f32[256,512]{1,0:T(8,128)S(1)} %get-tuple-element.29.upper, ...), custom_call_target="tpu_custom_call" | custom-call | flops 536870912 | tf_op jit(solution)/shard_map/mate/pallas_call | solution.py:330
  19.8 3.0 %flux.1 = (f32[6,8,16,128]{3,2,1,0:T(8,128)S(1)}, f32[3,8,16,128]{3,2,1,0:T(8,128)S(1)}, f32[16,128]{1,0:T(8,128)S(1)}) custom-call(f32[20,16,128]{2,1,0:T(8,128)S(1)} %collective-permute-done.b_mine, f32[28,16,128]{2,1,0:T(8,128)S(1)} %collective-permute-done.4.b_rest, f32[4,16,16,128]{3,2,1,0:T(8,128)S(1)} %get-tuple-element.31.a_raw, ...), custom_call_target="tpu_custom_call" | custom-call | tf_op jit(solution)/shard_map/flux/pallas_call | solution.py:330
  22.8 0.9 %collective-permute-start.9 = (f32[16,128]{1,0:T(8,128)S(1)}, f32[16,128]{1,0:T(8,128)S(1)}, u32[]{:S(2)}, u32[]{:S(2)}) collective-permute-start(f32[16,128]{1,0:T(8,128)S(1)} %get-tuple-element.35), channel_id=1, source_target_pairs={{0,16},{8,24},{16,0},{24,8},{1,17},{9,25},{17,1},{25,9},{2,18},{10... | collective-permute-start | bytes 24584 | tf_op jit(solution)/shard_map/ppermute | solution.py:436
  23.7 1.5 %collective-permute-start.8 = (f32[16,128]{1,0:T(8,128)S(1)}, f32[16,128]{1,0:T(8,128)S(1)}, u32[]{:S(2)}, u32[]{:S(2)}) collective-permute-start(f32[16,128]{1,0:T(8,128)S(1)} %get-tuple-element.35), channel_id=1, source_target_pairs={{0,24},{8,16},{16,8},{24,0},{1,25},{9,17},{17,9},{25,1},{2,26},{10... | collective-permute-start | bytes 24584 | tf_op jit(solution)/shard_map/ppermute | solution.py:436
  25.2 1.2 %collective-permute-start.7 = (f32[16,128]{1,0:T(8,128)S(1)}, f32[16,128]{1,0:T(8,128)S(1)}, u32[]{:S(2)}, u32[]{:S(2)}) collective-permute-start(f32[16,128]{1,0:T(8,128)S(1)} %get-tuple-element.35), channel_id=1, source_target_pairs={{0,8},{8,0},{16,24},{24,16},{1,9},{9,1},{17,25},{25,17},{2,10},{10... | collective-permute-start | bytes 24584 | tf_op jit(solution)/shard_map/ppermute | solution.py:436
  26.4 0.8 %collective-permute-start.11 = (f32[3,8,16,128]{3,2,1,0:T(8,128)S(1)}, f32[3,8,16,128]{3,2,1,0:T(8,128)S(1)}, u32[]{:S(2)}, u32[]{:S(2)}) collective-permute-start(f32[3,8,16,128]{3,2,1,0:T(8,128)S(1)} %get-tuple-element.37), channel_id=1, source_target_pairs={{0,1},{1,0},{2,3},{3,2},{4,5},{5,4},{6,7},{7,6},{8,9},{9,8},{10,11... | collective-permute-start | bytes 589832 | tf_op jit(solution)/shard_map/ppermute | solution.py:351
  27.2 0.3 collective-permute-done.9
  27.4 1.7 %collective-permute-done.8 = f32[16,128]{1,0:T(8,128)S(1)} collective-permute-done((f32[16,128]{1,0:T(8,128)S(1)}, f32[16,128]{1,0:T(8,128)S(1)}, u32[]{:S(2)}, u32[]{:S(2)}) %collective-permute-start.8) | collective-permute-done | bytes 8224 | tf_op jit(solution)/shard_map/ppermute | solution.py:436
  29.1 0.8 %collective-permute-start.10 = (f32[16,128]{1,0:T(8,128)S(1)}, f32[16,128]{1,0:T(8,128)S(1)}, u32[]{:S(2)}, u32[]{:S(2)}) collective-permute-start(f32[16,128]{1,0:T(8,128)S(1)} %add_add_fusion), channel_id=1, source_target_pairs={{0,1},{1,0},{2,3},{3,2},{4,5},{5,4},{6,7},{7,6},{8,9},{9,8},{10,11... | collective-permute-start | bytes 24584 | tf_op jit(solution)/shard_map/ppermute | solution.py:351
  29.9 3.7 %collective-permute-done.10 = f32[16,128]{1,0:T(8,128)S(1)} collective-permute-done((f32[16,128]{1,0:T(8,128)S(1)}, f32[16,128]{1,0:T(8,128)S(1)}, u32[]{:S(2)}, u32[]{:S(2)}) %collective-permute-start.10) | collective-permute-done | bytes 8224 | tf_op jit(solution)/shard_map/ppermute | solution.py:351
  33.6 1.0 %finish.1 = (f32[3,8,16,128]{3,2,1,0:T(8,128)}, f32[3,8,16,128]{3,2,1,0:T(8,128)}, f32[3,16]{1,0:T(4,128)}, f32[3,16]{1,0:T(4,128)}) custom-call(f32[16,128]{1,0:T(8,128)S(1)} %add.15.sums, f32[6,8,16,128]{3,2,1,0:T(8,128)S(1)} %get-tuple-element.36.keep, f32[3,8,16,128]{3,2,1,0:T(8,128)S(1)} %collective-permute-done.11.come), custom_call_target="tpu_custom_call" | custom-call | tf_op jit(solution)/shard_map/finish/pallas_call | solution.py:330
  (13 shorter events, 0.1 us)
Async XLA Ops:
  0.6 1.0 %copy-start.1 = (f32[4,8,16,128]{3,2,1,0:T(8,128)S(1)}, f32[4,8,16,128]{3,2,1,0:T(8,128)}, u32[]{:S(2)}) copy-start(f32[4,8,16,128]{3,2,1,0:T(8,128)} %own.1) | copy-start | bytes 786436
  2.0 7.7 %collective-permute-start.1 = (f32[20,16,128]{2,1,0:T(8,128)S(1)}, f32[20,16,128]{2,1,0:T(8,128)S(1)}, u32[]{:S(2)}, u32[]{:S(2)}) collective-permute-start(f32[20,16,128]{2,1,0:T(8,128)S(1)} %get-tuple-element.23), channel_id=1, source_target_pairs={{0,1},{1,0},{2,3},{3,2},{4,5},{5,4},{6,7},{7,6},{8,9},{9,8},{10,11... | collective-permute-start | bytes 491528 | tf_op jit(solution)/shard_map/ppermute | solution.py:351
  5.0 7.7 %collective-permute-start.2 = (f32[4,16,128]{2,1,0:T(8,128)S(1)}, f32[4,16,128]{2,1,0:T(8,128)S(1)}, u32[]{:S(2)}, u32[]{:S(2)}) collective-permute-start(f32[4,16,128]{2,1,0:T(8,128)S(1)} %get-tuple-element.24), channel_id=1, source_target_pairs={{1,25},{0,8},{9,1},{8,16},{17,9},{16,24},{25,17},{24,0},{3,27},{2,... | collective-permute-start | bytes 98312 | tf_op jit(solution)/shard_map/ppermute | solution.py:375
  6.5 6.6 %collective-permute-start.3 = (f32[4,16,128]{2,1,0:T(8,128)S(1)}, f32[4,16,128]{2,1,0:T(8,128)S(1)}, u32[]{:S(2)}, u32[]{:S(2)}) collective-permute-start(f32[4,16,128]{2,1,0:T(8,128)S(1)} %get-tuple-element.25), channel_id=1, source_target_pairs={{0,25},{1,8},{8,1},{9,16},{16,9},{17,24},{24,17},{25,0},{2,27},{3,... | collective-permute-start | bytes 98312 | tf_op jit(solution)/shard_map/ppermute | solution.py:374
  9.0 7.8 %collective-permute-start = (f32[20,16,128]{2,1,0:T(8,128)S(1)}, f32[20,16,128]{2,1,0:T(8,128)S(1)}, u32[]{:S(2)}, u32[]{:S(2)}) collective-permute-start(f32[20,16,128]{2,1,0:T(8,128)S(1)} %get-tuple-element.28.mine), channel_id=1, source_target_pairs={{0,0},{2,4},{4,2},{6,6},{1,1},{3,5},{5,3},{7,7},{8,8},{10,12},{12,... | collective-permute-start | bytes 491528 | tf_op jit(solution)/shard_map/ppermute | solution.py:357
  9.7 7.1 %copy-start = (bf16[768,1024]{1,0:T(8,128)(2,1)S(1)}, bf16[768,1024]{1,0:T(8,128)(2,1)}, u32[]{:S(2)}) copy-start(bf16[768,1024]{1,0:T(8,128)(2,1)} %constant.2.clone.weights) | copy-start | bytes 4718596
  9.7 8.2 %collective-permute-start.5 = (f32[40,16,128]{2,1,0:T(8,128)S(1)}, f32[40,16,128]{2,1,0:T(8,128)S(1)}, u32[]{:S(2)}, u32[]{:S(2)}) collective-permute-start(f32[40,16,128]{2,1,0:T(8,128)S(1)} %join.1), channel_id=1, source_target_pairs={{0,2},{2,0},{4,6},{6,4},{1,3},{3,1},{5,7},{7,5},{8,10},{10,8},{12,... | collective-permute-start | bytes 983048 | tf_op jit(solution)/shard_map/ppermute | solution.py:354
  13.2 6.6 %collective-permute-start.4 = (f32[28,16,128]{2,1,0:T(8,128)S(1)}, f32[28,16,128]{2,1,0:T(8,128)S(1)}, u32[]{:S(2)}, u32[]{:S(2)}) collective-permute-start(f32[28,16,128]{2,1,0:T(8,128)S(1)} %get-tuple-element.26), channel_id=1, source_target_pairs={{0,0},{2,4},{4,2},{6,6},{1,1},{3,5},{5,3},{7,7},{8,8},{10,12},{12,... | collective-permute-start | bytes 688136 | tf_op jit(solution)/shard_map/ppermute | solution.py:357
  13.9 4.0 %collective-permute-start.6 = (f32[8,16,128]{2,1,0:T(8,128)S(1)}, f32[8,16,128]{2,1,0:T(8,128)S(1)}, u32[]{:S(2)}, u32[]{:S(2)}) collective-permute-start(f32[8,16,128]{2,1,0:T(8,128)S(1)} %get-tuple-element.27.outer), channel_id=1, source_target_pairs={{0,2},{2,0},{4,6},{6,4},{1,3},{3,1},{5,7},{7,5},{8,10},{10,8},{12,... | collective-permute-start | bytes 196616 | tf_op jit(solution)/shard_map/ppermute | solution.py:354
  22.8 4.6 %collective-permute-start.9 = (f32[16,128]{1,0:T(8,128)S(1)}, f32[16,128]{1,0:T(8,128)S(1)}, u32[]{:S(2)}, u32[]{:S(2)}) collective-permute-start(f32[16,128]{1,0:T(8,128)S(1)} %get-tuple-element.35), channel_id=1, source_target_pairs={{0,16},{8,24},{16,0},{24,8},{1,17},{9,25},{17,1},{25,9},{2,18},{10... | collective-permute-start | bytes 24584 | tf_op jit(solution)/shard_map/ppermute | solution.py:436
  23.7 5.4 %collective-permute-start.8 = (f32[16,128]{1,0:T(8,128)S(1)}, f32[16,128]{1,0:T(8,128)S(1)}, u32[]{:S(2)}, u32[]{:S(2)}) collective-permute-start(f32[16,128]{1,0:T(8,128)S(1)} %get-tuple-element.35), channel_id=1, source_target_pairs={{0,24},{8,16},{16,8},{24,0},{1,25},{9,17},{17,9},{25,1},{2,26},{10... | collective-permute-start | bytes 24584 | tf_op jit(solution)/shard_map/ppermute | solution.py:436
  25.2 4.0 %collective-permute-start.7 = (f32[16,128]{1,0:T(8,128)S(1)}, f32[16,128]{1,0:T(8,128)S(1)}, u32[]{:S(2)}, u32[]{:S(2)}) collective-permute-start(f32[16,128]{1,0:T(8,128)S(1)} %get-tuple-element.35), channel_id=1, source_target_pairs={{0,8},{8,0},{16,24},{24,16},{1,9},{9,1},{17,25},{25,17},{2,10},{10... | collective-permute-start | bytes 24584 | tf_op jit(solution)/shard_map/ppermute | solution.py:436
  26.4 7.3 %collective-permute-start.11 = (f32[3,8,16,128]{3,2,1,0:T(8,128)S(1)}, f32[3,8,16,128]{3,2,1,0:T(8,128)S(1)}, u32[]{:S(2)}, u32[]{:S(2)}) collective-permute-start(f32[3,8,16,128]{3,2,1,0:T(8,128)S(1)} %get-tuple-element.37), channel_id=1, source_target_pairs={{0,1},{1,0},{2,3},{3,2},{4,5},{5,4},{6,7},{7,6},{8,9},{9,8},{10,11... | collective-permute-start | bytes 589832 | tf_op jit(solution)/shard_map/ppermute | solution.py:351
  29.1 4.5 %collective-permute-start.10 = (f32[16,128]{1,0:T(8,128)S(1)}, f32[16,128]{1,0:T(8,128)S(1)}, u32[]{:S(2)}, u32[]{:S(2)}) collective-permute-start(f32[16,128]{1,0:T(8,128)S(1)} %add_add_fusion), channel_id=1, source_target_pairs={{0,1},{1,0},{2,3},{3,2},{4,5},{5,4},{6,7},{7,6},{8,9},{9,8},{10,11... | collective-permute-start | bytes 24584 | tf_op jit(solution)/shard_map/ppermute | solution.py:351

commit v17 on v16

--- a/solution.py
+++ b/solution.py
@@ -113,29 +113,23 @@
     to_same[...] = pack_strip(own, 7 * (1 - me_s))
 
 
-def rest_kernel(part, own_strip, part_strip, rest, outer):
+def rest_kernel(part, own_strip, part_strip, rest):
     count, half = part.shape[0], own_strip.shape[0]
-    outer[:half] = own_strip[...]
-    outer[half:] = part_strip[...]
     rest[:count] = part[...]
-    rest[count:] = outer[...]
-
-
-def join_kernel(mine, part, whole):
-    count = mine.shape[0]
-    whole[:count] = mine[...]
-    whole[count:] = part[...]
-
-
-def unpack(mine, part, outer, me_s):
-    layers, rows, width = outer.shape
+    rest[count : count + half] = own_strip[...]
+    rest[count + half :] = part_strip[...]
+
+
+def unpack(mine, rest, me_s):
+    count, rows, width = mine.shape
+    layers = rest.shape[0] - count
     half = layers // 2
     unit = unit_index((half, rows, width))
     first = 4 * (1 - me_s)
     in_strip = (unit == first) | (unit == first + 3)
-    for which, packed in enumerate((mine, part)):
-        far = outer[which * half : (which + 1) * half]
-        for k, strip in strip_tile(packed[2 * layers :], far, me_s):
+    for which, packed in enumerate((mine, rest)):
+        far = rest[count + which * half : count + (which + 1) * half]
+        for k, strip in strip_tile(packed[2 * layers : count], far, me_s):
             layer = (me_s if which == 0 else 1 - me_s) * layers + k * half
             for f in range(4):
                 start = f // 2 * layers + k * half
@@ -156,9 +150,9 @@
     return dot(plane_h, high) + dot(plane_l, high) + dot(plane_h, low)
 
 
-def bring(mine, part, outer, raw, high, low, keep=None):
-    rows, width = outer.shape[1:]
-    for f, layer, value in unpack(mine, part, outer, lax.axis_index("stream")):
+def bring(mine, rest, raw, high, low, keep=None):
+    rows, width = mine.shape[1:]
+    for f, layer, value in unpack(mine, rest, lax.axis_index("stream")):
         count = value.shape[0]
         value = value if keep is None else value * keep
         raw[f, pl.ds(layer, count)] = value
@@ -166,9 +160,9 @@
         high[down, column(f)], low[down, column(f)] = halves(value.reshape(-1, width))
 
 
-def centre_kernel(mine, part, outer, weights, upper, lower, products, centre, in_h, in_l, prod_h, prod_l):
-    cells, width = in_h.shape[0], outer.shape[-1]
-    bring(mine, part, outer, centre, in_h, in_l)
+def centre_kernel(mine, rest, weights, upper, lower, products, centre, in_h, in_l, prod_h, prod_l):
+    cells, width = in_h.shape[0], mine.shape[-1]
+    bring(mine, rest, centre, in_h, in_l)
     for i in range(3):
         value = (centre[i] * centre[3]).reshape(cells, width)
         prod_h[:, column(i)], prod_l[:, column(i)] = halves(value)
@@ -197,12 +191,11 @@
 
 
 def mate_kernel(
-    whole, outer, upper, lower, weights, raw, mean, second, in_h, in_l, mid_h, mid_l
+    a_mine, a_rest, upper, lower, weights, raw, mean, second, in_h, in_l, mid_h, mid_l
 ):
     both = raw.shape[1]
     odd = lax.rem(lax.axis_index("wall"), 2)
-    count = whole.shape[0] // 2
-    bring(whole.at[:count], whole.at[count:], outer, raw, in_h, in_l)
+    bring(a_mine, a_rest, raw, in_h, in_l)
     planes = jnp.where(odd == 1, upper[...], lower[...])
     planes = planes + planes_of(weights, 1 - odd, in_h[...], in_l[...])
     means = span_pass(weights, planes, both)
@@ -226,8 +219,7 @@
     at_end = (me_w == 0) | (me_w == walls - 1)
     keep_b = jnp.where(at_end, 0.0, 1.0).astype(jnp.float32)
 
-    count = b_mine.shape[0]
-    bring(b_mine, b_rest.at[:count], b_rest.at[count:], raw, in_h, in_l, keep_b)
+    bring(b_mine, b_rest, raw, in_h, in_l, keep_b)
 
     for t in range(4):
         mean[t, 0] = jnp.zeros((2 * rows, width), jnp.float32)
@@ -373,17 +365,15 @@
     part = swap(to_partner)
     part_strip = lax.ppermute(first, ("span", "stream"), to_other)
     own_strip = lax.ppermute(second, ("span", "stream"), to_same)
-    (whole,) = call(join_kernel, "join", (mine, part), ((2 * message[0], rows, width),))
-    a_whole = pair_a(whole)
-    mine_now, b_mine = lax.optimization_barrier((mine, pair_b(mine)))
-    rest, outer = call(
+    mine_now, b_mine, a_mine = lax.optimization_barrier((mine, pair_b(mine), pair_a(mine)))
+    (rest,) = call(
         rest_kernel,
         "rest",
         (part, own_strip, part_strip),
-        ((message[0] + layers, rows, width), (layers, rows, width)),
+        ((message[0] + layers, rows, width),),
         hint=2**35,
     )
-    b_rest, a_outer = pair_b(rest), pair_a(outer)
+    a_rest, b_rest = pair_a(rest), pair_b(rest)
 
     matrices = np.zeros((2 * cells + 2 * width, 4 * cells), ml_dtypes.bfloat16)
     matrices[:cells], matrices[cells : 2 * cells] = plane_constants(both, rows)
@@ -395,16 +385,16 @@
     upper, lower, products = call(
         centre_kernel,
         "centre",
-        (mine_now, part, outer, weights),
+        (mine_now, rest, weights),
         ((cells, 4 * width), (cells, 4 * width), (cells, 3 * width)),
         [(block, single), *pieces, ((cells, 3 * width), brief), ((cells, 3 * width), brief)],
         mib=16,
-        hint=2**29,
+        hint=2**31,
     )
     a_raw, a_mean, a_second = call(
         mate_kernel,
         "mate",
-        (a_whole, a_outer, upper, lower, weights),
+        (a_mine, a_rest, upper, lower, weights),
         (block, block, (cells, 7 * width)),
         [*pieces, ((cells, 7 * width), brief), ((cells, 7 * width), brief)],
         mib=16,

time: 34.8 us -> 33.4 us (0.960)
  the two profiles are of different devices: /device:TPU:0 before, /device:TPU:4 now
where the time goes in v17:
time: 33.4 us; the launch traced here: 33.2 us
  starting transfers between devices  15.5 us (46%)
  waiting for transfers between devices  8.63 us (26%)
  Pallas kernels  7.37 us (22%)
  local copies, waits for them, and re-layouts  0.95 us (3%)
  between operations  0.74 us (2%)
    pallas_call x6, Pallas kernels, call(): pl.pallas_call(kernel, out_shape=tuple((jax.ShapeDtypeStruct(shape, jnp.f...  7.37 us
    ppermute x2, starting transfers between devices, pair_b(): lax.ppermute(value, 'wall', [(w, min(max((w + 1 ^ 1) - 1, 0), walls - 1))...  5.02 us
    ppermute x3, starting transfers between devices, from_span(): return lax.ppermute(value, 'span', [(p, p ^ step) for p in range(spans)])  3.55 us
    ppermute x3, waiting for transfers between devices, swap(): return lax.ppermute(value, 'stream', [(0, 1), (1, 0)])  3.19 us
    ppermute x3, starting transfers between devices, swap(): return lax.ppermute(value, 'stream', [(0, 1), (1, 0)])  2.87 us
    ppermute x1, starting transfers between devices, shards(): part_strip = lax.ppermute(first, ('span', 'stream'), to_other)  2.45 us
    ppermute x3, waiting for transfers between devices, from_span(): return lax.ppermute(value, 'span', [(p, p ^ step) for p in range(spans)])  1.96 us
    ppermute x2, waiting for transfers between devices, pair_b(): lax.ppermute(value, 'wall', [(w, min(max((w + 1 ^ 1) - 1, 0), walls - 1))...  1.83 us
  transfers between devices with their start and end apart: 12, of which 5 were waited for; matrix products, arithmetic and copies ran while one was open for 0% of the time, Pallas kernels for 9%

profile of v17, /device:TPU:4, one launch (start us, length us, event | category | flops | bytes accessed | tf_op | source)
XLA Modules:
  0.0 33.2 jit_solution(12893978832092908028)
XLA Ops:
  0.6 0.9 %copy-done.1 = f32[4,8,16,128]{3,2,1,0:T(8,128)S(1)} copy-done((f32[4,8,16,128]{3,2,1,0:T(8,128)S(1)}, f32[4,8,16,128]{3,2,1,0:T(8,128)}, u32[]{:S(2)}) %copy-start.1) | copy-done | bytes 262168
  1.6 0.4 %pack.1 = (f32[20,16,128]{2,1,0:T(8,128)S(1)}, f32[20,16,128]{2,1,0:T(8,128)S(1)}, f32[4,16,128]{2,1,0:T(8,128)S(1)}, f32[4,16,128]{2,1,0:T(8,128)S(1)}) custom-call(f32[4,8,16,128]{3,2,1,0:T(8,128)S(1)} %copy-done.1), custom_call_target="tpu_custom_call" | custom-call | tf_op jit(solution)/shard_map/pack/pallas_call | solution.py:322
  2.0 1.6 %collective-permute-start.2 = (f32[20,16,128]{2,1,0:T(8,128)S(1)}, f32[20,16,128]{2,1,0:T(8,128)S(1)}, u32[]{:S(2)}, u32[]{:S(2)}) collective-permute-start(f32[20,16,128]{2,1,0:T(8,128)S(1)} %get-tuple-element.22), channel_id=1, source_target_pairs={{0,1},{1,0},{2,3},{3,2},{4,5},{5,4},{6,7},{7,6},{8,9},{9,8},{10,11... | collective-permute-start | bytes 491528 | tf_op jit(solution)/shard_map/ppermute | solution.py:343
  3.5 1.6 %collective-permute-start.3 = (f32[4,16,128]{2,1,0:T(8,128)S(1)}, f32[4,16,128]{2,1,0:T(8,128)S(1)}, u32[]{:S(2)}, u32[]{:S(2)}) collective-permute-start(f32[4,16,128]{2,1,0:T(8,128)S(1)} %get-tuple-element.23), channel_id=1, source_target_pairs={{1,25},{0,8},{9,1},{8,16},{17,9},{16,24},{25,17},{24,0},{3,27},{2,... | collective-permute-start | bytes 98312 | tf_op jit(solution)/shard_map/ppermute | solution.py:367
  5.1 2.4 %collective-permute-start.4 = (f32[4,16,128]{2,1,0:T(8,128)S(1)}, f32[4,16,128]{2,1,0:T(8,128)S(1)}, u32[]{:S(2)}, u32[]{:S(2)}) collective-permute-start(f32[4,16,128]{2,1,0:T(8,128)S(1)} %get-tuple-element.24), channel_id=1, source_target_pairs={{0,25},{1,8},{8,1},{9,16},{16,9},{17,24},{24,17},{25,0},{2,27},{3,... | collective-permute-start | bytes 98312 | tf_op jit(solution)/shard_map/ppermute | solution.py:366
  7.5 0.0 collective-permute-start.1
  7.5 2.5 %collective-permute-start = (f32[20,16,128]{2,1,0:T(8,128)S(1)}, f32[20,16,128]{2,1,0:T(8,128)S(1)}, u32[]{:S(2)}, u32[]{:S(2)}) collective-permute-start(f32[20,16,128]{2,1,0:T(8,128)S(1)} %get-tuple-element.26.mine), channel_id=1, source_target_pairs={{0,0},{2,4},{4,2},{6,6},{1,1},{3,5},{5,3},{7,7},{8,8},{10,12},{12,... | collective-permute-start | bytes 491528 | tf_op jit(solution)/shard_map/ppermute | solution.py:349
  10.1 1.6 %collective-permute-done.4.part_strip = f32[4,16,128]{2,1,0:T(8,128)S(1)} collective-permute-done((f32[4,16,128]{2,1,0:T(8,128)S(1)}, f32[4,16,128]{2,1,0:T(8,128)S(1)}, u32[]{:S(2)}, u32[]{:S(2)}) %collective-permute-start.4) | collective-permute-done | bytes 32800 | tf_op jit(solution)/shard_map/ppermute | solution.py:366
  11.7 0.1 collective-permute-start.6
  11.8 2.5 %collective-permute-start.5 = (f32[28,16,128]{2,1,0:T(8,128)S(1)}, f32[28,16,128]{2,1,0:T(8,128)S(1)}, u32[]{:S(2)}, u32[]{:S(2)}) collective-permute-start(f32[28,16,128]{2,1,0:T(8,128)S(1)} %rest.1), channel_id=1, source_target_pairs={{0,0},{2,4},{4,2},{6,6},{1,1},{3,5},{5,3},{7,7},{8,8},{10,12},{12,... | collective-permute-start | bytes 688136 | tf_op jit(solution)/shard_map/ppermute | solution.py:349
  14.3 0.0 collective-permute-done.1.a_mine
  14.3 1.1 %centre.1 = (f32[256,512]{1,0:T(8,128)S(1)}, f32[256,512]{1,0:T(8,128)S(1)}, f32[256,384]{1,0:T(8,128)S(1)}) custom-call(f32[20,16,128]{2,1,0:T(8,128)S(1)} %get-tuple-element.26.mine, f32[28,16,128]{2,1,0:T(8,128)S(1)} %rest.1, bf16[768,1024]{1,0:T(8,128)(2,1)S(1)} %copy-done), custom_call_target="tpu_custom_call" | custom-call | flops 2147483648 | tf_op jit(solution)/shard_map/centre/pallas_call | solution.py:322
  15.4 1.9 %mate.1 = (f32[4,16,16,128]{3,2,1,0:T(8,128)S(1)}, f32[4,16,16,128]{3,2,1,0:T(8,128)S(1)}, f32[256,896]{1,0:T(8,128)S(1)}) custom-call(f32[20,16,128]{2,1,0:T(8,128)S(1)} %collective-permute-done.1.a_mine, f32[28,16,128]{2,1,0:T(8,128)S(1)} %collective-permute-done.6.a_rest, f32[256,512]{1,0:T(8,128)S(1)} %get-tuple-element.27.upper, ...), custom_call_target="tpu_custom_call" | custom-call | flops 536870912 | tf_op jit(solution)/shard_map/mate/pallas_call | solution.py:322
  17.3 1.8 %collective-permute-done.5.b_rest = f32[28,16,128]{2,1,0:T(8,128)S(1)} collective-permute-done((f32[28,16,128]{2,1,0:T(8,128)S(1)}, f32[28,16,128]{2,1,0:T(8,128)S(1)}, u32[]{:S(2)}, u32[]{:S(2)}) %collective-permute-start.5) | collective-permute-done | bytes 229408 | tf_op jit(solution)/shard_map/ppermute | solution.py:349
  19.1 3.0 %flux.1 = (f32[6,8,16,128]{3,2,1,0:T(8,128)S(1)}, f32[3,8,16,128]{3,2,1,0:T(8,128)S(1)}, f32[16,128]{1,0:T(8,128)S(1)}) custom-call(f32[20,16,128]{2,1,0:T(8,128)S(1)} %collective-permute-done.b_mine, f32[28,16,128]{2,1,0:T(8,128)S(1)} %collective-permute-done.5.b_rest, f32[4,16,16,128]{3,2,1,0:T(8,128)S(1)} %get-tuple-element.29.a_raw, ...), custom_call_target="tpu_custom_call" | custom-call | tf_op jit(solution)/shard_map/flux/pallas_call | solution.py:322
  22.2 0.9 %collective-permute-start.9 = (f32[16,128]{1,0:T(8,128)S(1)}, f32[16,128]{1,0:T(8,128)S(1)}, u32[]{:S(2)}, u32[]{:S(2)}) collective-permute-start(f32[16,128]{1,0:T(8,128)S(1)} %get-tuple-element.33), channel_id=1, source_target_pairs={{0,16},{8,24},{16,0},{24,8},{1,17},{9,25},{17,1},{25,9},{2,18},{10... | collective-permute-start | bytes 24584 | tf_op jit(solution)/shard_map/ppermute | solution.py:426
  23.0 1.5 %collective-permute-start.8 = (f32[16,128]{1,0:T(8,128)S(1)}, f32[16,128]{1,0:T(8,128)S(1)}, u32[]{:S(2)}, u32[]{:S(2)}) collective-permute-start(f32[16,128]{1,0:T(8,128)S(1)} %get-tuple-element.33), channel_id=1, source_target_pairs={{0,24},{8,16},{16,8},{24,0},{1,25},{9,17},{17,9},{25,1},{2,26},{10... | collective-permute-start | bytes 24584 | tf_op jit(solution)/shard_map/ppermute | solution.py:426
  24.6 1.2 %collective-permute-start.7 = (f32[16,128]{1,0:T(8,128)S(1)}, f32[16,128]{1,0:T(8,128)S(1)}, u32[]{:S(2)}, u32[]{:S(2)}) collective-permute-start(f32[16,128]{1,0:T(8,128)S(1)} %get-tuple-element.33), channel_id=1, source_target_pairs={{0,8},{8,0},{16,24},{24,16},{1,9},{9,1},{17,25},{25,17},{2,10},{10... | collective-permute-start | bytes 24584 | tf_op jit(solution)/shard_map/ppermute | solution.py:426
  25.7 0.8 %collective-permute-start.11 = (f32[3,8,16,128]{3,2,1,0:T(8,128)S(1)}, f32[3,8,16,128]{3,2,1,0:T(8,128)S(1)}, u32[]{:S(2)}, u32[]{:S(2)}) collective-permute-start(f32[3,8,16,128]{3,2,1,0:T(8,128)S(1)} %get-tuple-element.35), channel_id=1, source_target_pairs={{0,1},{1,0},{2,3},{3,2},{4,5},{5,4},{6,7},{7,6},{8,9},{9,8},{10,11... | collective-permute-start | bytes 589832 | tf_op jit(solution)/shard_map/ppermute | solution.py:343
  26.5 0.3 collective-permute-done.9
  26.8 1.7 %collective-permute-done.8 = f32[16,128]{1,0:T(8,128)S(1)} collective-permute-done((f32[16,128]{1,0:T(8,128)S(1)}, f32[16,128]{1,0:T(8,128)S(1)}, u32[]{:S(2)}, u32[]{:S(2)}) %collective-permute-start.8) | collective-permute-done | bytes 8224 | tf_op jit(solution)/shard_map/ppermute | solution.py:426
  28.5 0.5 %collective-permute-start.10 = (f32[16,128]{1,0:T(8,128)S(1)}, f32[16,128]{1,0:T(8,128)S(1)}, u32[]{:S(2)}, u32[]{:S(2)}) collective-permute-start(f32[16,128]{1,0:T(8,128)S(1)} %add_add_fusion), channel_id=1, source_target_pairs={{0,1},{1,0},{2,3},{3,2},{4,5},{5,4},{6,7},{7,6},{8,9},{9,8},{10,11... | collective-permute-start | bytes 24584 | tf_op jit(solution)/shard_map/ppermute | solution.py:343
  29.0 3.2 %collective-permute-done.10 = f32[16,128]{1,0:T(8,128)S(1)} collective-permute-done((f32[16,128]{1,0:T(8,128)S(1)}, f32[16,128]{1,0:T(8,128)S(1)}, u32[]{:S(2)}, u32[]{:S(2)}) %collective-permute-start.10) | collective-permute-done | bytes 8224 | tf_op jit(solution)/shard_map/ppermute | solution.py:343
  32.2 1.0 %finish.1 = (f32[3,8,16,128]{3,2,1,0:T(8,128)}, f32[3,8,16,128]{3,2,1,0:T(8,128)}, f32[3,16]{1,0:T(4,128)}, f32[3,16]{1,0:T(4,128)}) custom-call(f32[16,128]{1,0:T(8,128)S(1)} %add.15.sums, f32[6,8,16,128]{3,2,1,0:T(8,128)S(1)} %get-tuple-element.34.keep, f32[3,8,16,128]{3,2,1,0:T(8,128)S(1)} %collective-permute-done.11.come), custom_call_target="tpu_custom_call" | custom-call | tf_op jit(solution)/shard_map/finish/pallas_call | solution.py:322
  (12 shorter events, 0.0 us)
Async XLA Ops:
  0.6 1.0 %copy-start.1 = (f32[4,8,16,128]{3,2,1,0:T(8,128)S(1)}, f32[4,8,16,128]{3,2,1,0:T(8,128)}, u32[]{:S(2)}) copy-start(f32[4,8,16,128]{3,2,1,0:T(8,128)} %own.1) | copy-start | bytes 786436
  2.0 9.7 %collective-permute-start.2 = (f32[20,16,128]{2,1,0:T(8,128)S(1)}, f32[20,16,128]{2,1,0:T(8,128)S(1)}, u32[]{:S(2)}, u32[]{:S(2)}) collective-permute-start(f32[20,16,128]{2,1,0:T(8,128)S(1)} %get-tuple-element.22), channel_id=1, source_target_pairs={{0,1},{1,0},{2,3},{3,2},{4,5},{5,4},{6,7},{7,6},{8,9},{9,8},{10,11... | collective-permute-start | bytes 491528 | tf_op jit(solution)/shard_map/ppermute | solution.py:343
  3.5 6.6 %collective-permute-start.3 = (f32[4,16,128]{2,1,0:T(8,128)S(1)}, f32[4,16,128]{2,1,0:T(8,128)S(1)}, u32[]{:S(2)}, u32[]{:S(2)}) collective-permute-start(f32[4,16,128]{2,1,0:T(8,128)S(1)} %get-tuple-element.23), channel_id=1, source_target_pairs={{1,25},{0,8},{9,1},{8,16},{17,9},{16,24},{25,17},{24,0},{3,27},{2,... | collective-permute-start | bytes 98312 | tf_op jit(solution)/shard_map/ppermute | solution.py:367
  5.1 6.6 %collective-permute-start.4 = (f32[4,16,128]{2,1,0:T(8,128)S(1)}, f32[4,16,128]{2,1,0:T(8,128)S(1)}, u32[]{:S(2)}, u32[]{:S(2)}) collective-permute-start(f32[4,16,128]{2,1,0:T(8,128)S(1)} %get-tuple-element.24), channel_id=1, source_target_pairs={{0,25},{1,8},{8,1},{9,16},{16,9},{17,24},{24,17},{25,0},{2,27},{3,... | collective-permute-start | bytes 98312 | tf_op jit(solution)/shard_map/ppermute | solution.py:366
  7.5 6.8 %copy-start = (bf16[768,1024]{1,0:T(8,128)(2,1)S(1)}, bf16[768,1024]{1,0:T(8,128)(2,1)}, u32[]{:S(2)}) copy-start(bf16[768,1024]{1,0:T(8,128)(2,1)} %constant.2.clone.weights) | copy-start | bytes 4718596
  7.5 6.8 %collective-permute-start.1 = (f32[20,16,128]{2,1,0:T(8,128)S(1)}, f32[20,16,128]{2,1,0:T(8,128)S(1)}, u32[]{:S(2)}, u32[]{:S(2)}) collective-permute-start(f32[20,16,128]{2,1,0:T(8,128)S(1)} %get-tuple-element.26.mine), channel_id=1, source_target_pairs={{0,2},{2,0},{4,6},{6,4},{1,3},{3,1},{5,7},{7,5},{8,10},{10,8},{12,... | collective-permute-start | bytes 491528 | tf_op jit(solution)/shard_map/ppermute | solution.py:346
  7.5 6.8 %collective-permute-start = (f32[20,16,128]{2,1,0:T(8,128)S(1)}, f32[20,16,128]{2,1,0:T(8,128)S(1)}, u32[]{:S(2)}, u32[]{:S(2)}) collective-permute-start(f32[20,16,128]{2,1,0:T(8,128)S(1)} %get-tuple-element.26.mine), channel_id=1, source_target_pairs={{0,0},{2,4},{4,2},{6,6},{1,1},{3,5},{5,3},{7,7},{8,8},{10,12},{12,... | collective-permute-start | bytes 491528 | tf_op jit(solution)/shard_map/ppermute | solution.py:349
  11.7 3.7 %collective-permute-start.6 = (f32[28,16,128]{2,1,0:T(8,128)S(1)}, f32[28,16,128]{2,1,0:T(8,128)S(1)}, u32[]{:S(2)}, u32[]{:S(2)}) collective-permute-start(f32[28,16,128]{2,1,0:T(8,128)S(1)} %rest.1), channel_id=1, source_target_pairs={{0,2},{2,0},{4,6},{6,4},{1,3},{3,1},{5,7},{7,5},{8,10},{10,8},{12,... | collective-permute-start | bytes 688136 | tf_op jit(solution)/shard_map/ppermute | solution.py:346
  11.8 7.3 %collective-permute-start.5 = (f32[28,16,128]{2,1,0:T(8,128)S(1)}, f32[28,16,128]{2,1,0:T(8,128)S(1)}, u32[]{:S(2)}, u32[]{:S(2)}) collective-permute-start(f32[28,16,128]{2,1,0:T(8,128)S(1)} %rest.1), channel_id=1, source_target_pairs={{0,0},{2,4},{4,2},{6,6},{1,1},{3,5},{5,3},{7,7},{8,8},{10,12},{12,... | collective-permute-start | bytes 688136 | tf_op jit(solution)/shard_map/ppermute | solution.py:349
  22.2 4.6 %collective-permute-start.9 = (f32[16,128]{1,0:T(8,128)S(1)}, f32[16,128]{1,0:T(8,128)S(1)}, u32[]{:S(2)}, u32[]{:S(2)}) collective-permute-start(f32[16,128]{1,0:T(8,128)S(1)} %get-tuple-element.33), channel_id=1, source_target_pairs={{0,16},{8,24},{16,0},{24,8},{1,17},{9,25},{17,1},{25,9},{2,18},{10... | collective-permute-start | bytes 24584 | tf_op jit(solution)/shard_map/ppermute | solution.py:426
  23.0 5.4 %collective-permute-start.8 = (f32[16,128]{1,0:T(8,128)S(1)}, f32[16,128]{1,0:T(8,128)S(1)}, u32[]{:S(2)}, u32[]{:S(2)}) collective-permute-start(f32[16,128]{1,0:T(8,128)S(1)} %get-tuple-element.33), channel_id=1, source_target_pairs={{0,24},{8,16},{16,8},{24,0},{1,25},{9,17},{17,9},{25,1},{2,26},{10... | collective-permute-start | bytes 24584 | tf_op jit(solution)/shard_map/ppermute | solution.py:426
  24.6 3.9 %collective-permute-start.7 = (f32[16,128]{1,0:T(8,128)S(1)}, f32[16,128]{1,0:T(8,128)S(1)}, u32[]{:S(2)}, u32[]{:S(2)}) collective-permute-start(f32[16,128]{1,0:T(8,128)S(1)} %get-tuple-element.33), channel_id=1, source_target_pairs={{0,8},{8,0},{16,24},{24,16},{1,9},{9,1},{17,25},{25,17},{2,10},{10... | collective-permute-start | bytes 24584 | tf_op jit(solution)/shard_map/ppermute | solution.py:426
  25.7 6.5 %collective-permute-start.11 = (f32[3,8,16,128]{3,2,1,0:T(8,128)S(1)}, f32[3,8,16,128]{3,2,1,0:T(8,128)S(1)}, u32[]{:S(2)}, u32[]{:S(2)}) collective-permute-start(f32[3,8,16,128]{3,2,1,0:T(8,128)S(1)} %get-tuple-element.35), channel_id=1, source_target_pairs={{0,1},{1,0},{2,3},{3,2},{4,5},{5,4},{6,7},{7,6},{8,9},{9,8},{10,11... | collective-permute-start | bytes 589832 | tf_op jit(solution)/shard_map/ppermute | solution.py:343
  28.5 3.7 %collective-permute-start.10 = (f32[16,128]{1,0:T(8,128)S(1)}, f32[16,128]{1,0:T(8,128)S(1)}, u32[]{:S(2)}, u32[]{:S(2)}) collective-permute-start(f32[16,128]{1,0:T(8,128)S(1)} %add_add_fusion), channel_id=1, source_target_pairs={{0,1},{1,0},{2,3},{3,2},{4,5},{5,4},{6,7},{7,6},{8,9},{9,8},{10,11... | collective-permute-start | bytes 24584 | tf_op jit(solution)/shard_map/ppermute | solution.py:343

commit v18 on v17

--- a/solution.py
+++ b/solution.py
@@ -50,8 +50,21 @@
     for o in range(width):
         for k in range(2 * reach + 1):
             circle[(o + k - reach) % width, o] = filter_taps[k]
-    high, low = split_constant(circle)
-    return np.block([[high, low], [high, np.zeros_like(low)]])
+    half = width // 2
+
+    def parts(matrix):
+        high, low = split_constant(matrix)
+        return np.block([[high, low], [high, np.zeros_like(low)]])
+
+    packed = []
+    for layers in range(2):
+        row = []
+        for s in range(2):
+            matrix = np.zeros((width, width))
+            matrix[:, layers * half : (layers + 1) * half] = circle[:, s * half : (s + 1) * half]
+            row.append(parts(matrix))
+        packed.append(np.concatenate(row, axis=1))
+    return parts(circle), np.concatenate(packed, axis=0)
 
 
 def halves(value):
@@ -175,7 +188,7 @@
     cells = planes.shape[0]
     rows = cells // both
     width = 128
-    span_w = weights[2 * cells :, : 2 * width]
+    span_w = weights[2 * cells : 2 * cells + 2 * width, : 2 * width]
     high, low = halves(planes)
     tiles = planes.shape[1] // width
     parts = [jnp.concatenate([high[:, column(t)], low[:, column(t)]], axis=1) for t in range(tiles)]
@@ -190,25 +203,65 @@
         high[:, column(t)], low[:, column(t)] = halves(value.reshape(-1, value.shape[-1]))
 
 
+def packed_pass(weights, planes):
+    cells = planes.shape[0]
+    some, width = cells // 2, 128
+    me_s = lax.axis_index("stream")
+    along = pl.ds(pl.multiple_of((1 + me_s) * 2 * width, 2 * width), 2 * width)
+    matrix = weights[2 * cells : 2 * cells + 4 * width, along]
+    high, low = halves(planes)
+    tiles = planes.shape[1] // width
+    parts = [
+        jnp.concatenate(
+            [high[:some, column(t)], low[:some, column(t)], high[some:, column(t)], low[some:, column(t)]],
+            axis=1,
+        )
+        for t in range(tiles)
+    ]
+    result = dot(jnp.concatenate(parts, axis=0), matrix)
+    result = result[:, :width] + result[:, width:]
+    return [result[t * some : (t + 1) * some] for t in range(tiles)]
+
+
+def pack_layers(own, other, me_s, shift=0):
+    width = own.shape[-1]
+    in_place = lane_index(own.shape) // (width // 2) == me_s
+    own = pltpu.roll(own, shift % width, 2) if shift else own
+    return jnp.where(in_place, own, pltpu.roll(other, (shift + width // 2) % width, 2))
+
+
+def pack_means(mean, means, rows_near):
+    for t, value in enumerate(means):
+        mean[t] = value
+    both = mean.shape[1]
+    me_s = lax.axis_index("stream")
+    own, other = pl.ds(me_s * (both // 2), both // 2), pl.ds((1 - me_s) * (both // 2), both // 2)
+    for t in range(4):
+        near = mean[t, own, rows_near, :], mean[t, other, rows_near, :]
+        slope = (pack_layers(*near, me_s, -1) - pack_layers(*near, me_s, 1)) * 0.5
+        yield t, pack_layers(mean[t, own], mean[t, other], me_s), slope
+
+
 def mate_kernel(
-    a_mine, a_rest, upper, lower, weights, raw, mean, second, in_h, in_l, mid_h, mid_l
+    a_mine, a_rest, upper, lower, weights, raw, packed, slopes, second, in_h, in_l, mid_h, mid_l, mean
 ):
-    both = raw.shape[1]
+    both, rows = raw.shape[1:3]
     odd = lax.rem(lax.axis_index("wall"), 2)
     bring(a_mine, a_rest, raw, in_h, in_l)
     planes = jnp.where(odd == 1, upper[...], lower[...])
     planes = planes + planes_of(weights, 1 - odd, in_h[...], in_l[...])
     means = span_pass(weights, planes, both)
-    for t, value in enumerate(means):
-        mean[t] = value
+    for t, value, slope in pack_means(mean, means, pl.ds(pl.multiple_of(odd * reach, reach), reach)):
+        packed[t] = value
+        slopes[t] = slope
     second_input(means, mid_h, mid_l)
     second[...] = planes_of(weights, 1 - odd, mid_h[...], mid_l[...])
 
 
 def flux_kernel(
-    walls, b_mine, b_rest, a_raw, a_mean, a_second, upper, lower, products, weights,
+    walls, b_mine, b_rest, a_raw, a_packed, a_slopes, a_second, upper, lower, products, weights,
     keep_ref, send_ref, sums_ref,
-    raw, in_h, in_l, prod_h, prod_l, mean, mid_h, mid_l, clark_all, similar_all,
+    raw, in_h, in_l, prod_h, prod_l, mean, mid_h, mid_l, packed, slopes,
 ):
     _, layers, rows, width = keep_ref.shape
     both = 2 * layers
@@ -221,9 +274,6 @@
 
     bring(b_mine, b_rest, raw, in_h, in_l, keep_b)
 
-    for t in range(4):
-        mean[t, 0] = jnp.zeros((2 * rows, width), jnp.float32)
-        mean[t, both + 1] = jnp.zeros((2 * rows, width), jnp.float32)
     planes = jnp.where(odd == 0, upper[...], lower[...])
     planes = planes + planes_of(weights, odd, in_h[...], in_l[...])
     row = lax.rem(lax.broadcasted_iota(jnp.int32, planes.shape, 0), rows)
@@ -232,11 +282,16 @@
     means = span_pass(weights, planes, both)
     rows_b = pl.ds(pl.multiple_of(odd * rows, rows), rows)
     rows_a = pl.ds(pl.multiple_of((1 - odd) * rows, rows), rows)
-    for t, value in enumerate(means):
-        mean[t, 1 : both + 1, rows_b, :] = value
-        mean[t, 1 : both + 1, rows_a, :] = a_mean[t]
+    near_b = pl.ds(pl.multiple_of(odd * reach, reach), reach)
+    near_a = pl.ds(pl.multiple_of((1 - odd) * reach, reach), reach)
+    for t, value, slope in pack_means(mean, means, near_a):
+        packed[t, :, rows_b, :] = value
+        packed[t, :, rows_a, :] = a_packed[t]
+        slopes[t, :, near_b, :] = slope
+        slopes[t, :, near_a, :] = a_slopes[t]
     second_input(means, mid_h, mid_l)
-    second = span_pass(weights, a_second[...] + planes_of(weights, odd, mid_h[...], mid_l[...]), both)
+    second = packed_pass(weights, a_second[...] + planes_of(weights, odd, mid_h[...], mid_l[...]))
+    second = [value.reshape(layers, rows, width) for value in second]
 
     def around(f):
         above = jnp.where(odd == 0, raw[f, :, rows - reach :, :], a_raw[f, :, rows - reach :, :])
@@ -247,45 +302,43 @@
     for i in range(3):
         value = (around(i) * temperature).reshape(cells, width)
         prod_h[:, column(i)], prod_l[:, column(i)] = halves(value)
-    flux = span_pass(weights, products[...] + planes_of(weights, 3, prod_h[...], prod_l[...]), both)
+    flux = packed_pass(weights, products[...] + planes_of(weights, 3, prod_h[...], prod_l[...]))
+    flux = [value.reshape(layers, rows, width) for value in flux]
 
     mid_rows = slice(reach, reach + rows)
-    centre, along_span, along_wall, along_stream = [], [], [], []
+    first = lane_index((1, rows, width)) < width // 2
+    centre, along_wall, along_stream = [], [], []
     for f in range(4):
-        here = mean[f, 1 : both + 1, mid_rows, :]
+        here = packed[f, :, mid_rows, :]
         centre.append(here)
-        along_span.append((pltpu.roll(here, width - 1, 2) - pltpu.roll(here, 1, 2)) * 0.5)
-        below = mean[f, 1 : both + 1, reach + 1 : reach + rows + 1, :]
-        above = mean[f, 1 : both + 1, reach - 1 : reach + rows - 1, :]
+        below = packed[f, :, reach + 1 : reach + rows + 1, :]
+        above = packed[f, :, reach - 1 : reach + rows - 1, :]
         along_wall.append((below - above) * 0.5)
-        along_stream.append((mean[f, 2 : both + 2, mid_rows, :] - mean[f, :both, mid_rows, :]) * 0.5)
+        after = jnp.where(first, pltpu.roll(here[:1], width // 2, 2), 0.0)
+        before = jnp.where(first, 0.0, pltpu.roll(here[layers - 1 :], width // 2, 2))
+        ahead = jnp.concatenate([here[1:], after], axis=0)
+        behind = jnp.concatenate([before, here[: layers - 1]], axis=0)
+        along_stream.append((ahead - behind) * 0.5)
 
     lane = lane_index((rows, width))
-    useful = lane // (width // 2) == me_s
     table = jnp.zeros((rows, width), jnp.float32)
+    first = lane_index((layers, rows, width)) < width // 2
+    in_first = me_s == 1
     for i in range(3):
         exact = flux[i] - centre[i] * centre[3]
         similar = second[4 + i] - second[i] * second[3]
-        total = along_span[i] * along_span[3] + along_wall[i] * along_wall[3]
+        total = slopes[i] * slopes[3] + along_wall[i] * along_wall[3]
         clark = clark_coef * (total + along_stream[i] * along_stream[3])
-        clark_all[i] = clark
-        similar_all[i] = similar
         terms = (exact * clark, exact * similar, exact * exact, clark * clark, similar * similar)
         for q, term in enumerate(terms):
-            value = jnp.where(useful, jnp.sum(term, axis=0), 0.0)
-            table = jnp.where(lane == 3 * q + i, jnp.sum(value, axis=1, keepdims=True), table)
+            value = jnp.sum(jnp.sum(term, axis=0), axis=1, keepdims=True)
+            table = jnp.where(lane == 3 * q + i, value, table)
+        keep_ref[i] = clark
+        keep_ref[3 + i] = similar
+        clark = jnp.where(in_first, clark, pltpu.roll(clark, width // 2, 2))
+        similar = jnp.where(in_first, pltpu.roll(similar, width // 2, 2), similar)
+        send_ref[i] = jnp.where(first, clark, similar)
     sums_ref[...] = table
-
-    first = lane_index((layers, rows, width)) < width // 2
-    for i in range(3):
-        keep_ref[i] = clark_all[i, pl.ds(me_s * layers, layers)]
-        keep_ref[3 + i] = similar_all[i, pl.ds(me_s * layers, layers)]
-        clark = clark_all[i, pl.ds((1 - me_s) * layers, layers)]
-        similar = similar_all[i, pl.ds((1 - me_s) * layers, layers)]
-        turn = me_s == 0
-        clark = jnp.where(turn, clark, pltpu.roll(clark, width // 2, 2))
-        similar = jnp.where(turn, pltpu.roll(similar, width // 2, 2), similar)
-        send_ref[i] = jnp.where(first, clark, similar)
 
 
 def finish_kernel(
@@ -375,9 +428,11 @@
     )
     a_rest, b_rest = pair_a(rest), pair_b(rest)
 
-    matrices = np.zeros((2 * cells + 2 * width, 4 * cells), ml_dtypes.bfloat16)
+    matrices = np.zeros((2 * cells + 4 * width, 4 * cells), ml_dtypes.bfloat16)
     matrices[:cells], matrices[cells : 2 * cells] = plane_constants(both, rows)
-    matrices[2 * cells :, : 2 * width] = span_constants(width)
+    single_pass, split_pass = span_constants(width)
+    matrices[2 * cells : 2 * cells + 2 * width, : 2 * width] = single_pass
+    matrices[2 * cells :, 2 * width : 6 * width] = split_pass
     weights = jnp.asarray(matrices)
     single, brief = jnp.float32, jnp.bfloat16
     block = (4, both, rows, width)
@@ -391,19 +446,20 @@
         mib=16,
         hint=2**31,
     )
-    a_raw, a_mean, a_second = call(
+    quarter = (4, layers, rows, width)
+    a_raw, a_packed, a_slopes, a_second = call(
         mate_kernel,
         "mate",
         (a_mine, a_rest, upper, lower, weights),
-        (block, block, (cells, 7 * width)),
-        [*pieces, ((cells, 7 * width), brief), ((cells, 7 * width), brief)],
+        (block, quarter, (4, layers, reach, width), (cells, 7 * width)),
+        [*pieces, ((cells, 7 * width), brief), ((cells, 7 * width), brief), (block, single)],
         mib=16,
         hint=2**29,
     )
     keep, send, sums = call(
         functools.partial(flux_kernel, walls),
         "flux",
-        (b_mine, b_rest, a_raw, a_mean, a_second, upper, lower, products, weights),
+        (b_mine, b_rest, a_raw, a_packed, a_slopes, a_second, upper, lower, products, weights),
         ((6, layers, rows, width), (3, layers, rows, width), (rows, width)),
         [
             (block, single),
@@ -411,11 +467,11 @@
             ((cells, 4 * width), brief),
             ((cells, 3 * width), brief),
             ((cells, 3 * width), brief),
-            ((4, both + 2, 2 * rows, width), single),
+            (block, single),
             ((cells, 7 * width), brief),
             ((cells, 7 * width), brief),
-            ((3, both, rows, width), single),
-            ((3, both, rows, width), single),
+            ((4, layers, 2 * rows, width), single),
+            (quarter, single),
         ],
         mib=24,
     )

time: 33.4 us -> 33.2 us (level)
  no operation moved by 1% of the time
where the time goes in v18:
time: 33.2 us; the launch traced here: 33 us
  starting transfers between devices  15.5 us (47%)
  waiting for transfers between devices  8.65 us (26%)
  Pallas kernels  7.18 us (22%)
  local copies, waits for them, and re-layouts  0.95 us (3%)
  between operations  0.74 us (2%)
    pallas_call x6, Pallas kernels, call(): pl.pallas_call(kernel, out_shape=tuple((jax.ShapeDtypeStruct(shape, jnp.f...  7.18 us
    ppermute x2, starting transfers between devices, pair_b(): lax.ppermute(value, 'wall', [(w, min(max((w + 1 ^ 1) - 1, 0), walls - 1))...  5.02 us
    ppermute x3, starting transfers between devices, from_span(): return lax.ppermute(value, 'span', [(p, p ^ step) for p in range(spans)])  3.55 us
    ppermute x3, waiting for transfers between devices, swap(): return lax.ppermute(value, 'stream', [(0, 1), (1, 0)])  3.22 us
    ppermute x3, starting transfers between devices, swap(): return lax.ppermute(value, 'stream', [(0, 1), (1, 0)])  2.83 us
    ppermute x1, starting transfers between devices, shards(): part_strip = lax.ppermute(first, ('span', 'stream'), to_other)  2.45 us
    ppermute x3, waiting for transfers between devices, from_span(): return lax.ppermute(value, 'span', [(p, p ^ step) for p in range(spans)])  1.98 us
    ppermute x2, waiting for transfers between devices, pair_b(): lax.ppermute(value, 'wall', [(w, min(max((w + 1 ^ 1) - 1, 0), walls - 1))...  1.81 us
  transfers between devices with their start and end apart: 12, of which 5 were waited for; matrix products, arithmetic and copies ran while one was open for 0% of the time, Pallas kernels for 9%

profile of v18, /device:TPU:4, one launch (start us, length us, event | category | flops | bytes accessed | tf_op | source)
XLA Modules:
  0.0 33.0 jit_solution(11316809179972303700)
XLA Ops:
  0.6 0.9 %copy-done.1 = f32[4,8,16,128]{3,2,1,0:T(8,128)S(1)} copy-done((f32[4,8,16,128]{3,2,1,0:T(8,128)S(1)}, f32[4,8,16,128]{3,2,1,0:T(8,128)}, u32[]{:S(2)}) %copy-start.1) | copy-done | bytes 262168
  1.6 0.4 %pack.1 = (f32[20,16,128]{2,1,0:T(8,128)S(1)}, f32[20,16,128]{2,1,0:T(8,128)S(1)}, f32[4,16,128]{2,1,0:T(8,128)S(1)}, f32[4,16,128]{2,1,0:T(8,128)S(1)}) custom-call(f32[4,8,16,128]{3,2,1,0:T(8,128)S(1)} %copy-done.1), custom_call_target="tpu_custom_call" | custom-call | tf_op jit(solution)/shard_map/pack/pallas_call | solution.py:375
  2.0 1.6 %collective-permute-start.2 = (f32[20,16,128]{2,1,0:T(8,128)S(1)}, f32[20,16,128]{2,1,0:T(8,128)S(1)}, u32[]{:S(2)}, u32[]{:S(2)}) collective-permute-start(f32[20,16,128]{2,1,0:T(8,128)S(1)} %get-tuple-element.23), channel_id=1, source_target_pairs={{0,1},{1,0},{2,3},{3,2},{4,5},{5,4},{6,7},{7,6},{8,9},{9,8},{10,11... | collective-permute-start | bytes 491528 | tf_op jit(solution)/shard_map/ppermute | solution.py:396
  3.5 1.6 %collective-permute-start.3 = (f32[4,16,128]{2,1,0:T(8,128)S(1)}, f32[4,16,128]{2,1,0:T(8,128)S(1)}, u32[]{:S(2)}, u32[]{:S(2)}) collective-permute-start(f32[4,16,128]{2,1,0:T(8,128)S(1)} %get-tuple-element.24), channel_id=1, source_target_pairs={{1,25},{0,8},{9,1},{8,16},{17,9},{16,24},{25,17},{24,0},{3,27},{2,... | collective-permute-start | bytes 98312 | tf_op jit(solution)/shard_map/ppermute | solution.py:420
  5.1 2.4 %collective-permute-start.4 = (f32[4,16,128]{2,1,0:T(8,128)S(1)}, f32[4,16,128]{2,1,0:T(8,128)S(1)}, u32[]{:S(2)}, u32[]{:S(2)}) collective-permute-start(f32[4,16,128]{2,1,0:T(8,128)S(1)} %get-tuple-element.25), channel_id=1, source_target_pairs={{0,25},{1,8},{8,1},{9,16},{16,9},{17,24},{24,17},{25,0},{2,27},{3,... | collective-permute-start | bytes 98312 | tf_op jit(solution)/shard_map/ppermute | solution.py:419
  7.5 0.0 collective-permute-start.1
  7.5 2.5 %collective-permute-start = (f32[20,16,128]{2,1,0:T(8,128)S(1)}, f32[20,16,128]{2,1,0:T(8,128)S(1)}, u32[]{:S(2)}, u32[]{:S(2)}) collective-permute-start(f32[20,16,128]{2,1,0:T(8,128)S(1)} %get-tuple-element.27.mine), channel_id=1, source_target_pairs={{0,0},{2,4},{4,2},{6,6},{1,1},{3,5},{5,3},{7,7},{8,8},{10,12},{12,... | collective-permute-start | bytes 491528 | tf_op jit(solution)/shard_map/ppermute | solution.py:402
  10.1 1.6 %collective-permute-done.4.part_strip = f32[4,16,128]{2,1,0:T(8,128)S(1)} collective-permute-done((f32[4,16,128]{2,1,0:T(8,128)S(1)}, f32[4,16,128]{2,1,0:T(8,128)S(1)}, u32[]{:S(2)}, u32[]{:S(2)}) %collective-permute-start.4) | collective-permute-done | bytes 32800 | tf_op jit(solution)/shard_map/ppermute | solution.py:419
  11.7 0.1 collective-permute-start.6
  11.8 2.5 %collective-permute-start.5 = (f32[28,16,128]{2,1,0:T(8,128)S(1)}, f32[28,16,128]{2,1,0:T(8,128)S(1)}, u32[]{:S(2)}, u32[]{:S(2)}) collective-permute-start(f32[28,16,128]{2,1,0:T(8,128)S(1)} %rest.1), channel_id=1, source_target_pairs={{0,0},{2,4},{4,2},{6,6},{1,1},{3,5},{5,3},{7,7},{8,8},{10,12},{12,... | collective-permute-start | bytes 688136 | tf_op jit(solution)/shard_map/ppermute | solution.py:402
  14.3 0.0 collective-permute-done.1.a_mine
  14.3 1.1 %centre.1 = (f32[256,512]{1,0:T(8,128)S(1)}, f32[256,512]{1,0:T(8,128)S(1)}, f32[256,384]{1,0:T(8,128)S(1)}) custom-call(f32[20,16,128]{2,1,0:T(8,128)S(1)} %get-tuple-element.27.mine, f32[28,16,128]{2,1,0:T(8,128)S(1)} %rest.1, bf16[1024,1024]{1,0:T(8,128)(2,1)S(1)} %copy-done), custom_call_target="tpu_custom_call" | custom-call | flops 2147483648 | tf_op jit(solution)/shard_map/centre/pallas_call | solution.py:375
  15.4 1.9 %mate.1 = (f32[4,16,16,128]{3,2,1,0:T(8,128)S(1)}, f32[4,8,16,128]{3,2,1,0:T(8,128)S(1)}, f32[4,8,8,128]{3,2,1,0:T(8,128)S(1)}, f32[256,896]{1,0:T(8,128)S(1)}) custom-call(f32[20,16,128]{2,1,0:T(8,128)S(1)} %collective-permute-done.1.a_mine, f32[28,16,128]{2,1,0:T(8,128)S(1)} %collective-permute-done.6.a_rest, f32[256,512]{1,0:T(8,128)S(1)} %get-tuple-element.28.upper, ...), custom_call_target="tpu_custom_call" | custom-call | flops 536870912 | tf_op jit(solution)/shard_map/mate/pallas_call | solution.py:375
  17.3 1.8 %collective-permute-done.5.b_rest = f32[28,16,128]{2,1,0:T(8,128)S(1)} collective-permute-done((f32[28,16,128]{2,1,0:T(8,128)S(1)}, f32[28,16,128]{2,1,0:T(8,128)S(1)}, u32[]{:S(2)}, u32[]{:S(2)}) %collective-permute-start.5) | collective-permute-done | bytes 229408 | tf_op jit(solution)/shard_map/ppermute | solution.py:402
  19.1 2.8 %flux.1 = (f32[6,8,16,128]{3,2,1,0:T(8,128)S(1)}, f32[3,8,16,128]{3,2,1,0:T(8,128)S(1)}, f32[16,128]{1,0:T(8,128)S(1)}) custom-call(f32[20,16,128]{2,1,0:T(8,128)S(1)} %collective-permute-done.b_mine, f32[28,16,128]{2,1,0:T(8,128)S(1)} %collective-permute-done.5.b_rest, f32[4,16,16,128]{3,2,1,0:T(8,128)S(1)} %get-tuple-element.30.a_raw, ...), custom_call_target="tpu_custom_call" | custom-call | tf_op jit(solution)/shard_map/flux/pallas_call | solution.py:375
  22.0 0.9 %collective-permute-start.9 = (f32[16,128]{1,0:T(8,128)S(1)}, f32[16,128]{1,0:T(8,128)S(1)}, u32[]{:S(2)}, u32[]{:S(2)}) collective-permute-start(f32[16,128]{1,0:T(8,128)S(1)} %get-tuple-element.35), channel_id=1, source_target_pairs={{0,16},{8,24},{16,0},{24,8},{1,17},{9,25},{17,1},{25,9},{2,18},{10... | collective-permute-start | bytes 24584 | tf_op jit(solution)/shard_map/ppermute | solution.py:482
  22.8 1.5 %collective-permute-start.8 = (f32[16,128]{1,0:T(8,128)S(1)}, f32[16,128]{1,0:T(8,128)S(1)}, u32[]{:S(2)}, u32[]{:S(2)}) collective-permute-start(f32[16,128]{1,0:T(8,128)S(1)} %get-tuple-element.35), channel_id=1, source_target_pairs={{0,24},{8,16},{16,8},{24,0},{1,25},{9,17},{17,9},{25,1},{2,26},{10... | collective-permute-start | bytes 24584 | tf_op jit(solution)/shard_map/ppermute | solution.py:482
  24.4 1.2 %collective-permute-start.7 = (f32[16,128]{1,0:T(8,128)S(1)}, f32[16,128]{1,0:T(8,128)S(1)}, u32[]{:S(2)}, u32[]{:S(2)}) collective-permute-start(f32[16,128]{1,0:T(8,128)S(1)} %get-tuple-element.35), channel_id=1, source_target_pairs={{0,8},{8,0},{16,24},{24,16},{1,9},{9,1},{17,25},{25,17},{2,10},{10... | collective-permute-start | bytes 24584 | tf_op jit(solution)/shard_map/ppermute | solution.py:482
  25.5 0.8 %collective-permute-start.11 = (f32[3,8,16,128]{3,2,1,0:T(8,128)S(1)}, f32[3,8,16,128]{3,2,1,0:T(8,128)S(1)}, u32[]{:S(2)}, u32[]{:S(2)}) collective-permute-start(f32[3,8,16,128]{3,2,1,0:T(8,128)S(1)} %get-tuple-element.37), channel_id=1, source_target_pairs={{0,1},{1,0},{2,3},{3,2},{4,5},{5,4},{6,7},{7,6},{8,9},{9,8},{10,11... | collective-permute-start | bytes 589832 | tf_op jit(solution)/shard_map/ppermute | solution.py:396
  26.3 0.3 collective-permute-done.9
  26.6 1.7 %collective-permute-done.8 = f32[16,128]{1,0:T(8,128)S(1)} collective-permute-done((f32[16,128]{1,0:T(8,128)S(1)}, f32[16,128]{1,0:T(8,128)S(1)}, u32[]{:S(2)}, u32[]{:S(2)}) %collective-permute-start.8) | collective-permute-done | bytes 8224 | tf_op jit(solution)/shard_map/ppermute | solution.py:482
  28.3 0.5 %collective-permute-start.10 = (f32[16,128]{1,0:T(8,128)S(1)}, f32[16,128]{1,0:T(8,128)S(1)}, u32[]{:S(2)}, u32[]{:S(2)}) collective-permute-start(f32[16,128]{1,0:T(8,128)S(1)} %add_add_fusion), channel_id=1, source_target_pairs={{0,1},{1,0},{2,3},{3,2},{4,5},{5,4},{6,7},{7,6},{8,9},{9,8},{10,11... | collective-permute-start | bytes 24584 | tf_op jit(solution)/shard_map/ppermute | solution.py:396
  28.8 3.2 %collective-permute-done.10 = f32[16,128]{1,0:T(8,128)S(1)} collective-permute-done((f32[16,128]{1,0:T(8,128)S(1)}, f32[16,128]{1,0:T(8,128)S(1)}, u32[]{:S(2)}, u32[]{:S(2)}) %collective-permute-start.10) | collective-permute-done | bytes 8224 | tf_op jit(solution)/shard_map/ppermute | solution.py:396
  32.0 1.0 %finish.1 = (f32[3,8,16,128]{3,2,1,0:T(8,128)}, f32[3,8,16,128]{3,2,1,0:T(8,128)}, f32[3,16]{1,0:T(4,128)}, f32[3,16]{1,0:T(4,128)}) custom-call(f32[16,128]{1,0:T(8,128)S(1)} %add.15.sums, f32[6,8,16,128]{3,2,1,0:T(8,128)S(1)} %get-tuple-element.36.keep, f32[3,8,16,128]{3,2,1,0:T(8,128)S(1)} %collective-permute-done.11.come), custom_call_target="tpu_custom_call" | custom-call | tf_op jit(solution)/shard_map/finish/pallas_call | solution.py:375
  (12 shorter events, 0.0 us)
Async XLA Ops:
  0.6 1.0 %copy-start.1 = (f32[4,8,16,128]{3,2,1,0:T(8,128)S(1)}, f32[4,8,16,128]{3,2,1,0:T(8,128)}, u32[]{:S(2)}) copy-start(f32[4,8,16,128]{3,2,1,0:T(8,128)} %own.1) | copy-start | bytes 786436
  2.0 9.7 %collective-permute-start.2 = (f32[20,16,128]{2,1,0:T(8,128)S(1)}, f32[20,16,128]{2,1,0:T(8,128)S(1)}, u32[]{:S(2)}, u32[]{:S(2)}) collective-permute-start(f32[20,16,128]{2,1,0:T(8,128)S(1)} %get-tuple-element.23), channel_id=1, source_target_pairs={{0,1},{1,0},{2,3},{3,2},{4,5},{5,4},{6,7},{7,6},{8,9},{9,8},{10,11... | collective-permute-start | bytes 491528 | tf_op jit(solution)/shard_map/ppermute | solution.py:396
  3.5 6.6 %collective-permute-start.3 = (f32[4,16,128]{2,1,0:T(8,128)S(1)}, f32[4,16,128]{2,1,0:T(8,128)S(1)}, u32[]{:S(2)}, u32[]{:S(2)}) collective-permute-start(f32[4,16,128]{2,1,0:T(8,128)S(1)} %get-tuple-element.24), channel_id=1, source_target_pairs={{1,25},{0,8},{9,1},{8,16},{17,9},{16,24},{25,17},{24,0},{3,27},{2,... | collective-permute-start | bytes 98312 | tf_op jit(solution)/shard_map/ppermute | solution.py:420
  5.1 6.6 %collective-permute-start.4 = (f32[4,16,128]{2,1,0:T(8,128)S(1)}, f32[4,16,128]{2,1,0:T(8,128)S(1)}, u32[]{:S(2)}, u32[]{:S(2)}) collective-permute-start(f32[4,16,128]{2,1,0:T(8,128)S(1)} %get-tuple-element.25), channel_id=1, source_target_pairs={{0,25},{1,8},{8,1},{9,16},{16,9},{17,24},{24,17},{25,0},{2,27},{3,... | collective-permute-start | bytes 98312 | tf_op jit(solution)/shard_map/ppermute | solution.py:419
  7.5 6.8 %copy-start = (bf16[1024,1024]{1,0:T(8,128)(2,1)S(1)}, bf16[1024,1024]{1,0:T(8,128)(2,1)}, u32[]{:S(2)}) copy-start(bf16[1024,1024]{1,0:T(8,128)(2,1)} %constant.2.clone.weights) | copy-start | bytes 6291460
  7.5 6.8 %collective-permute-start.1 = (f32[20,16,128]{2,1,0:T(8,128)S(1)}, f32[20,16,128]{2,1,0:T(8,128)S(1)}, u32[]{:S(2)}, u32[]{:S(2)}) collective-permute-start(f32[20,16,128]{2,1,0:T(8,128)S(1)} %get-tuple-element.27.mine), channel_id=1, source_target_pairs={{0,2},{2,0},{4,6},{6,4},{1,3},{3,1},{5,7},{7,5},{8,10},{10,8},{12,... | collective-permute-start | bytes 491528 | tf_op jit(solution)/shard_map/ppermute | solution.py:399
  7.5 6.8 %collective-permute-start = (f32[20,16,128]{2,1,0:T(8,128)S(1)}, f32[20,16,128]{2,1,0:T(8,128)S(1)}, u32[]{:S(2)}, u32[]{:S(2)}) collective-permute-start(f32[20,16,128]{2,1,0:T(8,128)S(1)} %get-tuple-element.27.mine), channel_id=1, source_target_pairs={{0,0},{2,4},{4,2},{6,6},{1,1},{3,5},{5,3},{7,7},{8,8},{10,12},{12,... | collective-permute-start | bytes 491528 | tf_op jit(solution)/shard_map/ppermute | solution.py:402
  11.7 3.7 %collective-permute-start.6 = (f32[28,16,128]{2,1,0:T(8,128)S(1)}, f32[28,16,128]{2,1,0:T(8,128)S(1)}, u32[]{:S(2)}, u32[]{:S(2)}) collective-permute-start(f32[28,16,128]{2,1,0:T(8,128)S(1)} %rest.1), channel_id=1, source_target_pairs={{0,2},{2,0},{4,6},{6,4},{1,3},{3,1},{5,7},{7,5},{8,10},{10,8},{12,... | collective-permute-start | bytes 688136 | tf_op jit(solution)/shard_map/ppermute | solution.py:399
  11.8 7.3 %collective-permute-start.5 = (f32[28,16,128]{2,1,0:T(8,128)S(1)}, f32[28,16,128]{2,1,0:T(8,128)S(1)}, u32[]{:S(2)}, u32[]{:S(2)}) collective-permute-start(f32[28,16,128]{2,1,0:T(8,128)S(1)} %rest.1), channel_id=1, source_target_pairs={{0,0},{2,4},{4,2},{6,6},{1,1},{3,5},{5,3},{7,7},{8,8},{10,12},{12,... | collective-permute-start | bytes 688136 | tf_op jit(solution)/shard_map/ppermute | solution.py:402
  22.0 4.6 %collective-permute-start.9 = (f32[16,128]{1,0:T(8,128)S(1)}, f32[16,128]{1,0:T(8,128)S(1)}, u32[]{:S(2)}, u32[]{:S(2)}) collective-permute-start(f32[16,128]{1,0:T(8,128)S(1)} %get-tuple-element.35), channel_id=1, source_target_pairs={{0,16},{8,24},{16,0},{24,8},{1,17},{9,25},{17,1},{25,9},{2,18},{10... | collective-permute-start | bytes 24584 | tf_op jit(solution)/shard_map/ppermute | solution.py:482
  22.8 5.4 %collective-permute-start.8 = (f32[16,128]{1,0:T(8,128)S(1)}, f32[16,128]{1,0:T(8,128)S(1)}, u32[]{:S(2)}, u32[]{:S(2)}) collective-permute-start(f32[16,128]{1,0:T(8,128)S(1)} %get-tuple-element.35), channel_id=1, source_target_pairs={{0,24},{8,16},{16,8},{24,0},{1,25},{9,17},{17,9},{25,1},{2,26},{10... | collective-permute-start | bytes 24584 | tf_op jit(solution)/shard_map/ppermute | solution.py:482
  24.4 3.9 %collective-permute-start.7 = (f32[16,128]{1,0:T(8,128)S(1)}, f32[16,128]{1,0:T(8,128)S(1)}, u32[]{:S(2)}, u32[]{:S(2)}) collective-permute-start(f32[16,128]{1,0:T(8,128)S(1)} %get-tuple-element.35), channel_id=1, source_target_pairs={{0,8},{8,0},{16,24},{24,16},{1,9},{9,1},{17,25},{25,17},{2,10},{10... | collective-permute-start | bytes 24584 | tf_op jit(solution)/shard_map/ppermute | solution.py:482
  25.5 6.5 %collective-permute-start.11 = (f32[3,8,16,128]{3,2,1,0:T(8,128)S(1)}, f32[3,8,16,128]{3,2,1,0:T(8,128)S(1)}, u32[]{:S(2)}, u32[]{:S(2)}) collective-permute-start(f32[3,8,16,128]{3,2,1,0:T(8,128)S(1)} %get-tuple-element.37), channel_id=1, source_target_pairs={{0,1},{1,0},{2,3},{3,2},{4,5},{5,4},{6,7},{7,6},{8,9},{9,8},{10,11... | collective-permute-start | bytes 589832 | tf_op jit(solution)/shard_map/ppermute | solution.py:396
  28.3 3.7 %collective-permute-start.10 = (f32[16,128]{1,0:T(8,128)S(1)}, f32[16,128]{1,0:T(8,128)S(1)}, u32[]{:S(2)}, u32[]{:S(2)}) collective-permute-start(f32[16,128]{1,0:T(8,128)S(1)} %add_add_fusion), channel_id=1, source_target_pairs={{0,1},{1,0},{2,3},{3,2},{4,5},{5,4},{6,7},{7,6},{8,9},{9,8},{10,11... | collective-permute-start | bytes 24584 | tf_op jit(solution)/shard_map/ppermute | solution.py:396

commit v19 on v18

--- a/solution.py
+++ b/solution.py
@@ -156,39 +156,46 @@
     return slice(t * width, (t + 1) * width)
 
 
-def planes_of(weights, part, high, low):
-    cells = weights.shape[1] // 4
-    along = pl.ds(part * cells if isinstance(part, int) else pl.multiple_of(part * cells, cells), cells)
-    plane_h, plane_l = weights[:cells, along], weights[cells : 2 * cells, along]
-    return dot(plane_h, high) + dot(plane_l, high) + dot(plane_h, low)
-
-
-def bring(mine, rest, raw, high, low, keep=None):
+def put_parts(parts, down, across, value):
+    third = parts.shape[0] // 3
+    high, low = halves(value)
+    for k, part in enumerate((high, high, low)):
+        parts[pl.ds(k * third + down, value.shape[0]), across] = part
+
+
+def planes_of(planes, part, parts):
+    depth = parts.shape[0]
+    start = part * depth if isinstance(part, int) else pl.multiple_of(part * depth, depth)
+    return dot(planes[:, pl.ds(start, depth)], parts[...])
+
+
+def bring(mine, rest, raw, parts, keep=None):
     rows, width = mine.shape[1:]
     for f, layer, value in unpack(mine, rest, lax.axis_index("stream")):
         count = value.shape[0]
         value = value if keep is None else value * keep
         raw[f, pl.ds(layer, count)] = value
-        down = pl.ds(pl.multiple_of(layer * rows, count * rows), count * rows)
-        high[down, column(f)], low[down, column(f)] = halves(value.reshape(-1, width))
-
-
-def centre_kernel(mine, rest, weights, upper, lower, products, centre, in_h, in_l, prod_h, prod_l):
-    cells, width = in_h.shape[0], mine.shape[-1]
-    bring(mine, rest, centre, in_h, in_l)
+        down = pl.multiple_of(layer * rows, count * rows)
+        put_parts(parts, down, column(f), value.reshape(-1, width))
+
+
+def centre_kernel(
+    mine, rest, planes, upper, lower, products, centre, parts, prod
+):
+    bring(mine, rest, centre, parts)
     for i in range(3):
-        value = (centre[i] * centre[3]).reshape(cells, width)
-        prod_h[:, column(i)], prod_l[:, column(i)] = halves(value)
-    upper[...] = planes_of(weights, 1, in_h[...], in_l[...])
-    lower[...] = planes_of(weights, 0, in_h[...], in_l[...])
-    products[...] = planes_of(weights, 2, prod_h[...], prod_l[...])
-
-
-def span_pass(weights, planes, both):
+        value = centre[i] * centre[3]
+        put_parts(prod, 0, column(i), value.reshape(-1, value.shape[-1]))
+    upper[...] = planes_of(planes, 1, parts)
+    lower[...] = planes_of(planes, 0, parts)
+    products[...] = planes_of(planes, 2, prod)
+
+
+def span_pass(spans, planes, both):
     cells = planes.shape[0]
     rows = cells // both
     width = 128
-    span_w = weights[2 * cells : 2 * cells + 2 * width, : 2 * width]
+    span_w = spans[: 2 * width, : 2 * width]
     high, low = halves(planes)
     tiles = planes.shape[1] // width
     parts = [jnp.concatenate([high[:, column(t)], low[:, column(t)]], axis=1) for t in range(tiles)]
@@ -197,18 +204,18 @@
     return [result[t * cells : (t + 1) * cells].reshape(both, rows, width) for t in range(tiles)]
 
 
-def second_input(means, high, low):
+def second_input(means, parts):
     tiles = means + [means[i] * means[3] for i in range(3)]
     for t, value in enumerate(tiles):
-        high[:, column(t)], low[:, column(t)] = halves(value.reshape(-1, value.shape[-1]))
-
-
-def packed_pass(weights, planes):
+        put_parts(parts, 0, column(t), value.reshape(-1, value.shape[-1]))
+
+
+def packed_pass(spans, planes):
     cells = planes.shape[0]
     some, width = cells // 2, 128
     me_s = lax.axis_index("stream")
     along = pl.ds(pl.multiple_of((1 + me_s) * 2 * width, 2 * width), 2 * width)
-    matrix = weights[2 * cells : 2 * cells + 4 * width, along]
+    matrix = spans[:, along]
     high, low = halves(planes)
     tiles = planes.shape[1] // width
     parts = [
@@ -243,25 +250,25 @@
 
 
 def mate_kernel(
-    a_mine, a_rest, upper, lower, weights, raw, packed, slopes, second, in_h, in_l, mid_h, mid_l, mean
+    a_mine, a_rest, upper, lower, matrices, spans, raw, packed, slopes, second, parts, mid, mean
 ):
     both, rows = raw.shape[1:3]
     odd = lax.rem(lax.axis_index("wall"), 2)
-    bring(a_mine, a_rest, raw, in_h, in_l)
+    bring(a_mine, a_rest, raw, parts)
     planes = jnp.where(odd == 1, upper[...], lower[...])
-    planes = planes + planes_of(weights, 1 - odd, in_h[...], in_l[...])
-    means = span_pass(weights, planes, both)
+    planes = planes + planes_of(matrices, 1 - odd, parts)
+    means = span_pass(spans, planes, both)
     for t, value, slope in pack_means(mean, means, pl.ds(pl.multiple_of(odd * reach, reach), reach)):
         packed[t] = value
         slopes[t] = slope
-    second_input(means, mid_h, mid_l)
-    second[...] = planes_of(weights, 1 - odd, mid_h[...], mid_l[...])
+    second_input(means, mid)
+    second[...] = planes_of(matrices, 1 - odd, mid)
 
 
 def flux_kernel(
-    walls, b_mine, b_rest, a_raw, a_packed, a_slopes, a_second, upper, lower, products, weights,
+    walls, b_mine, b_rest, a_raw, a_packed, a_slopes, a_second, upper, lower, products, matrices, spans,
     keep_ref, send_ref, sums_ref,
-    raw, in_h, in_l, prod_h, prod_l, mean, mid_h, mid_l, packed, slopes,
+    raw, parts, prod, mean, mid, packed, slopes,
 ):
     _, layers, rows, width = keep_ref.shape
     both = 2 * layers
@@ -272,14 +279,14 @@
     at_end = (me_w == 0) | (me_w == walls - 1)
     keep_b = jnp.where(at_end, 0.0, 1.0).astype(jnp.float32)
 
-    bring(b_mine, b_rest, raw, in_h, in_l, keep_b)
+    bring(b_mine, b_rest, raw, parts, keep_b)
 
     planes = jnp.where(odd == 0, upper[...], lower[...])
-    planes = planes + planes_of(weights, odd, in_h[...], in_l[...])
+    planes = planes + planes_of(matrices, odd, parts)
     row = lax.rem(lax.broadcasted_iota(jnp.int32, planes.shape, 0), rows)
     inside = (row < reach) == (odd == 1)
     planes = jnp.where(jnp.logical_or(inside, jnp.logical_not(at_end)), planes, 0.0)
-    means = span_pass(weights, planes, both)
+    means = span_pass(spans, planes, both)
     rows_b = pl.ds(pl.multiple_of(odd * rows, rows), rows)
     rows_a = pl.ds(pl.multiple_of((1 - odd) * rows, rows), rows)
     near_b = pl.ds(pl.multiple_of(odd * reach, reach), reach)
@@ -289,8 +296,8 @@
         packed[t, :, rows_a, :] = a_packed[t]
         slopes[t, :, near_b, :] = slope
         slopes[t, :, near_a, :] = a_slopes[t]
-    second_input(means, mid_h, mid_l)
-    second = packed_pass(weights, a_second[...] + planes_of(weights, odd, mid_h[...], mid_l[...]))
+    second_input(means, mid)
+    second = packed_pass(spans, a_second[...] + planes_of(matrices, odd, mid))
     second = [value.reshape(layers, rows, width) for value in second]
 
     def around(f):
@@ -301,8 +308,8 @@
     temperature = around(3)
     for i in range(3):
         value = (around(i) * temperature).reshape(cells, width)
-        prod_h[:, column(i)], prod_l[:, column(i)] = halves(value)
-    flux = packed_pass(weights, products[...] + planes_of(weights, 3, prod_h[...], prod_l[...]))
+        put_parts(prod, 0, column(i), value)
+    flux = packed_pass(spans, products[...] + planes_of(matrices, 3, prod))
     flux = [value.reshape(layers, rows, width) for value in flux]
 
     mid_rows = slice(reach, reach + rows)
@@ -428,48 +435,46 @@
     )
     a_rest, b_rest = pair_a(rest), pair_b(rest)
 
-    matrices = np.zeros((2 * cells + 4 * width, 4 * cells), ml_dtypes.bfloat16)
-    matrices[:cells], matrices[cells : 2 * cells] = plane_constants(both, rows)
+    high, low = plane_constants(both, rows)
+    thirds = [(high[:, k : k + cells], low[:, k : k + cells], high[:, k : k + cells]) for k in range(0, 4 * cells, cells)]
+    matrices = jnp.asarray(np.concatenate([part for third in thirds for part in third], axis=1))
     single_pass, split_pass = span_constants(width)
-    matrices[2 * cells : 2 * cells + 2 * width, : 2 * width] = single_pass
-    matrices[2 * cells :, 2 * width : 6 * width] = split_pass
-    weights = jnp.asarray(matrices)
+    both_passes = np.zeros((4 * width, 6 * width), ml_dtypes.bfloat16)
+    both_passes[: 2 * width, : 2 * width] = single_pass
+    both_passes[:, 2 * width :] = split_pass
+    passes = jnp.asarray(both_passes)
     single, brief = jnp.float32, jnp.bfloat16
-    block = (4, both, rows, width)
-    pieces = [((cells, 4 * width), brief), ((cells, 4 * width), brief)]
+    block, quarter = (4, both, rows, width), (4, layers, rows, width)
+    four, three, seven = (((3 * cells, n * width), brief) for n in (4, 3, 7))
     upper, lower, products = call(
         centre_kernel,
         "centre",
-        (mine_now, rest, weights),
+        (mine_now, rest, matrices),
         ((cells, 4 * width), (cells, 4 * width), (cells, 3 * width)),
-        [(block, single), *pieces, ((cells, 3 * width), brief), ((cells, 3 * width), brief)],
+        [(block, single), four, three],
         mib=16,
         hint=2**31,
     )
-    quarter = (4, layers, rows, width)
     a_raw, a_packed, a_slopes, a_second = call(
         mate_kernel,
         "mate",
-        (a_mine, a_rest, upper, lower, weights),
+        (a_mine, a_rest, upper, lower, matrices, passes),
         (block, quarter, (4, layers, reach, width), (cells, 7 * width)),
-        [*pieces, ((cells, 7 * width), brief), ((cells, 7 * width), brief), (block, single)],
+        [four, seven, (block, single)],
         mib=16,
         hint=2**29,
     )
     keep, send, sums = call(
         functools.partial(flux_kernel, walls),
         "flux",
-        (b_mine, b_rest, a_raw, a_packed, a_slopes, a_second, upper, lower, products, weights),
+        (b_mine, b_rest, a_raw, a_packed, a_slopes, a_second, upper, lower, products, matrices, passes),
         ((6, layers, rows, width), (3, layers, rows, width), (rows, width)),
         [
             (block, single),
-            ((cells, 4 * width), brief),
-            ((cells, 4 * width), brief),
-            ((cells, 3 * width), brief),
-            ((cells, 3 * width), brief),
+            four,
+            three,
             (block, single),
-            ((cells, 7 * width), brief),
-            ((cells, 7 * width), brief),
+            seven,
             ((4, layers, 2 * rows, width), single),
             (quarter, single),
         ],

time: 33.2 us -> 33.1 us (level)
  Pallas kernels: 7.18 us -> 6.67 us
  waiting for transfers between devices: 8.65 us -> 9.01 us
    pallas_call x6, Pallas kernels: 7.18 us -> 6.67 us  [call(): pl.pallas_call(kernel, out_shape=tuple((jax.ShapeDtypeStruct(shape, jnp.f...]
    ppermute x2, waiting for transfers between devices: 1.81 us -> 2.17 us  [pair_b(): lax.ppermute(value, 'wall', [(w, min(max((w + 1 ^ 1) - 1, 0), walls - 1))...]
    unnamed x4 -> x6, local copies, waits for them, and re-layouts: 0.95 us -> 0.95 us
  transfers between devices with their start and end apart: 12 -> 12, of which waited for: 5 -> 5; matrix products, arithmetic and copies ran while one was open for 0% -> 0% of each run, Pallas kernels for 9% -> 8%
where the time goes in v19:
time: 33.1 us; the launch traced here: 32.9 us
  starting transfers between devices  15.5 us (47%)
  waiting for transfers between devices  9.01 us (27%)
  Pallas kernels  6.67 us (20%)
  local copies, waits for them, and re-layouts  0.95 us (3%)
  between operations  0.76 us (2%)
    pallas_call x6, Pallas kernels, call(): pl.pallas_call(kernel, out_shape=tuple((jax.ShapeDtypeStruct(shape, jnp.f...  6.67 us
    ppermute x2, starting transfers between devices, pair_b(): lax.ppermute(value, 'wall', [(w, min(max((w + 1 ^ 1) - 1, 0), walls - 1))...  5.02 us
    ppermute x3, starting transfers between devices, from_span(): return lax.ppermute(value, 'span', [(p, p ^ step) for p in range(spans)])  3.55 us
    ppermute x3, waiting for transfers between devices, swap(): return lax.ppermute(value, 'stream', [(0, 1), (1, 0)])  3.22 us
    ppermute x3, starting transfers between devices, swap(): return lax.ppermute(value, 'stream', [(0, 1), (1, 0)])  2.83 us
    ppermute x1, starting transfers between devices, shards(): part_strip = lax.ppermute(first, ('span', 'stream'), to_other)  2.45 us
    ppermute x2, waiting for transfers between devices, pair_b(): lax.ppermute(value, 'wall', [(w, min(max((w + 1 ^ 1) - 1, 0), walls - 1))...  2.17 us
    ppermute x3, waiting for transfers between devices, from_span(): return lax.ppermute(value, 'span', [(p, p ^ step) for p in range(spans)])  1.98 us
  transfers between devices with their start and end apart: 12, of which 5 were waited for; matrix products, arithmetic and copies ran while one was open for 0% of the time, Pallas kernels for 8%

profile of v19, /device:TPU:4, one launch (start us, length us, event | category | flops | bytes accessed | tf_op | source)
XLA Modules:
  0.0 32.9 jit_solution(13832142915241176089)
XLA Ops:
  0.6 0.9 %copy-done.2 = f32[4,8,16,128]{3,2,1,0:T(8,128)S(1)} copy-done((f32[4,8,16,128]{3,2,1,0:T(8,128)S(1)}, f32[4,8,16,128]{3,2,1,0:T(8,128)}, u32[]{:S(2)}) %copy-start.2) | copy-done | bytes 262168
  1.6 0.4 %pack.1 = (f32[20,16,128]{2,1,0:T(8,128)S(1)}, f32[20,16,128]{2,1,0:T(8,128)S(1)}, f32[4,16,128]{2,1,0:T(8,128)S(1)}, f32[4,16,128]{2,1,0:T(8,128)S(1)}) custom-call(f32[4,8,16,128]{3,2,1,0:T(8,128)S(1)} %copy-done.2), custom_call_target="tpu_custom_call" | custom-call | tf_op jit(solution)/shard_map/pack/pallas_call | solution.py:382
  2.0 1.6 %collective-permute-start.2 = (f32[20,16,128]{2,1,0:T(8,128)S(1)}, f32[20,16,128]{2,1,0:T(8,128)S(1)}, u32[]{:S(2)}, u32[]{:S(2)}) collective-permute-start(f32[20,16,128]{2,1,0:T(8,128)S(1)} %get-tuple-element.23), channel_id=1, source_target_pairs={{0,1},{1,0},{2,3},{3,2},{4,5},{5,4},{6,7},{7,6},{8,9},{9,8},{10,11... | collective-permute-start | bytes 491528 | tf_op jit(solution)/shard_map/ppermute | solution.py:403
  3.5 1.6 %collective-permute-start.3 = (f32[4,16,128]{2,1,0:T(8,128)S(1)}, f32[4,16,128]{2,1,0:T(8,128)S(1)}, u32[]{:S(2)}, u32[]{:S(2)}) collective-permute-start(f32[4,16,128]{2,1,0:T(8,128)S(1)} %get-tuple-element.24), channel_id=1, source_target_pairs={{1,25},{0,8},{9,1},{8,16},{17,9},{16,24},{25,17},{24,0},{3,27},{2,... | collective-permute-start | bytes 98312 | tf_op jit(solution)/shard_map/ppermute | solution.py:427
  5.1 2.4 %collective-permute-start.4 = (f32[4,16,128]{2,1,0:T(8,128)S(1)}, f32[4,16,128]{2,1,0:T(8,128)S(1)}, u32[]{:S(2)}, u32[]{:S(2)}) collective-permute-start(f32[4,16,128]{2,1,0:T(8,128)S(1)} %get-tuple-element.25), channel_id=1, source_target_pairs={{0,25},{1,8},{8,1},{9,16},{16,9},{17,24},{24,17},{25,0},{2,27},{3,... | collective-permute-start | bytes 98312 | tf_op jit(solution)/shard_map/ppermute | solution.py:426
  7.5 0.0 collective-permute-start.1
  7.5 2.5 %collective-permute-start = (f32[20,16,128]{2,1,0:T(8,128)S(1)}, f32[20,16,128]{2,1,0:T(8,128)S(1)}, u32[]{:S(2)}, u32[]{:S(2)}) collective-permute-start(f32[20,16,128]{2,1,0:T(8,128)S(1)} %get-tuple-element.27.mine), channel_id=1, source_target_pairs={{0,0},{2,4},{4,2},{6,6},{1,1},{3,5},{5,3},{7,7},{8,8},{10,12},{12,... | collective-permute-start | bytes 491528 | tf_op jit(solution)/shard_map/ppermute | solution.py:409
  10.1 1.6 %collective-permute-done.4.part_strip = f32[4,16,128]{2,1,0:T(8,128)S(1)} collective-permute-done((f32[4,16,128]{2,1,0:T(8,128)S(1)}, f32[4,16,128]{2,1,0:T(8,128)S(1)}, u32[]{:S(2)}, u32[]{:S(2)}) %collective-permute-start.4) | collective-permute-done | bytes 32800 | tf_op jit(solution)/shard_map/ppermute | solution.py:426
  11.7 0.0 copy-start.1
  11.7 0.1 collective-permute-start.6
  11.8 2.5 %collective-permute-start.5 = (f32[28,16,128]{2,1,0:T(8,128)S(1)}, f32[28,16,128]{2,1,0:T(8,128)S(1)}, u32[]{:S(2)}, u32[]{:S(2)}) collective-permute-start(f32[28,16,128]{2,1,0:T(8,128)S(1)} %rest.1), channel_id=1, source_target_pairs={{0,0},{2,4},{4,2},{6,6},{1,1},{3,5},{5,3},{7,7},{8,8},{10,12},{12,... | collective-permute-start | bytes 688136 | tf_op jit(solution)/shard_map/ppermute | solution.py:409
  14.4 1.1 %centre.1 = (f32[256,512]{1,0:T(8,128)S(1)}, f32[256,512]{1,0:T(8,128)S(1)}, f32[256,384]{1,0:T(8,128)S(1)}) custom-call(f32[20,16,128]{2,1,0:T(8,128)S(1)} %get-tuple-element.27.mine, f32[28,16,128]{2,1,0:T(8,128)S(1)} %rest.1, bf16[256,3072]{1,0:T(8,128)(2,1)S(1)} %copy-done), custom_call_target="tpu_custom_call" | custom-call | flops 2147483648 | tf_op jit(solution)/shard_map/centre/pallas_call | solution.py:382
  15.5 1.6 %mate.1 = (f32[4,16,16,128]{3,2,1,0:T(8,128)S(1)}, f32[4,8,16,128]{3,2,1,0:T(8,128)S(1)}, f32[4,8,8,128]{3,2,1,0:T(8,128)S(1)}, f32[256,896]{1,0:T(8,128)S(1)}) custom-call(f32[20,16,128]{2,1,0:T(8,128)S(1)} %collective-permute-done.1.a_mine, f32[28,16,128]{2,1,0:T(8,128)S(1)} %collective-permute-done.6.a_rest, f32[256,512]{1,0:T(8,128)S(1)} %get-tuple-element.28.upper, ...), custom_call_target="tpu_custom_call" | custom-call | flops 536870912 | tf_op jit(solution)/shard_map/mate/pallas_call | solution.py:382
  17.1 2.2 %collective-permute-done.5.b_rest = f32[28,16,128]{2,1,0:T(8,128)S(1)} collective-permute-done((f32[28,16,128]{2,1,0:T(8,128)S(1)}, f32[28,16,128]{2,1,0:T(8,128)S(1)}, u32[]{:S(2)}, u32[]{:S(2)}) %collective-permute-start.5) | collective-permute-done | bytes 229408 | tf_op jit(solution)/shard_map/ppermute | solution.py:409
  19.3 2.6 %flux.1 = (f32[6,8,16,128]{3,2,1,0:T(8,128)S(1)}, f32[3,8,16,128]{3,2,1,0:T(8,128)S(1)}, f32[16,128]{1,0:T(8,128)S(1)}) custom-call(f32[20,16,128]{2,1,0:T(8,128)S(1)} %collective-permute-done.b_mine, f32[28,16,128]{2,1,0:T(8,128)S(1)} %collective-permute-done.5.b_rest, f32[4,16,16,128]{3,2,1,0:T(8,128)S(1)} %get-tuple-element.30.a_raw, ...), custom_call_target="tpu_custom_call" | custom-call | tf_op jit(solution)/shard_map/flux/pallas_call | solution.py:382
  21.8 0.9 %collective-permute-start.9 = (f32[16,128]{1,0:T(8,128)S(1)}, f32[16,128]{1,0:T(8,128)S(1)}, u32[]{:S(2)}, u32[]{:S(2)}) collective-permute-start(f32[16,128]{1,0:T(8,128)S(1)} %get-tuple-element.35), channel_id=1, source_target_pairs={{0,16},{8,24},{16,0},{24,8},{1,17},{9,25},{17,1},{25,9},{2,18},{10... | collective-permute-start | bytes 24584 | tf_op jit(solution)/shard_map/ppermute | solution.py:487
  22.7 1.5 %collective-permute-start.8 = (f32[16,128]{1,0:T(8,128)S(1)}, f32[16,128]{1,0:T(8,128)S(1)}, u32[]{:S(2)}, u32[]{:S(2)}) collective-permute-start(f32[16,128]{1,0:T(8,128)S(1)} %get-tuple-element.35), channel_id=1, source_target_pairs={{0,24},{8,16},{16,8},{24,0},{1,25},{9,17},{17,9},{25,1},{2,26},{10... | collective-permute-start | bytes 24584 | tf_op jit(solution)/shard_map/ppermute | solution.py:487
  24.2 1.2 %collective-permute-start.7 = (f32[16,128]{1,0:T(8,128)S(1)}, f32[16,128]{1,0:T(8,128)S(1)}, u32[]{:S(2)}, u32[]{:S(2)}) collective-permute-start(f32[16,128]{1,0:T(8,128)S(1)} %get-tuple-element.35), channel_id=1, source_target_pairs={{0,8},{8,0},{16,24},{24,16},{1,9},{9,1},{17,25},{25,17},{2,10},{10... | collective-permute-start | bytes 24584 | tf_op jit(solution)/shard_map/ppermute | solution.py:487
  25.4 0.8 %collective-permute-start.11 = (f32[3,8,16,128]{3,2,1,0:T(8,128)S(1)}, f32[3,8,16,128]{3,2,1,0:T(8,128)S(1)}, u32[]{:S(2)}, u32[]{:S(2)}) collective-permute-start(f32[3,8,16,128]{3,2,1,0:T(8,128)S(1)} %get-tuple-element.37), channel_id=1, source_target_pairs={{0,1},{1,0},{2,3},{3,2},{4,5},{5,4},{6,7},{7,6},{8,9},{9,8},{10,11... | collective-permute-start | bytes 589832 | tf_op jit(solution)/shard_map/ppermute | solution.py:403
  26.2 0.3 collective-permute-done.9
  26.5 1.7 %collective-permute-done.8 = f32[16,128]{1,0:T(8,128)S(1)} collective-permute-done((f32[16,128]{1,0:T(8,128)S(1)}, f32[16,128]{1,0:T(8,128)S(1)}, u32[]{:S(2)}, u32[]{:S(2)}) %collective-permute-start.8) | collective-permute-done | bytes 8224 | tf_op jit(solution)/shard_map/ppermute | solution.py:487
  28.2 0.5 %collective-permute-start.10 = (f32[16,128]{1,0:T(8,128)S(1)}, f32[16,128]{1,0:T(8,128)S(1)}, u32[]{:S(2)}, u32[]{:S(2)}) collective-permute-start(f32[16,128]{1,0:T(8,128)S(1)} %add_add_fusion), channel_id=1, source_target_pairs={{0,1},{1,0},{2,3},{3,2},{4,5},{5,4},{6,7},{7,6},{8,9},{9,8},{10,11... | collective-permute-start | bytes 24584 | tf_op jit(solution)/shard_map/ppermute | solution.py:403
  28.7 3.2 %collective-permute-done.10 = f32[16,128]{1,0:T(8,128)S(1)} collective-permute-done((f32[16,128]{1,0:T(8,128)S(1)}, f32[16,128]{1,0:T(8,128)S(1)}, u32[]{:S(2)}, u32[]{:S(2)}) %collective-permute-start.10) | collective-permute-done | bytes 8224 | tf_op jit(solution)/shard_map/ppermute | solution.py:403
  31.9 1.0 %finish.1 = (f32[3,8,16,128]{3,2,1,0:T(8,128)}, f32[3,8,16,128]{3,2,1,0:T(8,128)}, f32[3,16]{1,0:T(4,128)}, f32[3,16]{1,0:T(4,128)}) custom-call(f32[16,128]{1,0:T(8,128)S(1)} %add.15.sums, f32[6,8,16,128]{3,2,1,0:T(8,128)S(1)} %get-tuple-element.36.keep, f32[3,8,16,128]{3,2,1,0:T(8,128)S(1)} %collective-permute-done.11.come), custom_call_target="tpu_custom_call" | custom-call | tf_op jit(solution)/shard_map/finish/pallas_call | solution.py:382
  (14 shorter events, 0.1 us)
Async XLA Ops:
  0.6 1.0 %copy-start.2 = (f32[4,8,16,128]{3,2,1,0:T(8,128)S(1)}, f32[4,8,16,128]{3,2,1,0:T(8,128)}, u32[]{:S(2)}) copy-start(f32[4,8,16,128]{3,2,1,0:T(8,128)} %own.1) | copy-start | bytes 786436
  2.0 9.7 %collective-permute-start.2 = (f32[20,16,128]{2,1,0:T(8,128)S(1)}, f32[20,16,128]{2,1,0:T(8,128)S(1)}, u32[]{:S(2)}, u32[]{:S(2)}) collective-permute-start(f32[20,16,128]{2,1,0:T(8,128)S(1)} %get-tuple-element.23), channel_id=1, source_target_pairs={{0,1},{1,0},{2,3},{3,2},{4,5},{5,4},{6,7},{7,6},{8,9},{9,8},{10,11... | collective-permute-start | bytes 491528 | tf_op jit(solution)/shard_map/ppermute | solution.py:403
  3.5 6.6 %collective-permute-start.3 = (f32[4,16,128]{2,1,0:T(8,128)S(1)}, f32[4,16,128]{2,1,0:T(8,128)S(1)}, u32[]{:S(2)}, u32[]{:S(2)}) collective-permute-start(f32[4,16,128]{2,1,0:T(8,128)S(1)} %get-tuple-element.24), channel_id=1, source_target_pairs={{1,25},{0,8},{9,1},{8,16},{17,9},{16,24},{25,17},{24,0},{3,27},{2,... | collective-permute-start | bytes 98312 | tf_op jit(solution)/shard_map/ppermute | solution.py:427
  5.1 6.6 %collective-permute-start.4 = (f32[4,16,128]{2,1,0:T(8,128)S(1)}, f32[4,16,128]{2,1,0:T(8,128)S(1)}, u32[]{:S(2)}, u32[]{:S(2)}) collective-permute-start(f32[4,16,128]{2,1,0:T(8,128)S(1)} %get-tuple-element.25), channel_id=1, source_target_pairs={{0,25},{1,8},{8,1},{9,16},{16,9},{17,24},{24,17},{25,0},{2,27},{3,... | collective-permute-start | bytes 98312 | tf_op jit(solution)/shard_map/ppermute | solution.py:426
  7.5 6.8 %copy-start = (bf16[256,3072]{1,0:T(8,128)(2,1)S(1)}, bf16[256,3072]{1,0:T(8,128)(2,1)}, u32[]{:S(2)}) copy-start(bf16[256,3072]{1,0:T(8,128)(2,1)} %constant.4.clone.planes.matrices) | copy-start | bytes 4718596
  7.5 6.8 %collective-permute-start.1 = (f32[20,16,128]{2,1,0:T(8,128)S(1)}, f32[20,16,128]{2,1,0:T(8,128)S(1)}, u32[]{:S(2)}, u32[]{:S(2)}) collective-permute-start(f32[20,16,128]{2,1,0:T(8,128)S(1)} %get-tuple-element.27.mine), channel_id=1, source_target_pairs={{0,2},{2,0},{4,6},{6,4},{1,3},{3,1},{5,7},{7,5},{8,10},{10,8},{12,... | collective-permute-start | bytes 491528 | tf_op jit(solution)/shard_map/ppermute | solution.py:406
  7.5 6.8 %collective-permute-start = (f32[20,16,128]{2,1,0:T(8,128)S(1)}, f32[20,16,128]{2,1,0:T(8,128)S(1)}, u32[]{:S(2)}, u32[]{:S(2)}) collective-permute-start(f32[20,16,128]{2,1,0:T(8,128)S(1)} %get-tuple-element.27.mine), channel_id=1, source_target_pairs={{0,0},{2,4},{4,2},{6,6},{1,1},{3,5},{5,3},{7,7},{8,8},{10,12},{12,... | collective-permute-start | bytes 491528 | tf_op jit(solution)/shard_map/ppermute | solution.py:409
  11.7 3.7 %copy-start.1 = (bf16[512,768]{1,0:T(8,128)(2,1)S(1)}, bf16[512,768]{1,0:T(8,128)(2,1)}, u32[]{:S(2)}) copy-start(bf16[512,768]{1,0:T(8,128)(2,1)} %constant.5.clone.spans) | copy-start | bytes 2359300
  11.7 3.7 %collective-permute-start.6 = (f32[28,16,128]{2,1,0:T(8,128)S(1)}, f32[28,16,128]{2,1,0:T(8,128)S(1)}, u32[]{:S(2)}, u32[]{:S(2)}) collective-permute-start(f32[28,16,128]{2,1,0:T(8,128)S(1)} %rest.1), channel_id=1, source_target_pairs={{0,2},{2,0},{4,6},{6,4},{1,3},{3,1},{5,7},{7,5},{8,10},{10,8},{12,... | collective-permute-start | bytes 688136 | tf_op jit(solution)/shard_map/ppermute | solution.py:406
  11.8 7.5 %collective-permute-start.5 = (f32[28,16,128]{2,1,0:T(8,128)S(1)}, f32[28,16,128]{2,1,0:T(8,128)S(1)}, u32[]{:S(2)}, u32[]{:S(2)}) collective-permute-start(f32[28,16,128]{2,1,0:T(8,128)S(1)} %rest.1), channel_id=1, source_target_pairs={{0,0},{2,4},{4,2},{6,6},{1,1},{3,5},{5,3},{7,7},{8,8},{10,12},{12,... | collective-permute-start | bytes 688136 | tf_op jit(solution)/shard_map/ppermute | solution.py:409
  21.8 4.6 %collective-permute-start.9 = (f32[16,128]{1,0:T(8,128)S(1)}, f32[16,128]{1,0:T(8,128)S(1)}, u32[]{:S(2)}, u32[]{:S(2)}) collective-permute-start(f32[16,128]{1,0:T(8,128)S(1)} %get-tuple-element.35), channel_id=1, source_target_pairs={{0,16},{8,24},{16,0},{24,8},{1,17},{9,25},{17,1},{25,9},{2,18},{10... | collective-permute-start | bytes 24584 | tf_op jit(solution)/shard_map/ppermute | solution.py:487
  22.7 5.4 %collective-permute-start.8 = (f32[16,128]{1,0:T(8,128)S(1)}, f32[16,128]{1,0:T(8,128)S(1)}, u32[]{:S(2)}, u32[]{:S(2)}) collective-permute-start(f32[16,128]{1,0:T(8,128)S(1)} %get-tuple-element.35), channel_id=1, source_target_pairs={{0,24},{8,16},{16,8},{24,0},{1,25},{9,17},{17,9},{25,1},{2,26},{10... | collective-permute-start | bytes 24584 | tf_op jit(solution)/shard_map/ppermute | solution.py:487
  24.2 3.9 %collective-permute-start.7 = (f32[16,128]{1,0:T(8,128)S(1)}, f32[16,128]{1,0:T(8,128)S(1)}, u32[]{:S(2)}, u32[]{:S(2)}) collective-permute-start(f32[16,128]{1,0:T(8,128)S(1)} %get-tuple-element.35), channel_id=1, source_target_pairs={{0,8},{8,0},{16,24},{24,16},{1,9},{9,1},{17,25},{25,17},{2,10},{10... | collective-permute-start | bytes 24584 | tf_op jit(solution)/shard_map/ppermute | solution.py:487
  25.4 6.5 %collective-permute-start.11 = (f32[3,8,16,128]{3,2,1,0:T(8,128)S(1)}, f32[3,8,16,128]{3,2,1,0:T(8,128)S(1)}, u32[]{:S(2)}, u32[]{:S(2)}) collective-permute-start(f32[3,8,16,128]{3,2,1,0:T(8,128)S(1)} %get-tuple-element.37), channel_id=1, source_target_pairs={{0,1},{1,0},{2,3},{3,2},{4,5},{5,4},{6,7},{7,6},{8,9},{9,8},{10,11... | collective-permute-start | bytes 589832 | tf_op jit(solution)/shard_map/ppermute | solution.py:403
  28.2 3.7 %collective-permute-start.10 = (f32[16,128]{1,0:T(8,128)S(1)}, f32[16,128]{1,0:T(8,128)S(1)}, u32[]{:S(2)}, u32[]{:S(2)}) collective-permute-start(f32[16,128]{1,0:T(8,128)S(1)} %add_add_fusion), channel_id=1, source_target_pairs={{0,1},{1,0},{2,3},{3,2},{4,5},{5,4},{6,7},{7,6},{8,9},{9,8},{10,11... | collective-permute-start | bytes 24584 | tf_op jit(solution)/shard_map/ppermute | solution.py:403

commit v20 on v19

--- a/solution.py
+++ b/solution.py
@@ -126,7 +126,7 @@
     to_same[...] = pack_strip(own, 7 * (1 - me_s))
 
 
-def rest_kernel(part, own_strip, part_strip, rest):
+def rest_kernel(part, part_strip, own_strip, rest):
     count, half = part.shape[0], own_strip.shape[0]
     rest[:count] = part[...]
     rest[count : count + half] = own_strip[...]
@@ -429,7 +429,7 @@
     (rest,) = call(
         rest_kernel,
         "rest",
-        (part, own_strip, part_strip),
+        (part, part_strip, own_strip),
         ((message[0] + layers, rows, width),),
         hint=2**35,
     )
@@ -489,7 +489,7 @@
     step = 1
     while step < spans:
         if 2 * step < spans:
-            far = from_span(sums, 3 * step) + from_span(sums, 2 * step)
+            far = from_span(sums, 2 * step) + from_span(sums, 3 * step)
             sums = (sums + from_span(sums, step)) + far
         else:
             sums = sums + from_span(sums, step)

time: 33.1 us -> 34.4 us (1.039)
  waiting for transfers between devices: 9.01 us -> 10.6 us
    ppermute x1, waiting for transfers between devices: 0.01 us -> 2.43 us  [shards(): own_strip = lax.ppermute(second, ('span', 'stream'), to_same)]
    ppermute x1, starting transfers between devices: 1.58 us -> 0.01 us  [shards(): own_strip = lax.ppermute(second, ('span', 'stream'), to_same)]
    ppermute x1, starting transfers between devices: 2.45 us -> 3.57 us  [shards(): part_strip = lax.ppermute(first, ('span', 'stream'), to_other)]
    ppermute x3, starting transfers between devices: 3.55 us -> 4.45 us  [from_span(): return lax.ppermute(value, 'span', [(p, p ^ step) for p in range(spans)])]
    ppermute x1, waiting for transfers between devices: 1.63 us -> 0.75 us  [shards(): part_strip = lax.ppermute(first, ('span', 'stream'), to_other)]
    ppermute x3, starting transfers between devices: 2.83 us -> 2.04 us  [swap(): return lax.ppermute(value, 'stream', [(0, 1), (1, 0)])]
    ppermute x3, waiting for transfers between devices: 3.22 us -> 3.64 us  [swap(): return lax.ppermute(value, 'stream', [(0, 1), (1, 0)])]
    ppermute x3, waiting for transfers between devices: 1.98 us -> 1.62 us  [from_span(): return lax.ppermute(value, 'span', [(p, p ^ step) for p in range(spans)])]
  transfers between devices with their start and end apart: 12 -> 12, of which waited for: 5 -> 6; matrix products, arithmetic and copies ran while one was open for 0% -> 0% of each run, Pallas kernels for 8% -> 8%
where the time goes in v20:
time: 34.4 us; the launch traced here: 34.2 us
  starting transfers between devices  15.2 us (44%)
  waiting for transfers between devices  10.6 us (31%)
  Pallas kernels  6.67 us (19%)
  local copies, waits for them, and re-layouts  0.95 us (3%)
  between operations  0.75 us (2%)
    pallas_call x6, Pallas kernels, call(): pl.pallas_call(kernel, out_shape=tuple((jax.ShapeDtypeStruct(shape, jnp.f...  6.67 us
    ppermute x2, starting transfers between devices, pair_b(): lax.ppermute(value, 'wall', [(w, min(max((w + 1 ^ 1) - 1, 0), walls - 1))...  5.02 us
    ppermute x3, starting transfers between devices, from_span(): return lax.ppermute(value, 'span', [(p, p ^ step) for p in range(spans)])  4.45 us
    ppermute x3, waiting for transfers between devices, swap(): return lax.ppermute(value, 'stream', [(0, 1), (1, 0)])  3.64 us
    ppermute x1, starting transfers between devices, shards(): part_strip = lax.ppermute(first, ('span', 'stream'), to_other)  3.57 us
    ppermute x1, waiting for transfers between devices, shards(): own_strip = lax.ppermute(second, ('span', 'stream'), to_same)  2.43 us
    ppermute x2, waiting for transfers between devices, pair_b(): lax.ppermute(value, 'wall', [(w, min(max((w + 1 ^ 1) - 1, 0), walls - 1))...  2.17 us
    ppermute x3, starting transfers between devices, swap(): return lax.ppermute(value, 'stream', [(0, 1), (1, 0)])  2.04 us
  transfers between devices with their start and end apart: 12, of which 6 were waited for; matrix products, arithmetic and copies ran while one was open for 0% of the time, Pallas kernels for 8%

profile of v20, /device:TPU:4, one launch (start us, length us, event | category | flops | bytes accessed | tf_op | source)
XLA Modules:
  0.0 34.2 jit_solution(8160081862097235503)
XLA Ops:
  0.6 0.9 %copy-done.2 = f32[4,8,16,128]{3,2,1,0:T(8,128)S(1)} copy-done((f32[4,8,16,128]{3,2,1,0:T(8,128)S(1)}, f32[4,8,16,128]{3,2,1,0:T(8,128)}, u32[]{:S(2)}) %copy-start.2) | copy-done | bytes 262168
  1.6 0.4 %pack.1 = (f32[20,16,128]{2,1,0:T(8,128)S(1)}, f32[20,16,128]{2,1,0:T(8,128)S(1)}, f32[4,16,128]{2,1,0:T(8,128)S(1)}, f32[4,16,128]{2,1,0:T(8,128)S(1)}) custom-call(f32[4,8,16,128]{3,2,1,0:T(8,128)S(1)} %copy-done.2), custom_call_target="tpu_custom_call" | custom-call | tf_op jit(solution)/shard_map/pack/pallas_call | solution.py:382
  2.0 1.6 %collective-permute-start.2 = (f32[20,16,128]{2,1,0:T(8,128)S(1)}, f32[20,16,128]{2,1,0:T(8,128)S(1)}, u32[]{:S(2)}, u32[]{:S(2)}) collective-permute-start(f32[20,16,128]{2,1,0:T(8,128)S(1)} %get-tuple-element.23), channel_id=1, source_target_pairs={{0,1},{1,0},{2,3},{3,2},{4,5},{5,4},{6,7},{7,6},{8,9},{9,8},{10,11... | collective-permute-start | bytes 491528 | tf_op jit(solution)/shard_map/ppermute | solution.py:403
  3.5 3.6 %collective-permute-start.3 = (f32[4,16,128]{2,1,0:T(8,128)S(1)}, f32[4,16,128]{2,1,0:T(8,128)S(1)}, u32[]{:S(2)}, u32[]{:S(2)}) collective-permute-start(f32[4,16,128]{2,1,0:T(8,128)S(1)} %get-tuple-element.24), channel_id=1, source_target_pairs={{0,25},{1,8},{8,1},{9,16},{16,9},{17,24},{24,17},{25,0},{2,27},{3,... | collective-permute-start | bytes 98312 | tf_op jit(solution)/shard_map/ppermute | solution.py:426
  7.1 2.5 %collective-permute-start = (f32[20,16,128]{2,1,0:T(8,128)S(1)}, f32[20,16,128]{2,1,0:T(8,128)S(1)}, u32[]{:S(2)}, u32[]{:S(2)}) collective-permute-start(f32[20,16,128]{2,1,0:T(8,128)S(1)} %get-tuple-element.27.mine), channel_id=1, source_target_pairs={{0,0},{2,4},{4,2},{6,6},{1,1},{3,5},{5,3},{7,7},{8,8},{10,12},{12,... | collective-permute-start | bytes 491528 | tf_op jit(solution)/shard_map/ppermute | solution.py:409
  9.6 0.7 %collective-permute-done.3.part_strip = f32[4,16,128]{2,1,0:T(8,128)S(1)} collective-permute-done((f32[4,16,128]{2,1,0:T(8,128)S(1)}, f32[4,16,128]{2,1,0:T(8,128)S(1)}, u32[]{:S(2)}, u32[]{:S(2)}) %collective-permute-start.3) | collective-permute-done | bytes 32800 | tf_op jit(solution)/shard_map/ppermute | solution.py:426
  10.4 2.4 %collective-permute-done.4.own_strip = f32[4,16,128]{2,1,0:T(8,128)S(1)} collective-permute-done((f32[4,16,128]{2,1,0:T(8,128)S(1)}, f32[4,16,128]{2,1,0:T(8,128)S(1)}, u32[]{:S(2)}, u32[]{:S(2)}) %collective-permute-start.4) | collective-permute-done | bytes 32800 | tf_op jit(solution)/shard_map/ppermute | solution.py:427
  12.8 0.0 copy-start.1
  12.8 0.1 collective-permute-start.6
  12.9 2.5 %collective-permute-start.5 = (f32[28,16,128]{2,1,0:T(8,128)S(1)}, f32[28,16,128]{2,1,0:T(8,128)S(1)}, u32[]{:S(2)}, u32[]{:S(2)}) collective-permute-start(f32[28,16,128]{2,1,0:T(8,128)S(1)} %rest.1), channel_id=1, source_target_pairs={{0,0},{2,4},{4,2},{6,6},{1,1},{3,5},{5,3},{7,7},{8,8},{10,12},{12,... | collective-permute-start | bytes 688136 | tf_op jit(solution)/shard_map/ppermute | solution.py:409
  15.4 0.0 collective-permute-done.1.a_mine
  15.4 0.0 collective-permute-done.b_mine
  15.5 1.1 %centre.1 = (f32[256,512]{1,0:T(8,128)S(1)}, f32[256,512]{1,0:T(8,128)S(1)}, f32[256,384]{1,0:T(8,128)S(1)}) custom-call(f32[20,16,128]{2,1,0:T(8,128)S(1)} %get-tuple-element.27.mine, f32[28,16,128]{2,1,0:T(8,128)S(1)} %rest.1, bf16[256,3072]{1,0:T(8,128)(2,1)S(1)} %copy-done), custom_call_target="tpu_custom_call" | custom-call | flops 2147483648 | tf_op jit(solution)/shard_map/centre/pallas_call | solution.py:382
  16.6 1.6 %mate.1 = (f32[4,16,16,128]{3,2,1,0:T(8,128)S(1)}, f32[4,8,16,128]{3,2,1,0:T(8,128)S(1)}, f32[4,8,8,128]{3,2,1,0:T(8,128)S(1)}, f32[256,896]{1,0:T(8,128)S(1)}) custom-call(f32[20,16,128]{2,1,0:T(8,128)S(1)} %collective-permute-done.1.a_mine, f32[28,16,128]{2,1,0:T(8,128)S(1)} %collective-permute-done.6.a_rest, f32[256,512]{1,0:T(8,128)S(1)} %get-tuple-element.28.upper, ...), custom_call_target="tpu_custom_call" | custom-call | flops 536870912 | tf_op jit(solution)/shard_map/mate/pallas_call | solution.py:382
  18.2 2.2 %collective-permute-done.5.b_rest = f32[28,16,128]{2,1,0:T(8,128)S(1)} collective-permute-done((f32[28,16,128]{2,1,0:T(8,128)S(1)}, f32[28,16,128]{2,1,0:T(8,128)S(1)}, u32[]{:S(2)}, u32[]{:S(2)}) %collective-permute-start.5) | collective-permute-done | bytes 229408 | tf_op jit(solution)/shard_map/ppermute | solution.py:409
  20.4 2.6 %flux.1 = (f32[6,8,16,128]{3,2,1,0:T(8,128)S(1)}, f32[3,8,16,128]{3,2,1,0:T(8,128)S(1)}, f32[16,128]{1,0:T(8,128)S(1)}) custom-call(f32[20,16,128]{2,1,0:T(8,128)S(1)} %collective-permute-done.b_mine, f32[28,16,128]{2,1,0:T(8,128)S(1)} %collective-permute-done.5.b_rest, f32[4,16,16,128]{3,2,1,0:T(8,128)S(1)} %get-tuple-element.30.a_raw, ...), custom_call_target="tpu_custom_call" | custom-call | tf_op jit(solution)/shard_map/flux/pallas_call | solution.py:382
  22.9 0.7 %collective-permute-start.9 = (f32[16,128]{1,0:T(8,128)S(1)}, f32[16,128]{1,0:T(8,128)S(1)}, u32[]{:S(2)}, u32[]{:S(2)}) collective-permute-start(f32[16,128]{1,0:T(8,128)S(1)} %get-tuple-element.35), channel_id=1, source_target_pairs={{0,24},{8,16},{16,8},{24,0},{1,25},{9,17},{17,9},{25,1},{2,26},{10... | collective-permute-start | bytes 24584 | tf_op jit(solution)/shard_map/ppermute | solution.py:487
  23.7 0.0 collective-permute-start.8
  23.7 3.7 %collective-permute-start.7 = (f32[16,128]{1,0:T(8,128)S(1)}, f32[16,128]{1,0:T(8,128)S(1)}, u32[]{:S(2)}, u32[]{:S(2)}) collective-permute-start(f32[16,128]{1,0:T(8,128)S(1)} %get-tuple-element.35), channel_id=1, source_target_pairs={{0,8},{8,0},{16,24},{24,16},{1,9},{9,1},{17,25},{25,17},{2,10},{10... | collective-permute-start | bytes 24584 | tf_op jit(solution)/shard_map/ppermute | solution.py:487
  27.4 1.1 %collective-permute-done.9 = f32[16,128]{1,0:T(8,128)S(1)} collective-permute-done((f32[16,128]{1,0:T(8,128)S(1)}, f32[16,128]{1,0:T(8,128)S(1)}, u32[]{:S(2)}, u32[]{:S(2)}) %collective-permute-start.9) | collective-permute-done | bytes 8224 | tf_op jit(solution)/shard_map/ppermute | solution.py:487
  28.5 0.6 %collective-permute-done.7 = f32[16,128]{1,0:T(8,128)S(1)} collective-permute-done((f32[16,128]{1,0:T(8,128)S(1)}, f32[16,128]{1,0:T(8,128)S(1)}, u32[]{:S(2)}, u32[]{:S(2)}) %collective-permute-start.7) | collective-permute-done | bytes 8224 | tf_op jit(solution)/shard_map/ppermute | solution.py:487
  29.0 0.5 %collective-permute-start.10 = (f32[16,128]{1,0:T(8,128)S(1)}, f32[16,128]{1,0:T(8,128)S(1)}, u32[]{:S(2)}, u32[]{:S(2)}) collective-permute-start(f32[16,128]{1,0:T(8,128)S(1)} %add_add_fusion), channel_id=1, source_target_pairs={{0,1},{1,0},{2,3},{3,2},{4,5},{5,4},{6,7},{7,6},{8,9},{9,8},{10,11... | collective-permute-start | bytes 24584 | tf_op jit(solution)/shard_map/ppermute | solution.py:403
  29.5 3.6 %collective-permute-done.10 = f32[16,128]{1,0:T(8,128)S(1)} collective-permute-done((f32[16,128]{1,0:T(8,128)S(1)}, f32[16,128]{1,0:T(8,128)S(1)}, u32[]{:S(2)}, u32[]{:S(2)}) %collective-permute-start.10) | collective-permute-done | bytes 8224 | tf_op jit(solution)/shard_map/ppermute | solution.py:403
  33.2 1.0 %finish.1 = (f32[3,8,16,128]{3,2,1,0:T(8,128)}, f32[3,8,16,128]{3,2,1,0:T(8,128)}, f32[3,16]{1,0:T(4,128)}, f32[3,16]{1,0:T(4,128)}) custom-call(f32[16,128]{1,0:T(8,128)S(1)} %add.15.sums, f32[6,8,16,128]{3,2,1,0:T(8,128)S(1)} %get-tuple-element.36.keep, f32[3,8,16,128]{3,2,1,0:T(8,128)S(1)} %collective-permute-done.11.come), custom_call_target="tpu_custom_call" | custom-call | tf_op jit(solution)/shard_map/finish/pallas_call | solution.py:382
  (14 shorter events, 0.1 us)
Async XLA Ops:
  0.6 1.0 %copy-start.2 = (f32[4,8,16,128]{3,2,1,0:T(8,128)S(1)}, f32[4,8,16,128]{3,2,1,0:T(8,128)}, u32[]{:S(2)}) copy-start(f32[4,8,16,128]{3,2,1,0:T(8,128)} %own.1) | copy-start | bytes 786436
  2.0 10.8 %collective-permute-start.2 = (f32[20,16,128]{2,1,0:T(8,128)S(1)}, f32[20,16,128]{2,1,0:T(8,128)S(1)}, u32[]{:S(2)}, u32[]{:S(2)}) collective-permute-start(f32[20,16,128]{2,1,0:T(8,128)S(1)} %get-tuple-element.23), channel_id=1, source_target_pairs={{0,1},{1,0},{2,3},{3,2},{4,5},{5,4},{6,7},{7,6},{8,9},{9,8},{10,11... | collective-permute-start | bytes 491528 | tf_op jit(solution)/shard_map/ppermute | solution.py:403
  3.5 6.9 %collective-permute-start.3 = (f32[4,16,128]{2,1,0:T(8,128)S(1)}, f32[4,16,128]{2,1,0:T(8,128)S(1)}, u32[]{:S(2)}, u32[]{:S(2)}) collective-permute-start(f32[4,16,128]{2,1,0:T(8,128)S(1)} %get-tuple-element.24), channel_id=1, source_target_pairs={{0,25},{1,8},{8,1},{9,16},{16,9},{17,24},{24,17},{25,0},{2,27},{3,... | collective-permute-start | bytes 98312 | tf_op jit(solution)/shard_map/ppermute | solution.py:426
  7.1 5.7 %collective-permute-start.4 = (f32[4,16,128]{2,1,0:T(8,128)S(1)}, f32[4,16,128]{2,1,0:T(8,128)S(1)}, u32[]{:S(2)}, u32[]{:S(2)}) collective-permute-start(f32[4,16,128]{2,1,0:T(8,128)S(1)} %get-tuple-element.25), channel_id=1, source_target_pairs={{1,25},{0,8},{9,1},{8,16},{17,9},{16,24},{25,17},{24,0},{3,27},{2,... | collective-permute-start | bytes 98312 | tf_op jit(solution)/shard_map/ppermute | solution.py:427
  7.1 8.4 %copy-start = (bf16[256,3072]{1,0:T(8,128)(2,1)S(1)}, bf16[256,3072]{1,0:T(8,128)(2,1)}, u32[]{:S(2)}) copy-start(bf16[256,3072]{1,0:T(8,128)(2,1)} %constant.4.clone.planes.matrices) | copy-start | bytes 4718596
  7.1 8.3 %collective-permute-start.1 = (f32[20,16,128]{2,1,0:T(8,128)S(1)}, f32[20,16,128]{2,1,0:T(8,128)S(1)}, u32[]{:S(2)}, u32[]{:S(2)}) collective-permute-start(f32[20,16,128]{2,1,0:T(8,128)S(1)} %get-tuple-element.27.mine), channel_id=1, source_target_pairs={{0,2},{2,0},{4,6},{6,4},{1,3},{3,1},{5,7},{7,5},{8,10},{10,8},{12,... | collective-permute-start | bytes 491528 | tf_op jit(solution)/shard_map/ppermute | solution.py:406
  7.1 8.3 %collective-permute-start = (f32[20,16,128]{2,1,0:T(8,128)S(1)}, f32[20,16,128]{2,1,0:T(8,128)S(1)}, u32[]{:S(2)}, u32[]{:S(2)}) collective-permute-start(f32[20,16,128]{2,1,0:T(8,128)S(1)} %get-tuple-element.27.mine), channel_id=1, source_target_pairs={{0,0},{2,4},{4,2},{6,6},{1,1},{3,5},{5,3},{7,7},{8,8},{10,12},{12,... | collective-permute-start | bytes 491528 | tf_op jit(solution)/shard_map/ppermute | solution.py:409
  12.8 3.8 %copy-start.1 = (bf16[512,768]{1,0:T(8,128)(2,1)S(1)}, bf16[512,768]{1,0:T(8,128)(2,1)}, u32[]{:S(2)}) copy-start(bf16[512,768]{1,0:T(8,128)(2,1)} %constant.5.clone.spans) | copy-start | bytes 2359300
  12.8 3.7 %collective-permute-start.6 = (f32[28,16,128]{2,1,0:T(8,128)S(1)}, f32[28,16,128]{2,1,0:T(8,128)S(1)}, u32[]{:S(2)}, u32[]{:S(2)}) collective-permute-start(f32[28,16,128]{2,1,0:T(8,128)S(1)} %rest.1), channel_id=1, source_target_pairs={{0,2},{2,0},{4,6},{6,4},{1,3},{3,1},{5,7},{7,5},{8,10},{10,8},{12,... | collective-permute-start | bytes 688136 | tf_op jit(solution)/shard_map/ppermute | solution.py:406
  12.9 7.5 %collective-permute-start.5 = (f32[28,16,128]{2,1,0:T(8,128)S(1)}, f32[28,16,128]{2,1,0:T(8,128)S(1)}, u32[]{:S(2)}, u32[]{:S(2)}) collective-permute-start(f32[28,16,128]{2,1,0:T(8,128)S(1)} %rest.1), channel_id=1, source_target_pairs={{0,0},{2,4},{4,2},{6,6},{1,1},{3,5},{5,3},{7,7},{8,8},{10,12},{12,... | collective-permute-start | bytes 688136 | tf_op jit(solution)/shard_map/ppermute | solution.py:409
  22.9 5.5 %collective-permute-start.9 = (f32[16,128]{1,0:T(8,128)S(1)}, f32[16,128]{1,0:T(8,128)S(1)}, u32[]{:S(2)}, u32[]{:S(2)}) collective-permute-start(f32[16,128]{1,0:T(8,128)S(1)} %get-tuple-element.35), channel_id=1, source_target_pairs={{0,24},{8,16},{16,8},{24,0},{1,25},{9,17},{17,9},{25,1},{2,26},{10... | collective-permute-start | bytes 24584 | tf_op jit(solution)/shard_map/ppermute | solution.py:487
  23.7 4.8 %collective-permute-start.8 = (f32[16,128]{1,0:T(8,128)S(1)}, f32[16,128]{1,0:T(8,128)S(1)}, u32[]{:S(2)}, u32[]{:S(2)}) collective-permute-start(f32[16,128]{1,0:T(8,128)S(1)} %get-tuple-element.35), channel_id=1, source_target_pairs={{0,16},{8,24},{16,0},{24,8},{1,17},{9,25},{17,1},{25,9},{2,18},{10... | collective-permute-start | bytes 24584 | tf_op jit(solution)/shard_map/ppermute | solution.py:487
  23.7 5.3 %collective-permute-start.7 = (f32[16,128]{1,0:T(8,128)S(1)}, f32[16,128]{1,0:T(8,128)S(1)}, u32[]{:S(2)}, u32[]{:S(2)}) collective-permute-start(f32[16,128]{1,0:T(8,128)S(1)} %get-tuple-element.35), channel_id=1, source_target_pairs={{0,8},{8,0},{16,24},{24,16},{1,9},{9,1},{17,25},{25,17},{2,10},{10... | collective-permute-start | bytes 24584 | tf_op jit(solution)/shard_map/ppermute | solution.py:487
  27.4 5.8 %collective-permute-start.11 = (f32[3,8,16,128]{3,2,1,0:T(8,128)S(1)}, f32[3,8,16,128]{3,2,1,0:T(8,128)S(1)}, u32[]{:S(2)}, u32[]{:S(2)}) collective-permute-start(f32[3,8,16,128]{3,2,1,0:T(8,128)S(1)} %get-tuple-element.37), channel_id=1, source_target_pairs={{0,1},{1,0},{2,3},{3,2},{4,5},{5,4},{6,7},{7,6},{8,9},{9,8},{10,11... | collective-permute-start | bytes 589832 | tf_op jit(solution)/shard_map/ppermute | solution.py:403
  29.0 4.1 %collective-permute-start.10 = (f32[16,128]{1,0:T(8,128)S(1)}, f32[16,128]{1,0:T(8,128)S(1)}, u32[]{:S(2)}, u32[]{:S(2)}) collective-permute-start(f32[16,128]{1,0:T(8,128)S(1)} %add_add_fusion), channel_id=1, source_target_pairs={{0,1},{1,0},{2,3},{3,2},{4,5},{5,4},{6,7},{7,6},{8,9},{9,8},{10,11... | collective-permute-start | bytes 24584 | tf_op jit(solution)/shard_map/ppermute | solution.py:403

commit v21 on v19

--- a/solution.py
+++ b/solution.py
@@ -38,11 +38,12 @@
 def plane_constants(layers, rows):
     stream = band(layers, layers, 0)
     wall = band(rows, 2 * rows, reach)
-    near = np.arange(reach, reach + rows)
-    far = np.setdiff1d(np.arange(2 * rows), near)
-    parts = [np.arange(rows), np.arange(rows, 2 * rows), near, far]
+    ends = [0, reach, reach + rows, 2 * rows]
+    thirds = [np.arange(ends[k], ends[k + 1]) for k in range(3)]
+    parts = [np.arange(rows), np.arange(rows, 2 * rows), thirds[1], thirds[0], thirds[2]]
     blocks = [np.kron(stream, wall[:, part]) for part in parts]
-    return split_constant(np.concatenate(blocks, axis=1))
+    parts = [split_constant(block) for block in blocks]
+    return np.concatenate([np.concatenate([high, low, high], axis=1) for high, low in parts], axis=1)
 
 
 def span_constants(width):
@@ -167,6 +168,15 @@
     depth = parts.shape[0]
     start = part * depth if isinstance(part, int) else pl.multiple_of(part * depth, depth)
     return dot(planes[:, pl.ds(start, depth)], parts[...])
+
+
+def add_products(planes, which, raw, base, parts):
+    near = pl.ds(pl.multiple_of((1 - which) * reach, reach), reach)
+    temperature = raw[3, :, near, :]
+    for i in range(3):
+        value = raw[i, :, near, :] * temperature
+        put_parts(parts, 0, column(i), value.reshape(-1, value.shape[-1]))
+    return base + planes_of(planes, 6 + which, parts)
 
 
 def bring(mine, rest, raw, parts, keep=None):
@@ -250,7 +260,8 @@
 
 
 def mate_kernel(
-    a_mine, a_rest, upper, lower, matrices, spans, raw, packed, slopes, second, parts, mid, mean
+    a_mine, a_rest, upper, lower, products, matrices, spans,
+    base, packed, slopes, second, products_a, raw, parts, mid, mean, prod,
 ):
     both, rows = raw.shape[1:3]
     odd = lax.rem(lax.axis_index("wall"), 2)
@@ -263,10 +274,12 @@
         slopes[t] = slope
     second_input(means, mid)
     second[...] = planes_of(matrices, 1 - odd, mid)
+    base[...] = jnp.where(odd == 0, upper[...], lower[...])
+    products_a[...] = add_products(matrices, 1 - odd, raw, products[...], prod)
 
 
 def flux_kernel(
-    walls, b_mine, b_rest, a_raw, a_packed, a_slopes, a_second, upper, lower, products, matrices, spans,
+    walls, b_mine, b_rest, base, a_packed, a_slopes, a_second, products, matrices, spans,
     keep_ref, send_ref, sums_ref,
     raw, parts, prod, mean, mid, packed, slopes,
 ):
@@ -281,8 +294,7 @@
 
     bring(b_mine, b_rest, raw, parts, keep_b)
 
-    planes = jnp.where(odd == 0, upper[...], lower[...])
-    planes = planes + planes_of(matrices, odd, parts)
+    planes = base[...] + planes_of(matrices, odd, parts)
     row = lax.rem(lax.broadcasted_iota(jnp.int32, planes.shape, 0), rows)
     inside = (row < reach) == (odd == 1)
     planes = jnp.where(jnp.logical_or(inside, jnp.logical_not(at_end)), planes, 0.0)
@@ -300,16 +312,7 @@
     second = packed_pass(spans, a_second[...] + planes_of(matrices, odd, mid))
     second = [value.reshape(layers, rows, width) for value in second]
 
-    def around(f):
-        above = jnp.where(odd == 0, raw[f, :, rows - reach :, :], a_raw[f, :, rows - reach :, :])
-        below = jnp.where(odd == 1, raw[f, :, :reach, :], a_raw[f, :, :reach, :])
-        return jnp.concatenate([above, below], axis=1)
-
-    temperature = around(3)
-    for i in range(3):
-        value = (around(i) * temperature).reshape(cells, width)
-        put_parts(prod, 0, column(i), value)
-    flux = packed_pass(spans, products[...] + planes_of(matrices, 3, prod))
+    flux = packed_pass(spans, add_products(matrices, odd, raw, products[...], prod))
     flux = [value.reshape(layers, rows, width) for value in flux]
 
     mid_rows = slice(reach, reach + rows)
@@ -435,9 +438,7 @@
     )
     a_rest, b_rest = pair_a(rest), pair_b(rest)
 
-    high, low = plane_constants(both, rows)
-    thirds = [(high[:, k : k + cells], low[:, k : k + cells], high[:, k : k + cells]) for k in range(0, 4 * cells, cells)]
-    matrices = jnp.asarray(np.concatenate([part for third in thirds for part in third], axis=1))
+    matrices = jnp.asarray(plane_constants(both, rows))
     single_pass, split_pass = span_constants(width)
     both_passes = np.zeros((4 * width, 6 * width), ml_dtypes.bfloat16)
     both_passes[: 2 * width, : 2 * width] = single_pass
@@ -446,6 +447,7 @@
     single, brief = jnp.float32, jnp.bfloat16
     block, quarter = (4, both, rows, width), (4, layers, rows, width)
     four, three, seven = (((3 * cells, n * width), brief) for n in (4, 3, 7))
+    few = ((3 * both * reach, 3 * width), brief)
     upper, lower, products = call(
         centre_kernel,
         "centre",
@@ -455,24 +457,27 @@
         mib=16,
         hint=2**31,
     )
-    a_raw, a_packed, a_slopes, a_second = call(
+    base, a_packed, a_slopes, a_second, products = call(
         mate_kernel,
         "mate",
-        (a_mine, a_rest, upper, lower, matrices, passes),
-        (block, quarter, (4, layers, reach, width), (cells, 7 * width)),
-        [four, seven, (block, single)],
+        (a_mine, a_rest, upper, lower, products, matrices, passes),
+        (
+            (cells, 4 * width), quarter, (4, layers, reach, width), (cells, 7 * width),
+            (cells, 3 * width),
+        ),
+        [(block, single), four, seven, (block, single), few],
         mib=16,
         hint=2**29,
     )
     keep, send, sums = call(
         functools.partial(flux_kernel, walls),
         "flux",
-        (b_mine, b_rest, a_raw, a_packed, a_slopes, a_second, upper, lower, products, matrices, passes),
+        (b_mine, b_rest, base, a_packed, a_slopes, a_second, products, matrices, passes),
         ((6, layers, rows, width), (3, layers, rows, width), (rows, width)),
         [
             (block, single),
             four,
-            three,
+            few,
             (block, single),
             seven,
             ((4, layers, 2 * rows, width), single),

time: 33.1 us -> 32.9 us (level)
  transfers between devices with their start and end apart: 12 -> 12, of which waited for: 5 -> 5; matrix products, arithmetic and copies ran while one was open for 0% -> 0% of each run, Pallas kernels for 8% -> 9%
where the time goes in v21:
time: 32.9 us; the launch traced here: 32.7 us
  starting transfers between devices  15.5 us (47%)
  waiting for transfers between devices  8.79 us (27%)
  Pallas kernels  6.72 us (20%)
  local copies, waits for them, and re-layouts  0.95 us (3%)
  between operations  0.76 us (2%)
    pallas_call x6, Pallas kernels, call(): pl.pallas_call(kernel, out_shape=tuple((jax.ShapeDtypeStruct(shape, jnp.f...  6.72 us
    ppermute x2, starting transfers between devices, pair_b(): lax.ppermute(value, 'wall', [(w, min(max((w + 1 ^ 1) - 1, 0), walls - 1))...  5.02 us
    ppermute x3, starting transfers between devices, from_span(): return lax.ppermute(value, 'span', [(p, p ^ step) for p in range(spans)])  3.55 us
    ppermute x3, waiting for transfers between devices, swap(): return lax.ppermute(value, 'stream', [(0, 1), (1, 0)])  3.21 us
    ppermute x3, starting transfers between devices, swap(): return lax.ppermute(value, 'stream', [(0, 1), (1, 0)])  2.84 us
    ppermute x1, starting transfers between devices, shards(): part_strip = lax.ppermute(first, ('span', 'stream'), to_other)  2.45 us
    ppermute x3, waiting for transfers between devices, from_span(): return lax.ppermute(value, 'span', [(p, p ^ step) for p in range(spans)])  1.98 us
    ppermute x2, waiting for transfers between devices, pair_b(): lax.ppermute(value, 'wall', [(w, min(max((w + 1 ^ 1) - 1, 0), walls - 1))...  1.96 us
  transfers between devices with their start and end apart: 12, of which 5 were waited for; matrix products, arithmetic and copies ran while one was open for 0% of the time, Pallas kernels for 9%

profile of v21, /device:TPU:4, one launch (start us, length us, event | category | flops | bytes accessed | tf_op | source)
XLA Modules:
  0.0 32.7 jit_solution(16277991358249699474)
XLA Ops:
  0.6 0.9 %copy-done.2 = f32[4,8,16,128]{3,2,1,0:T(8,128)S(1)} copy-done((f32[4,8,16,128]{3,2,1,0:T(8,128)S(1)}, f32[4,8,16,128]{3,2,1,0:T(8,128)}, u32[]{:S(2)}) %copy-start.2) | copy-done | bytes 262168
  1.6 0.4 %pack.1 = (f32[20,16,128]{2,1,0:T(8,128)S(1)}, f32[20,16,128]{2,1,0:T(8,128)S(1)}, f32[4,16,128]{2,1,0:T(8,128)S(1)}, f32[4,16,128]{2,1,0:T(8,128)S(1)}) custom-call(f32[4,8,16,128]{3,2,1,0:T(8,128)S(1)} %copy-done.2), custom_call_target="tpu_custom_call" | custom-call | tf_op jit(solution)/shard_map/pack/pallas_call | solution.py:385
  2.0 1.6 %collective-permute-start.2 = (f32[20,16,128]{2,1,0:T(8,128)S(1)}, f32[20,16,128]{2,1,0:T(8,128)S(1)}, u32[]{:S(2)}, u32[]{:S(2)}) collective-permute-start(f32[20,16,128]{2,1,0:T(8,128)S(1)} %get-tuple-element.24), channel_id=1, source_target_pairs={{0,1},{1,0},{2,3},{3,2},{4,5},{5,4},{6,7},{7,6},{8,9},{9,8},{10,11... | collective-permute-start | bytes 491528 | tf_op jit(solution)/shard_map/ppermute | solution.py:406
  3.5 1.6 %collective-permute-start.3 = (f32[4,16,128]{2,1,0:T(8,128)S(1)}, f32[4,16,128]{2,1,0:T(8,128)S(1)}, u32[]{:S(2)}, u32[]{:S(2)}) collective-permute-start(f32[4,16,128]{2,1,0:T(8,128)S(1)} %get-tuple-element.25), channel_id=1, source_target_pairs={{1,25},{0,8},{9,1},{8,16},{17,9},{16,24},{25,17},{24,0},{3,27},{2,... | collective-permute-start | bytes 98312 | tf_op jit(solution)/shard_map/ppermute | solution.py:430
  5.1 2.4 %collective-permute-start.4 = (f32[4,16,128]{2,1,0:T(8,128)S(1)}, f32[4,16,128]{2,1,0:T(8,128)S(1)}, u32[]{:S(2)}, u32[]{:S(2)}) collective-permute-start(f32[4,16,128]{2,1,0:T(8,128)S(1)} %get-tuple-element.26), channel_id=1, source_target_pairs={{0,25},{1,8},{8,1},{9,16},{16,9},{17,24},{24,17},{25,0},{2,27},{3,... | collective-permute-start | bytes 98312 | tf_op jit(solution)/shard_map/ppermute | solution.py:429
  7.5 0.0 collective-permute-start.1
  7.5 2.5 %collective-permute-start = (f32[20,16,128]{2,1,0:T(8,128)S(1)}, f32[20,16,128]{2,1,0:T(8,128)S(1)}, u32[]{:S(2)}, u32[]{:S(2)}) collective-permute-start(f32[20,16,128]{2,1,0:T(8,128)S(1)} %get-tuple-element.28.mine), channel_id=1, source_target_pairs={{0,0},{2,4},{4,2},{6,6},{1,1},{3,5},{5,3},{7,7},{8,8},{10,12},{12,... | collective-permute-start | bytes 491528 | tf_op jit(solution)/shard_map/ppermute | solution.py:412
  10.1 1.6 %collective-permute-done.4.part_strip = f32[4,16,128]{2,1,0:T(8,128)S(1)} collective-permute-done((f32[4,16,128]{2,1,0:T(8,128)S(1)}, f32[4,16,128]{2,1,0:T(8,128)S(1)}, u32[]{:S(2)}, u32[]{:S(2)}) %collective-permute-start.4) | collective-permute-done | bytes 32800 | tf_op jit(solution)/shard_map/ppermute | solution.py:429
  11.7 0.0 copy-start.1
  11.7 0.1 collective-permute-start.6
  11.8 2.5 %collective-permute-start.5 = (f32[28,16,128]{2,1,0:T(8,128)S(1)}, f32[28,16,128]{2,1,0:T(8,128)S(1)}, u32[]{:S(2)}, u32[]{:S(2)}) collective-permute-start(f32[28,16,128]{2,1,0:T(8,128)S(1)} %rest.1), channel_id=1, source_target_pairs={{0,0},{2,4},{4,2},{6,6},{1,1},{3,5},{5,3},{7,7},{8,8},{10,12},{12,... | collective-permute-start | bytes 688136 | tf_op jit(solution)/shard_map/ppermute | solution.py:412
  14.4 1.1 %centre.1 = (f32[256,512]{1,0:T(8,128)S(1)}, f32[256,512]{1,0:T(8,128)S(1)}, f32[256,384]{1,0:T(8,128)S(1)}) custom-call(f32[20,16,128]{2,1,0:T(8,128)S(1)} %get-tuple-element.28.mine, f32[28,16,128]{2,1,0:T(8,128)S(1)} %rest.1, bf16[256,3072]{1,0:T(8,128)(2,1)S(1)} %copy-done), custom_call_target="tpu_custom_call" | custom-call | flops 2147483648 | tf_op jit(solution)/shard_map/centre/pallas_call | solution.py:385
  15.5 1.8 %mate.1 = (f32[256,512]{1,0:T(8,128)S(1)}, f32[4,8,16,128]{3,2,1,0:T(8,128)S(1)}, f32[4,8,8,128]{3,2,1,0:T(8,128)S(1)}, f32[256,896]{1,0:T(8,128)S(1)}, f32[256,384]{1,0:T(8,128)S(1)}) custom-call(f32[20,16,128]{2,1,0:T(8,128)S(1)} %collective-permute-done.1.a_mine, f32[28,16,128]{2,1,0:T(8,128)S(1)} %collective-permute-done.6.a_rest, ...), custom_call_target="tpu_custom_call" | custom-call | flops 536870912 | tf_op jit(solution)/shard_map/mate/pallas_call | solution.py:385
  17.3 2.0 %collective-permute-done.5.b_rest = f32[28,16,128]{2,1,0:T(8,128)S(1)} collective-permute-done((f32[28,16,128]{2,1,0:T(8,128)S(1)}, f32[28,16,128]{2,1,0:T(8,128)S(1)}, u32[]{:S(2)}, u32[]{:S(2)}) %collective-permute-start.5) | collective-permute-done | bytes 229408 | tf_op jit(solution)/shard_map/ppermute | solution.py:412
  19.3 2.4 %flux.1 = (f32[6,8,16,128]{3,2,1,0:T(8,128)S(1)}, f32[3,8,16,128]{3,2,1,0:T(8,128)S(1)}, f32[16,128]{1,0:T(8,128)S(1)}) custom-call(f32[20,16,128]{2,1,0:T(8,128)S(1)} %collective-permute-done.b_mine, f32[28,16,128]{2,1,0:T(8,128)S(1)} %collective-permute-done.5.b_rest, f32[256,512]{1,0:T(8,128)S(1)} %get-tuple-element.32.base, ...), custom_call_target="tpu_custom_call" | custom-call | tf_op jit(solution)/shard_map/flux/pallas_call | solution.py:385
  21.7 0.9 %collective-permute-start.9 = (f32[16,128]{1,0:T(8,128)S(1)}, f32[16,128]{1,0:T(8,128)S(1)}, u32[]{:S(2)}, u32[]{:S(2)}) collective-permute-start(f32[16,128]{1,0:T(8,128)S(1)} %get-tuple-element.37), channel_id=1, source_target_pairs={{0,16},{8,24},{16,0},{24,8},{1,17},{9,25},{17,1},{25,9},{2,18},{10... | collective-permute-start | bytes 24584 | tf_op jit(solution)/shard_map/ppermute | solution.py:492
  22.5 1.5 %collective-permute-start.8 = (f32[16,128]{1,0:T(8,128)S(1)}, f32[16,128]{1,0:T(8,128)S(1)}, u32[]{:S(2)}, u32[]{:S(2)}) collective-permute-start(f32[16,128]{1,0:T(8,128)S(1)} %get-tuple-element.37), channel_id=1, source_target_pairs={{0,24},{8,16},{16,8},{24,0},{1,25},{9,17},{17,9},{25,1},{2,26},{10... | collective-permute-start | bytes 24584 | tf_op jit(solution)/shard_map/ppermute | solution.py:492
  24.1 1.2 %collective-permute-start.7 = (f32[16,128]{1,0:T(8,128)S(1)}, f32[16,128]{1,0:T(8,128)S(1)}, u32[]{:S(2)}, u32[]{:S(2)}) collective-permute-start(f32[16,128]{1,0:T(8,128)S(1)} %get-tuple-element.37), channel_id=1, source_target_pairs={{0,8},{8,0},{16,24},{24,16},{1,9},{9,1},{17,25},{25,17},{2,10},{10... | collective-permute-start | bytes 24584 | tf_op jit(solution)/shard_map/ppermute | solution.py:492
  25.2 0.8 %collective-permute-start.11 = (f32[3,8,16,128]{3,2,1,0:T(8,128)S(1)}, f32[3,8,16,128]{3,2,1,0:T(8,128)S(1)}, u32[]{:S(2)}, u32[]{:S(2)}) collective-permute-start(f32[3,8,16,128]{3,2,1,0:T(8,128)S(1)} %get-tuple-element.39), channel_id=1, source_target_pairs={{0,1},{1,0},{2,3},{3,2},{4,5},{5,4},{6,7},{7,6},{8,9},{9,8},{10,11... | collective-permute-start | bytes 589832 | tf_op jit(solution)/shard_map/ppermute | solution.py:406
  26.0 0.3 collective-permute-done.9
  26.3 1.7 %collective-permute-done.8 = f32[16,128]{1,0:T(8,128)S(1)} collective-permute-done((f32[16,128]{1,0:T(8,128)S(1)}, f32[16,128]{1,0:T(8,128)S(1)}, u32[]{:S(2)}, u32[]{:S(2)}) %collective-permute-start.8) | collective-permute-done | bytes 8224 | tf_op jit(solution)/shard_map/ppermute | solution.py:492
  28.0 0.5 %collective-permute-start.10 = (f32[16,128]{1,0:T(8,128)S(1)}, f32[16,128]{1,0:T(8,128)S(1)}, u32[]{:S(2)}, u32[]{:S(2)}) collective-permute-start(f32[16,128]{1,0:T(8,128)S(1)} %add_add_fusion), channel_id=1, source_target_pairs={{0,1},{1,0},{2,3},{3,2},{4,5},{5,4},{6,7},{7,6},{8,9},{9,8},{10,11... | collective-permute-start | bytes 24584 | tf_op jit(solution)/shard_map/ppermute | solution.py:406
  28.5 3.2 %collective-permute-done.10 = f32[16,128]{1,0:T(8,128)S(1)} collective-permute-done((f32[16,128]{1,0:T(8,128)S(1)}, f32[16,128]{1,0:T(8,128)S(1)}, u32[]{:S(2)}, u32[]{:S(2)}) %collective-permute-start.10) | collective-permute-done | bytes 8224 | tf_op jit(solution)/shard_map/ppermute | solution.py:406
  31.7 1.0 %finish.1 = (f32[3,8,16,128]{3,2,1,0:T(8,128)}, f32[3,8,16,128]{3,2,1,0:T(8,128)}, f32[3,16]{1,0:T(4,128)}, f32[3,16]{1,0:T(4,128)}) custom-call(f32[16,128]{1,0:T(8,128)S(1)} %add.15.sums, f32[6,8,16,128]{3,2,1,0:T(8,128)S(1)} %get-tuple-element.38.keep, f32[3,8,16,128]{3,2,1,0:T(8,128)S(1)} %collective-permute-done.11.come), custom_call_target="tpu_custom_call" | custom-call | tf_op jit(solution)/shard_map/finish/pallas_call | solution.py:385
  (14 shorter events, 0.1 us)
Async XLA Ops:
  0.6 1.0 %copy-start.2 = (f32[4,8,16,128]{3,2,1,0:T(8,128)S(1)}, f32[4,8,16,128]{3,2,1,0:T(8,128)}, u32[]{:S(2)}) copy-start(f32[4,8,16,128]{3,2,1,0:T(8,128)} %own.1) | copy-start | bytes 786436
  2.0 9.7 %collective-permute-start.2 = (f32[20,16,128]{2,1,0:T(8,128)S(1)}, f32[20,16,128]{2,1,0:T(8,128)S(1)}, u32[]{:S(2)}, u32[]{:S(2)}) collective-permute-start(f32[20,16,128]{2,1,0:T(8,128)S(1)} %get-tuple-element.24), channel_id=1, source_target_pairs={{0,1},{1,0},{2,3},{3,2},{4,5},{5,4},{6,7},{7,6},{8,9},{9,8},{10,11... | collective-permute-start | bytes 491528 | tf_op jit(solution)/shard_map/ppermute | solution.py:406
  3.5 6.6 %collective-permute-start.3 = (f32[4,16,128]{2,1,0:T(8,128)S(1)}, f32[4,16,128]{2,1,0:T(8,128)S(1)}, u32[]{:S(2)}, u32[]{:S(2)}) collective-permute-start(f32[4,16,128]{2,1,0:T(8,128)S(1)} %get-tuple-element.25), channel_id=1, source_target_pairs={{1,25},{0,8},{9,1},{8,16},{17,9},{16,24},{25,17},{24,0},{3,27},{2,... | collective-permute-start | bytes 98312 | tf_op jit(solution)/shard_map/ppermute | solution.py:430
  5.1 6.6 %collective-permute-start.4 = (f32[4,16,128]{2,1,0:T(8,128)S(1)}, f32[4,16,128]{2,1,0:T(8,128)S(1)}, u32[]{:S(2)}, u32[]{:S(2)}) collective-permute-start(f32[4,16,128]{2,1,0:T(8,128)S(1)} %get-tuple-element.26), channel_id=1, source_target_pairs={{0,25},{1,8},{8,1},{9,16},{16,9},{17,24},{24,17},{25,0},{2,27},{3,... | collective-permute-start | bytes 98312 | tf_op jit(solution)/shard_map/ppermute | solution.py:429
  7.5 6.8 %copy-start = (bf16[256,3072]{1,0:T(8,128)(2,1)S(1)}, bf16[256,3072]{1,0:T(8,128)(2,1)}, u32[]{:S(2)}) copy-start(bf16[256,3072]{1,0:T(8,128)(2,1)} %constant.4.clone.planes.matrices) | copy-start | bytes 4718596
  7.5 6.8 %collective-permute-start.1 = (f32[20,16,128]{2,1,0:T(8,128)S(1)}, f32[20,16,128]{2,1,0:T(8,128)S(1)}, u32[]{:S(2)}, u32[]{:S(2)}) collective-permute-start(f32[20,16,128]{2,1,0:T(8,128)S(1)} %get-tuple-element.28.mine), channel_id=1, source_target_pairs={{0,2},{2,0},{4,6},{6,4},{1,3},{3,1},{5,7},{7,5},{8,10},{10,8},{12,... | collective-permute-start | bytes 491528 | tf_op jit(solution)/shard_map/ppermute | solution.py:409
  7.5 6.8 %collective-permute-start = (f32[20,16,128]{2,1,0:T(8,128)S(1)}, f32[20,16,128]{2,1,0:T(8,128)S(1)}, u32[]{:S(2)}, u32[]{:S(2)}) collective-permute-start(f32[20,16,128]{2,1,0:T(8,128)S(1)} %get-tuple-element.28.mine), channel_id=1, source_target_pairs={{0,0},{2,4},{4,2},{6,6},{1,1},{3,5},{5,3},{7,7},{8,8},{10,12},{12,... | collective-permute-start | bytes 491528 | tf_op jit(solution)/shard_map/ppermute | solution.py:412
  11.7 3.7 %copy-start.1 = (bf16[512,768]{1,0:T(8,128)(2,1)S(1)}, bf16[512,768]{1,0:T(8,128)(2,1)}, u32[]{:S(2)}) copy-start(bf16[512,768]{1,0:T(8,128)(2,1)} %constant.5.clone.spans) | copy-start | bytes 2359300
  11.7 3.7 %collective-permute-start.6 = (f32[28,16,128]{2,1,0:T(8,128)S(1)}, f32[28,16,128]{2,1,0:T(8,128)S(1)}, u32[]{:S(2)}, u32[]{:S(2)}) collective-permute-start(f32[28,16,128]{2,1,0:T(8,128)S(1)} %rest.1), channel_id=1, source_target_pairs={{0,2},{2,0},{4,6},{6,4},{1,3},{3,1},{5,7},{7,5},{8,10},{10,8},{12,... | collective-permute-start | bytes 688136 | tf_op jit(solution)/shard_map/ppermute | solution.py:409
  11.8 7.5 %collective-permute-start.5 = (f32[28,16,128]{2,1,0:T(8,128)S(1)}, f32[28,16,128]{2,1,0:T(8,128)S(1)}, u32[]{:S(2)}, u32[]{:S(2)}) collective-permute-start(f32[28,16,128]{2,1,0:T(8,128)S(1)} %rest.1), channel_id=1, source_target_pairs={{0,0},{2,4},{4,2},{6,6},{1,1},{3,5},{5,3},{7,7},{8,8},{10,12},{12,... | collective-permute-start | bytes 688136 | tf_op jit(solution)/shard_map/ppermute | solution.py:412
  21.7 4.6 %collective-permute-start.9 = (f32[16,128]{1,0:T(8,128)S(1)}, f32[16,128]{1,0:T(8,128)S(1)}, u32[]{:S(2)}, u32[]{:S(2)}) collective-permute-start(f32[16,128]{1,0:T(8,128)S(1)} %get-tuple-element.37), channel_id=1, source_target_pairs={{0,16},{8,24},{16,0},{24,8},{1,17},{9,25},{17,1},{25,9},{2,18},{10... | collective-permute-start | bytes 24584 | tf_op jit(solution)/shard_map/ppermute | solution.py:492
  22.5 5.4 %collective-permute-start.8 = (f32[16,128]{1,0:T(8,128)S(1)}, f32[16,128]{1,0:T(8,128)S(1)}, u32[]{:S(2)}, u32[]{:S(2)}) collective-permute-start(f32[16,128]{1,0:T(8,128)S(1)} %get-tuple-element.37), channel_id=1, source_target_pairs={{0,24},{8,16},{16,8},{24,0},{1,25},{9,17},{17,9},{25,1},{2,26},{10... | collective-permute-start | bytes 24584 | tf_op jit(solution)/shard_map/ppermute | solution.py:492
  24.1 3.9 %collective-permute-start.7 = (f32[16,128]{1,0:T(8,128)S(1)}, f32[16,128]{1,0:T(8,128)S(1)}, u32[]{:S(2)}, u32[]{:S(2)}) collective-permute-start(f32[16,128]{1,0:T(8,128)S(1)} %get-tuple-element.37), channel_id=1, source_target_pairs={{0,8},{8,0},{16,24},{24,16},{1,9},{9,1},{17,25},{25,17},{2,10},{10... | collective-permute-start | bytes 24584 | tf_op jit(solution)/shard_map/ppermute | solution.py:492
  25.2 6.5 %collective-permute-start.11 = (f32[3,8,16,128]{3,2,1,0:T(8,128)S(1)}, f32[3,8,16,128]{3,2,1,0:T(8,128)S(1)}, u32[]{:S(2)}, u32[]{:S(2)}) collective-permute-start(f32[3,8,16,128]{3,2,1,0:T(8,128)S(1)} %get-tuple-element.39), channel_id=1, source_target_pairs={{0,1},{1,0},{2,3},{3,2},{4,5},{5,4},{6,7},{7,6},{8,9},{9,8},{10,11... | collective-permute-start | bytes 589832 | tf_op jit(solution)/shard_map/ppermute | solution.py:406
  28.0 3.7 %collective-permute-start.10 = (f32[16,128]{1,0:T(8,128)S(1)}, f32[16,128]{1,0:T(8,128)S(1)}, u32[]{:S(2)}, u32[]{:S(2)}) collective-permute-start(f32[16,128]{1,0:T(8,128)S(1)} %add_add_fusion), channel_id=1, source_target_pairs={{0,1},{1,0},{2,3},{3,2},{4,5},{5,4},{6,7},{7,6},{8,9},{9,8},{10,11... | collective-permute-start | bytes 24584 | tf_op jit(solution)/shard_map/ppermute | solution.py:406

commit v22 on v21

--- a/solution.py
+++ b/solution.py
@@ -352,7 +352,8 @@
 
 
 def finish_kernel(
-    plane_cells, sums, keep, come, clark_model, similar_model, clark_corr, similar_corr
+    plane_cells, sums, keep, come, clark_model, similar_model, clark_corr, similar_corr,
+    clark_done, similar_done, corr_done, sent,
 ):
     _, layers, rows, width = keep.shape
     me_s = lax.axis_index("stream")
@@ -360,6 +361,12 @@
     lane = lane_index((rows, width))
     useful = lane // (width // 2) == me_s
     corr = jnp.zeros((rows, width), jnp.float32)
+    copies = []
+
+    def send(source, target):
+        copies.append(pltpu.make_async_copy(source, target, sent.at[len(copies)]))
+        copies[-1].start()
+
     for i in range(3):
         cross_c, cross_s, power_e, power_c, power_s = (
             table[:, 3 * q + i : 3 * q + i + 1] for q in range(5)
@@ -367,27 +374,36 @@
         packed = come[i]
         turned = pltpu.roll(packed, width // 2, 2)
         clark = jnp.where(useful[None], keep[i], jnp.where(me_s == 0, turned, packed))
+        clark_done[i] = clark / jnp.sqrt(power_c + small_eps)[None]
+        send(clark_done.at[i], clark_model.at[i])
         similar = jnp.where(useful[None], keep[3 + i], jnp.where(me_s == 0, packed, turned))
-        clark_model[i] = clark / jnp.sqrt(power_c + small_eps)[None]
-        similar_model[i] = similar / jnp.sqrt(power_s + small_eps)[None]
+        similar_done[i] = similar / jnp.sqrt(power_s + small_eps)[None]
+        send(similar_done.at[i], similar_model.at[i])
         value = cross_c / jnp.sqrt((power_e + small_eps) * (power_c + small_eps))
         corr = jnp.where(lane == i, value, corr)
         value = cross_s / jnp.sqrt((power_e + small_eps) * (power_s + small_eps))
         corr = jnp.where(lane == 8 + i, value, corr)
     square = jnp.concatenate([corr, jnp.zeros((width - rows, width), jnp.float32)], axis=0)
     turned = square.T
-    clark_corr[...] = turned[:3, :rows]
-    similar_corr[...] = turned[8:11, :rows]
-
-
-def call(kernel, name, ins, outs, scratch=(), mib=4, hint=None):
+    corr_done[0] = turned[:3, :rows]
+    send(corr_done.at[0], clark_corr)
+    corr_done[1] = turned[8:11, :rows]
+    send(corr_done.at[1], similar_corr)
+    for copy in copies:
+        copy.wait()
+
+
+def call(kernel, name, ins, outs, scratch=(), mib=4, hint=None, space=pltpu.VMEM):
     cost = hint and pl.CostEstimate(flops=hint, bytes_accessed=0, transcendentals=0)
     return pl.pallas_call(
         kernel,
         out_shape=tuple(jax.ShapeDtypeStruct(shape, jnp.float32) for shape in outs),
         in_specs=[pl.BlockSpec(memory_space=pltpu.VMEM)] * len(ins),
-        out_specs=tuple(pl.BlockSpec(memory_space=pltpu.VMEM) for _ in outs),
-        scratch_shapes=[pltpu.VMEM(shape, dtype) for shape, dtype in scratch],
+        out_specs=tuple(pl.BlockSpec(memory_space=space) for _ in outs),
+        scratch_shapes=[
+            pltpu.SemaphoreType.DMA(shape) if dtype is None else pltpu.VMEM(shape, dtype)
+            for shape, dtype in scratch
+        ],
         compiler_params=pltpu.CompilerParams(vmem_limit_bytes=mib * 1024 * 1024),
         cost_estimate=cost,
         name=name,
@@ -506,6 +522,8 @@
         "finish",
         (sums, keep, come),
         (block, block, corr, corr),
+        [(block, single), (block, single), ((2, *corr), single), ((8,), None)],
+        space=pl.ANY,
     )
 
 

time: 32.9 us -> 32.9 us (level)
  no operation moved by 1% of the time
where the time goes in v22:
time: 32.9 us; the launch traced here: 32.7 us
  starting transfers between devices  15.5 us (47%)
  waiting for transfers between devices  8.79 us (27%)
  Pallas kernels  6.7 us (20%)
  local copies, waits for them, and re-layouts  0.95 us (3%)
  between operations  0.76 us (2%)
    pallas_call x6, Pallas kernels, call(): pl.pallas_call(kernel, out_shape=tuple((jax.ShapeDtypeStruct(shape, jnp.f...  6.7 us
    ppermute x2, starting transfers between devices, pair_b(): lax.ppermute(value, 'wall', [(w, min(max((w + 1 ^ 1) - 1, 0), walls - 1))...  5.02 us
    ppermute x3, starting transfers between devices, from_span(): return lax.ppermute(value, 'span', [(p, p ^ step) for p in range(spans)])  3.55 us
    ppermute x3, waiting for transfers between devices, swap(): return lax.ppermute(value, 'stream', [(0, 1), (1, 0)])  3.21 us
    ppermute x3, starting transfers between devices, swap(): return lax.ppermute(value, 'stream', [(0, 1), (1, 0)])  2.84 us
    ppermute x1, starting transfers between devices, shards(): part_strip = lax.ppermute(first, ('span', 'stream'), to_other)  2.45 us
    ppermute x3, waiting for transfers between devices, from_span(): return lax.ppermute(value, 'span', [(p, p ^ step) for p in range(spans)])  1.98 us
    ppermute x2, waiting for transfers between devices, pair_b(): lax.ppermute(value, 'wall', [(w, min(max((w + 1 ^ 1) - 1, 0), walls - 1))...  1.96 us
  transfers between devices with their start and end apart: 12, of which 5 were waited for; matrix products, arithmetic and copies ran while one was open for 0% of the time, Pallas kernels for 9%

profile of v22, /device:TPU:4, one launch (start us, length us, event | category | flops | bytes accessed | tf_op | source)
XLA Modules:
  0.0 32.7 jit_solution(2329451893831847711)
XLA Ops:
  0.6 0.9 %copy-done.2 = f32[4,8,16,128]{3,2,1,0:T(8,128)S(1)} copy-done((f32[4,8,16,128]{3,2,1,0:T(8,128)S(1)}, f32[4,8,16,128]{3,2,1,0:T(8,128)}, u32[]{:S(2)}) %copy-start.2) | copy-done | bytes 262168
  1.6 0.4 %pack.1 = (f32[20,16,128]{2,1,0:T(8,128)S(1)}, f32[20,16,128]{2,1,0:T(8,128)S(1)}, f32[4,16,128]{2,1,0:T(8,128)S(1)}, f32[4,16,128]{2,1,0:T(8,128)S(1)}) custom-call(f32[4,8,16,128]{3,2,1,0:T(8,128)S(1)} %copy-done.2), custom_call_target="tpu_custom_call" | custom-call | tf_op jit(solution)/shard_map/pack/pallas_call | solution.py:398
  2.0 1.6 %collective-permute-start.2 = (f32[20,16,128]{2,1,0:T(8,128)S(1)}, f32[20,16,128]{2,1,0:T(8,128)S(1)}, u32[]{:S(2)}, u32[]{:S(2)}) collective-permute-start(f32[20,16,128]{2,1,0:T(8,128)S(1)} %get-tuple-element.24), channel_id=1, source_target_pairs={{0,1},{1,0},{2,3},{3,2},{4,5},{5,4},{6,7},{7,6},{8,9},{9,8},{10,11... | collective-permute-start | bytes 491528 | tf_op jit(solution)/shard_map/ppermute | solution.py:422
  3.5 1.6 %collective-permute-start.3 = (f32[4,16,128]{2,1,0:T(8,128)S(1)}, f32[4,16,128]{2,1,0:T(8,128)S(1)}, u32[]{:S(2)}, u32[]{:S(2)}) collective-permute-start(f32[4,16,128]{2,1,0:T(8,128)S(1)} %get-tuple-element.25), channel_id=1, source_target_pairs={{1,25},{0,8},{9,1},{8,16},{17,9},{16,24},{25,17},{24,0},{3,27},{2,... | collective-permute-start | bytes 98312 | tf_op jit(solution)/shard_map/ppermute | solution.py:446
  5.1 2.4 %collective-permute-start.4 = (f32[4,16,128]{2,1,0:T(8,128)S(1)}, f32[4,16,128]{2,1,0:T(8,128)S(1)}, u32[]{:S(2)}, u32[]{:S(2)}) collective-permute-start(f32[4,16,128]{2,1,0:T(8,128)S(1)} %get-tuple-element.26), channel_id=1, source_target_pairs={{0,25},{1,8},{8,1},{9,16},{16,9},{17,24},{24,17},{25,0},{2,27},{3,... | collective-permute-start | bytes 98312 | tf_op jit(solution)/shard_map/ppermute | solution.py:445
  7.5 0.0 collective-permute-start.1
  7.5 2.5 %collective-permute-start = (f32[20,16,128]{2,1,0:T(8,128)S(1)}, f32[20,16,128]{2,1,0:T(8,128)S(1)}, u32[]{:S(2)}, u32[]{:S(2)}) collective-permute-start(f32[20,16,128]{2,1,0:T(8,128)S(1)} %get-tuple-element.28.mine), channel_id=1, source_target_pairs={{0,0},{2,4},{4,2},{6,6},{1,1},{3,5},{5,3},{7,7},{8,8},{10,12},{12,... | collective-permute-start | bytes 491528 | tf_op jit(solution)/shard_map/ppermute | solution.py:428
  10.1 1.6 %collective-permute-done.4.part_strip = f32[4,16,128]{2,1,0:T(8,128)S(1)} collective-permute-done((f32[4,16,128]{2,1,0:T(8,128)S(1)}, f32[4,16,128]{2,1,0:T(8,128)S(1)}, u32[]{:S(2)}, u32[]{:S(2)}) %collective-permute-start.4) | collective-permute-done | bytes 32800 | tf_op jit(solution)/shard_map/ppermute | solution.py:445
  11.7 0.0 copy-start.1
  11.7 0.1 collective-permute-start.6
  11.8 2.5 %collective-permute-start.5 = (f32[28,16,128]{2,1,0:T(8,128)S(1)}, f32[28,16,128]{2,1,0:T(8,128)S(1)}, u32[]{:S(2)}, u32[]{:S(2)}) collective-permute-start(f32[28,16,128]{2,1,0:T(8,128)S(1)} %rest.1), channel_id=1, source_target_pairs={{0,0},{2,4},{4,2},{6,6},{1,1},{3,5},{5,3},{7,7},{8,8},{10,12},{12,... | collective-permute-start | bytes 688136 | tf_op jit(solution)/shard_map/ppermute | solution.py:428
  14.4 1.1 %centre.1 = (f32[256,512]{1,0:T(8,128)S(1)}, f32[256,512]{1,0:T(8,128)S(1)}, f32[256,384]{1,0:T(8,128)S(1)}) custom-call(f32[20,16,128]{2,1,0:T(8,128)S(1)} %get-tuple-element.28.mine, f32[28,16,128]{2,1,0:T(8,128)S(1)} %rest.1, bf16[256,3072]{1,0:T(8,128)(2,1)S(1)} %copy-done), custom_call_target="tpu_custom_call" | custom-call | flops 2147483648 | tf_op jit(solution)/shard_map/centre/pallas_call | solution.py:398
  15.5 1.8 %mate.1 = (f32[256,512]{1,0:T(8,128)S(1)}, f32[4,8,16,128]{3,2,1,0:T(8,128)S(1)}, f32[4,8,8,128]{3,2,1,0:T(8,128)S(1)}, f32[256,896]{1,0:T(8,128)S(1)}, f32[256,384]{1,0:T(8,128)S(1)}) custom-call(f32[20,16,128]{2,1,0:T(8,128)S(1)} %collective-permute-done.1.a_mine, f32[28,16,128]{2,1,0:T(8,128)S(1)} %collective-permute-done.6.a_rest, ...), custom_call_target="tpu_custom_call" | custom-call | flops 536870912 | tf_op jit(solution)/shard_map/mate/pallas_call | solution.py:398
  17.3 2.0 %collective-permute-done.5.b_rest = f32[28,16,128]{2,1,0:T(8,128)S(1)} collective-permute-done((f32[28,16,128]{2,1,0:T(8,128)S(1)}, f32[28,16,128]{2,1,0:T(8,128)S(1)}, u32[]{:S(2)}, u32[]{:S(2)}) %collective-permute-start.5) | collective-permute-done | bytes 229408 | tf_op jit(solution)/shard_map/ppermute | solution.py:428
  19.3 2.4 %flux.1 = (f32[6,8,16,128]{3,2,1,0:T(8,128)S(1)}, f32[3,8,16,128]{3,2,1,0:T(8,128)S(1)}, f32[16,128]{1,0:T(8,128)S(1)}) custom-call(f32[20,16,128]{2,1,0:T(8,128)S(1)} %collective-permute-done.b_mine, f32[28,16,128]{2,1,0:T(8,128)S(1)} %collective-permute-done.5.b_rest, f32[256,512]{1,0:T(8,128)S(1)} %get-tuple-element.32.base, ...), custom_call_target="tpu_custom_call" | custom-call | tf_op jit(solution)/shard_map/flux/pallas_call | solution.py:398
  21.7 0.9 %collective-permute-start.9 = (f32[16,128]{1,0:T(8,128)S(1)}, f32[16,128]{1,0:T(8,128)S(1)}, u32[]{:S(2)}, u32[]{:S(2)}) collective-permute-start(f32[16,128]{1,0:T(8,128)S(1)} %get-tuple-element.37), channel_id=1, source_target_pairs={{0,16},{8,24},{16,0},{24,8},{1,17},{9,25},{17,1},{25,9},{2,18},{10... | collective-permute-start | bytes 24584 | tf_op jit(solution)/shard_map/ppermute | solution.py:508
  22.5 1.5 %collective-permute-start.8 = (f32[16,128]{1,0:T(8,128)S(1)}, f32[16,128]{1,0:T(8,128)S(1)}, u32[]{:S(2)}, u32[]{:S(2)}) collective-permute-start(f32[16,128]{1,0:T(8,128)S(1)} %get-tuple-element.37), channel_id=1, source_target_pairs={{0,24},{8,16},{16,8},{24,0},{1,25},{9,17},{17,9},{25,1},{2,26},{10... | collective-permute-start | bytes 24584 | tf_op jit(solution)/shard_map/ppermute | solution.py:508
  24.1 1.2 %collective-permute-start.7 = (f32[16,128]{1,0:T(8,128)S(1)}, f32[16,128]{1,0:T(8,128)S(1)}, u32[]{:S(2)}, u32[]{:S(2)}) collective-permute-start(f32[16,128]{1,0:T(8,128)S(1)} %get-tuple-element.37), channel_id=1, source_target_pairs={{0,8},{8,0},{16,24},{24,16},{1,9},{9,1},{17,25},{25,17},{2,10},{10... | collective-permute-start | bytes 24584 | tf_op jit(solution)/shard_map/ppermute | solution.py:508
  25.2 0.8 %collective-permute-start.11 = (f32[3,8,16,128]{3,2,1,0:T(8,128)S(1)}, f32[3,8,16,128]{3,2,1,0:T(8,128)S(1)}, u32[]{:S(2)}, u32[]{:S(2)}) collective-permute-start(f32[3,8,16,128]{3,2,1,0:T(8,128)S(1)} %get-tuple-element.39), channel_id=1, source_target_pairs={{0,1},{1,0},{2,3},{3,2},{4,5},{5,4},{6,7},{7,6},{8,9},{9,8},{10,11... | collective-permute-start | bytes 589832 | tf_op jit(solution)/shard_map/ppermute | solution.py:422
  26.0 0.3 collective-permute-done.9
  26.3 1.7 %collective-permute-done.8 = f32[16,128]{1,0:T(8,128)S(1)} collective-permute-done((f32[16,128]{1,0:T(8,128)S(1)}, f32[16,128]{1,0:T(8,128)S(1)}, u32[]{:S(2)}, u32[]{:S(2)}) %collective-permute-start.8) | collective-permute-done | bytes 8224 | tf_op jit(solution)/shard_map/ppermute | solution.py:508
  28.0 0.5 %collective-permute-start.10 = (f32[16,128]{1,0:T(8,128)S(1)}, f32[16,128]{1,0:T(8,128)S(1)}, u32[]{:S(2)}, u32[]{:S(2)}) collective-permute-start(f32[16,128]{1,0:T(8,128)S(1)} %add_add_fusion), channel_id=1, source_target_pairs={{0,1},{1,0},{2,3},{3,2},{4,5},{5,4},{6,7},{7,6},{8,9},{9,8},{10,11... | collective-permute-start | bytes 24584 | tf_op jit(solution)/shard_map/ppermute | solution.py:422
  28.5 3.2 %collective-permute-done.10 = f32[16,128]{1,0:T(8,128)S(1)} collective-permute-done((f32[16,128]{1,0:T(8,128)S(1)}, f32[16,128]{1,0:T(8,128)S(1)}, u32[]{:S(2)}, u32[]{:S(2)}) %collective-permute-start.10) | collective-permute-done | bytes 8224 | tf_op jit(solution)/shard_map/ppermute | solution.py:422
  31.7 1.0 %finish.1 = (f32[3,8,16,128]{3,2,1,0:T(8,128)}, f32[3,8,16,128]{3,2,1,0:T(8,128)}, f32[3,16]{1,0:T(4,128)}, f32[3,16]{1,0:T(4,128)}) custom-call(f32[16,128]{1,0:T(8,128)S(1)} %add.15.sums, f32[6,8,16,128]{3,2,1,0:T(8,128)S(1)} %get-tuple-element.38.keep, f32[3,8,16,128]{3,2,1,0:T(8,128)S(1)} %collective-permute-done.11.come), custom_call_target="tpu_custom_call" | custom-call | tf_op jit(solution)/shard_map/finish/pallas_call | solution.py:398
  (14 shorter events, 0.1 us)
Async XLA Ops:
  0.6 1.0 %copy-start.2 = (f32[4,8,16,128]{3,2,1,0:T(8,128)S(1)}, f32[4,8,16,128]{3,2,1,0:T(8,128)}, u32[]{:S(2)}) copy-start(f32[4,8,16,128]{3,2,1,0:T(8,128)} %own.1) | copy-start | bytes 786436
  2.0 9.7 %collective-permute-start.2 = (f32[20,16,128]{2,1,0:T(8,128)S(1)}, f32[20,16,128]{2,1,0:T(8,128)S(1)}, u32[]{:S(2)}, u32[]{:S(2)}) collective-permute-start(f32[20,16,128]{2,1,0:T(8,128)S(1)} %get-tuple-element.24), channel_id=1, source_target_pairs={{0,1},{1,0},{2,3},{3,2},{4,5},{5,4},{6,7},{7,6},{8,9},{9,8},{10,11... | collective-permute-start | bytes 491528 | tf_op jit(solution)/shard_map/ppermute | solution.py:422
  3.5 6.6 %collective-permute-start.3 = (f32[4,16,128]{2,1,0:T(8,128)S(1)}, f32[4,16,128]{2,1,0:T(8,128)S(1)}, u32[]{:S(2)}, u32[]{:S(2)}) collective-permute-start(f32[4,16,128]{2,1,0:T(8,128)S(1)} %get-tuple-element.25), channel_id=1, source_target_pairs={{1,25},{0,8},{9,1},{8,16},{17,9},{16,24},{25,17},{24,0},{3,27},{2,... | collective-permute-start | bytes 98312 | tf_op jit(solution)/shard_map/ppermute | solution.py:446
  5.1 6.6 %collective-permute-start.4 = (f32[4,16,128]{2,1,0:T(8,128)S(1)}, f32[4,16,128]{2,1,0:T(8,128)S(1)}, u32[]{:S(2)}, u32[]{:S(2)}) collective-permute-start(f32[4,16,128]{2,1,0:T(8,128)S(1)} %get-tuple-element.26), channel_id=1, source_target_pairs={{0,25},{1,8},{8,1},{9,16},{16,9},{17,24},{24,17},{25,0},{2,27},{3,... | collective-permute-start | bytes 98312 | tf_op jit(solution)/shard_map/ppermute | solution.py:445
  7.5 6.8 %copy-start = (bf16[256,3072]{1,0:T(8,128)(2,1)S(1)}, bf16[256,3072]{1,0:T(8,128)(2,1)}, u32[]{:S(2)}) copy-start(bf16[256,3072]{1,0:T(8,128)(2,1)} %constant.4.clone.planes.matrices) | copy-start | bytes 4718596
  7.5 6.8 %collective-permute-start.1 = (f32[20,16,128]{2,1,0:T(8,128)S(1)}, f32[20,16,128]{2,1,0:T(8,128)S(1)}, u32[]{:S(2)}, u32[]{:S(2)}) collective-permute-start(f32[20,16,128]{2,1,0:T(8,128)S(1)} %get-tuple-element.28.mine), channel_id=1, source_target_pairs={{0,2},{2,0},{4,6},{6,4},{1,3},{3,1},{5,7},{7,5},{8,10},{10,8},{12,... | collective-permute-start | bytes 491528 | tf_op jit(solution)/shard_map/ppermute | solution.py:425
  7.5 6.8 %collective-permute-start = (f32[20,16,128]{2,1,0:T(8,128)S(1)}, f32[20,16,128]{2,1,0:T(8,128)S(1)}, u32[]{:S(2)}, u32[]{:S(2)}) collective-permute-start(f32[20,16,128]{2,1,0:T(8,128)S(1)} %get-tuple-element.28.mine), channel_id=1, source_target_pairs={{0,0},{2,4},{4,2},{6,6},{1,1},{3,5},{5,3},{7,7},{8,8},{10,12},{12,... | collective-permute-start | bytes 491528 | tf_op jit(solution)/shard_map/ppermute | solution.py:428
  11.7 3.7 %copy-start.1 = (bf16[512,768]{1,0:T(8,128)(2,1)S(1)}, bf16[512,768]{1,0:T(8,128)(2,1)}, u32[]{:S(2)}) copy-start(bf16[512,768]{1,0:T(8,128)(2,1)} %constant.5.clone.spans) | copy-start | bytes 2359300
  11.7 3.7 %collective-permute-start.6 = (f32[28,16,128]{2,1,0:T(8,128)S(1)}, f32[28,16,128]{2,1,0:T(8,128)S(1)}, u32[]{:S(2)}, u32[]{:S(2)}) collective-permute-start(f32[28,16,128]{2,1,0:T(8,128)S(1)} %rest.1), channel_id=1, source_target_pairs={{0,2},{2,0},{4,6},{6,4},{1,3},{3,1},{5,7},{7,5},{8,10},{10,8},{12,... | collective-permute-start | bytes 688136 | tf_op jit(solution)/shard_map/ppermute | solution.py:425
  11.8 7.5 %collective-permute-start.5 = (f32[28,16,128]{2,1,0:T(8,128)S(1)}, f32[28,16,128]{2,1,0:T(8,128)S(1)}, u32[]{:S(2)}, u32[]{:S(2)}) collective-permute-start(f32[28,16,128]{2,1,0:T(8,128)S(1)} %rest.1), channel_id=1, source_target_pairs={{0,0},{2,4},{4,2},{6,6},{1,1},{3,5},{5,3},{7,7},{8,8},{10,12},{12,... | collective-permute-start | bytes 688136 | tf_op jit(solution)/shard_map/ppermute | solution.py:428
  21.7 4.6 %collective-permute-start.9 = (f32[16,128]{1,0:T(8,128)S(1)}, f32[16,128]{1,0:T(8,128)S(1)}, u32[]{:S(2)}, u32[]{:S(2)}) collective-permute-start(f32[16,128]{1,0:T(8,128)S(1)} %get-tuple-element.37), channel_id=1, source_target_pairs={{0,16},{8,24},{16,0},{24,8},{1,17},{9,25},{17,1},{25,9},{2,18},{10... | collective-permute-start | bytes 24584 | tf_op jit(solution)/shard_map/ppermute | solution.py:508
  22.5 5.4 %collective-permute-start.8 = (f32[16,128]{1,0:T(8,128)S(1)}, f32[16,128]{1,0:T(8,128)S(1)}, u32[]{:S(2)}, u32[]{:S(2)}) collective-permute-start(f32[16,128]{1,0:T(8,128)S(1)} %get-tuple-element.37), channel_id=1, source_target_pairs={{0,24},{8,16},{16,8},{24,0},{1,25},{9,17},{17,9},{25,1},{2,26},{10... | collective-permute-start | bytes 24584 | tf_op jit(solution)/shard_map/ppermute | solution.py:508
  24.1 3.9 %collective-permute-start.7 = (f32[16,128]{1,0:T(8,128)S(1)}, f32[16,128]{1,0:T(8,128)S(1)}, u32[]{:S(2)}, u32[]{:S(2)}) collective-permute-start(f32[16,128]{1,0:T(8,128)S(1)} %get-tuple-element.37), channel_id=1, source_target_pairs={{0,8},{8,0},{16,24},{24,16},{1,9},{9,1},{17,25},{25,17},{2,10},{10... | collective-permute-start | bytes 24584 | tf_op jit(solution)/shard_map/ppermute | solution.py:508
  25.2 6.5 %collective-permute-start.11 = (f32[3,8,16,128]{3,2,1,0:T(8,128)S(1)}, f32[3,8,16,128]{3,2,1,0:T(8,128)S(1)}, u32[]{:S(2)}, u32[]{:S(2)}) collective-permute-start(f32[3,8,16,128]{3,2,1,0:T(8,128)S(1)} %get-tuple-element.39), channel_id=1, source_target_pairs={{0,1},{1,0},{2,3},{3,2},{4,5},{5,4},{6,7},{7,6},{8,9},{9,8},{10,11... | collective-permute-start | bytes 589832 | tf_op jit(solution)/shard_map/ppermute | solution.py:422
  28.0 3.7 %collective-permute-start.10 = (f32[16,128]{1,0:T(8,128)S(1)}, f32[16,128]{1,0:T(8,128)S(1)}, u32[]{:S(2)}, u32[]{:S(2)}) collective-permute-start(f32[16,128]{1,0:T(8,128)S(1)} %add_add_fusion), channel_id=1, source_target_pairs={{0,1},{1,0},{2,3},{3,2},{4,5},{5,4},{6,7},{7,6},{8,9},{9,8},{10,11... | collective-permute-start | bytes 24584 | tf_op jit(solution)/shard_map/ppermute | solution.py:422

commit v23 on v21

--- a/solution.py
+++ b/solution.py
@@ -408,10 +408,10 @@
     def pair_a(value):
         return lax.ppermute(value, "wall", [(w, w ^ 1) for w in range(walls)])
 
-    def pair_b(value):
-        return lax.ppermute(
-            value, "wall", [(w, min(max(((w + 1) ^ 1) - 1, 0), walls - 1)) for w in range(walls)]
-        )
+    def pass_on(value):
+        ups = [(w, w + 2) for w in range(0, walls - 2, 2)]
+        downs = [(w, w - 2) for w in range(3, walls, 2)]
+        return lax.ppermute(value, "wall", ups + downs)
 
     def place(p, s):
         return (p % spans) * streams + s
@@ -428,7 +428,9 @@
     part = swap(to_partner)
     part_strip = lax.ppermute(first, ("span", "stream"), to_other)
     own_strip = lax.ppermute(second, ("span", "stream"), to_same)
-    mine_now, b_mine, a_mine = lax.optimization_barrier((mine, pair_b(mine), pair_a(mine)))
+    a_mine = pair_a(mine)
+    own_strip, part_strip, a_mine = lax.optimization_barrier((own_strip, part_strip, a_mine))
+    b_mine = pass_on(a_mine)
     (rest,) = call(
         rest_kernel,
         "rest",
@@ -436,7 +438,8 @@
         ((message[0] + layers, rows, width),),
         hint=2**35,
     )
-    a_rest, b_rest = pair_a(rest), pair_b(rest)
+    a_rest = pair_a(rest)
+    b_rest = pass_on(a_rest)
 
     matrices = jnp.asarray(plane_constants(both, rows))
     single_pass, split_pass = span_constants(width)
@@ -451,7 +454,7 @@
     upper, lower, products = call(
         centre_kernel,
         "centre",
-        (mine_now, rest, matrices),
+        (mine, rest, matrices),
         ((cells, 4 * width), (cells, 4 * width), (cells, 3 * width)),
         [(block, single), four, three],
         mib=16,

time: 32.9 us -> 36.3 us (1.10); the launches traced: 32.7 us -> 35.6 us
  waiting for transfers between devices: 8.79 us -> 13.6 us
  starting transfers between devices: 15.5 us -> 13.6 us
    ppermute x2, starting transfers between devices: 5.02 us -> 2.7 us  [pass_on(): return lax.ppermute(value, 'wall', ups + downs)]
    ppermute x2, waiting for transfers between devices: 1.96 us -> 4.07 us  [pass_on(): return lax.ppermute(value, 'wall', ups + downs)]
    ppermute x1, waiting for transfers between devices: 0.01 us -> 1.69 us  [shards(): own_strip = lax.ppermute(second, ('span', 'stream'), to_same)]
    ppermute x1, waiting for transfers between devices: 1.63 us -> 2.48 us  [shards(): part_strip = lax.ppermute(first, ('span', 'stream'), to_other)]
    ppermute x3, waiting for transfers between devices: 1.98 us -> 2.54 us  [from_span(): return lax.ppermute(value, 'span', [(p, p ^ step) for p in range(spans)])]
    ppermute x3, waiting for transfers between devices: 3.21 us -> 2.79 us  [swap(): return lax.ppermute(value, 'stream', [(0, 1), (1, 0)])]
  transfers between devices with their start and end apart: 12 -> 12, of which waited for: 5 -> 7; matrix products, arithmetic and copies ran while one was open for 0% -> 0% of each run, Pallas kernels for 9% -> 8%
where the time goes in v23:
time: 36.3 us; the launch traced here: 35.6 us
  starting transfers between devices  13.6 us (37%)
  waiting for transfers between devices  13.6 us (37%)
  Pallas kernels  6.72 us (19%)
  local copies, waits for them, and re-layouts  0.95 us (3%)
  between operations  0.75 us (2%)
    pallas_call x6, Pallas kernels, call(): pl.pallas_call(kernel, out_shape=tuple((jax.ShapeDtypeStruct(shape, jnp.f...  6.72 us
    ppermute x2, waiting for transfers between devices, pass_on(): return lax.ppermute(value, 'wall', ups + downs)  4.07 us
    ppermute x3, starting transfers between devices, from_span(): return lax.ppermute(value, 'span', [(p, p ^ step) for p in range(spans)])  3.55 us
    ppermute x3, starting transfers between devices, swap(): return lax.ppermute(value, 'stream', [(0, 1), (1, 0)])  3.21 us
    ppermute x3, waiting for transfers between devices, swap(): return lax.ppermute(value, 'stream', [(0, 1), (1, 0)])  2.79 us
    ppermute x2, starting transfers between devices, pass_on(): return lax.ppermute(value, 'wall', ups + downs)  2.7 us
    ppermute x3, waiting for transfers between devices, from_span(): return lax.ppermute(value, 'span', [(p, p ^ step) for p in range(spans)])  2.54 us
    ppermute x1, waiting for transfers between devices, shards(): part_strip = lax.ppermute(first, ('span', 'stream'), to_other)  2.48 us
  transfers between devices with their start and end apart: 12, of which 7 were waited for; matrix products, arithmetic and copies ran while one was open for 0% of the time, Pallas kernels for 8%

profile of v23, /device:TPU:4, one launch (start us, length us, event | category | flops | bytes accessed | tf_op | source)
XLA Modules:
  0.0 35.6 jit_solution(13037705474172651129)
XLA Ops:
  0.6 0.9 %copy-done.2 = f32[4,8,16,128]{3,2,1,0:T(8,128)S(1)} copy-done((f32[4,8,16,128]{3,2,1,0:T(8,128)S(1)}, f32[4,8,16,128]{3,2,1,0:T(8,128)}, u32[]{:S(2)}) %copy-start.2) | copy-done | bytes 262168
  1.6 0.4 %pack.1 = (f32[20,16,128]{2,1,0:T(8,128)S(1)}, f32[20,16,128]{2,1,0:T(8,128)S(1)}, f32[4,16,128]{2,1,0:T(8,128)S(1)}, f32[4,16,128]{2,1,0:T(8,128)S(1)}) custom-call(f32[4,8,16,128]{3,2,1,0:T(8,128)S(1)} %copy-done.2), custom_call_target="tpu_custom_call" | custom-call | tf_op jit(solution)/shard_map/pack/pallas_call | solution.py:385
  2.0 1.6 %collective-permute-start.4 = (f32[20,16,128]{2,1,0:T(8,128)S(1)}, f32[20,16,128]{2,1,0:T(8,128)S(1)}, u32[]{:S(2)}, u32[]{:S(2)}) collective-permute-start(f32[20,16,128]{2,1,0:T(8,128)S(1)} %get-tuple-element.26), channel_id=1, source_target_pairs={{0,1},{1,0},{2,3},{3,2},{4,5},{5,4},{6,7},{7,6},{8,9},{9,8},{10,11... | collective-permute-start | bytes 491528 | tf_op jit(solution)/shard_map/ppermute | solution.py:406
  3.6 1.6 %collective-permute-start = (f32[4,16,128]{2,1,0:T(8,128)S(1)}, f32[4,16,128]{2,1,0:T(8,128)S(1)}, u32[]{:S(2)}, u32[]{:S(2)}) collective-permute-start(f32[4,16,128]{2,1,0:T(8,128)S(1)} %get-tuple-element.22), channel_id=1, source_target_pairs={{1,25},{0,8},{9,1},{8,16},{17,9},{16,24},{25,17},{24,0},{3,27},{2,... | collective-permute-start | bytes 98312 | tf_op jit(solution)/shard_map/ppermute | solution.py:430
  5.2 2.4 %collective-permute-start.1 = (f32[4,16,128]{2,1,0:T(8,128)S(1)}, f32[4,16,128]{2,1,0:T(8,128)S(1)}, u32[]{:S(2)}, u32[]{:S(2)}) collective-permute-start(f32[4,16,128]{2,1,0:T(8,128)S(1)} %get-tuple-element.23), channel_id=1, source_target_pairs={{0,25},{1,8},{8,1},{9,16},{16,9},{17,24},{24,17},{25,0},{2,27},{3,... | collective-permute-start | bytes 98312 | tf_op jit(solution)/shard_map/ppermute | solution.py:429
  7.6 1.7 %collective-permute-done.own_strip = f32[4,16,128]{2,1,0:T(8,128)S(1)} collective-permute-done((f32[4,16,128]{2,1,0:T(8,128)S(1)}, f32[4,16,128]{2,1,0:T(8,128)S(1)}, u32[]{:S(2)}, u32[]{:S(2)}) %collective-permute-start) | collective-permute-done | bytes 32800 | tf_op jit(solution)/shard_map/ppermute | solution.py:430
  9.3 2.5 %collective-permute-done.1.part_strip = f32[4,16,128]{2,1,0:T(8,128)S(1)} collective-permute-done((f32[4,16,128]{2,1,0:T(8,128)S(1)}, f32[4,16,128]{2,1,0:T(8,128)S(1)}, u32[]{:S(2)}, u32[]{:S(2)}) %collective-permute-start.1) | collective-permute-done | bytes 32800 | tf_op jit(solution)/shard_map/ppermute | solution.py:429
  11.8 0.1 collective-permute-start.5
  11.9 1.4 %collective-permute-start.3 = (f32[20,16,128]{2,1,0:T(8,128)S(1)}, f32[20,16,128]{2,1,0:T(8,128)S(1)}, u32[]{:S(2)}, u32[]{:S(2)}) collective-permute-start(f32[20,16,128]{2,1,0:T(8,128)S(1)} %collective-permute-done.2.a_mine), channel_id=1, source_target_pairs={{0,4},{6,2},{1,5},{7,3},{8,12},{14,10},{9,13},{15,11},{16,20},{22,... | collective-permute-start | bytes 491528 | tf_op jit(solution)/shard_map/ppermute | solution.py:414
  13.4 1.3 %collective-permute-start.6 = (f32[28,16,128]{2,1,0:T(8,128)S(1)}, f32[28,16,128]{2,1,0:T(8,128)S(1)}, u32[]{:S(2)}, u32[]{:S(2)}) collective-permute-start(f32[28,16,128]{2,1,0:T(8,128)S(1)} %collective-permute-done.5.a_rest), channel_id=1, source_target_pairs={{0,4},{6,2},{1,5},{7,3},{8,12},{14,10},{9,13},{15,11},{16,20},{22,... | collective-permute-start | bytes 688136 | tf_op jit(solution)/shard_map/ppermute | solution.py:414
  14.7 1.1 %centre.1 = (f32[256,512]{1,0:T(8,128)S(1)}, f32[256,512]{1,0:T(8,128)S(1)}, f32[256,384]{1,0:T(8,128)S(1)}) custom-call(f32[20,16,128]{2,1,0:T(8,128)S(1)} %get-tuple-element.24.mine, f32[28,16,128]{2,1,0:T(8,128)S(1)} %rest.1, bf16[256,3072]{1,0:T(8,128)(2,1)S(1)} %copy-done), custom_call_target="tpu_custom_call" | custom-call | flops 2147483648 | tf_op jit(solution)/shard_map/centre/pallas_call | solution.py:385
  15.8 1.8 %mate.1 = (f32[256,512]{1,0:T(8,128)S(1)}, f32[4,8,16,128]{3,2,1,0:T(8,128)S(1)}, f32[4,8,8,128]{3,2,1,0:T(8,128)S(1)}, f32[256,896]{1,0:T(8,128)S(1)}, f32[256,384]{1,0:T(8,128)S(1)}) custom-call(f32[20,16,128]{2,1,0:T(8,128)S(1)} %collective-permute-done.2.a_mine, f32[28,16,128]{2,1,0:T(8,128)S(1)} %collective-permute-done.5.a_rest, ...), custom_call_target="tpu_custom_call" | custom-call | flops 536870912 | tf_op jit(solution)/shard_map/mate/pallas_call | solution.py:385
  17.6 1.6 %collective-permute-done.3.b_mine = f32[20,16,128]{2,1,0:T(8,128)S(1)} collective-permute-done((f32[20,16,128]{2,1,0:T(8,128)S(1)}, f32[20,16,128]{2,1,0:T(8,128)S(1)}, u32[]{:S(2)}, u32[]{:S(2)}) %collective-permute-start.3) | collective-permute-done | bytes 163872 | tf_op jit(solution)/shard_map/ppermute | solution.py:414
  19.2 2.5 %collective-permute-done.6.b_rest = f32[28,16,128]{2,1,0:T(8,128)S(1)} collective-permute-done((f32[28,16,128]{2,1,0:T(8,128)S(1)}, f32[28,16,128]{2,1,0:T(8,128)S(1)}, u32[]{:S(2)}, u32[]{:S(2)}) %collective-permute-start.6) | collective-permute-done | bytes 229408 | tf_op jit(solution)/shard_map/ppermute | solution.py:414
  21.7 2.4 %flux.1 = (f32[6,8,16,128]{3,2,1,0:T(8,128)S(1)}, f32[3,8,16,128]{3,2,1,0:T(8,128)S(1)}, f32[16,128]{1,0:T(8,128)S(1)}) custom-call(f32[20,16,128]{2,1,0:T(8,128)S(1)} %collective-permute-done.3.b_mine, f32[28,16,128]{2,1,0:T(8,128)S(1)} %collective-permute-done.6.b_rest, f32[256,512]{1,0:T(8,128)S(1)} %get-tuple-element.32.base, ...), custom_call_target="tpu_custom_call" | custom-call | tf_op jit(solution)/shard_map/flux/pallas_call | solution.py:385
  24.1 0.1 collective-permute-start.7
  24.2 2.2 %collective-permute-start.8 = (f32[16,128]{1,0:T(8,128)S(1)}, f32[16,128]{1,0:T(8,128)S(1)}, u32[]{:S(2)}, u32[]{:S(2)}) collective-permute-start(f32[16,128]{1,0:T(8,128)S(1)} %get-tuple-element.37), channel_id=1, source_target_pairs={{0,24},{8,16},{16,8},{24,0},{1,25},{9,17},{17,9},{25,1},{2,26},{10... | collective-permute-start | bytes 24584 | tf_op jit(solution)/shard_map/ppermute | solution.py:495
  26.4 1.2 %collective-permute-start.9 = (f32[16,128]{1,0:T(8,128)S(1)}, f32[16,128]{1,0:T(8,128)S(1)}, u32[]{:S(2)}, u32[]{:S(2)}) collective-permute-start(f32[16,128]{1,0:T(8,128)S(1)} %get-tuple-element.37), channel_id=1, source_target_pairs={{0,16},{8,24},{16,0},{24,8},{1,17},{9,25},{17,1},{25,9},{2,18},{10... | collective-permute-start | bytes 24584 | tf_op jit(solution)/shard_map/ppermute | solution.py:495
  27.7 0.8 %collective-permute-start.11 = (f32[3,8,16,128]{3,2,1,0:T(8,128)S(1)}, f32[3,8,16,128]{3,2,1,0:T(8,128)S(1)}, u32[]{:S(2)}, u32[]{:S(2)}) collective-permute-start(f32[3,8,16,128]{3,2,1,0:T(8,128)S(1)} %get-tuple-element.39), channel_id=1, source_target_pairs={{0,1},{1,0},{2,3},{3,2},{4,5},{5,4},{6,7},{7,6},{8,9},{9,8},{10,11... | collective-permute-start | bytes 589832 | tf_op jit(solution)/shard_map/ppermute | solution.py:406
  28.4 1.3 %collective-permute-done.8 = f32[16,128]{1,0:T(8,128)S(1)} collective-permute-done((f32[16,128]{1,0:T(8,128)S(1)}, f32[16,128]{1,0:T(8,128)S(1)}, u32[]{:S(2)}, u32[]{:S(2)}) %collective-permute-start.8) | collective-permute-done | bytes 8224 | tf_op jit(solution)/shard_map/ppermute | solution.py:495
  29.7 1.3 %collective-permute-done.9 = f32[16,128]{1,0:T(8,128)S(1)} collective-permute-done((f32[16,128]{1,0:T(8,128)S(1)}, f32[16,128]{1,0:T(8,128)S(1)}, u32[]{:S(2)}, u32[]{:S(2)}) %collective-permute-start.9) | collective-permute-done | bytes 8224 | tf_op jit(solution)/shard_map/ppermute | solution.py:495
  31.0 0.9 %collective-permute-start.10 = (f32[16,128]{1,0:T(8,128)S(1)}, f32[16,128]{1,0:T(8,128)S(1)}, u32[]{:S(2)}, u32[]{:S(2)}) collective-permute-start(f32[16,128]{1,0:T(8,128)S(1)} %add_add_fusion), channel_id=1, source_target_pairs={{0,1},{1,0},{2,3},{3,2},{4,5},{5,4},{6,7},{7,6},{8,9},{9,8},{10,11... | collective-permute-start | bytes 24584 | tf_op jit(solution)/shard_map/ppermute | solution.py:406
  31.9 2.8 %collective-permute-done.10 = f32[16,128]{1,0:T(8,128)S(1)} collective-permute-done((f32[16,128]{1,0:T(8,128)S(1)}, f32[16,128]{1,0:T(8,128)S(1)}, u32[]{:S(2)}, u32[]{:S(2)}) %collective-permute-start.10) | collective-permute-done | bytes 8224 | tf_op jit(solution)/shard_map/ppermute | solution.py:406
  34.6 1.0 %finish.1 = (f32[3,8,16,128]{3,2,1,0:T(8,128)}, f32[3,8,16,128]{3,2,1,0:T(8,128)}, f32[3,16]{1,0:T(4,128)}, f32[3,16]{1,0:T(4,128)}) custom-call(f32[16,128]{1,0:T(8,128)S(1)} %add.15.sums, f32[6,8,16,128]{3,2,1,0:T(8,128)S(1)} %get-tuple-element.38.keep, f32[3,8,16,128]{3,2,1,0:T(8,128)S(1)} %collective-permute-done.11.come), custom_call_target="tpu_custom_call" | custom-call | tf_op jit(solution)/shard_map/finish/pallas_call | solution.py:385
  (14 shorter events, 0.2 us)
Async XLA Ops:
  0.6 1.0 %copy-start.2 = (f32[4,8,16,128]{3,2,1,0:T(8,128)S(1)}, f32[4,8,16,128]{3,2,1,0:T(8,128)}, u32[]{:S(2)}) copy-start(f32[4,8,16,128]{3,2,1,0:T(8,128)} %own.1) | copy-start | bytes 786436
  2.0 9.8 %collective-permute-start.2 = (f32[20,16,128]{2,1,0:T(8,128)S(1)}, f32[20,16,128]{2,1,0:T(8,128)S(1)}, u32[]{:S(2)}, u32[]{:S(2)}) collective-permute-start(f32[20,16,128]{2,1,0:T(8,128)S(1)} %get-tuple-element.24.mine), channel_id=1, source_target_pairs={{0,2},{2,0},{4,6},{6,4},{1,3},{3,1},{5,7},{7,5},{8,10},{10,8},{12,... | collective-permute-start | bytes 491528 | tf_op jit(solution)/shard_map/ppermute | solution.py:409
  2.0 9.8 %collective-permute-start.4 = (f32[20,16,128]{2,1,0:T(8,128)S(1)}, f32[20,16,128]{2,1,0:T(8,128)S(1)}, u32[]{:S(2)}, u32[]{:S(2)}) collective-permute-start(f32[20,16,128]{2,1,0:T(8,128)S(1)} %get-tuple-element.26), channel_id=1, source_target_pairs={{0,1},{1,0},{2,3},{3,2},{4,5},{5,4},{6,7},{7,6},{8,9},{9,8},{10,11... | collective-permute-start | bytes 491528 | tf_op jit(solution)/shard_map/ppermute | solution.py:406
  3.6 5.7 %collective-permute-start = (f32[4,16,128]{2,1,0:T(8,128)S(1)}, f32[4,16,128]{2,1,0:T(8,128)S(1)}, u32[]{:S(2)}, u32[]{:S(2)}) collective-permute-start(f32[4,16,128]{2,1,0:T(8,128)S(1)} %get-tuple-element.22), channel_id=1, source_target_pairs={{1,25},{0,8},{9,1},{8,16},{17,9},{16,24},{25,17},{24,0},{3,27},{2,... | collective-permute-start | bytes 98312 | tf_op jit(solution)/shard_map/ppermute | solution.py:430
  5.2 9.5 %copy-start = (bf16[256,3072]{1,0:T(8,128)(2,1)S(1)}, bf16[256,3072]{1,0:T(8,128)(2,1)}, u32[]{:S(2)}) copy-start(bf16[256,3072]{1,0:T(8,128)(2,1)} %constant.4.clone.planes.matrices) | copy-start | bytes 4718596
  5.2 6.6 %collective-permute-start.1 = (f32[4,16,128]{2,1,0:T(8,128)S(1)}, f32[4,16,128]{2,1,0:T(8,128)S(1)}, u32[]{:S(2)}, u32[]{:S(2)}) collective-permute-start(f32[4,16,128]{2,1,0:T(8,128)S(1)} %get-tuple-element.23), channel_id=1, source_target_pairs={{0,25},{1,8},{8,1},{9,16},{16,9},{17,24},{24,17},{25,0},{2,27},{3,... | collective-permute-start | bytes 98312 | tf_op jit(solution)/shard_map/ppermute | solution.py:429
  11.8 4.0 %copy-start.1 = (bf16[512,768]{1,0:T(8,128)(2,1)S(1)}, bf16[512,768]{1,0:T(8,128)(2,1)}, u32[]{:S(2)}) copy-start(bf16[512,768]{1,0:T(8,128)(2,1)} %constant.5.clone.spans) | copy-start | bytes 2359300
  11.8 1.6 %collective-permute-start.5 = (f32[28,16,128]{2,1,0:T(8,128)S(1)}, f32[28,16,128]{2,1,0:T(8,128)S(1)}, u32[]{:S(2)}, u32[]{:S(2)}) collective-permute-start(f32[28,16,128]{2,1,0:T(8,128)S(1)} %rest.1), channel_id=1, source_target_pairs={{0,2},{2,0},{4,6},{6,4},{1,3},{3,1},{5,7},{7,5},{8,10},{10,8},{12,... | collective-permute-start | bytes 688136 | tf_op jit(solution)/shard_map/ppermute | solution.py:409
  11.9 7.3 %collective-permute-start.3 = (f32[20,16,128]{2,1,0:T(8,128)S(1)}, f32[20,16,128]{2,1,0:T(8,128)S(1)}, u32[]{:S(2)}, u32[]{:S(2)}) collective-permute-start(f32[20,16,128]{2,1,0:T(8,128)S(1)} %collective-permute-done.2.a_mine), channel_id=1, source_target_pairs={{0,4},{6,2},{1,5},{7,3},{8,12},{14,10},{9,13},{15,11},{16,20},{22,... | collective-permute-start | bytes 491528 | tf_op jit(solution)/shard_map/ppermute | solution.py:414
  13.4 8.3 %collective-permute-start.6 = (f32[28,16,128]{2,1,0:T(8,128)S(1)}, f32[28,16,128]{2,1,0:T(8,128)S(1)}, u32[]{:S(2)}, u32[]{:S(2)}) collective-permute-start(f32[28,16,128]{2,1,0:T(8,128)S(1)} %collective-permute-done.5.a_rest), channel_id=1, source_target_pairs={{0,4},{6,2},{1,5},{7,3},{8,12},{14,10},{9,13},{15,11},{16,20},{22,... | collective-permute-start | bytes 688136 | tf_op jit(solution)/shard_map/ppermute | solution.py:414
  24.1 4.3 %collective-permute-start.7 = (f32[16,128]{1,0:T(8,128)S(1)}, f32[16,128]{1,0:T(8,128)S(1)}, u32[]{:S(2)}, u32[]{:S(2)}) collective-permute-start(f32[16,128]{1,0:T(8,128)S(1)} %get-tuple-element.37), channel_id=1, source_target_pairs={{0,8},{8,0},{16,24},{24,16},{1,9},{9,1},{17,25},{25,17},{2,10},{10... | collective-permute-start | bytes 24584 | tf_op jit(solution)/shard_map/ppermute | solution.py:495
  24.2 5.5 %collective-permute-start.8 = (f32[16,128]{1,0:T(8,128)S(1)}, f32[16,128]{1,0:T(8,128)S(1)}, u32[]{:S(2)}, u32[]{:S(2)}) collective-permute-start(f32[16,128]{1,0:T(8,128)S(1)} %get-tuple-element.37), channel_id=1, source_target_pairs={{0,24},{8,16},{16,8},{24,0},{1,25},{9,17},{17,9},{25,1},{2,26},{10... | collective-permute-start | bytes 24584 | tf_op jit(solution)/shard_map/ppermute | solution.py:495
  26.4 4.5 %collective-permute-start.9 = (f32[16,128]{1,0:T(8,128)S(1)}, f32[16,128]{1,0:T(8,128)S(1)}, u32[]{:S(2)}, u32[]{:S(2)}) collective-permute-start(f32[16,128]{1,0:T(8,128)S(1)} %get-tuple-element.37), channel_id=1, source_target_pairs={{0,16},{8,24},{16,0},{24,8},{1,17},{9,25},{17,1},{25,9},{2,18},{10... | collective-permute-start | bytes 24584 | tf_op jit(solution)/shard_map/ppermute | solution.py:495
  27.7 7.0 %collective-permute-start.11 = (f32[3,8,16,128]{3,2,1,0:T(8,128)S(1)}, f32[3,8,16,128]{3,2,1,0:T(8,128)S(1)}, u32[]{:S(2)}, u32[]{:S(2)}) collective-permute-start(f32[3,8,16,128]{3,2,1,0:T(8,128)S(1)} %get-tuple-element.39), channel_id=1, source_target_pairs={{0,1},{1,0},{2,3},{3,2},{4,5},{5,4},{6,7},{7,6},{8,9},{9,8},{10,11... | collective-permute-start | bytes 589832 | tf_op jit(solution)/shard_map/ppermute | solution.py:406
  31.0 3.7 %collective-permute-start.10 = (f32[16,128]{1,0:T(8,128)S(1)}, f32[16,128]{1,0:T(8,128)S(1)}, u32[]{:S(2)}, u32[]{:S(2)}) collective-permute-start(f32[16,128]{1,0:T(8,128)S(1)} %add_add_fusion), channel_id=1, source_target_pairs={{0,1},{1,0},{2,3},{3,2},{4,5},{5,4},{6,7},{7,6},{8,9},{9,8},{10,11... | collective-permute-start | bytes 24584 | tf_op jit(solution)/shard_map/ppermute | solution.py:406

commit v24 on v23

--- a/solution.py
+++ b/solution.py
@@ -429,8 +429,7 @@
     part_strip = lax.ppermute(first, ("span", "stream"), to_other)
     own_strip = lax.ppermute(second, ("span", "stream"), to_same)
     a_mine = pair_a(mine)
-    own_strip, part_strip, a_mine = lax.optimization_barrier((own_strip, part_strip, a_mine))
-    b_mine = pass_on(a_mine)
+    mine_now, b_mine = lax.optimization_barrier((mine, pass_on(a_mine)))
     (rest,) = call(
         rest_kernel,
         "rest",
@@ -439,7 +438,6 @@
         hint=2**35,
     )
     a_rest = pair_a(rest)
-    b_rest = pass_on(a_rest)
 
     matrices = jnp.asarray(plane_constants(both, rows))
     single_pass, split_pass = span_constants(width)
@@ -454,12 +452,14 @@
     upper, lower, products = call(
         centre_kernel,
         "centre",
-        (mine, rest, matrices),
+        (mine_now, rest, matrices),
         ((cells, 4 * width), (cells, 4 * width), (cells, 3 * width)),
         [(block, single), four, three],
         mib=16,
         hint=2**31,
     )
+    a_rest, upper = lax.optimization_barrier((a_rest, upper))
+    b_rest = pass_on(a_rest)
     base, a_packed, a_slopes, a_second, products = call(
         mate_kernel,
         "mate",

time: 36.3 us -> 38.8 us (1.069)
  waiting for transfers between devices: 13.6 us -> 16.4 us
    ppermute x2, waiting for transfers between devices: 4.07 us -> 7.68 us  [pass_on(): return lax.ppermute(value, 'wall', ups + downs)]
    ppermute x1, waiting for transfers between devices: 1.69 us -> 0.4 us  [shards(): own_strip = lax.ppermute(second, ('span', 'stream'), to_same)]
    ppermute x3, waiting for transfers between devices: 2.54 us -> 2.93 us  [from_span(): return lax.ppermute(value, 'span', [(p, p ^ step) for p in range(spans)])]
  transfers between devices with their start and end apart: 12 -> 12, of which waited for: 7 -> 6; matrix products, arithmetic and copies ran while one was open for 0% -> 0% of each run, Pallas kernels for 8% -> 8%
where the time goes in v24:
time: 38.8 us; the launch traced here: 38.1 us
  waiting for transfers between devices  16.4 us (42%)
  starting transfers between devices  13.3 us (34%)
  Pallas kernels  6.72 us (17%)
  local copies, waits for them, and re-layouts  0.95 us (2%)
  between operations  0.74 us (2%)
    ppermute x2, waiting for transfers between devices, pass_on(): return lax.ppermute(value, 'wall', ups + downs)  7.68 us
    pallas_call x6, Pallas kernels, call(): pl.pallas_call(kernel, out_shape=tuple((jax.ShapeDtypeStruct(shape, jnp.f...  6.72 us
    ppermute x3, starting transfers between devices, from_span(): return lax.ppermute(value, 'span', [(p, p ^ step) for p in range(spans)])  3.55 us
    ppermute x3, starting transfers between devices, swap(): return lax.ppermute(value, 'stream', [(0, 1), (1, 0)])  2.99 us
    ppermute x3, waiting for transfers between devices, from_span(): return lax.ppermute(value, 'span', [(p, p ^ step) for p in range(spans)])  2.93 us
    ppermute x3, waiting for transfers between devices, swap(): return lax.ppermute(value, 'stream', [(0, 1), (1, 0)])  2.89 us
    ppermute x2, starting transfers between devices, pass_on(): return lax.ppermute(value, 'wall', ups + downs)  2.57 us
    ppermute x1, waiting for transfers between devices, shards(): part_strip = lax.ppermute(first, ('span', 'stream'), to_other)  2.48 us
  transfers between devices with their start and end apart: 12, of which 6 were waited for; matrix products, arithmetic and copies ran while one was open for 0% of the time, Pallas kernels for 8%

profile of v24, /device:TPU:4, one launch (start us, length us, event | category | flops | bytes accessed | tf_op | source)
XLA Modules:
  0.0 38.1 jit_solution(12813542668741928404)
XLA Ops:
  0.6 0.9 %copy-done.2 = f32[4,8,16,128]{3,2,1,0:T(8,128)S(1)} copy-done((f32[4,8,16,128]{3,2,1,0:T(8,128)S(1)}, f32[4,8,16,128]{3,2,1,0:T(8,128)}, u32[]{:S(2)}) %copy-start.2) | copy-done | bytes 262168
  1.6 0.4 pack.1
  2.0 0.1 collective-permute-start
  2.0 1.6 %collective-permute-start.2 = (f32[20,16,128]{2,1,0:T(8,128)S(1)}, f32[20,16,128]{2,1,0:T(8,128)S(1)}, u32[]{:S(2)}, u32[]{:S(2)}) collective-permute-start(f32[20,16,128]{2,1,0:T(8,128)S(1)} %get-tuple-element.25), channel_id=1, source_target_pairs={{0,1},{1,0},{2,3},{3,2},{4,5},{5,4},{6,7},{7,6},{8,9},{9,8},{10,11... | collective-permute-start | bytes 491528 | tf_op jit(solution)/shard_map/ppermute | solution.py:406
  3.6 1.6 %collective-permute-start.3 = (f32[4,16,128]{2,1,0:T(8,128)S(1)}, f32[4,16,128]{2,1,0:T(8,128)S(1)}, u32[]{:S(2)}, u32[]{:S(2)}) collective-permute-start(f32[4,16,128]{2,1,0:T(8,128)S(1)} %get-tuple-element.26), channel_id=1, source_target_pairs={{1,25},{0,8},{9,1},{8,16},{17,9},{16,24},{25,17},{24,0},{3,27},{2,... | collective-permute-start | bytes 98312 | tf_op jit(solution)/shard_map/ppermute | solution.py:430
  5.2 2.4 %collective-permute-start.4 = (f32[4,16,128]{2,1,0:T(8,128)S(1)}, f32[4,16,128]{2,1,0:T(8,128)S(1)}, u32[]{:S(2)}, u32[]{:S(2)}) collective-permute-start(f32[4,16,128]{2,1,0:T(8,128)S(1)} %get-tuple-element.27), channel_id=1, source_target_pairs={{0,25},{1,8},{8,1},{9,16},{16,9},{17,24},{24,17},{25,0},{2,27},{3,... | collective-permute-start | bytes 98312 | tf_op jit(solution)/shard_map/ppermute | solution.py:429
  7.6 1.3 %collective-permute-start.1 = (f32[20,16,128]{2,1,0:T(8,128)S(1)}, f32[20,16,128]{2,1,0:T(8,128)S(1)}, u32[]{:S(2)}, u32[]{:S(2)}) collective-permute-start(f32[20,16,128]{2,1,0:T(8,128)S(1)} %collective-permute-done.a_mine), channel_id=1, source_target_pairs={{0,4},{6,2},{1,5},{7,3},{8,12},{14,10},{9,13},{15,11},{16,20},{22,... | collective-permute-start | bytes 491528 | tf_op jit(solution)/shard_map/ppermute | solution.py:414
  8.9 0.4 %collective-permute-done.3.own_strip = f32[4,16,128]{2,1,0:T(8,128)S(1)} collective-permute-done((f32[4,16,128]{2,1,0:T(8,128)S(1)}, f32[4,16,128]{2,1,0:T(8,128)S(1)}, u32[]{:S(2)}, u32[]{:S(2)}) %collective-permute-start.3) | collective-permute-done | bytes 32800 | tf_op jit(solution)/shard_map/ppermute | solution.py:430
  9.3 2.5 %collective-permute-done.4.part_strip = f32[4,16,128]{2,1,0:T(8,128)S(1)} collective-permute-done((f32[4,16,128]{2,1,0:T(8,128)S(1)}, f32[4,16,128]{2,1,0:T(8,128)S(1)}, u32[]{:S(2)}, u32[]{:S(2)}) %collective-permute-start.4) | collective-permute-done | bytes 32800 | tf_op jit(solution)/shard_map/ppermute | solution.py:429
  11.8 0.1 collective-permute-start.5
  11.9 2.9 %collective-permute-done.1.b_mine = f32[20,16,128]{2,1,0:T(8,128)S(1)} collective-permute-done((f32[20,16,128]{2,1,0:T(8,128)S(1)}, f32[20,16,128]{2,1,0:T(8,128)S(1)}, u32[]{:S(2)}, u32[]{:S(2)}) %collective-permute-start.1) | collective-permute-done | bytes 163872 | tf_op jit(solution)/shard_map/ppermute | solution.py:414
  14.8 1.1 %centre.1 = (f32[256,512]{1,0:T(8,128)S(1)}, f32[256,512]{1,0:T(8,128)S(1)}, f32[256,384]{1,0:T(8,128)S(1)}) custom-call(f32[20,16,128]{2,1,0:T(8,128)S(1)} %get-tuple-element.28.mine, f32[28,16,128]{2,1,0:T(8,128)S(1)} %rest.1, bf16[256,3072]{1,0:T(8,128)(2,1)S(1)} %copy-done), custom_call_target="tpu_custom_call" | custom-call | flops 2147483648 | tf_op jit(solution)/shard_map/centre/pallas_call | solution.py:385
  15.9 1.3 %collective-permute-start.6 = (f32[28,16,128]{2,1,0:T(8,128)S(1)}, f32[28,16,128]{2,1,0:T(8,128)S(1)}, u32[]{:S(2)}, u32[]{:S(2)}) collective-permute-start(f32[28,16,128]{2,1,0:T(8,128)S(1)} %collective-permute-done.5.a_rest), channel_id=1, source_target_pairs={{0,4},{6,2},{1,5},{7,3},{8,12},{14,10},{9,13},{15,11},{16,20},{22,... | collective-permute-start | bytes 688136 | tf_op jit(solution)/shard_map/ppermute | solution.py:414
  17.2 1.8 %mate.1 = (f32[256,512]{1,0:T(8,128)S(1)}, f32[4,8,16,128]{3,2,1,0:T(8,128)S(1)}, f32[4,8,8,128]{3,2,1,0:T(8,128)S(1)}, f32[256,896]{1,0:T(8,128)S(1)}, f32[256,384]{1,0:T(8,128)S(1)}) custom-call(f32[20,16,128]{2,1,0:T(8,128)S(1)} %collective-permute-done.a_mine, f32[28,16,128]{2,1,0:T(8,128)S(1)} %collective-permute-done.5.a_rest, ...), custom_call_target="tpu_custom_call" | custom-call | flops 536870912 | tf_op jit(solution)/shard_map/mate/pallas_call | solution.py:385
  19.1 4.8 %collective-permute-done.6.b_rest = f32[28,16,128]{2,1,0:T(8,128)S(1)} collective-permute-done((f32[28,16,128]{2,1,0:T(8,128)S(1)}, f32[28,16,128]{2,1,0:T(8,128)S(1)}, u32[]{:S(2)}, u32[]{:S(2)}) %collective-permute-start.6) | collective-permute-done | bytes 229408 | tf_op jit(solution)/shard_map/ppermute | solution.py:414
  23.8 2.4 %flux.1 = (f32[6,8,16,128]{3,2,1,0:T(8,128)S(1)}, f32[3,8,16,128]{3,2,1,0:T(8,128)S(1)}, f32[16,128]{1,0:T(8,128)S(1)}) custom-call(f32[20,16,128]{2,1,0:T(8,128)S(1)} %collective-permute-done.1.b_mine, f32[28,16,128]{2,1,0:T(8,128)S(1)} %collective-permute-done.6.b_rest, f32[256,512]{1,0:T(8,128)S(1)} %get-tuple-element.34.base, ...), custom_call_target="tpu_custom_call" | custom-call | tf_op jit(solution)/shard_map/flux/pallas_call | solution.py:385
  26.3 1.6 %collective-permute-start.7 = (f32[16,128]{1,0:T(8,128)S(1)}, f32[16,128]{1,0:T(8,128)S(1)}, u32[]{:S(2)}, u32[]{:S(2)}) collective-permute-start(f32[16,128]{1,0:T(8,128)S(1)} %get-tuple-element.39), channel_id=1, source_target_pairs={{0,8},{8,0},{16,24},{24,16},{1,9},{9,1},{17,25},{25,17},{2,10},{10... | collective-permute-start | bytes 24584 | tf_op jit(solution)/shard_map/ppermute | solution.py:495
  27.9 0.2 collective-permute-start.8
  28.1 1.7 %collective-permute-start.9 = (f32[16,128]{1,0:T(8,128)S(1)}, f32[16,128]{1,0:T(8,128)S(1)}, u32[]{:S(2)}, u32[]{:S(2)}) collective-permute-start(f32[16,128]{1,0:T(8,128)S(1)} %get-tuple-element.39), channel_id=1, source_target_pairs={{0,16},{8,24},{16,0},{24,8},{1,17},{9,25},{17,1},{25,9},{2,18},{10... | collective-permute-start | bytes 24584 | tf_op jit(solution)/shard_map/ppermute | solution.py:495
  29.8 0.6 %collective-permute-start.11 = (f32[3,8,16,128]{3,2,1,0:T(8,128)S(1)}, f32[3,8,16,128]{3,2,1,0:T(8,128)S(1)}, u32[]{:S(2)}, u32[]{:S(2)}) collective-permute-start(f32[3,8,16,128]{3,2,1,0:T(8,128)S(1)} %get-tuple-element.41), channel_id=1, source_target_pairs={{0,1},{1,0},{2,3},{3,2},{4,5},{5,4},{6,7},{7,6},{8,9},{9,8},{10,11... | collective-permute-start | bytes 589832 | tf_op jit(solution)/shard_map/ppermute | solution.py:406
  30.4 2.9 %collective-permute-done.8 = f32[16,128]{1,0:T(8,128)S(1)} collective-permute-done((f32[16,128]{1,0:T(8,128)S(1)}, f32[16,128]{1,0:T(8,128)S(1)}, u32[]{:S(2)}, u32[]{:S(2)}) %collective-permute-start.8) | collective-permute-done | bytes 8224 | tf_op jit(solution)/shard_map/ppermute | solution.py:495
  33.4 0.8 %collective-permute-start.10 = (f32[16,128]{1,0:T(8,128)S(1)}, f32[16,128]{1,0:T(8,128)S(1)}, u32[]{:S(2)}, u32[]{:S(2)}) collective-permute-start(f32[16,128]{1,0:T(8,128)S(1)} %add_add_fusion), channel_id=1, source_target_pairs={{0,1},{1,0},{2,3},{3,2},{4,5},{5,4},{6,7},{7,6},{8,9},{9,8},{10,11... | collective-permute-start | bytes 24584 | tf_op jit(solution)/shard_map/ppermute | solution.py:406
  34.2 2.9 %collective-permute-done.10 = f32[16,128]{1,0:T(8,128)S(1)} collective-permute-done((f32[16,128]{1,0:T(8,128)S(1)}, f32[16,128]{1,0:T(8,128)S(1)}, u32[]{:S(2)}, u32[]{:S(2)}) %collective-permute-start.10) | collective-permute-done | bytes 8224 | tf_op jit(solution)/shard_map/ppermute | solution.py:406
  37.1 1.0 %finish.1 = (f32[3,8,16,128]{3,2,1,0:T(8,128)}, f32[3,8,16,128]{3,2,1,0:T(8,128)}, f32[3,16]{1,0:T(4,128)}, f32[3,16]{1,0:T(4,128)}) custom-call(f32[16,128]{1,0:T(8,128)S(1)} %add.15.sums, f32[6,8,16,128]{3,2,1,0:T(8,128)S(1)} %get-tuple-element.40.keep, f32[3,8,16,128]{3,2,1,0:T(8,128)S(1)} %collective-permute-done.11.come), custom_call_target="tpu_custom_call" | custom-call | tf_op jit(solution)/shard_map/finish/pallas_call | solution.py:385
  (14 shorter events, 0.1 us)
Async XLA Ops:
  0.6 1.0 %copy-start.2 = (f32[4,8,16,128]{3,2,1,0:T(8,128)S(1)}, f32[4,8,16,128]{3,2,1,0:T(8,128)}, u32[]{:S(2)}) copy-start(f32[4,8,16,128]{3,2,1,0:T(8,128)} %own.1) | copy-start | bytes 786436
  2.0 5.7 %collective-permute-start = (f32[20,16,128]{2,1,0:T(8,128)S(1)}, f32[20,16,128]{2,1,0:T(8,128)S(1)}, u32[]{:S(2)}, u32[]{:S(2)}) collective-permute-start(f32[20,16,128]{2,1,0:T(8,128)S(1)} %get-tuple-element.28.mine), channel_id=1, source_target_pairs={{0,2},{2,0},{4,6},{6,4},{1,3},{3,1},{5,7},{7,5},{8,10},{10,8},{12,... | collective-permute-start | bytes 491528 | tf_op jit(solution)/shard_map/ppermute | solution.py:409
  2.0 9.8 %collective-permute-start.2 = (f32[20,16,128]{2,1,0:T(8,128)S(1)}, f32[20,16,128]{2,1,0:T(8,128)S(1)}, u32[]{:S(2)}, u32[]{:S(2)}) collective-permute-start(f32[20,16,128]{2,1,0:T(8,128)S(1)} %get-tuple-element.25), channel_id=1, source_target_pairs={{0,1},{1,0},{2,3},{3,2},{4,5},{5,4},{6,7},{7,6},{8,9},{9,8},{10,11... | collective-permute-start | bytes 491528 | tf_op jit(solution)/shard_map/ppermute | solution.py:406
  3.6 5.7 %collective-permute-start.3 = (f32[4,16,128]{2,1,0:T(8,128)S(1)}, f32[4,16,128]{2,1,0:T(8,128)S(1)}, u32[]{:S(2)}, u32[]{:S(2)}) collective-permute-start(f32[4,16,128]{2,1,0:T(8,128)S(1)} %get-tuple-element.26), channel_id=1, source_target_pairs={{1,25},{0,8},{9,1},{8,16},{17,9},{16,24},{25,17},{24,0},{3,27},{2,... | collective-permute-start | bytes 98312 | tf_op jit(solution)/shard_map/ppermute | solution.py:430
  5.2 9.7 %copy-start = (bf16[256,3072]{1,0:T(8,128)(2,1)S(1)}, bf16[256,3072]{1,0:T(8,128)(2,1)}, u32[]{:S(2)}) copy-start(bf16[256,3072]{1,0:T(8,128)(2,1)} %constant.4.clone.planes.matrices) | copy-start | bytes 4718596
  5.2 6.6 %collective-permute-start.4 = (f32[4,16,128]{2,1,0:T(8,128)S(1)}, f32[4,16,128]{2,1,0:T(8,128)S(1)}, u32[]{:S(2)}, u32[]{:S(2)}) collective-permute-start(f32[4,16,128]{2,1,0:T(8,128)S(1)} %get-tuple-element.27), channel_id=1, source_target_pairs={{0,25},{1,8},{8,1},{9,16},{16,9},{17,24},{24,17},{25,0},{2,27},{3,... | collective-permute-start | bytes 98312 | tf_op jit(solution)/shard_map/ppermute | solution.py:429
  7.6 7.2 %collective-permute-start.1 = (f32[20,16,128]{2,1,0:T(8,128)S(1)}, f32[20,16,128]{2,1,0:T(8,128)S(1)}, u32[]{:S(2)}, u32[]{:S(2)}) collective-permute-start(f32[20,16,128]{2,1,0:T(8,128)S(1)} %collective-permute-done.a_mine), channel_id=1, source_target_pairs={{0,4},{6,2},{1,5},{7,3},{8,12},{14,10},{9,13},{15,11},{16,20},{22,... | collective-permute-start | bytes 491528 | tf_op jit(solution)/shard_map/ppermute | solution.py:414
  11.8 5.4 %copy-start.1 = (bf16[512,768]{1,0:T(8,128)(2,1)S(1)}, bf16[512,768]{1,0:T(8,128)(2,1)}, u32[]{:S(2)}) copy-start(bf16[512,768]{1,0:T(8,128)(2,1)} %constant.5.clone.spans) | copy-start | bytes 2359300
  11.8 4.1 %collective-permute-start.5 = (f32[28,16,128]{2,1,0:T(8,128)S(1)}, f32[28,16,128]{2,1,0:T(8,128)S(1)}, u32[]{:S(2)}, u32[]{:S(2)}) collective-permute-start(f32[28,16,128]{2,1,0:T(8,128)S(1)} %rest.1), channel_id=1, source_target_pairs={{0,2},{2,0},{4,6},{6,4},{1,3},{3,1},{5,7},{7,5},{8,10},{10,8},{12,... | collective-permute-start | bytes 688136 | tf_op jit(solution)/shard_map/ppermute | solution.py:409
  15.9 7.9 %collective-permute-start.6 = (f32[28,16,128]{2,1,0:T(8,128)S(1)}, f32[28,16,128]{2,1,0:T(8,128)S(1)}, u32[]{:S(2)}, u32[]{:S(2)}) collective-permute-start(f32[28,16,128]{2,1,0:T(8,128)S(1)} %collective-permute-done.5.a_rest), channel_id=1, source_target_pairs={{0,4},{6,2},{1,5},{7,3},{8,12},{14,10},{9,13},{15,11},{16,20},{22,... | collective-permute-start | bytes 688136 | tf_op jit(solution)/shard_map/ppermute | solution.py:414
  26.3 4.2 %collective-permute-start.7 = (f32[16,128]{1,0:T(8,128)S(1)}, f32[16,128]{1,0:T(8,128)S(1)}, u32[]{:S(2)}, u32[]{:S(2)}) collective-permute-start(f32[16,128]{1,0:T(8,128)S(1)} %get-tuple-element.39), channel_id=1, source_target_pairs={{0,8},{8,0},{16,24},{24,16},{1,9},{9,1},{17,25},{25,17},{2,10},{10... | collective-permute-start | bytes 24584 | tf_op jit(solution)/shard_map/ppermute | solution.py:495
  27.9 5.4 %collective-permute-start.8 = (f32[16,128]{1,0:T(8,128)S(1)}, f32[16,128]{1,0:T(8,128)S(1)}, u32[]{:S(2)}, u32[]{:S(2)}) collective-permute-start(f32[16,128]{1,0:T(8,128)S(1)} %get-tuple-element.39), channel_id=1, source_target_pairs={{0,24},{8,16},{16,8},{24,0},{1,25},{9,17},{17,9},{25,1},{2,26},{10... | collective-permute-start | bytes 24584 | tf_op jit(solution)/shard_map/ppermute | solution.py:495
  28.1 5.3 %collective-permute-start.9 = (f32[16,128]{1,0:T(8,128)S(1)}, f32[16,128]{1,0:T(8,128)S(1)}, u32[]{:S(2)}, u32[]{:S(2)}) collective-permute-start(f32[16,128]{1,0:T(8,128)S(1)} %get-tuple-element.39), channel_id=1, source_target_pairs={{0,16},{8,24},{16,0},{24,8},{1,17},{9,25},{17,1},{25,9},{2,18},{10... | collective-permute-start | bytes 24584 | tf_op jit(solution)/shard_map/ppermute | solution.py:495
  29.8 7.3 %collective-permute-start.11 = (f32[3,8,16,128]{3,2,1,0:T(8,128)S(1)}, f32[3,8,16,128]{3,2,1,0:T(8,128)S(1)}, u32[]{:S(2)}, u32[]{:S(2)}) collective-permute-start(f32[3,8,16,128]{3,2,1,0:T(8,128)S(1)} %get-tuple-element.41), channel_id=1, source_target_pairs={{0,1},{1,0},{2,3},{3,2},{4,5},{5,4},{6,7},{7,6},{8,9},{9,8},{10,11... | collective-permute-start | bytes 589832 | tf_op jit(solution)/shard_map/ppermute | solution.py:406
  33.4 3.7 %collective-permute-start.10 = (f32[16,128]{1,0:T(8,128)S(1)}, f32[16,128]{1,0:T(8,128)S(1)}, u32[]{:S(2)}, u32[]{:S(2)}) collective-permute-start(f32[16,128]{1,0:T(8,128)S(1)} %add_add_fusion), channel_id=1, source_target_pairs={{0,1},{1,0},{2,3},{3,2},{4,5},{5,4},{6,7},{7,6},{8,9},{9,8},{10,11... | collective-permute-start | bytes 24584 | tf_op jit(solution)/shard_map/ppermute | solution.py:406

commit v25 on v21

--- a/solution.py
+++ b/solution.py
@@ -428,7 +428,8 @@
     part = swap(to_partner)
     part_strip = lax.ppermute(first, ("span", "stream"), to_other)
     own_strip = lax.ppermute(second, ("span", "stream"), to_same)
-    mine_now, b_mine, a_mine = lax.optimization_barrier((mine, pair_b(mine), pair_a(mine)))
+    own_strip, part_strip, a_mine = lax.optimization_barrier((own_strip, part_strip, pair_a(mine)))
+    mine_now, b_mine = lax.optimization_barrier((mine, pair_b(mine)))
     (rest,) = call(
         rest_kernel,
         "rest",

time: 32.9 us -> 33 us (level)
    ppermute x1, waiting for transfers between devices: 1.63 us -> 2.24 us  [shards(): part_strip = lax.ppermute(first, ('span', 'stream'), to_other)]
    ppermute x2, starting transfers between devices: 5.02 us -> 4.41 us  [pair_b(): lax.ppermute(value, 'wall', [(w, min(max((w + 1 ^ 1) - 1, 0), walls - 1))...]
    ppermute x3, starting transfers between devices: 2.84 us -> 3.27 us  [swap(): return lax.ppermute(value, 'stream', [(0, 1), (1, 0)])]
    ppermute x3, waiting for transfers between devices: 3.21 us -> 2.79 us  [swap(): return lax.ppermute(value, 'stream', [(0, 1), (1, 0)])]
where the time goes in v25:
time: 33 us; the launch traced here: 32.8 us
  starting transfers between devices  15.4 us (47%)
  waiting for transfers between devices  8.98 us (27%)
  Pallas kernels  6.72 us (20%)
  local copies, waits for them, and re-layouts  0.95 us (3%)
  between operations  0.76 us (2%)
    pallas_call x6, Pallas kernels, call(): pl.pallas_call(kernel, out_shape=tuple((jax.ShapeDtypeStruct(shape, jnp.f...  6.72 us
    ppermute x2, starting transfers between devices, pair_b(): lax.ppermute(value, 'wall', [(w, min(max((w + 1 ^ 1) - 1, 0), walls - 1))...  4.41 us
    ppermute x3, starting transfers between devices, from_span(): return lax.ppermute(value, 'span', [(p, p ^ step) for p in range(spans)])  3.55 us
    ppermute x3, starting transfers between devices, swap(): return lax.ppermute(value, 'stream', [(0, 1), (1, 0)])  3.27 us
    ppermute x3, waiting for transfers between devices, swap(): return lax.ppermute(value, 'stream', [(0, 1), (1, 0)])  2.79 us
    ppermute x1, starting transfers between devices, shards(): part_strip = lax.ppermute(first, ('span', 'stream'), to_other)  2.45 us
    ppermute x1, waiting for transfers between devices, shards(): part_strip = lax.ppermute(first, ('span', 'stream'), to_other)  2.24 us
    ppermute x3, waiting for transfers between devices, from_span(): return lax.ppermute(value, 'span', [(p, p ^ step) for p in range(spans)])  1.97 us
  transfers between devices with their start and end apart: 12, of which 5 were waited for; matrix products, arithmetic and copies ran while one was open for 0% of the time, Pallas kernels for 9%

profile of v25, /device:TPU:4, one launch (start us, length us, event | category | flops | bytes accessed | tf_op | source)
XLA Modules:
  0.0 32.8 jit_solution(5432870274695514671)
XLA Ops:
  0.6 0.9 %copy-done.2 = f32[4,8,16,128]{3,2,1,0:T(8,128)S(1)} copy-done((f32[4,8,16,128]{3,2,1,0:T(8,128)S(1)}, f32[4,8,16,128]{3,2,1,0:T(8,128)}, u32[]{:S(2)}) %copy-start.2) | copy-done | bytes 262168
  1.6 0.4 %pack.1 = (f32[20,16,128]{2,1,0:T(8,128)S(1)}, f32[20,16,128]{2,1,0:T(8,128)S(1)}, f32[4,16,128]{2,1,0:T(8,128)S(1)}, f32[4,16,128]{2,1,0:T(8,128)S(1)}) custom-call(f32[4,8,16,128]{3,2,1,0:T(8,128)S(1)} %copy-done.2), custom_call_target="tpu_custom_call" | custom-call | tf_op jit(solution)/shard_map/pack/pallas_call | solution.py:385
  2.0 0.1 collective-permute-start.4
  2.0 1.6 %collective-permute-start.1 = (f32[20,16,128]{2,1,0:T(8,128)S(1)}, f32[20,16,128]{2,1,0:T(8,128)S(1)}, u32[]{:S(2)}, u32[]{:S(2)}) collective-permute-start(f32[20,16,128]{2,1,0:T(8,128)S(1)} %get-tuple-element.26), channel_id=1, source_target_pairs={{0,1},{1,0},{2,3},{3,2},{4,5},{5,4},{6,7},{7,6},{8,9},{9,8},{10,11... | collective-permute-start | bytes 491528 | tf_op jit(solution)/shard_map/ppermute | solution.py:406
  3.6 1.6 %collective-permute-start.2 = (f32[4,16,128]{2,1,0:T(8,128)S(1)}, f32[4,16,128]{2,1,0:T(8,128)S(1)}, u32[]{:S(2)}, u32[]{:S(2)}) collective-permute-start(f32[4,16,128]{2,1,0:T(8,128)S(1)} %get-tuple-element.27), channel_id=1, source_target_pairs={{1,25},{0,8},{9,1},{8,16},{17,9},{16,24},{25,17},{24,0},{3,27},{2,... | collective-permute-start | bytes 98312 | tf_op jit(solution)/shard_map/ppermute | solution.py:430
  5.2 2.4 %collective-permute-start.3 = (f32[4,16,128]{2,1,0:T(8,128)S(1)}, f32[4,16,128]{2,1,0:T(8,128)S(1)}, u32[]{:S(2)}, u32[]{:S(2)}) collective-permute-start(f32[4,16,128]{2,1,0:T(8,128)S(1)} %get-tuple-element.28), channel_id=1, source_target_pairs={{0,25},{1,8},{8,1},{9,16},{16,9},{17,24},{24,17},{25,0},{2,27},{3,... | collective-permute-start | bytes 98312 | tf_op jit(solution)/shard_map/ppermute | solution.py:429
  7.6 1.9 %collective-permute-start = (f32[20,16,128]{2,1,0:T(8,128)S(1)}, f32[20,16,128]{2,1,0:T(8,128)S(1)}, u32[]{:S(2)}, u32[]{:S(2)}) collective-permute-start(f32[20,16,128]{2,1,0:T(8,128)S(1)} %get-tuple-element.32.mine), channel_id=1, source_target_pairs={{0,0},{2,4},{4,2},{6,6},{1,1},{3,5},{5,3},{7,7},{8,8},{10,12},{12,... | collective-permute-start | bytes 491528 | tf_op jit(solution)/shard_map/ppermute | solution.py:412
  9.5 2.2 %collective-permute-done.3.part_strip = f32[4,16,128]{2,1,0:T(8,128)S(1)} collective-permute-done((f32[4,16,128]{2,1,0:T(8,128)S(1)}, f32[4,16,128]{2,1,0:T(8,128)S(1)}, u32[]{:S(2)}, u32[]{:S(2)}) %collective-permute-start.3) | collective-permute-done | bytes 32800 | tf_op jit(solution)/shard_map/ppermute | solution.py:429
  11.8 0.0 copy-start.1
  11.8 0.1 collective-permute-start.6
  11.9 2.5 %collective-permute-start.5 = (f32[28,16,128]{2,1,0:T(8,128)S(1)}, f32[28,16,128]{2,1,0:T(8,128)S(1)}, u32[]{:S(2)}, u32[]{:S(2)}) collective-permute-start(f32[28,16,128]{2,1,0:T(8,128)S(1)} %rest.1), channel_id=1, source_target_pairs={{0,0},{2,4},{4,2},{6,6},{1,1},{3,5},{5,3},{7,7},{8,8},{10,12},{12,... | collective-permute-start | bytes 688136 | tf_op jit(solution)/shard_map/ppermute | solution.py:412
  14.4 1.1 %centre.1 = (f32[256,512]{1,0:T(8,128)S(1)}, f32[256,512]{1,0:T(8,128)S(1)}, f32[256,384]{1,0:T(8,128)S(1)}) custom-call(f32[20,16,128]{2,1,0:T(8,128)S(1)} %get-tuple-element.32.mine, f32[28,16,128]{2,1,0:T(8,128)S(1)} %rest.1, bf16[256,3072]{1,0:T(8,128)(2,1)S(1)} %copy-done), custom_call_target="tpu_custom_call" | custom-call | flops 2147483648 | tf_op jit(solution)/shard_map/centre/pallas_call | solution.py:385
  15.6 1.8 %mate.1 = (f32[256,512]{1,0:T(8,128)S(1)}, f32[4,8,16,128]{3,2,1,0:T(8,128)S(1)}, f32[4,8,8,128]{3,2,1,0:T(8,128)S(1)}, f32[256,896]{1,0:T(8,128)S(1)}, f32[256,384]{1,0:T(8,128)S(1)}) custom-call(f32[20,16,128]{2,1,0:T(8,128)S(1)} %collective-permute-done.4.a_mine, f32[28,16,128]{2,1,0:T(8,128)S(1)} %collective-permute-done.6.a_rest, ...), custom_call_target="tpu_custom_call" | custom-call | flops 536870912 | tf_op jit(solution)/shard_map/mate/pallas_call | solution.py:385
  17.4 2.0 %collective-permute-done.5.b_rest = f32[28,16,128]{2,1,0:T(8,128)S(1)} collective-permute-done((f32[28,16,128]{2,1,0:T(8,128)S(1)}, f32[28,16,128]{2,1,0:T(8,128)S(1)}, u32[]{:S(2)}, u32[]{:S(2)}) %collective-permute-start.5) | collective-permute-done | bytes 229408 | tf_op jit(solution)/shard_map/ppermute | solution.py:412
  19.4 2.4 %flux.1 = (f32[6,8,16,128]{3,2,1,0:T(8,128)S(1)}, f32[3,8,16,128]{3,2,1,0:T(8,128)S(1)}, f32[16,128]{1,0:T(8,128)S(1)}) custom-call(f32[20,16,128]{2,1,0:T(8,128)S(1)} %collective-permute-done.b_mine, f32[28,16,128]{2,1,0:T(8,128)S(1)} %collective-permute-done.5.b_rest, f32[256,512]{1,0:T(8,128)S(1)} %get-tuple-element.36.base, ...), custom_call_target="tpu_custom_call" | custom-call | tf_op jit(solution)/shard_map/flux/pallas_call | solution.py:385
  21.8 0.9 %collective-permute-start.9 = (f32[16,128]{1,0:T(8,128)S(1)}, f32[16,128]{1,0:T(8,128)S(1)}, u32[]{:S(2)}, u32[]{:S(2)}) collective-permute-start(f32[16,128]{1,0:T(8,128)S(1)} %get-tuple-element.41), channel_id=1, source_target_pairs={{0,16},{8,24},{16,0},{24,8},{1,17},{9,25},{17,1},{25,9},{2,18},{10... | collective-permute-start | bytes 24584 | tf_op jit(solution)/shard_map/ppermute | solution.py:493
  22.6 1.3 %collective-permute-start.8 = (f32[16,128]{1,0:T(8,128)S(1)}, f32[16,128]{1,0:T(8,128)S(1)}, u32[]{:S(2)}, u32[]{:S(2)}) collective-permute-start(f32[16,128]{1,0:T(8,128)S(1)} %get-tuple-element.41), channel_id=1, source_target_pairs={{0,24},{8,16},{16,8},{24,0},{1,25},{9,17},{17,9},{25,1},{2,26},{10... | collective-permute-start | bytes 24584 | tf_op jit(solution)/shard_map/ppermute | solution.py:493
  24.0 1.3 %collective-permute-start.7 = (f32[16,128]{1,0:T(8,128)S(1)}, f32[16,128]{1,0:T(8,128)S(1)}, u32[]{:S(2)}, u32[]{:S(2)}) collective-permute-start(f32[16,128]{1,0:T(8,128)S(1)} %get-tuple-element.41), channel_id=1, source_target_pairs={{0,8},{8,0},{16,24},{24,16},{1,9},{9,1},{17,25},{25,17},{2,10},{10... | collective-permute-start | bytes 24584 | tf_op jit(solution)/shard_map/ppermute | solution.py:493
  25.3 0.8 %collective-permute-start.11 = (f32[3,8,16,128]{3,2,1,0:T(8,128)S(1)}, f32[3,8,16,128]{3,2,1,0:T(8,128)S(1)}, u32[]{:S(2)}, u32[]{:S(2)}) collective-permute-start(f32[3,8,16,128]{3,2,1,0:T(8,128)S(1)} %get-tuple-element.43), channel_id=1, source_target_pairs={{0,1},{1,0},{2,3},{3,2},{4,5},{5,4},{6,7},{7,6},{8,9},{9,8},{10,11... | collective-permute-start | bytes 589832 | tf_op jit(solution)/shard_map/ppermute | solution.py:406
  26.1 0.3 collective-permute-done.9
  26.4 1.7 %collective-permute-done.8 = f32[16,128]{1,0:T(8,128)S(1)} collective-permute-done((f32[16,128]{1,0:T(8,128)S(1)}, f32[16,128]{1,0:T(8,128)S(1)}, u32[]{:S(2)}, u32[]{:S(2)}) %collective-permute-start.8) | collective-permute-done | bytes 8224 | tf_op jit(solution)/shard_map/ppermute | solution.py:493
  28.1 0.9 %collective-permute-start.10 = (f32[16,128]{1,0:T(8,128)S(1)}, f32[16,128]{1,0:T(8,128)S(1)}, u32[]{:S(2)}, u32[]{:S(2)}) collective-permute-start(f32[16,128]{1,0:T(8,128)S(1)} %add_add_fusion), channel_id=1, source_target_pairs={{0,1},{1,0},{2,3},{3,2},{4,5},{5,4},{6,7},{7,6},{8,9},{9,8},{10,11... | collective-permute-start | bytes 24584 | tf_op jit(solution)/shard_map/ppermute | solution.py:406
  29.0 2.8 %collective-permute-done.10 = f32[16,128]{1,0:T(8,128)S(1)} collective-permute-done((f32[16,128]{1,0:T(8,128)S(1)}, f32[16,128]{1,0:T(8,128)S(1)}, u32[]{:S(2)}, u32[]{:S(2)}) %collective-permute-start.10) | collective-permute-done | bytes 8224 | tf_op jit(solution)/shard_map/ppermute | solution.py:406
  31.8 1.0 %finish.1 = (f32[3,8,16,128]{3,2,1,0:T(8,128)}, f32[3,8,16,128]{3,2,1,0:T(8,128)}, f32[3,16]{1,0:T(4,128)}, f32[3,16]{1,0:T(4,128)}) custom-call(f32[16,128]{1,0:T(8,128)S(1)} %add.15.sums, f32[6,8,16,128]{3,2,1,0:T(8,128)S(1)} %get-tuple-element.42.keep, f32[3,8,16,128]{3,2,1,0:T(8,128)S(1)} %collective-permute-done.11.come), custom_call_target="tpu_custom_call" | custom-call | tf_op jit(solution)/shard_map/finish/pallas_call | solution.py:385
  (14 shorter events, 0.1 us)
Async XLA Ops:
  0.6 1.0 %copy-start.2 = (f32[4,8,16,128]{3,2,1,0:T(8,128)S(1)}, f32[4,8,16,128]{3,2,1,0:T(8,128)}, u32[]{:S(2)}) copy-start(f32[4,8,16,128]{3,2,1,0:T(8,128)} %own.1) | copy-start | bytes 786436
  2.0 9.8 %collective-permute-start.4 = (f32[20,16,128]{2,1,0:T(8,128)S(1)}, f32[20,16,128]{2,1,0:T(8,128)S(1)}, u32[]{:S(2)}, u32[]{:S(2)}) collective-permute-start(f32[20,16,128]{2,1,0:T(8,128)S(1)} %get-tuple-element.32.mine), channel_id=1, source_target_pairs={{0,2},{2,0},{4,6},{6,4},{1,3},{3,1},{5,7},{7,5},{8,10},{10,8},{12,... | collective-permute-start | bytes 491528 | tf_op jit(solution)/shard_map/ppermute | solution.py:409
  2.0 9.8 %collective-permute-start.1 = (f32[20,16,128]{2,1,0:T(8,128)S(1)}, f32[20,16,128]{2,1,0:T(8,128)S(1)}, u32[]{:S(2)}, u32[]{:S(2)}) collective-permute-start(f32[20,16,128]{2,1,0:T(8,128)S(1)} %get-tuple-element.26), channel_id=1, source_target_pairs={{0,1},{1,0},{2,3},{3,2},{4,5},{5,4},{6,7},{7,6},{8,9},{9,8},{10,11... | collective-permute-start | bytes 491528 | tf_op jit(solution)/shard_map/ppermute | solution.py:406
  3.6 5.9 %collective-permute-start.2 = (f32[4,16,128]{2,1,0:T(8,128)S(1)}, f32[4,16,128]{2,1,0:T(8,128)S(1)}, u32[]{:S(2)}, u32[]{:S(2)}) collective-permute-start(f32[4,16,128]{2,1,0:T(8,128)S(1)} %get-tuple-element.27), channel_id=1, source_target_pairs={{1,25},{0,8},{9,1},{8,16},{17,9},{16,24},{25,17},{24,0},{3,27},{2,... | collective-permute-start | bytes 98312 | tf_op jit(solution)/shard_map/ppermute | solution.py:430
  5.2 9.3 %copy-start = (bf16[256,3072]{1,0:T(8,128)(2,1)S(1)}, bf16[256,3072]{1,0:T(8,128)(2,1)}, u32[]{:S(2)}) copy-start(bf16[256,3072]{1,0:T(8,128)(2,1)} %constant.4.clone.planes.matrices) | copy-start | bytes 4718596
  5.2 6.6 %collective-permute-start.3 = (f32[4,16,128]{2,1,0:T(8,128)S(1)}, f32[4,16,128]{2,1,0:T(8,128)S(1)}, u32[]{:S(2)}, u32[]{:S(2)}) collective-permute-start(f32[4,16,128]{2,1,0:T(8,128)S(1)} %get-tuple-element.28), channel_id=1, source_target_pairs={{0,25},{1,8},{8,1},{9,16},{16,9},{17,24},{24,17},{25,0},{2,27},{3,... | collective-permute-start | bytes 98312 | tf_op jit(solution)/shard_map/ppermute | solution.py:429
  7.6 6.8 %collective-permute-start = (f32[20,16,128]{2,1,0:T(8,128)S(1)}, f32[20,16,128]{2,1,0:T(8,128)S(1)}, u32[]{:S(2)}, u32[]{:S(2)}) collective-permute-start(f32[20,16,128]{2,1,0:T(8,128)S(1)} %get-tuple-element.32.mine), channel_id=1, source_target_pairs={{0,0},{2,4},{4,2},{6,6},{1,1},{3,5},{5,3},{7,7},{8,8},{10,12},{12,... | collective-permute-start | bytes 491528 | tf_op jit(solution)/shard_map/ppermute | solution.py:412
  11.8 3.7 %copy-start.1 = (bf16[512,768]{1,0:T(8,128)(2,1)S(1)}, bf16[512,768]{1,0:T(8,128)(2,1)}, u32[]{:S(2)}) copy-start(bf16[512,768]{1,0:T(8,128)(2,1)} %constant.5.clone.spans) | copy-start | bytes 2359300
  11.8 3.7 %collective-permute-start.6 = (f32[28,16,128]{2,1,0:T(8,128)S(1)}, f32[28,16,128]{2,1,0:T(8,128)S(1)}, u32[]{:S(2)}, u32[]{:S(2)}) collective-permute-start(f32[28,16,128]{2,1,0:T(8,128)S(1)} %rest.1), channel_id=1, source_target_pairs={{0,2},{2,0},{4,6},{6,4},{1,3},{3,1},{5,7},{7,5},{8,10},{10,8},{12,... | collective-permute-start | bytes 688136 | tf_op jit(solution)/shard_map/ppermute | solution.py:409
  11.9 7.5 %collective-permute-start.5 = (f32[28,16,128]{2,1,0:T(8,128)S(1)}, f32[28,16,128]{2,1,0:T(8,128)S(1)}, u32[]{:S(2)}, u32[]{:S(2)}) collective-permute-start(f32[28,16,128]{2,1,0:T(8,128)S(1)} %rest.1), channel_id=1, source_target_pairs={{0,0},{2,4},{4,2},{6,6},{1,1},{3,5},{5,3},{7,7},{8,8},{10,12},{12,... | collective-permute-start | bytes 688136 | tf_op jit(solution)/shard_map/ppermute | solution.py:412
  21.8 4.6 %collective-permute-start.9 = (f32[16,128]{1,0:T(8,128)S(1)}, f32[16,128]{1,0:T(8,128)S(1)}, u32[]{:S(2)}, u32[]{:S(2)}) collective-permute-start(f32[16,128]{1,0:T(8,128)S(1)} %get-tuple-element.41), channel_id=1, source_target_pairs={{0,16},{8,24},{16,0},{24,8},{1,17},{9,25},{17,1},{25,9},{2,18},{10... | collective-permute-start | bytes 24584 | tf_op jit(solution)/shard_map/ppermute | solution.py:493
  22.6 5.4 %collective-permute-start.8 = (f32[16,128]{1,0:T(8,128)S(1)}, f32[16,128]{1,0:T(8,128)S(1)}, u32[]{:S(2)}, u32[]{:S(2)}) collective-permute-start(f32[16,128]{1,0:T(8,128)S(1)} %get-tuple-element.41), channel_id=1, source_target_pairs={{0,24},{8,16},{16,8},{24,0},{1,25},{9,17},{17,9},{25,1},{2,26},{10... | collective-permute-start | bytes 24584 | tf_op jit(solution)/shard_map/ppermute | solution.py:493
  24.0 4.1 %collective-permute-start.7 = (f32[16,128]{1,0:T(8,128)S(1)}, f32[16,128]{1,0:T(8,128)S(1)}, u32[]{:S(2)}, u32[]{:S(2)}) collective-permute-start(f32[16,128]{1,0:T(8,128)S(1)} %get-tuple-element.41), channel_id=1, source_target_pairs={{0,8},{8,0},{16,24},{24,16},{1,9},{9,1},{17,25},{25,17},{2,10},{10... | collective-permute-start | bytes 24584 | tf_op jit(solution)/shard_map/ppermute | solution.py:493
  25.3 6.5 %collective-permute-start.11 = (f32[3,8,16,128]{3,2,1,0:T(8,128)S(1)}, f32[3,8,16,128]{3,2,1,0:T(8,128)S(1)}, u32[]{:S(2)}, u32[]{:S(2)}) collective-permute-start(f32[3,8,16,128]{3,2,1,0:T(8,128)S(1)} %get-tuple-element.43), channel_id=1, source_target_pairs={{0,1},{1,0},{2,3},{3,2},{4,5},{5,4},{6,7},{7,6},{8,9},{9,8},{10,11... | collective-permute-start | bytes 589832 | tf_op jit(solution)/shard_map/ppermute | solution.py:406
  28.1 3.7 %collective-permute-start.10 = (f32[16,128]{1,0:T(8,128)S(1)}, f32[16,128]{1,0:T(8,128)S(1)}, u32[]{:S(2)}, u32[]{:S(2)}) collective-permute-start(f32[16,128]{1,0:T(8,128)S(1)} %add_add_fusion), channel_id=1, source_target_pairs={{0,1},{1,0},{2,3},{3,2},{4,5},{5,4},{6,7},{7,6},{8,9},{9,8},{10,11... | collective-permute-start | bytes 24584 | tf_op jit(solution)/shard_map/ppermute | solution.py:406

commit v26 on v21

--- a/solution.py
+++ b/solution.py
@@ -127,11 +127,10 @@
     to_same[...] = pack_strip(own, 7 * (1 - me_s))
 
 
-def rest_kernel(part, own_strip, part_strip, rest):
-    count, half = part.shape[0], own_strip.shape[0]
+def rest_kernel(part, strips, rest):
+    count = part.shape[0]
     rest[:count] = part[...]
-    rest[count : count + half] = own_strip[...]
-    rest[count + half :] = part_strip[...]
+    rest[count:] = strips[...]
 
 
 def unpack(mine, rest, me_s):
@@ -416,9 +415,8 @@
     def place(p, s):
         return (p % spans) * streams + s
 
-    to_other, to_same = [], []
+    to_same = []
     for p in range(spans):
-        to_other += [(place(p, 0), place(p - 1, 1)), (place(p, 1), place(p + 1, 0))]
         to_same += [(place(p, 1), place(p - 1, 1)), (place(p, 0), place(p + 1, 0))]
 
     message, strip = (2 * layers + layers // 2, rows, width), (layers // 2, rows, width)
@@ -426,13 +424,12 @@
         pack_kernel, "pack", (fields,), (message, message, strip, strip)
     )
     part = swap(to_partner)
-    part_strip = lax.ppermute(first, ("span", "stream"), to_other)
-    own_strip = lax.ppermute(second, ("span", "stream"), to_same)
+    strips = lax.ppermute(jnp.concatenate([second, swap(first)]), ("span", "stream"), to_same)
     mine_now, b_mine, a_mine = lax.optimization_barrier((mine, pair_b(mine), pair_a(mine)))
     (rest,) = call(
         rest_kernel,
         "rest",
-        (part, own_strip, part_strip),
+        (part, strips),
         ((message[0] + layers, rows, width),),
         hint=2**35,
     )

time: 32.9 us -> 34.6 us (1.052)
  the two profiles are of different devices: /device:TPU:4 before, /device:TPU:6 now
where the time goes in v26:
time: 34.6 us; the launch traced here: 34.4 us
  starting transfers between devices  15.7 us (45%)
  waiting for transfers between devices  10.3 us (30%)
  Pallas kernels  6.74 us (19%)
  local copies, waits for them, and re-layouts  0.95 us (3%)
  between operations  0.76 us (2%)
    pallas_call x6, Pallas kernels, call(): pl.pallas_call(kernel, out_shape=tuple((jax.ShapeDtypeStruct(shape, jnp.f...  6.74 us
    ppermute x4, waiting for transfers between devices, swap(): return lax.ppermute(value, 'stream', [(0, 1), (1, 0)])  5.9 us
    ppermute x2, starting transfers between devices, pair_b(): lax.ppermute(value, 'wall', [(w, min(max((w + 1 ^ 1) - 1, 0), walls - 1))...  5.81 us
    ppermute x3, starting transfers between devices, from_span(): return lax.ppermute(value, 'span', [(p, p ^ step) for p in range(spans)])  4.14 us
    ppermute x1, starting transfers between devices, shards(): lax.ppermute(jnp.concatenate([second, swap(first)]), ('span', 'stream'),...  3.6 us
    ppermute x3, waiting for transfers between devices, from_span(): return lax.ppermute(value, 'span', [(p, p ^ step) for p in range(spans)])  3.16 us
    ppermute x4, starting transfers between devices, swap(): return lax.ppermute(value, 'stream', [(0, 1), (1, 0)])  2.1 us
    ppermute x2, waiting for transfers between devices, pair_b(): lax.ppermute(value, 'wall', [(w, min(max((w + 1 ^ 1) - 1, 0), walls - 1))...  1.19 us
  transfers between devices with their start and end apart: 12, of which 7 were waited for; matrix products, arithmetic and copies ran while one was open for 0% of the time, Pallas kernels for 9%

profile of v26, /device:TPU:6, one launch (start us, length us, event | category | flops | bytes accessed | tf_op | source)
XLA Modules:
  0.0 34.4 jit_solution(14043110015417439468)
XLA Ops:
  0.6 0.9 %copy-done.2 = f32[4,8,16,128]{3,2,1,0:T(8,128)S(1)} copy-done((f32[4,8,16,128]{3,2,1,0:T(8,128)S(1)}, f32[4,8,16,128]{3,2,1,0:T(8,128)}, u32[]{:S(2)}) %copy-start.2) | copy-done | bytes 262168
  1.6 0.4 %pack.1 = (f32[20,16,128]{2,1,0:T(8,128)S(1)}, f32[20,16,128]{2,1,0:T(8,128)S(1)}, f32[4,16,128]{2,1,0:T(8,128)S(1)}, f32[4,16,128]{2,1,0:T(8,128)S(1)}) custom-call(f32[4,8,16,128]{3,2,1,0:T(8,128)S(1)} %copy-done.2), custom_call_target="tpu_custom_call" | custom-call | tf_op jit(solution)/shard_map/pack/pallas_call | solution.py:384
  2.0 0.6 %collective-permute-start.3 = (f32[4,16,128]{2,1,0:T(8,128)S(1)}, f32[4,16,128]{2,1,0:T(8,128)S(1)}, u32[]{:S(2)}, u32[]{:S(2)}) collective-permute-start(f32[4,16,128]{2,1,0:T(8,128)S(1)} %get-tuple-element.26), channel_id=1, source_target_pairs={{0,1},{1,0},{2,3},{3,2},{4,5},{5,4},{6,7},{7,6},{8,9},{9,8},{10,11... | collective-permute-start | bytes 98312 | tf_op jit(solution)/shard_map/ppermute | solution.py:405
  2.6 1.5 %collective-permute-start.2 = (f32[20,16,128]{2,1,0:T(8,128)S(1)}, f32[20,16,128]{2,1,0:T(8,128)S(1)}, u32[]{:S(2)}, u32[]{:S(2)}) collective-permute-start(f32[20,16,128]{2,1,0:T(8,128)S(1)} %get-tuple-element.24), channel_id=1, source_target_pairs={{0,1},{1,0},{2,3},{3,2},{4,5},{5,4},{6,7},{7,6},{8,9},{9,8},{10,11... | collective-permute-start | bytes 491528 | tf_op jit(solution)/shard_map/ppermute | solution.py:405
  4.0 2.2 %collective-permute-done.3 = f32[4,16,128]{2,1,0:T(8,128)S(1)} collective-permute-done((f32[4,16,128]{2,1,0:T(8,128)S(1)}, f32[4,16,128]{2,1,0:T(8,128)S(1)}, u32[]{:S(2)}, u32[]{:S(2)}) %collective-permute-start.3) | collective-permute-done | bytes 32800 | tf_op jit(solution)/shard_map/ppermute | solution.py:405
  6.3 3.6 %collective-permute-start.4 = (f32[8,16,128]{2,1,0:T(8,128)S(1)}, f32[8,16,128]{2,1,0:T(8,128)S(1)}, u32[]{:S(2)}, u32[]{:S(2)}) collective-permute-start(f32[8,16,128]{2,1,0:T(8,128)S(1)} %pad_maximum_fusion), channel_id=1, source_target_pairs={{1,25},{0,8},{9,1},{8,16},{17,9},{16,24},{25,17},{24,0},{3,27},{2,... | collective-permute-start | bytes 196616 | tf_op jit(solution)/shard_map/ppermute | solution.py:427
  9.9 2.5 %collective-permute-start = (f32[20,16,128]{2,1,0:T(8,128)S(1)}, f32[20,16,128]{2,1,0:T(8,128)S(1)}, u32[]{:S(2)}, u32[]{:S(2)}) collective-permute-start(f32[20,16,128]{2,1,0:T(8,128)S(1)} %get-tuple-element.28.mine), channel_id=1, source_target_pairs={{0,0},{2,4},{4,2},{6,6},{1,1},{3,5},{5,3},{7,7},{8,8},{10,12},{12,... | collective-permute-start | bytes 491528 | tf_op jit(solution)/shard_map/ppermute | solution.py:411
  12.4 0.0 collective-permute-done.4.strips
  12.5 0.0 copy-start.1
  12.5 0.1 collective-permute-start.6
  12.6 3.3 %collective-permute-start.5 = (f32[28,16,128]{2,1,0:T(8,128)S(1)}, f32[28,16,128]{2,1,0:T(8,128)S(1)}, u32[]{:S(2)}, u32[]{:S(2)}) collective-permute-start(f32[28,16,128]{2,1,0:T(8,128)S(1)} %rest.1), channel_id=1, source_target_pairs={{0,0},{2,4},{4,2},{6,6},{1,1},{3,5},{5,3},{7,7},{8,8},{10,12},{12,... | collective-permute-start | bytes 688136 | tf_op jit(solution)/shard_map/ppermute | solution.py:411
  15.9 0.8 %collective-permute-done.b_mine = f32[20,16,128]{2,1,0:T(8,128)S(1)} collective-permute-done((f32[20,16,128]{2,1,0:T(8,128)S(1)}, f32[20,16,128]{2,1,0:T(8,128)S(1)}, u32[]{:S(2)}, u32[]{:S(2)}) %collective-permute-start) | collective-permute-done | bytes 163872 | tf_op jit(solution)/shard_map/ppermute | solution.py:411
  16.7 1.1 %centre.1 = (f32[256,512]{1,0:T(8,128)S(1)}, f32[256,512]{1,0:T(8,128)S(1)}, f32[256,384]{1,0:T(8,128)S(1)}) custom-call(f32[20,16,128]{2,1,0:T(8,128)S(1)} %get-tuple-element.28.mine, f32[28,16,128]{2,1,0:T(8,128)S(1)} %rest.1, bf16[256,3072]{1,0:T(8,128)(2,1)S(1)} %copy-done), custom_call_target="tpu_custom_call" | custom-call | flops 2147483648 | tf_op jit(solution)/shard_map/centre/pallas_call | solution.py:384
  17.8 1.8 %mate.1 = (f32[256,512]{1,0:T(8,128)S(1)}, f32[4,8,16,128]{3,2,1,0:T(8,128)S(1)}, f32[4,8,8,128]{3,2,1,0:T(8,128)S(1)}, f32[256,896]{1,0:T(8,128)S(1)}, f32[256,384]{1,0:T(8,128)S(1)}) custom-call(f32[20,16,128]{2,1,0:T(8,128)S(1)} %collective-permute-done.1.a_mine, f32[28,16,128]{2,1,0:T(8,128)S(1)} %collective-permute-done.6.a_rest, ...), custom_call_target="tpu_custom_call" | custom-call | flops 536870912 | tf_op jit(solution)/shard_map/mate/pallas_call | solution.py:384
  19.6 0.4 %collective-permute-done.5.b_rest = f32[28,16,128]{2,1,0:T(8,128)S(1)} collective-permute-done((f32[28,16,128]{2,1,0:T(8,128)S(1)}, f32[28,16,128]{2,1,0:T(8,128)S(1)}, u32[]{:S(2)}, u32[]{:S(2)}) %collective-permute-start.5) | collective-permute-done | bytes 229408 | tf_op jit(solution)/shard_map/ppermute | solution.py:411
  20.0 2.4 %flux.1 = (f32[6,8,16,128]{3,2,1,0:T(8,128)S(1)}, f32[3,8,16,128]{3,2,1,0:T(8,128)S(1)}, f32[16,128]{1,0:T(8,128)S(1)}) custom-call(f32[20,16,128]{2,1,0:T(8,128)S(1)} %collective-permute-done.b_mine, f32[28,16,128]{2,1,0:T(8,128)S(1)} %collective-permute-done.5.b_rest, f32[256,512]{1,0:T(8,128)S(1)} %get-tuple-element.32.base, ...), custom_call_target="tpu_custom_call" | custom-call | tf_op jit(solution)/shard_map/flux/pallas_call | solution.py:384
  22.5 0.8 %collective-permute-start.9 = (f32[16,128]{1,0:T(8,128)S(1)}, f32[16,128]{1,0:T(8,128)S(1)}, u32[]{:S(2)}, u32[]{:S(2)}) collective-permute-start(f32[16,128]{1,0:T(8,128)S(1)} %get-tuple-element.37), channel_id=1, source_target_pairs={{0,16},{8,24},{16,0},{24,8},{1,17},{9,25},{17,1},{25,9},{2,18},{10... | collective-permute-start | bytes 24584 | tf_op jit(solution)/shard_map/ppermute | solution.py:489
  23.2 2.9 %collective-permute-start.8 = (f32[16,128]{1,0:T(8,128)S(1)}, f32[16,128]{1,0:T(8,128)S(1)}, u32[]{:S(2)}, u32[]{:S(2)}) collective-permute-start(f32[16,128]{1,0:T(8,128)S(1)} %get-tuple-element.37), channel_id=1, source_target_pairs={{0,24},{8,16},{16,8},{24,0},{1,25},{9,17},{17,9},{25,1},{2,26},{10... | collective-permute-start | bytes 24584 | tf_op jit(solution)/shard_map/ppermute | solution.py:489
  26.1 0.5 %collective-permute-start.7 = (f32[16,128]{1,0:T(8,128)S(1)}, f32[16,128]{1,0:T(8,128)S(1)}, u32[]{:S(2)}, u32[]{:S(2)}) collective-permute-start(f32[16,128]{1,0:T(8,128)S(1)} %get-tuple-element.37), channel_id=1, source_target_pairs={{0,8},{8,0},{16,24},{24,16},{1,9},{9,1},{17,25},{25,17},{2,10},{10... | collective-permute-start | bytes 24584 | tf_op jit(solution)/shard_map/ppermute | solution.py:489
  26.6 0.5 %collective-permute-done.9 = f32[16,128]{1,0:T(8,128)S(1)} collective-permute-done((f32[16,128]{1,0:T(8,128)S(1)}, f32[16,128]{1,0:T(8,128)S(1)}, u32[]{:S(2)}, u32[]{:S(2)}) %collective-permute-start.9) | collective-permute-done | bytes 8224 | tf_op jit(solution)/shard_map/ppermute | solution.py:489
  27.1 1.6 %collective-permute-done.8 = f32[16,128]{1,0:T(8,128)S(1)} collective-permute-done((f32[16,128]{1,0:T(8,128)S(1)}, f32[16,128]{1,0:T(8,128)S(1)}, u32[]{:S(2)}, u32[]{:S(2)}) %collective-permute-start.8) | collective-permute-done | bytes 8224 | tf_op jit(solution)/shard_map/ppermute | solution.py:489
  28.7 1.1 %collective-permute-done.7 = f32[16,128]{1,0:T(8,128)S(1)} collective-permute-done((f32[16,128]{1,0:T(8,128)S(1)}, f32[16,128]{1,0:T(8,128)S(1)}, u32[]{:S(2)}, u32[]{:S(2)}) %collective-permute-start.7) | collective-permute-done | bytes 8224 | tf_op jit(solution)/shard_map/ppermute | solution.py:489
  29.8 3.6 %collective-permute-done.10 = f32[16,128]{1,0:T(8,128)S(1)} collective-permute-done((f32[16,128]{1,0:T(8,128)S(1)}, f32[16,128]{1,0:T(8,128)S(1)}, u32[]{:S(2)}, u32[]{:S(2)}) %collective-permute-start.10) | collective-permute-done | bytes 8224 | tf_op jit(solution)/shard_map/ppermute | solution.py:405
  33.4 1.0 %finish.1 = (f32[3,8,16,128]{3,2,1,0:T(8,128)}, f32[3,8,16,128]{3,2,1,0:T(8,128)}, f32[3,16]{1,0:T(4,128)}, f32[3,16]{1,0:T(4,128)}) custom-call(f32[16,128]{1,0:T(8,128)S(1)} %add.15.sums, f32[6,8,16,128]{3,2,1,0:T(8,128)S(1)} %get-tuple-element.38.keep, f32[3,8,16,128]{3,2,1,0:T(8,128)S(1)} %collective-permute-done.11.come), custom_call_target="tpu_custom_call" | custom-call | tf_op jit(solution)/shard_map/finish/pallas_call | solution.py:384
  (15 shorter events, 0.1 us)
Async XLA Ops:
  0.6 1.0 %copy-start.2 = (f32[4,8,16,128]{3,2,1,0:T(8,128)S(1)}, f32[4,8,16,128]{3,2,1,0:T(8,128)}, u32[]{:S(2)}) copy-start(f32[4,8,16,128]{3,2,1,0:T(8,128)} %own.1) | copy-start | bytes 786436
  2.0 4.3 %collective-permute-start.3 = (f32[4,16,128]{2,1,0:T(8,128)S(1)}, f32[4,16,128]{2,1,0:T(8,128)S(1)}, u32[]{:S(2)}, u32[]{:S(2)}) collective-permute-start(f32[4,16,128]{2,1,0:T(8,128)S(1)} %get-tuple-element.26), channel_id=1, source_target_pairs={{0,1},{1,0},{2,3},{3,2},{4,5},{5,4},{6,7},{7,6},{8,9},{9,8},{10,11... | collective-permute-start | bytes 98312 | tf_op jit(solution)/shard_map/ppermute | solution.py:405
  2.6 9.9 %collective-permute-start.2 = (f32[20,16,128]{2,1,0:T(8,128)S(1)}, f32[20,16,128]{2,1,0:T(8,128)S(1)}, u32[]{:S(2)}, u32[]{:S(2)}) collective-permute-start(f32[20,16,128]{2,1,0:T(8,128)S(1)} %get-tuple-element.24), channel_id=1, source_target_pairs={{0,1},{1,0},{2,3},{3,2},{4,5},{5,4},{6,7},{7,6},{8,9},{9,8},{10,11... | collective-permute-start | bytes 491528 | tf_op jit(solution)/shard_map/ppermute | solution.py:405
  6.3 6.1 %collective-permute-start.4 = (f32[8,16,128]{2,1,0:T(8,128)S(1)}, f32[8,16,128]{2,1,0:T(8,128)S(1)}, u32[]{:S(2)}, u32[]{:S(2)}) collective-permute-start(f32[8,16,128]{2,1,0:T(8,128)S(1)} %pad_maximum_fusion), channel_id=1, source_target_pairs={{1,25},{0,8},{9,1},{8,16},{17,9},{16,24},{25,17},{24,0},{3,27},{2,... | collective-permute-start | bytes 196616 | tf_op jit(solution)/shard_map/ppermute | solution.py:427
  9.9 6.8 %copy-start = (bf16[256,3072]{1,0:T(8,128)(2,1)S(1)}, bf16[256,3072]{1,0:T(8,128)(2,1)}, u32[]{:S(2)}) copy-start(bf16[256,3072]{1,0:T(8,128)(2,1)} %constant.4.clone.planes.matrices) | copy-start | bytes 4718596
  9.9 6.0 %collective-permute-start.1 = (f32[20,16,128]{2,1,0:T(8,128)S(1)}, f32[20,16,128]{2,1,0:T(8,128)S(1)}, u32[]{:S(2)}, u32[]{:S(2)}) collective-permute-start(f32[20,16,128]{2,1,0:T(8,128)S(1)} %get-tuple-element.28.mine), channel_id=1, source_target_pairs={{0,2},{2,0},{4,6},{6,4},{1,3},{3,1},{5,7},{7,5},{8,10},{10,8},{12,... | collective-permute-start | bytes 491528 | tf_op jit(solution)/shard_map/ppermute | solution.py:408
  9.9 6.8 %collective-permute-start = (f32[20,16,128]{2,1,0:T(8,128)S(1)}, f32[20,16,128]{2,1,0:T(8,128)S(1)}, u32[]{:S(2)}, u32[]{:S(2)}) collective-permute-start(f32[20,16,128]{2,1,0:T(8,128)S(1)} %get-tuple-element.28.mine), channel_id=1, source_target_pairs={{0,0},{2,4},{4,2},{6,6},{1,1},{3,5},{5,3},{7,7},{8,8},{10,12},{12,... | collective-permute-start | bytes 491528 | tf_op jit(solution)/shard_map/ppermute | solution.py:411
  12.5 5.3 %copy-start.1 = (bf16[512,768]{1,0:T(8,128)(2,1)S(1)}, bf16[512,768]{1,0:T(8,128)(2,1)}, u32[]{:S(2)}) copy-start(bf16[512,768]{1,0:T(8,128)(2,1)} %constant.5.clone.spans) | copy-start | bytes 2359300
  12.5 5.3 %collective-permute-start.6 = (f32[28,16,128]{2,1,0:T(8,128)S(1)}, f32[28,16,128]{2,1,0:T(8,128)S(1)}, u32[]{:S(2)}, u32[]{:S(2)}) collective-permute-start(f32[28,16,128]{2,1,0:T(8,128)S(1)} %rest.1), channel_id=1, source_target_pairs={{0,2},{2,0},{4,6},{6,4},{1,3},{3,1},{5,7},{7,5},{8,10},{10,8},{12,... | collective-permute-start | bytes 688136 | tf_op jit(solution)/shard_map/ppermute | solution.py:408
  12.6 7.5 %collective-permute-start.5 = (f32[28,16,128]{2,1,0:T(8,128)S(1)}, f32[28,16,128]{2,1,0:T(8,128)S(1)}, u32[]{:S(2)}, u32[]{:S(2)}) collective-permute-start(f32[28,16,128]{2,1,0:T(8,128)S(1)} %rest.1), channel_id=1, source_target_pairs={{0,0},{2,4},{4,2},{6,6},{1,1},{3,5},{5,3},{7,7},{8,8},{10,12},{12,... | collective-permute-start | bytes 688136 | tf_op jit(solution)/shard_map/ppermute | solution.py:411
  22.5 4.6 %collective-permute-start.9 = (f32[16,128]{1,0:T(8,128)S(1)}, f32[16,128]{1,0:T(8,128)S(1)}, u32[]{:S(2)}, u32[]{:S(2)}) collective-permute-start(f32[16,128]{1,0:T(8,128)S(1)} %get-tuple-element.37), channel_id=1, source_target_pairs={{0,16},{8,24},{16,0},{24,8},{1,17},{9,25},{17,1},{25,9},{2,18},{10... | collective-permute-start | bytes 24584 | tf_op jit(solution)/shard_map/ppermute | solution.py:489
  23.2 5.4 %collective-permute-start.8 = (f32[16,128]{1,0:T(8,128)S(1)}, f32[16,128]{1,0:T(8,128)S(1)}, u32[]{:S(2)}, u32[]{:S(2)}) collective-permute-start(f32[16,128]{1,0:T(8,128)S(1)} %get-tuple-element.37), channel_id=1, source_target_pairs={{0,24},{8,16},{16,8},{24,0},{1,25},{9,17},{17,9},{25,1},{2,26},{10... | collective-permute-start | bytes 24584 | tf_op jit(solution)/shard_map/ppermute | solution.py:489
  26.1 3.7 %collective-permute-start.7 = (f32[16,128]{1,0:T(8,128)S(1)}, f32[16,128]{1,0:T(8,128)S(1)}, u32[]{:S(2)}, u32[]{:S(2)}) collective-permute-start(f32[16,128]{1,0:T(8,128)S(1)} %get-tuple-element.37), channel_id=1, source_target_pairs={{0,8},{8,0},{16,24},{24,16},{1,9},{9,1},{17,25},{25,17},{2,10},{10... | collective-permute-start | bytes 24584 | tf_op jit(solution)/shard_map/ppermute | solution.py:489
  26.6 6.8 %collective-permute-start.11 = (f32[3,8,16,128]{3,2,1,0:T(8,128)S(1)}, f32[3,8,16,128]{3,2,1,0:T(8,128)S(1)}, u32[]{:S(2)}, u32[]{:S(2)}) collective-permute-start(f32[3,8,16,128]{3,2,1,0:T(8,128)S(1)} %get-tuple-element.39), channel_id=1, source_target_pairs={{0,1},{1,0},{2,3},{3,2},{4,5},{5,4},{6,7},{7,6},{8,9},{9,8},{10,11... | collective-permute-start | bytes 589832 | tf_op jit(solution)/shard_map/ppermute | solution.py:405
  29.8 3.7 %collective-permute-start.10 = (f32[16,128]{1,0:T(8,128)S(1)}, f32[16,128]{1,0:T(8,128)S(1)}, u32[]{:S(2)}, u32[]{:S(2)}) collective-permute-start(f32[16,128]{1,0:T(8,128)S(1)} %add_add_fusion), channel_id=1, source_target_pairs={{0,1},{1,0},{2,3},{3,2},{4,5},{5,4},{6,7},{7,6},{8,9},{9,8},{10,11... | collective-permute-start | bytes 24584 | tf_op jit(solution)/shard_map/ppermute | solution.py:405

commit v27 on v21

--- a/solution.py
+++ b/solution.py
@@ -171,20 +171,20 @@
 
 
 def add_products(planes, which, raw, base, parts):
-    near = pl.ds(pl.multiple_of((1 - which) * reach, reach), reach)
-    temperature = raw[3, :, near, :]
+    temperature = raw[3]
     for i in range(3):
-        value = raw[i, :, near, :] * temperature
+        value = raw[i] * temperature
         put_parts(parts, 0, column(i), value.reshape(-1, value.shape[-1]))
     return base + planes_of(planes, 6 + which, parts)
 
 
-def bring(mine, rest, raw, parts, keep=None):
+def bring(mine, rest, raw, parts, keep=None, which=None):
     rows, width = mine.shape[1:]
     for f, layer, value in unpack(mine, rest, lax.axis_index("stream")):
         count = value.shape[0]
         value = value if keep is None else value * keep
-        raw[f, pl.ds(layer, count)] = value
+        near = value if which is None else jnp.where(which == 0, value[:, rows - reach :], value[:, :reach])
+        raw[f, pl.ds(layer, count)] = near
         down = pl.multiple_of(layer * rows, count * rows)
         put_parts(parts, down, column(f), value.reshape(-1, width))
 
@@ -265,7 +265,7 @@
 ):
     both, rows = raw.shape[1:3]
     odd = lax.rem(lax.axis_index("wall"), 2)
-    bring(a_mine, a_rest, raw, parts)
+    bring(a_mine, a_rest, raw, parts, which=1 - odd)
     planes = jnp.where(odd == 1, upper[...], lower[...])
     planes = planes + planes_of(matrices, 1 - odd, parts)
     means = span_pass(spans, planes, both)
@@ -292,7 +292,7 @@
     at_end = (me_w == 0) | (me_w == walls - 1)
     keep_b = jnp.where(at_end, 0.0, 1.0).astype(jnp.float32)
 
-    bring(b_mine, b_rest, raw, parts, keep_b)
+    bring(b_mine, b_rest, raw, parts, keep_b, odd)
 
     planes = base[...] + planes_of(matrices, odd, parts)
     row = lax.rem(lax.broadcasted_iota(jnp.int32, planes.shape, 0), rows)
@@ -447,7 +447,7 @@
     single, brief = jnp.float32, jnp.bfloat16
     block, quarter = (4, both, rows, width), (4, layers, rows, width)
     four, three, seven = (((3 * cells, n * width), brief) for n in (4, 3, 7))
-    few = ((3 * both * reach, 3 * width), brief)
+    few, near = ((3 * both * reach, 3 * width), brief), ((4, both, reach, width), single)
     upper, lower, products = call(
         centre_kernel,
         "centre",
@@ -465,7 +465,7 @@
             (cells, 4 * width), quarter, (4, layers, reach, width), (cells, 7 * width),
             (cells, 3 * width),
         ),
-        [(block, single), four, seven, (block, single), few],
+        [near, four, seven, (block, single), few],
         mib=16,
         hint=2**29,
     )
@@ -475,7 +475,7 @@
         (b_mine, b_rest, base, a_packed, a_slopes, a_second, products, matrices, passes),
         ((6, layers, rows, width), (3, layers, rows, width), (rows, width)),
         [
-            (block, single),
+            near,
             four,
             few,
             (block, single),

time: 32.9 us -> 32.9 us (level)
  no operation moved by 1% of the time
where the time goes in v27:
time: 32.9 us; the launch traced here: 32.7 us
  starting transfers between devices  15.5 us (47%)
  waiting for transfers between devices  8.78 us (27%)
  Pallas kernels  6.73 us (20%)
  local copies, waits for them, and re-layouts  0.95 us (3%)
  between operations  0.76 us (2%)
    pallas_call x6, Pallas kernels, call(): pl.pallas_call(kernel, out_shape=tuple((jax.ShapeDtypeStruct(shape, jnp.f...  6.73 us
    ppermute x2, starting transfers between devices, pair_b(): lax.ppermute(value, 'wall', [(w, min(max((w + 1 ^ 1) - 1, 0), walls - 1))...  5.02 us
    ppermute x3, starting transfers between devices, from_span(): return lax.ppermute(value, 'span', [(p, p ^ step) for p in range(spans)])  3.55 us
    ppermute x3, waiting for transfers between devices, swap(): return lax.ppermute(value, 'stream', [(0, 1), (1, 0)])  3.21 us
    ppermute x3, starting transfers between devices, swap(): return lax.ppermute(value, 'stream', [(0, 1), (1, 0)])  2.84 us
    ppermute x1, starting transfers between devices, shards(): part_strip = lax.ppermute(first, ('span', 'stream'), to_other)  2.45 us
    ppermute x3, waiting for transfers between devices, from_span(): return lax.ppermute(value, 'span', [(p, p ^ step) for p in range(spans)])  1.97 us
    ppermute x2, waiting for transfers between devices, pair_b(): lax.ppermute(value, 'wall', [(w, min(max((w + 1 ^ 1) - 1, 0), walls - 1))...  1.96 us
  transfers between devices with their start and end apart: 12, of which 5 were waited for; matrix products, arithmetic and copies ran while one was open for 0% of the time, Pallas kernels for 9%

profile of v27, /device:TPU:4, one launch (start us, length us, event | category | flops | bytes accessed | tf_op | source)
XLA Modules:
  0.0 32.7 jit_solution(5329581969318292096)
XLA Ops:
  0.6 0.9 %copy-done.2 = f32[4,8,16,128]{3,2,1,0:T(8,128)S(1)} copy-done((f32[4,8,16,128]{3,2,1,0:T(8,128)S(1)}, f32[4,8,16,128]{3,2,1,0:T(8,128)}, u32[]{:S(2)}) %copy-start.2) | copy-done | bytes 262168
  1.6 0.4 %pack.1 = (f32[20,16,128]{2,1,0:T(8,128)S(1)}, f32[20,16,128]{2,1,0:T(8,128)S(1)}, f32[4,16,128]{2,1,0:T(8,128)S(1)}, f32[4,16,128]{2,1,0:T(8,128)S(1)}) custom-call(f32[4,8,16,128]{3,2,1,0:T(8,128)S(1)} %copy-done.2), custom_call_target="tpu_custom_call" | custom-call | tf_op jit(solution)/shard_map/pack/pallas_call | solution.py:385
  2.0 1.6 %collective-permute-start.2 = (f32[20,16,128]{2,1,0:T(8,128)S(1)}, f32[20,16,128]{2,1,0:T(8,128)S(1)}, u32[]{:S(2)}, u32[]{:S(2)}) collective-permute-start(f32[20,16,128]{2,1,0:T(8,128)S(1)} %get-tuple-element.24), channel_id=1, source_target_pairs={{0,1},{1,0},{2,3},{3,2},{4,5},{5,4},{6,7},{7,6},{8,9},{9,8},{10,11... | collective-permute-start | bytes 491528 | tf_op jit(solution)/shard_map/ppermute | solution.py:406
  3.5 1.6 %collective-permute-start.3 = (f32[4,16,128]{2,1,0:T(8,128)S(1)}, f32[4,16,128]{2,1,0:T(8,128)S(1)}, u32[]{:S(2)}, u32[]{:S(2)}) collective-permute-start(f32[4,16,128]{2,1,0:T(8,128)S(1)} %get-tuple-element.25), channel_id=1, source_target_pairs={{1,25},{0,8},{9,1},{8,16},{17,9},{16,24},{25,17},{24,0},{3,27},{2,... | collective-permute-start | bytes 98312 | tf_op jit(solution)/shard_map/ppermute | solution.py:430
  5.1 2.4 %collective-permute-start.4 = (f32[4,16,128]{2,1,0:T(8,128)S(1)}, f32[4,16,128]{2,1,0:T(8,128)S(1)}, u32[]{:S(2)}, u32[]{:S(2)}) collective-permute-start(f32[4,16,128]{2,1,0:T(8,128)S(1)} %get-tuple-element.26), channel_id=1, source_target_pairs={{0,25},{1,8},{8,1},{9,16},{16,9},{17,24},{24,17},{25,0},{2,27},{3,... | collective-permute-start | bytes 98312 | tf_op jit(solution)/shard_map/ppermute | solution.py:429
  7.5 0.0 collective-permute-start.1
  7.5 2.5 %collective-permute-start = (f32[20,16,128]{2,1,0:T(8,128)S(1)}, f32[20,16,128]{2,1,0:T(8,128)S(1)}, u32[]{:S(2)}, u32[]{:S(2)}) collective-permute-start(f32[20,16,128]{2,1,0:T(8,128)S(1)} %get-tuple-element.28.mine), channel_id=1, source_target_pairs={{0,0},{2,4},{4,2},{6,6},{1,1},{3,5},{5,3},{7,7},{8,8},{10,12},{12,... | collective-permute-start | bytes 491528 | tf_op jit(solution)/shard_map/ppermute | solution.py:412
  10.1 1.6 %collective-permute-done.4.part_strip = f32[4,16,128]{2,1,0:T(8,128)S(1)} collective-permute-done((f32[4,16,128]{2,1,0:T(8,128)S(1)}, f32[4,16,128]{2,1,0:T(8,128)S(1)}, u32[]{:S(2)}, u32[]{:S(2)}) %collective-permute-start.4) | collective-permute-done | bytes 32800 | tf_op jit(solution)/shard_map/ppermute | solution.py:429
  11.7 0.0 copy-start.1
  11.7 0.1 collective-permute-start.6
  11.8 2.5 %collective-permute-start.5 = (f32[28,16,128]{2,1,0:T(8,128)S(1)}, f32[28,16,128]{2,1,0:T(8,128)S(1)}, u32[]{:S(2)}, u32[]{:S(2)}) collective-permute-start(f32[28,16,128]{2,1,0:T(8,128)S(1)} %rest.1), channel_id=1, source_target_pairs={{0,0},{2,4},{4,2},{6,6},{1,1},{3,5},{5,3},{7,7},{8,8},{10,12},{12,... | collective-permute-start | bytes 688136 | tf_op jit(solution)/shard_map/ppermute | solution.py:412
  14.4 1.1 %centre.1 = (f32[256,512]{1,0:T(8,128)S(1)}, f32[256,512]{1,0:T(8,128)S(1)}, f32[256,384]{1,0:T(8,128)S(1)}) custom-call(f32[20,16,128]{2,1,0:T(8,128)S(1)} %get-tuple-element.28.mine, f32[28,16,128]{2,1,0:T(8,128)S(1)} %rest.1, bf16[256,3072]{1,0:T(8,128)(2,1)S(1)} %copy-done), custom_call_target="tpu_custom_call" | custom-call | flops 2147483648 | tf_op jit(solution)/shard_map/centre/pallas_call | solution.py:385
  15.5 1.8 %mate.1 = (f32[256,512]{1,0:T(8,128)S(1)}, f32[4,8,16,128]{3,2,1,0:T(8,128)S(1)}, f32[4,8,8,128]{3,2,1,0:T(8,128)S(1)}, f32[256,896]{1,0:T(8,128)S(1)}, f32[256,384]{1,0:T(8,128)S(1)}) custom-call(f32[20,16,128]{2,1,0:T(8,128)S(1)} %collective-permute-done.1.a_mine, f32[28,16,128]{2,1,0:T(8,128)S(1)} %collective-permute-done.6.a_rest, ...), custom_call_target="tpu_custom_call" | custom-call | flops 536870912 | tf_op jit(solution)/shard_map/mate/pallas_call | solution.py:385
  17.3 2.0 %collective-permute-done.5.b_rest = f32[28,16,128]{2,1,0:T(8,128)S(1)} collective-permute-done((f32[28,16,128]{2,1,0:T(8,128)S(1)}, f32[28,16,128]{2,1,0:T(8,128)S(1)}, u32[]{:S(2)}, u32[]{:S(2)}) %collective-permute-start.5) | collective-permute-done | bytes 229408 | tf_op jit(solution)/shard_map/ppermute | solution.py:412
  19.3 2.4 %flux.1 = (f32[6,8,16,128]{3,2,1,0:T(8,128)S(1)}, f32[3,8,16,128]{3,2,1,0:T(8,128)S(1)}, f32[16,128]{1,0:T(8,128)S(1)}) custom-call(f32[20,16,128]{2,1,0:T(8,128)S(1)} %collective-permute-done.b_mine, f32[28,16,128]{2,1,0:T(8,128)S(1)} %collective-permute-done.5.b_rest, f32[256,512]{1,0:T(8,128)S(1)} %get-tuple-element.32.base, ...), custom_call_target="tpu_custom_call" | custom-call | tf_op jit(solution)/shard_map/flux/pallas_call | solution.py:385
  21.7 0.9 %collective-permute-start.9 = (f32[16,128]{1,0:T(8,128)S(1)}, f32[16,128]{1,0:T(8,128)S(1)}, u32[]{:S(2)}, u32[]{:S(2)}) collective-permute-start(f32[16,128]{1,0:T(8,128)S(1)} %get-tuple-element.37), channel_id=1, source_target_pairs={{0,16},{8,24},{16,0},{24,8},{1,17},{9,25},{17,1},{25,9},{2,18},{10... | collective-permute-start | bytes 24584 | tf_op jit(solution)/shard_map/ppermute | solution.py:492
  22.6 1.5 %collective-permute-start.8 = (f32[16,128]{1,0:T(8,128)S(1)}, f32[16,128]{1,0:T(8,128)S(1)}, u32[]{:S(2)}, u32[]{:S(2)}) collective-permute-start(f32[16,128]{1,0:T(8,128)S(1)} %get-tuple-element.37), channel_id=1, source_target_pairs={{0,24},{8,16},{16,8},{24,0},{1,25},{9,17},{17,9},{25,1},{2,26},{10... | collective-permute-start | bytes 24584 | tf_op jit(solution)/shard_map/ppermute | solution.py:492
  24.1 1.2 %collective-permute-start.7 = (f32[16,128]{1,0:T(8,128)S(1)}, f32[16,128]{1,0:T(8,128)S(1)}, u32[]{:S(2)}, u32[]{:S(2)}) collective-permute-start(f32[16,128]{1,0:T(8,128)S(1)} %get-tuple-element.37), channel_id=1, source_target_pairs={{0,8},{8,0},{16,24},{24,16},{1,9},{9,1},{17,25},{25,17},{2,10},{10... | collective-permute-start | bytes 24584 | tf_op jit(solution)/shard_map/ppermute | solution.py:492
  25.3 0.8 %collective-permute-start.11 = (f32[3,8,16,128]{3,2,1,0:T(8,128)S(1)}, f32[3,8,16,128]{3,2,1,0:T(8,128)S(1)}, u32[]{:S(2)}, u32[]{:S(2)}) collective-permute-start(f32[3,8,16,128]{3,2,1,0:T(8,128)S(1)} %get-tuple-element.39), channel_id=1, source_target_pairs={{0,1},{1,0},{2,3},{3,2},{4,5},{5,4},{6,7},{7,6},{8,9},{9,8},{10,11... | collective-permute-start | bytes 589832 | tf_op jit(solution)/shard_map/ppermute | solution.py:406
  26.0 0.3 collective-permute-done.9
  26.3 1.7 %collective-permute-done.8 = f32[16,128]{1,0:T(8,128)S(1)} collective-permute-done((f32[16,128]{1,0:T(8,128)S(1)}, f32[16,128]{1,0:T(8,128)S(1)}, u32[]{:S(2)}, u32[]{:S(2)}) %collective-permute-start.8) | collective-permute-done | bytes 8224 | tf_op jit(solution)/shard_map/ppermute | solution.py:492
  28.0 0.5 %collective-permute-start.10 = (f32[16,128]{1,0:T(8,128)S(1)}, f32[16,128]{1,0:T(8,128)S(1)}, u32[]{:S(2)}, u32[]{:S(2)}) collective-permute-start(f32[16,128]{1,0:T(8,128)S(1)} %add_add_fusion), channel_id=1, source_target_pairs={{0,1},{1,0},{2,3},{3,2},{4,5},{5,4},{6,7},{7,6},{8,9},{9,8},{10,11... | collective-permute-start | bytes 24584 | tf_op jit(solution)/shard_map/ppermute | solution.py:406
  28.5 3.2 %collective-permute-done.10 = f32[16,128]{1,0:T(8,128)S(1)} collective-permute-done((f32[16,128]{1,0:T(8,128)S(1)}, f32[16,128]{1,0:T(8,128)S(1)}, u32[]{:S(2)}, u32[]{:S(2)}) %collective-permute-start.10) | collective-permute-done | bytes 8224 | tf_op jit(solution)/shard_map/ppermute | solution.py:406
  31.7 1.0 %finish.1 = (f32[3,8,16,128]{3,2,1,0:T(8,128)}, f32[3,8,16,128]{3,2,1,0:T(8,128)}, f32[3,16]{1,0:T(4,128)}, f32[3,16]{1,0:T(4,128)}) custom-call(f32[16,128]{1,0:T(8,128)S(1)} %add.15.sums, f32[6,8,16,128]{3,2,1,0:T(8,128)S(1)} %get-tuple-element.38.keep, f32[3,8,16,128]{3,2,1,0:T(8,128)S(1)} %collective-permute-done.11.come), custom_call_target="tpu_custom_call" | custom-call | tf_op jit(solution)/shard_map/finish/pallas_call | solution.py:385
  (14 shorter events, 0.1 us)
Async XLA Ops:
  0.6 1.0 %copy-start.2 = (f32[4,8,16,128]{3,2,1,0:T(8,128)S(1)}, f32[4,8,16,128]{3,2,1,0:T(8,128)}, u32[]{:S(2)}) copy-start(f32[4,8,16,128]{3,2,1,0:T(8,128)} %own.1) | copy-start | bytes 786436
  2.0 9.7 %collective-permute-start.2 = (f32[20,16,128]{2,1,0:T(8,128)S(1)}, f32[20,16,128]{2,1,0:T(8,128)S(1)}, u32[]{:S(2)}, u32[]{:S(2)}) collective-permute-start(f32[20,16,128]{2,1,0:T(8,128)S(1)} %get-tuple-element.24), channel_id=1, source_target_pairs={{0,1},{1,0},{2,3},{3,2},{4,5},{5,4},{6,7},{7,6},{8,9},{9,8},{10,11... | collective-permute-start | bytes 491528 | tf_op jit(solution)/shard_map/ppermute | solution.py:406
  3.5 6.6 %collective-permute-start.3 = (f32[4,16,128]{2,1,0:T(8,128)S(1)}, f32[4,16,128]{2,1,0:T(8,128)S(1)}, u32[]{:S(2)}, u32[]{:S(2)}) collective-permute-start(f32[4,16,128]{2,1,0:T(8,128)S(1)} %get-tuple-element.25), channel_id=1, source_target_pairs={{1,25},{0,8},{9,1},{8,16},{17,9},{16,24},{25,17},{24,0},{3,27},{2,... | collective-permute-start | bytes 98312 | tf_op jit(solution)/shard_map/ppermute | solution.py:430
  5.1 6.6 %collective-permute-start.4 = (f32[4,16,128]{2,1,0:T(8,128)S(1)}, f32[4,16,128]{2,1,0:T(8,128)S(1)}, u32[]{:S(2)}, u32[]{:S(2)}) collective-permute-start(f32[4,16,128]{2,1,0:T(8,128)S(1)} %get-tuple-element.26), channel_id=1, source_target_pairs={{0,25},{1,8},{8,1},{9,16},{16,9},{17,24},{24,17},{25,0},{2,27},{3,... | collective-permute-start | bytes 98312 | tf_op jit(solution)/shard_map/ppermute | solution.py:429
  7.5 6.8 %copy-start = (bf16[256,3072]{1,0:T(8,128)(2,1)S(1)}, bf16[256,3072]{1,0:T(8,128)(2,1)}, u32[]{:S(2)}) copy-start(bf16[256,3072]{1,0:T(8,128)(2,1)} %constant.4.clone.planes.matrices) | copy-start | bytes 4718596
  7.5 6.8 %collective-permute-start.1 = (f32[20,16,128]{2,1,0:T(8,128)S(1)}, f32[20,16,128]{2,1,0:T(8,128)S(1)}, u32[]{:S(2)}, u32[]{:S(2)}) collective-permute-start(f32[20,16,128]{2,1,0:T(8,128)S(1)} %get-tuple-element.28.mine), channel_id=1, source_target_pairs={{0,2},{2,0},{4,6},{6,4},{1,3},{3,1},{5,7},{7,5},{8,10},{10,8},{12,... | collective-permute-start | bytes 491528 | tf_op jit(solution)/shard_map/ppermute | solution.py:409
  7.5 6.8 %collective-permute-start = (f32[20,16,128]{2,1,0:T(8,128)S(1)}, f32[20,16,128]{2,1,0:T(8,128)S(1)}, u32[]{:S(2)}, u32[]{:S(2)}) collective-permute-start(f32[20,16,128]{2,1,0:T(8,128)S(1)} %get-tuple-element.28.mine), channel_id=1, source_target_pairs={{0,0},{2,4},{4,2},{6,6},{1,1},{3,5},{5,3},{7,7},{8,8},{10,12},{12,... | collective-permute-start | bytes 491528 | tf_op jit(solution)/shard_map/ppermute | solution.py:412
  11.7 3.7 %copy-start.1 = (bf16[512,768]{1,0:T(8,128)(2,1)S(1)}, bf16[512,768]{1,0:T(8,128)(2,1)}, u32[]{:S(2)}) copy-start(bf16[512,768]{1,0:T(8,128)(2,1)} %constant.5.clone.spans) | copy-start | bytes 2359300
  11.7 3.7 %collective-permute-start.6 = (f32[28,16,128]{2,1,0:T(8,128)S(1)}, f32[28,16,128]{2,1,0:T(8,128)S(1)}, u32[]{:S(2)}, u32[]{:S(2)}) collective-permute-start(f32[28,16,128]{2,1,0:T(8,128)S(1)} %rest.1), channel_id=1, source_target_pairs={{0,2},{2,0},{4,6},{6,4},{1,3},{3,1},{5,7},{7,5},{8,10},{10,8},{12,... | collective-permute-start | bytes 688136 | tf_op jit(solution)/shard_map/ppermute | solution.py:409
  11.8 7.5 %collective-permute-start.5 = (f32[28,16,128]{2,1,0:T(8,128)S(1)}, f32[28,16,128]{2,1,0:T(8,128)S(1)}, u32[]{:S(2)}, u32[]{:S(2)}) collective-permute-start(f32[28,16,128]{2,1,0:T(8,128)S(1)} %rest.1), channel_id=1, source_target_pairs={{0,0},{2,4},{4,2},{6,6},{1,1},{3,5},{5,3},{7,7},{8,8},{10,12},{12,... | collective-permute-start | bytes 688136 | tf_op jit(solution)/shard_map/ppermute | solution.py:412
  21.7 4.6 %collective-permute-start.9 = (f32[16,128]{1,0:T(8,128)S(1)}, f32[16,128]{1,0:T(8,128)S(1)}, u32[]{:S(2)}, u32[]{:S(2)}) collective-permute-start(f32[16,128]{1,0:T(8,128)S(1)} %get-tuple-element.37), channel_id=1, source_target_pairs={{0,16},{8,24},{16,0},{24,8},{1,17},{9,25},{17,1},{25,9},{2,18},{10... | collective-permute-start | bytes 24584 | tf_op jit(solution)/shard_map/ppermute | solution.py:492
  22.6 5.4 %collective-permute-start.8 = (f32[16,128]{1,0:T(8,128)S(1)}, f32[16,128]{1,0:T(8,128)S(1)}, u32[]{:S(2)}, u32[]{:S(2)}) collective-permute-start(f32[16,128]{1,0:T(8,128)S(1)} %get-tuple-element.37), channel_id=1, source_target_pairs={{0,24},{8,16},{16,8},{24,0},{1,25},{9,17},{17,9},{25,1},{2,26},{10... | collective-permute-start | bytes 24584 | tf_op jit(solution)/shard_map/ppermute | solution.py:492
  24.1 3.9 %collective-permute-start.7 = (f32[16,128]{1,0:T(8,128)S(1)}, f32[16,128]{1,0:T(8,128)S(1)}, u32[]{:S(2)}, u32[]{:S(2)}) collective-permute-start(f32[16,128]{1,0:T(8,128)S(1)} %get-tuple-element.37), channel_id=1, source_target_pairs={{0,8},{8,0},{16,24},{24,16},{1,9},{9,1},{17,25},{25,17},{2,10},{10... | collective-permute-start | bytes 24584 | tf_op jit(solution)/shard_map/ppermute | solution.py:492
  25.3 6.5 %collective-permute-start.11 = (f32[3,8,16,128]{3,2,1,0:T(8,128)S(1)}, f32[3,8,16,128]{3,2,1,0:T(8,128)S(1)}, u32[]{:S(2)}, u32[]{:S(2)}) collective-permute-start(f32[3,8,16,128]{3,2,1,0:T(8,128)S(1)} %get-tuple-element.39), channel_id=1, source_target_pairs={{0,1},{1,0},{2,3},{3,2},{4,5},{5,4},{6,7},{7,6},{8,9},{9,8},{10,11... | collective-permute-start | bytes 589832 | tf_op jit(solution)/shard_map/ppermute | solution.py:406
  28.0 3.7 %collective-permute-start.10 = (f32[16,128]{1,0:T(8,128)S(1)}, f32[16,128]{1,0:T(8,128)S(1)}, u32[]{:S(2)}, u32[]{:S(2)}) collective-permute-start(f32[16,128]{1,0:T(8,128)S(1)} %add_add_fusion), channel_id=1, source_target_pairs={{0,1},{1,0},{2,3},{3,2},{4,5},{5,4},{6,7},{7,6},{8,9},{9,8},{10,11... | collective-permute-start | bytes 24584 | tf_op jit(solution)/shard_map/ppermute | solution.py:406
